TPU v7x, 512 devices: a whole 4x4x16 slice. The times are simulated.
512 devices in a mesh: aux: 8 (over y, core), orb: 64 (over z, x).
Axes of the slice: x: 4, y: 4, z: 16, core: 2. Of those that a mesh axis runs over, the one named last changes fastest.
Arguments:
- occupied: bfloat16 [8192, 2048], P('orb'), may hold values from -1.25 to 1.25
- integrals: bfloat16 [8, 64, 15, 128, 128], P('aux', 'orb'), may hold values from -0.1875 to 0.1875
- pair_mask: int32 [64, 15], P('orb'), may hold values from 0 to 1, as said below
Outputs:
- exchange: float32 [64, 15, 128, 128], P('orb', None, 'aux')
Inputs may be any that keep to these rules, and one draw needn't show every extreme that they name: The list is symmetric: pair_mask[a, s] = pair_mask[a + s - 7, 14 - s]; every block is paired with itself (slot 7); slots whose partner lies outside the grid are 0; the number of kept pairs differs from block to block.
All inputs are finite; a program needn't handle non-finite values.
Results may differ from a plain program's by a relative error of at most 0.0011.
Values may be sent and summed in bfloat16 or wider, within the bound.
No kernel may reach another device: no remote copies, remote signals or barrier semaphores. Data moves between devices by JAX's collectives and lax.ppermute only.
A program may use at most 64 MiB of HBM per device.

v0:
```python
import jax
import jax.numpy as jnp
from jax import lax
from jax.sharding import PartitionSpec as P

REACH = 7


def shifted(x, axis, by):
    devices = lax.axis_size(axis)
    pairs = [(i, i + by) for i in range(devices) if 0 <= i + by < devices]
    return lax.ppermute(x, axis, pairs)


def neighbours(block):
    pieces = [block[None]]
    for offset in range(1, REACH + 1):
        pieces.append(shifted(block, "orb", -offset)[None])
    below = [shifted(block, "orb", offset)[None] for offset in range(REACH, 0, -1)]
    pieces = below + pieces
    return jnp.concatenate(pieces, 0)


def per_device(occupied, integrals, pair_mask):
    mask_row = pair_mask[0]
    own_tiles = integrals[:, 0]
    near_orbitals = neighbours(occupied)
    masked = own_tiles * mask_row.astype(jnp.bfloat16)[None, :, None, None]
    halfway = jnp.einsum("pomn,onk->pmk", masked, near_orbitals, preferred_element_type=jnp.float32)
    halfway = halfway.astype(jnp.bfloat16)
    near_half = neighbours(halfway)
    partial_tiles = jnp.einsum(
        "pmk,opnk->omn", halfway, near_half, preferred_element_type=jnp.float32
    )
    partial_tiles = partial_tiles * mask_row.astype(jnp.float32)[:, None, None]
    summed = lax.psum_scatter(partial_tiles, "aux", scatter_dimension=1, tiled=True)
    return summed[None]


def solution(mesh):
    placed = (P("orb", None), P("aux", "orb", None, None, None), P("orb", None))
    return jax.shard_map(
        per_device,
        mesh=mesh,
        in_specs=placed,
        out_specs=P("orb", None, "aux", None),
        check_vma=False,
    )
```

profile of v0, /device:TPU:6, one launch (start us, length us, event | category | flops | bytes accessed | tf_op | source)
XLA Modules:
  0.0 450.7 jit_solution(6028087672964546524)
XLA Ops:
  6.5 5.6 %collective-permute-start = (bf16[128,2048]{1,0:T(8,128)(2,1)}, bf16[128,2048]{1,0:T(8,128)(2,1)S(1)}, u32[]{:S(2)}, u32[]{:S(2)}) collective-permute-start(bf16[128,2048]{1,0:T(8,128)(2,1)} %param.3), channel_id=1, source_target_pairs={{0,7},{1,8},{2,9},{3,10},{4,11},{5,12},{6,13},{7,14},{8,15},{9,16}... | collective-permute-start | bytes 1572872 | tf_op jit(solution)/shard_map/ppermute | solution.py:12
  12.1 6.9 %collective-permute-start.1 = (bf16[128,2048]{1,0:T(8,128)(2,1)}, bf16[128,2048]{1,0:T(8,128)(2,1)S(1)}, u32[]{:S(2)}, u32[]{:S(2)}) collective-permute-start(bf16[128,2048]{1,0:T(8,128)(2,1)} %param.3), channel_id=1, source_target_pairs={{0,6},{1,7},{2,8},{3,9},{4,10},{5,11},{6,12},{7,13},{8,14},{9,15},... | collective-permute-start | bytes 1572872 | tf_op jit(solution)/shard_map/ppermute | solution.py:12
  19.1 5.4 %collective-permute-start.2 = (bf16[128,2048]{1,0:T(8,128)(2,1)}, bf16[128,2048]{1,0:T(8,128)(2,1)S(1)}, u32[]{:S(2)}, u32[]{:S(2)}) collective-permute-start(bf16[128,2048]{1,0:T(8,128)(2,1)} %param.3), channel_id=1, source_target_pairs={{0,5},{1,6},{2,7},{3,8},{4,9},{5,10},{6,11},{7,12},{8,13},{9,14},{... | collective-permute-start | bytes 1572872 | tf_op jit(solution)/shard_map/ppermute | solution.py:12
  24.5 3.8 collective-permute-start.3
  28.3 3.2 collective-permute-start.4
  32.2 6.7 %collective-permute-start.5 = (bf16[128,2048]{1,0:T(8,128)(2,1)}, bf16[128,2048]{1,0:T(8,128)(2,1)S(1)}, u32[]{:S(2)}, u32[]{:S(2)}) collective-permute-start(bf16[128,2048]{1,0:T(8,128)(2,1)} %param.3), channel_id=1, source_target_pairs={{0,2},{1,3},{2,4},{3,5},{4,6},{5,7},{6,8},{7,9},{8,10},{9,11},{10,... | collective-permute-start | bytes 1572872 | tf_op jit(solution)/shard_map/ppermute | solution.py:12
  38.9 15.2 %collective-permute-start.6 = (bf16[128,2048]{1,0:T(8,128)(2,1)}, bf16[128,2048]{1,0:T(8,128)(2,1)S(1)}, u32[]{:S(2)}, u32[]{:S(2)}) collective-permute-start(bf16[128,2048]{1,0:T(8,128)(2,1)} %param.3), channel_id=1, source_target_pairs={{0,1},{1,2},{2,3},{3,4},{4,5},{5,6},{6,7},{7,8},{8,9},{9,10},{10,1... | collective-permute-start | bytes 1572872 | tf_op jit(solution)/shard_map/ppermute | solution.py:12
  54.2 1.9 collective-permute-start.7
  56.2 2.3 collective-permute-done.3
  58.5 3.8 collective-permute-start.8
  62.3 7.4 %collective-permute-done.4 = bf16[128,2048]{1,0:T(8,128)(2,1)S(1)} collective-permute-done((bf16[128,2048]{1,0:T(8,128)(2,1)}, bf16[128,2048]{1,0:T(8,128)(2,1)S(1)}, u32[]{:S(2)}, u32[]{:S(2)}) %collective-permute-start.4) | collective-permute-done | bytes 524320 | tf_op jit(solution)/shard_map/ppermute | solution.py:12
  71.7 9.3 %collective-permute-done.5 = bf16[128,2048]{1,0:T(8,128)(2,1)S(1)} collective-permute-done((bf16[128,2048]{1,0:T(8,128)(2,1)}, bf16[128,2048]{1,0:T(8,128)(2,1)S(1)}, u32[]{:S(2)}, u32[]{:S(2)}) %collective-permute-start.5) | collective-permute-done | bytes 524320 | tf_op jit(solution)/shard_map/ppermute | solution.py:12
  82.3 8.8 %collective-permute-done.6 = bf16[128,2048]{1,0:T(8,128)(2,1)S(1)} collective-permute-done((bf16[128,2048]{1,0:T(8,128)(2,1)}, bf16[128,2048]{1,0:T(8,128)(2,1)S(1)}, u32[]{:S(2)}, u32[]{:S(2)}) %collective-permute-start.6) | collective-permute-done | bytes 524320 | tf_op jit(solution)/shard_map/ppermute | solution.py:12
  96.2 10.6 %collective-permute-done.9 = bf16[128,2048]{1,0:T(8,128)(2,1)S(1)} collective-permute-done((bf16[128,2048]{1,0:T(8,128)(2,1)}, bf16[128,2048]{1,0:T(8,128)(2,1)S(1)}, u32[]{:S(2)}, u32[]{:S(2)}) %collective-permute-start.9) | collective-permute-done | bytes 524320 | tf_op jit(solution)/shard_map/ppermute | solution.py:12
  106.8 22.4 %collective-permute-done.10 = bf16[128,2048]{1,0:T(8,128)(2,1)S(1)} collective-permute-done((bf16[128,2048]{1,0:T(8,128)(2,1)}, bf16[128,2048]{1,0:T(8,128)(2,1)S(1)}, u32[]{:S(2)}, u32[]{:S(2)}) %collective-permute-start.10) | collective-permute-done | bytes 524320 | tf_op jit(solution)/shard_map/ppermute | solution.py:12
  129.3 50.7 %collective-permute-done.11 = bf16[128,2048]{1,0:T(8,128)(2,1)S(1)} collective-permute-done((bf16[128,2048]{1,0:T(8,128)(2,1)}, bf16[128,2048]{1,0:T(8,128)(2,1)S(1)}, u32[]{:S(2)}, u32[]{:S(2)}) %collective-permute-start.11) | collective-permute-done | bytes 524320 | tf_op jit(solution)/shard_map/ppermute | solution.py:12
  181.5 21.0 %collective-permute-start.14 = (bf16[1,128,2048]{2,1,0:T(8,128)(2,1)S(1)}, bf16[1,128,2048]{2,1,0:T(8,128)(2,1)S(1)}, u32[]{:S(2)}, u32[]{:S(2)}) collective-permute-start(bf16[1,128,2048]{2,1,0:T(8,128)(2,1)S(1)} %bitcast.86), channel_id=1, source_target_pairs={{0,7},{1,8},{2,9},{3,10},{4,11},{5,12},{6,13},{7,14},{8,15},{9,16}... | collective-permute-start | bytes 1572872 | tf_op jit(solution)/shard_map/ppermute | solution.py:12
  202.5 13.1 %collective-permute-start.15 = (bf16[1,128,2048]{2,1,0:T(8,128)(2,1)S(1)}, bf16[1,128,2048]{2,1,0:T(8,128)(2,1)S(1)}, u32[]{:S(2)}, u32[]{:S(2)}) collective-permute-start(bf16[1,128,2048]{2,1,0:T(8,128)(2,1)S(1)} %bitcast.87), channel_id=1, source_target_pairs={{0,6},{1,7},{2,8},{3,9},{4,10},{5,11},{6,12},{7,13},{8,14},{9,15},... | collective-permute-start | bytes 1572872 | tf_op jit(solution)/shard_map/ppermute | solution.py:12
  216.9 16.4 %collective-permute-start.17 = (bf16[1,128,2048]{2,1,0:T(8,128)(2,1)S(1)}, bf16[1,128,2048]{2,1,0:T(8,128)(2,1)S(1)}, u32[]{:S(2)}, u32[]{:S(2)}) collective-permute-start(bf16[1,128,2048]{2,1,0:T(8,128)(2,1)S(1)} %bitcast.89), channel_id=1, source_target_pairs={{0,4},{1,5},{2,6},{3,7},{4,8},{5,9},{6,10},{7,11},{8,12},{9,13},{1... | collective-permute-start | bytes 1572872 | tf_op jit(solution)/shard_map/ppermute | solution.py:12
  235.2 3.3 collective-permute-start.19
  238.7 3.1 collective-permute-start.20
  241.8 11.6 %collective-permute-done.16 = bf16[1,128,2048]{2,1,0:T(8,128)(2,1)S(1)} collective-permute-done((bf16[1,128,2048]{2,1,0:T(8,128)(2,1)S(1)}, bf16[1,128,2048]{2,1,0:T(8,128)(2,1)S(1)}, u32[]{:S(2)}, u32[]{:S(2)}) %collective-permute-start.16) | collective-permute-done | bytes 524320 | tf_op jit(solution)/shard_map/ppermute | solution.py:12
  253.4 6.9 %collective-permute-start.21 = (bf16[1,128,2048]{2,1,0:T(8,128)(2,1)S(1)}, bf16[1,128,2048]{2,1,0:T(8,128)(2,1)S(1)}, u32[]{:S(2)}, u32[]{:S(2)}) collective-permute-start(bf16[1,128,2048]{2,1,0:T(8,128)(2,1)S(1)} %bitcast.93), channel_id=1, source_target_pairs={{1,0},{2,1},{3,2},{4,3},{5,4},{6,5},{7,6},{8,7},{9,8},{10,9},{11,1... | collective-permute-start | bytes 1572872 | tf_op jit(solution)/shard_map/ppermute | solution.py:12
  260.4 4.2 collective-permute-done.17
  266.6 15.8 %collective-permute-done.18 = bf16[1,128,2048]{2,1,0:T(8,128)(2,1)S(1)} collective-permute-done((bf16[1,128,2048]{2,1,0:T(8,128)(2,1)S(1)}, bf16[1,128,2048]{2,1,0:T(8,128)(2,1)S(1)}, u32[]{:S(2)}, u32[]{:S(2)}) %collective-permute-start.18) | collective-permute-done | bytes 524320 | tf_op jit(solution)/shard_map/ppermute | solution.py:12
  284.4 6.3 %collective-permute-done.19 = bf16[1,128,2048]{2,1,0:T(8,128)(2,1)S(1)} collective-permute-done((bf16[1,128,2048]{2,1,0:T(8,128)(2,1)S(1)}, bf16[1,128,2048]{2,1,0:T(8,128)(2,1)S(1)}, u32[]{:S(2)}, u32[]{:S(2)}) %collective-permute-start.19) | collective-permute-done | bytes 524320 | tf_op jit(solution)/shard_map/ppermute | solution.py:12
  292.0 11.7 %collective-permute-done.20 = bf16[1,128,2048]{2,1,0:T(8,128)(2,1)S(1)} collective-permute-done((bf16[1,128,2048]{2,1,0:T(8,128)(2,1)S(1)}, bf16[1,128,2048]{2,1,0:T(8,128)(2,1)S(1)}, u32[]{:S(2)}, u32[]{:S(2)}) %collective-permute-start.20) | collective-permute-done | bytes 524320 | tf_op jit(solution)/shard_map/ppermute | solution.py:12
  307.8 8.9 %collective-permute-done.24 = bf16[1,128,2048]{2,1,0:T(8,128)(2,1)S(1)} collective-permute-done((bf16[1,128,2048]{2,1,0:T(8,128)(2,1)S(1)}, bf16[1,128,2048]{2,1,0:T(8,128)(2,1)S(1)}, u32[]{:S(2)}, u32[]{:S(2)}) %collective-permute-start.24) | collective-permute-done | bytes 524320 | tf_op jit(solution)/shard_map/ppermute | solution.py:12
  316.8 25.4 %collective-permute-done.25 = bf16[1,128,2048]{2,1,0:T(8,128)(2,1)S(1)} collective-permute-done((bf16[1,128,2048]{2,1,0:T(8,128)(2,1)S(1)}, bf16[1,128,2048]{2,1,0:T(8,128)(2,1)S(1)}, u32[]{:S(2)}, u32[]{:S(2)}) %collective-permute-start.25) | collective-permute-done | bytes 524320 | tf_op jit(solution)/shard_map/ppermute | solution.py:12
  342.3 22.0 %collective-permute-done.26 = bf16[1,128,2048]{2,1,0:T(8,128)(2,1)S(1)} collective-permute-done((bf16[1,128,2048]{2,1,0:T(8,128)(2,1)S(1)}, bf16[1,128,2048]{2,1,0:T(8,128)(2,1)S(1)}, u32[]{:S(2)}, u32[]{:S(2)}) %collective-permute-start.26) | collective-permute-done | bytes 524320 | tf_op jit(solution)/shard_map/ppermute | solution.py:12
  364.4 2.3 fusion.6
  368.1 74.2 %reduce-scatter.2.cloned.1.call-done = f32[15,16,128]{2,0,1:T(8,128)} async-done(((f32[15,128,128]{2,0,1:T(8,128)}), f32[15,16,128]{2,0,1:T(8,128)}) %reduce-scatter.2.cloned.1.call-update) | async-done | bytes 122896 | tf_op jit(solution)/shard_map/reduce_scatter | solution.py:36
  (66 shorter events, 26.5 us)
Async XLA Ops:
  6.5 87.0 %copy-start.1 = (bf16[128,2048]{1,0:T(8,128)(2,1)S(1)}, bf16[128,2048]{1,0:T(8,128)(2,1)}, u32[]{:S(2)}) copy-start(bf16[128,2048]{1,0:T(8,128)(2,1)} %param.3) | copy-start | bytes 1572868
  6.5 435.7 %reduce-scatter.2.cloned.1.call-start = ((), (), s32[]{:S(2)}) async-start(), calls=%async_computation.1 | async-start | bytes 1179648 | tf_op jit(solution)/shard_map/reduce_scatter | solution.py:36
  6.5 25.7 %collective-permute-start = (bf16[128,2048]{1,0:T(8,128)(2,1)}, bf16[128,2048]{1,0:T(8,128)(2,1)S(1)}, u32[]{:S(2)}, u32[]{:S(2)}) collective-permute-start(bf16[128,2048]{1,0:T(8,128)(2,1)} %param.3), channel_id=1, source_target_pairs={{0,7},{1,8},{2,9},{3,10},{4,11},{5,12},{6,13},{7,14},{8,15},{9,16}... | collective-permute-start | bytes 1572872 | tf_op jit(solution)/shard_map/ppermute | solution.py:12
  12.1 26.8 %collective-permute-start.1 = (bf16[128,2048]{1,0:T(8,128)(2,1)}, bf16[128,2048]{1,0:T(8,128)(2,1)S(1)}, u32[]{:S(2)}, u32[]{:S(2)}) collective-permute-start(bf16[128,2048]{1,0:T(8,128)(2,1)} %param.3), channel_id=1, source_target_pairs={{0,6},{1,7},{2,8},{3,9},{4,10},{5,11},{6,12},{7,13},{8,14},{9,15},... | collective-permute-start | bytes 1572872 | tf_op jit(solution)/shard_map/ppermute | solution.py:12
  19.1 35.1 %collective-permute-start.2 = (bf16[128,2048]{1,0:T(8,128)(2,1)}, bf16[128,2048]{1,0:T(8,128)(2,1)S(1)}, u32[]{:S(2)}, u32[]{:S(2)}) collective-permute-start(bf16[128,2048]{1,0:T(8,128)(2,1)} %param.3), channel_id=1, source_target_pairs={{0,5},{1,6},{2,7},{3,8},{4,9},{5,10},{6,11},{7,12},{8,13},{9,14},{... | collective-permute-start | bytes 1572872 | tf_op jit(solution)/shard_map/ppermute | solution.py:12
  24.5 34.0 %collective-permute-start.3 = (bf16[128,2048]{1,0:T(8,128)(2,1)}, bf16[128,2048]{1,0:T(8,128)(2,1)S(1)}, u32[]{:S(2)}, u32[]{:S(2)}) collective-permute-start(bf16[128,2048]{1,0:T(8,128)(2,1)} %param.3), channel_id=1, source_target_pairs={{0,4},{1,5},{2,6},{3,7},{4,8},{5,9},{6,10},{7,11},{8,12},{9,13},{1... | collective-permute-start | bytes 1572872 | tf_op jit(solution)/shard_map/ppermute | solution.py:12
  28.3 41.4 %collective-permute-start.4 = (bf16[128,2048]{1,0:T(8,128)(2,1)}, bf16[128,2048]{1,0:T(8,128)(2,1)S(1)}, u32[]{:S(2)}, u32[]{:S(2)}) collective-permute-start(bf16[128,2048]{1,0:T(8,128)(2,1)} %param.3), channel_id=1, source_target_pairs={{0,3},{1,4},{2,5},{3,6},{4,7},{5,8},{6,9},{7,10},{8,11},{9,12},{10... | collective-permute-start | bytes 1572872 | tf_op jit(solution)/shard_map/ppermute | solution.py:12
  32.2 147.9 %copy-start = (bf16[1,1,15,128,128]{4,3,2,1,0:T(8,128)(2,1)S(1)}, bf16[1,1,15,128,128]{4,3,2,1,0:T(8,128)(2,1)}, u32[]{:S(2)}) copy-start(bf16[1,1,15,128,128]{4,3,2,1,0:T(8,128)(2,1)} %param.4) | copy-start | bytes 1474564
  32.2 48.7 %collective-permute-start.5 = (bf16[128,2048]{1,0:T(8,128)(2,1)}, bf16[128,2048]{1,0:T(8,128)(2,1)S(1)}, u32[]{:S(2)}, u32[]{:S(2)}) collective-permute-start(bf16[128,2048]{1,0:T(8,128)(2,1)} %param.3), channel_id=1, source_target_pairs={{0,2},{1,3},{2,4},{3,5},{4,6},{5,7},{6,8},{7,9},{8,10},{9,11},{10,... | collective-permute-start | bytes 1572872 | tf_op jit(solution)/shard_map/ppermute | solution.py:12
  38.9 52.1 %collective-permute-start.6 = (bf16[128,2048]{1,0:T(8,128)(2,1)}, bf16[128,2048]{1,0:T(8,128)(2,1)S(1)}, u32[]{:S(2)}, u32[]{:S(2)}) collective-permute-start(bf16[128,2048]{1,0:T(8,128)(2,1)} %param.3), channel_id=1, source_target_pairs={{0,1},{1,2},{2,3},{3,4},{4,5},{5,6},{6,7},{7,8},{8,9},{9,10},{10,1... | collective-permute-start | bytes 1572872 | tf_op jit(solution)/shard_map/ppermute | solution.py:12
  54.2 39.2 %collective-permute-start.7 = (bf16[128,2048]{1,0:T(8,128)(2,1)}, bf16[128,2048]{1,0:T(8,128)(2,1)S(1)}, u32[]{:S(2)}, u32[]{:S(2)}) collective-permute-start(bf16[128,2048]{1,0:T(8,128)(2,1)} %param.3), channel_id=1, source_target_pairs={{1,0},{2,1},{3,2},{4,3},{5,4},{6,5},{7,6},{8,7},{9,8},{10,9},{11,1... | collective-permute-start | bytes 1572872 | tf_op jit(solution)/shard_map/ppermute | solution.py:12
  58.5 36.4 %collective-permute-start.8 = (bf16[128,2048]{1,0:T(8,128)(2,1)}, bf16[128,2048]{1,0:T(8,128)(2,1)S(1)}, u32[]{:S(2)}, u32[]{:S(2)}) collective-permute-start(bf16[128,2048]{1,0:T(8,128)(2,1)} %param.3), channel_id=1, source_target_pairs={{2,0},{3,1},{4,2},{5,3},{6,4},{7,5},{8,6},{9,7},{10,8},{11,9},{12,... | collective-permute-start | bytes 1572872 | tf_op jit(solution)/shard_map/ppermute | solution.py:12
  69.7 37.1 %collective-permute-start.9 = (bf16[128,2048]{1,0:T(8,128)(2,1)}, bf16[128,2048]{1,0:T(8,128)(2,1)S(1)}, u32[]{:S(2)}, u32[]{:S(2)}) collective-permute-start(bf16[128,2048]{1,0:T(8,128)(2,1)} %param.3), channel_id=1, source_target_pairs={{3,0},{4,1},{5,2},{6,3},{7,4},{8,5},{9,6},{10,7},{11,8},{12,9},{13... | collective-permute-start | bytes 1572872 | tf_op jit(solution)/shard_map/ppermute | solution.py:12
  81.0 48.3 %collective-permute-start.10 = (bf16[128,2048]{1,0:T(8,128)(2,1)}, bf16[128,2048]{1,0:T(8,128)(2,1)S(1)}, u32[]{:S(2)}, u32[]{:S(2)}) collective-permute-start(bf16[128,2048]{1,0:T(8,128)(2,1)} %param.3), channel_id=1, source_target_pairs={{4,0},{5,1},{6,2},{7,3},{8,4},{9,5},{10,6},{11,7},{12,8},{13,9},{1... | collective-permute-start | bytes 1572872 | tf_op jit(solution)/shard_map/ppermute | solution.py:12
  91.1 88.9 %collective-permute-start.11 = (bf16[128,2048]{1,0:T(8,128)(2,1)}, bf16[128,2048]{1,0:T(8,128)(2,1)S(1)}, u32[]{:S(2)}, u32[]{:S(2)}) collective-permute-start(bf16[128,2048]{1,0:T(8,128)(2,1)} %param.3), channel_id=1, source_target_pairs={{5,0},{6,1},{7,2},{8,3},{9,4},{10,5},{11,6},{12,7},{13,8},{14,9},{... | collective-permute-start | bytes 1572872 | tf_op jit(solution)/shard_map/ppermute | solution.py:12
  93.5 86.5 %collective-permute-start.12 = (bf16[128,2048]{1,0:T(8,128)(2,1)S(1)}, bf16[128,2048]{1,0:T(8,128)(2,1)S(1)}, u32[]{:S(2)}, u32[]{:S(2)}) collective-permute-start(bf16[128,2048]{1,0:T(8,128)(2,1)S(1)} %copy-done.1), channel_id=1, source_target_pairs={{6,0},{7,1},{8,2},{9,3},{10,4},{11,5},{12,6},{13,7},{14,8},{15,9},... | collective-permute-start | bytes 1572872 | tf_op jit(solution)/shard_map/ppermute | solution.py:12
  94.9 85.2 %collective-permute-start.13 = (bf16[128,2048]{1,0:T(8,128)(2,1)S(1)}, bf16[128,2048]{1,0:T(8,128)(2,1)S(1)}, u32[]{:S(2)}, u32[]{:S(2)}) collective-permute-start(bf16[128,2048]{1,0:T(8,128)(2,1)S(1)} %copy-done.1), channel_id=1, source_target_pairs={{7,0},{8,1},{9,2},{10,3},{11,4},{12,5},{13,6},{14,7},{15,8},{16,9}... | collective-permute-start | bytes 1572872 | tf_op jit(solution)/shard_map/ppermute | solution.py:12
  181.5 53.8 %collective-permute-start.14 = (bf16[1,128,2048]{2,1,0:T(8,128)(2,1)S(1)}, bf16[1,128,2048]{2,1,0:T(8,128)(2,1)S(1)}, u32[]{:S(2)}, u32[]{:S(2)}) collective-permute-start(bf16[1,128,2048]{2,1,0:T(8,128)(2,1)S(1)} %bitcast.86), channel_id=1, source_target_pairs={{0,7},{1,8},{2,9},{3,10},{4,11},{5,12},{6,13},{7,14},{8,15},{9,16}... | collective-permute-start | bytes 1572872 | tf_op jit(solution)/shard_map/ppermute | solution.py:12
  202.5 36.2 %collective-permute-start.15 = (bf16[1,128,2048]{2,1,0:T(8,128)(2,1)S(1)}, bf16[1,128,2048]{2,1,0:T(8,128)(2,1)S(1)}, u32[]{:S(2)}, u32[]{:S(2)}) collective-permute-start(bf16[1,128,2048]{2,1,0:T(8,128)(2,1)S(1)} %bitcast.87), channel_id=1, source_target_pairs={{0,6},{1,7},{2,8},{3,9},{4,10},{5,11},{6,12},{7,13},{8,14},{9,15},... | collective-permute-start | bytes 1572872 | tf_op jit(solution)/shard_map/ppermute | solution.py:12
  215.5 37.9 %collective-permute-start.16 = (bf16[1,128,2048]{2,1,0:T(8,128)(2,1)S(1)}, bf16[1,128,2048]{2,1,0:T(8,128)(2,1)S(1)}, u32[]{:S(2)}, u32[]{:S(2)}) collective-permute-start(bf16[1,128,2048]{2,1,0:T(8,128)(2,1)S(1)} %bitcast.88), channel_id=1, source_target_pairs={{0,5},{1,6},{2,7},{3,8},{4,9},{5,10},{6,11},{7,12},{8,13},{9,14},{... | collective-permute-start | bytes 1572872 | tf_op jit(solution)/shard_map/ppermute | solution.py:12
  216.9 47.8 %collective-permute-start.17 = (bf16[1,128,2048]{2,1,0:T(8,128)(2,1)S(1)}, bf16[1,128,2048]{2,1,0:T(8,128)(2,1)S(1)}, u32[]{:S(2)}, u32[]{:S(2)}) collective-permute-start(bf16[1,128,2048]{2,1,0:T(8,128)(2,1)S(1)} %bitcast.89), channel_id=1, source_target_pairs={{0,4},{1,5},{2,6},{3,7},{4,8},{5,9},{6,10},{7,11},{8,12},{9,13},{1... | collective-permute-start | bytes 1572872 | tf_op jit(solution)/shard_map/ppermute | solution.py:12
  233.3 49.1 %collective-permute-start.18 = (bf16[1,128,2048]{2,1,0:T(8,128)(2,1)S(1)}, bf16[1,128,2048]{2,1,0:T(8,128)(2,1)S(1)}, u32[]{:S(2)}, u32[]{:S(2)}) collective-permute-start(bf16[1,128,2048]{2,1,0:T(8,128)(2,1)S(1)} %bitcast.90), channel_id=1, source_target_pairs={{0,3},{1,4},{2,5},{3,6},{4,7},{5,8},{6,9},{7,10},{8,11},{9,12},{10... | collective-permute-start | bytes 1572872 | tf_op jit(solution)/shard_map/ppermute | solution.py:12
  235.2 55.4 %collective-permute-start.19 = (bf16[1,128,2048]{2,1,0:T(8,128)(2,1)S(1)}, bf16[1,128,2048]{2,1,0:T(8,128)(2,1)S(1)}, u32[]{:S(2)}, u32[]{:S(2)}) collective-permute-start(bf16[1,128,2048]{2,1,0:T(8,128)(2,1)S(1)} %bitcast.91), channel_id=1, source_target_pairs={{0,2},{1,3},{2,4},{3,5},{4,6},{5,7},{6,8},{7,9},{8,10},{9,11},{10,... | collective-permute-start | bytes 1572872 | tf_op jit(solution)/shard_map/ppermute | solution.py:12
  238.7 65.0 %collective-permute-start.20 = (bf16[1,128,2048]{2,1,0:T(8,128)(2,1)S(1)}, bf16[1,128,2048]{2,1,0:T(8,128)(2,1)S(1)}, u32[]{:S(2)}, u32[]{:S(2)}) collective-permute-start(bf16[1,128,2048]{2,1,0:T(8,128)(2,1)S(1)} %bitcast.92), channel_id=1, source_target_pairs={{0,1},{1,2},{2,3},{3,4},{4,5},{5,6},{6,7},{7,8},{8,9},{9,10},{10,1... | collective-permute-start | bytes 1572872 | tf_op jit(solution)/shard_map/ppermute | solution.py:12
  253.4 51.7 %collective-permute-start.21 = (bf16[1,128,2048]{2,1,0:T(8,128)(2,1)S(1)}, bf16[1,128,2048]{2,1,0:T(8,128)(2,1)S(1)}, u32[]{:S(2)}, u32[]{:S(2)}) collective-permute-start(bf16[1,128,2048]{2,1,0:T(8,128)(2,1)S(1)} %bitcast.93), channel_id=1, source_target_pairs={{1,0},{2,1},{3,2},{4,3},{5,4},{6,5},{7,6},{8,7},{9,8},{10,9},{11,1... | collective-permute-start | bytes 1572872 | tf_op jit(solution)/shard_map/ppermute | solution.py:12
  264.6 41.8 %collective-permute-start.22 = (bf16[1,128,2048]{2,1,0:T(8,128)(2,1)S(1)}, bf16[1,128,2048]{2,1,0:T(8,128)(2,1)S(1)}, u32[]{:S(2)}, u32[]{:S(2)}) collective-permute-start(bf16[1,128,2048]{2,1,0:T(8,128)(2,1)S(1)} %bitcast.94), channel_id=1, source_target_pairs={{2,0},{3,1},{4,2},{5,3},{6,4},{7,5},{8,6},{9,7},{10,8},{11,9},{12,... | collective-permute-start | bytes 1572872 | tf_op jit(solution)/shard_map/ppermute | solution.py:12
  282.4 25.3 %collective-permute-start.23 = (bf16[1,128,2048]{2,1,0:T(8,128)(2,1)S(1)}, bf16[1,128,2048]{2,1,0:T(8,128)(2,1)S(1)}, u32[]{:S(2)}, u32[]{:S(2)}) collective-permute-start(bf16[1,128,2048]{2,1,0:T(8,128)(2,1)S(1)} %bitcast.95), channel_id=1, source_target_pairs={{3,0},{4,1},{5,2},{6,3},{7,4},{8,5},{9,6},{10,7},{11,8},{12,9},{13... | collective-permute-start | bytes 1572872 | tf_op jit(solution)/shard_map/ppermute | solution.py:12
  290.7 26.1 %collective-permute-start.24 = (bf16[1,128,2048]{2,1,0:T(8,128)(2,1)S(1)}, bf16[1,128,2048]{2,1,0:T(8,128)(2,1)S(1)}, u32[]{:S(2)}, u32[]{:S(2)}) collective-permute-start(bf16[1,128,2048]{2,1,0:T(8,128)(2,1)S(1)} %bitcast.96), channel_id=1, source_target_pairs={{4,0},{5,1},{6,2},{7,3},{8,4},{9,5},{10,6},{11,7},{12,8},{13,9},{1... | collective-permute-start | bytes 1572872 | tf_op jit(solution)/shard_map/ppermute | solution.py:12
  303.7 38.5 %collective-permute-start.25 = (bf16[1,128,2048]{2,1,0:T(8,128)(2,1)S(1)}, bf16[1,128,2048]{2,1,0:T(8,128)(2,1)S(1)}, u32[]{:S(2)}, u32[]{:S(2)}) collective-permute-start(bf16[1,128,2048]{2,1,0:T(8,128)(2,1)S(1)} %bitcast.97), channel_id=1, source_target_pairs={{5,0},{6,1},{7,2},{8,3},{9,4},{10,5},{11,6},{12,7},{13,8},{14,9},{... | collective-permute-start | bytes 1572872 | tf_op jit(solution)/shard_map/ppermute | solution.py:12
  305.1 59.2 %collective-permute-start.26 = (bf16[1,128,2048]{2,1,0:T(8,128)(2,1)S(1)}, bf16[1,128,2048]{2,1,0:T(8,128)(2,1)S(1)}, u32[]{:S(2)}, u32[]{:S(2)}) collective-permute-start(bf16[1,128,2048]{2,1,0:T(8,128)(2,1)S(1)} %bitcast.98), channel_id=1, source_target_pairs={{6,0},{7,1},{8,2},{9,3},{10,4},{11,5},{12,6},{13,7},{14,8},{15,9},... | collective-permute-start | bytes 1572872 | tf_op jit(solution)/shard_map/ppermute | solution.py:12
  306.4 57.9 %collective-permute-start.27 = (bf16[1,128,2048]{2,1,0:T(8,128)(2,1)S(1)}, bf16[1,128,2048]{2,1,0:T(8,128)(2,1)S(1)}, u32[]{:S(2)}, u32[]{:S(2)}) collective-permute-start(bf16[1,128,2048]{2,1,0:T(8,128)(2,1)S(1)} %bitcast.99), channel_id=1, source_target_pairs={{7,0},{8,1},{9,2},{10,3},{11,4},{12,5},{13,6},{14,7},{15,8},{16,9}... | collective-permute-start | bytes 1572872 | tf_op jit(solution)/shard_map/ppermute | solution.py:12
Sparse Core Ops, SparseCore 0:
  368.2 73.9 reduce-scatter.1
where the time goes:
time: 452 us; the launch traced here: 451 us
  waiting for transfers between devices  292 us (65%)
  starting transfers between devices  136 us (30%)
  between operations  14 us (3%)
  local copies, waits for them, and re-layouts  5.13 us (1%)
    ppermute x28, waiting for transfers between devices, shifted(): return lax.ppermute(x, axis, pairs)  217 us
    ppermute x28, starting transfers between devices, shifted(): return lax.ppermute(x, axis, pairs)  136 us
    reduce_scatter x1, waiting for transfers between devices, per_device(): lax.psum_scatter(partial_tiles, 'aux', scatter_dimension=1, tiled=True)  74.2 us
  transfers between devices with their start and end apart: 29, of which 16 were waited for; matrix products, arithmetic and copies ran while one was open for 1% of the time, Pallas kernels for 0%

commit v1 on v0

v1 whole, which is shorter than its diff:
```python
import jax
import jax.numpy as jnp
from jax import lax
from jax.sharding import Mesh, PartitionSpec as P

ROWS = 128
WIDE = 256
SPAN = 15


def moved(x, axis, by):
    n = lax.axis_size(axis)
    return lax.ppermute(x, axis, [(i, (i + by) % n) for i in range(n)])


def per_device(occupied, integrals, pair_mask):
    x = lax.axis_index("x")
    core = lax.axis_index("core")
    mask_row = pair_mask[0]
    tiles = integrals[0, 0] * mask_row.astype(jnp.bfloat16)[:, None, None]

    from_left = moved(tiles, "x", 1)
    from_right = moved(tiles, "x", -1)
    from_far = moved(tiles, "x", 2)
    by_turn = [tiles, from_right, from_far, from_left]

    mine = lax.dynamic_index_in_dim(
        occupied.reshape(ROWS, 4, 2, WIDE), core, 2, keepdims=False
    )
    plane = lax.all_to_all(mine.transpose(1, 0, 2), "x", 0, 0)
    below = moved(plane, "z", 1)
    above = moved(plane, "z", -1)
    below2 = moved(plane[1:], "z", 2)
    above2 = moved(plane[:3], "z", -2)
    window = jnp.concatenate([below2, below, plane, above, above2], 0)

    halves = []
    for turn in range(4):
        both = jnp.stack([by_turn[turn], moved(by_turn[turn], "core", 1)])
        near = lax.dynamic_slice_in_dim(window, (x + turn) % 4, SPAN, 0)
        half = jnp.einsum("pomn,onk->mpk", both, near, preferred_element_type=jnp.float32)
        halves.append(half.astype(jnp.bfloat16).reshape(ROWS, 2 * WIDE))
    half = jnp.stack(halves)
    half = lax.dynamic_slice_in_dim(jnp.concatenate([half, half]), 4 - x, 4, 0)

    down = moved(half, "z", 1)
    up = moved(half, "z", -1)
    three = jnp.stack([down, half, up])
    other = moved(three, "core", 1)
    full = jnp.concatenate([three, other], -1)
    rows = lax.dynamic_index_in_dim(
        full.reshape(3, 4, 4, 2, 16, 4 * WIDE), core, 3, keepdims=False
    )
    home = jnp.einsum(
        "xyrk,pbnk->xyrpbn", rows[1], full, preferred_element_type=jnp.float32
    ).reshape(4, 4, 16, 12, ROWS)
    to_below = jnp.einsum(
        "xyrk,bnk->xyrbn", rows[0], full[2, :3], preferred_element_type=jnp.float32
    )
    to_above = jnp.einsum(
        "xyrk,bnk->xyrbn", rows[2], full[0, 1:], preferred_element_type=jnp.float32
    )
    first = jnp.arange(3)[None, :] < jnp.arange(4)[:, None]
    far = jnp.where(first[:, None, None, :, None], to_below, to_above)
    partial = jnp.concatenate([home, far], 3).astype(jnp.bfloat16)
    partial = lax.all_to_all(partial.reshape(16, 16, SPAN, ROWS), ("x", "y"), 0, 0)
    total = partial.astype(jnp.float32).sum(0).transpose(1, 0, 2)
    far = total[12:]
    line = jnp.concatenate([moved(far, "z", 1), total[:12], moved(far, "z", -1)], 0)
    out = lax.dynamic_slice_in_dim(line, x, SPAN, 0)
    return (out * mask_row.astype(jnp.float32)[:, None, None])[None]


def solution(mesh):
    split = Mesh(mesh.devices.reshape(4, 2, 16, 4), ("y", "core", "z", "x"))
    aux, orb = ("y", "core"), ("z", "x")
    return jax.shard_map(
        per_device,
        mesh=split,
        in_specs=(P(orb, None), P(aux, orb, None, None, None), P(orb, None)),
        out_specs=P(orb, None, aux, None),
        check_vma=False,
    )
```

time: 452 us -> 126 us (0.28)
  the two profiles are of different devices: /device:TPU:6 before, /device:TPU:96 now
where the time goes in v1:
time: 126 us; the launch traced here: 125 us
  starting transfers between devices  51.5 us (41%)
  waiting for transfers between devices  35.5 us (28%)
  blocking collectives  22 us (17%)
  matrix products  8.25 us (7%)
  local copies, waits for them, and re-layouts  4.53 us (4%)
  other arithmetic  2.91 us (2%)
    ppermute x16, starting transfers between devices, moved(): return lax.ppermute(x, axis, [(i, (i + by) % n) for i in range(n)])  47.2 us
    ppermute x16, waiting for transfers between devices, moved(): return lax.ppermute(x, axis, [(i, (i + by) % n) for i in range(n)])  28.8 us
    all_to_all x1, blocking collectives, per_device(): lax.all_to_all(partial.reshape(16, 16, SPAN, ROWS), ('x', 'y'), 0, 0)  22 us
    all_to_all x1, waiting for transfers between devices, per_device(): plane = lax.all_to_all(mine.transpose(1, 0, 2), 'x', 0, 0)  6.67 us
    dot_general x4, matrix products, per_device(): jnp.einsum('pomn,onk->mpk', both, near, preferred_element_type=jnp.float32)  6.32 us
    all_to_all x1, starting transfers between devices, per_device(): plane = lax.all_to_all(mine.transpose(1, 0, 2), 'x', 0, 0)  4.29 us
  transfers between devices with their start and end apart: 17, of which 8 were waited for; matrix products, arithmetic and copies ran while one was open for 4% of the time, Pallas kernels for 0%

profile of v1, /device:TPU:96, one launch (start us, length us, event | category | flops | bytes accessed | tf_op | source)
XLA Modules:
  0.0 125.3 jit_solution(17343524562171336192)
XLA Ops:
  0.0 1.5 %reshape.54 = bf16[128,4,2,256]{3,2,1,0:T(2,128)(2,1)S(1)} reshape(bf16[128,2048]{1,0:T(8,128)(2,1)} %param.3) | data formatting | bytes 1048576 | tf_op jit(solution)/shard_map/reshape | solution.py:28
  2.0 1.1 copy.23
  3.1 4.3 %all-to-all-start = ((bf16[4,128,256]{1,2,0:T(8,128)(2,1)}), bf16[4,128,256]{1,2,0:T(8,128)(2,1)S(1)}, u32[]{:S(2)}, u32[]{:S(2)}) async-start(bf16[4,128,256]{1,2,0:T(8,128)(2,1)} %bitcast.1), calls=%async_computation | async-start | bytes 524288 | tf_op jit(solution)/shard_map/all_to_all | solution.py:30
  7.4 6.7 %all-to-all-done = bf16[4,128,256]{1,2,0:T(8,128)(2,1)S(1)} async-done(((bf16[4,128,256]{1,2,0:T(8,128)(2,1)}), bf16[4,128,256]{1,2,0:T(8,128)(2,1)S(1)}, u32[]{:S(2)}, u32[]{:S(2)}) %all-to-all-start) | async-done | bytes 262176 | tf_op jit(solution)/shard_map/all_to_all | solution.py:30
  14.1 6.4 %collective-permute-start = (bf16[3,128,256]{1,2,0:T(8,128)(2,1)S(1)}, bf16[3,128,256]{1,2,0:T(8,128)(2,1)S(1)}, u32[]{:S(2)}, u32[]{:S(2)}) collective-permute-start(bf16[3,128,256]{1,2,0:T(8,128)(2,1)S(1)} %get-tuple-element.6), channel_id=1, source_target_pairs={{0,8},{4,12},{8,16},{12,20},{16,24},{20,28},{24,32},{28,36},{32,40... | collective-permute-start | bytes 589832 | tf_op jit(solution)/shard_map/ppermute | solution.py:13
  20.5 3.8 %collective-permute-start.1 = (bf16[4,128,256]{1,2,0:T(8,128)(2,1)S(1)}, bf16[4,128,256]{1,2,0:T(8,128)(2,1)S(1)}, u32[]{:S(2)}, u32[]{:S(2)}) collective-permute-start(bf16[4,128,256]{1,2,0:T(8,128)(2,1)S(1)} %all-to-all-done), channel_id=1, source_target_pairs={{0,4},{4,8},{8,12},{12,16},{16,20},{20,24},{24,28},{28,32},{32,36}... | collective-permute-start | bytes 786440 | tf_op jit(solution)/shard_map/ppermute | solution.py:13
  24.5 3.1 %collective-permute-start.5 = (bf16[15,128,128]{2,1,0:T(8,128)(2,1)S(1)}, bf16[15,128,128]{2,1,0:T(8,128)(2,1)}, u32[]{:S(2)}, u32[]{:S(2)}) collective-permute-start(bf16[15,128,128]{2,1,0:T(8,128)(2,1)S(1)} %bitcast_multiply_fusion), channel_id=1, source_target_pairs={{0,3},{1,0},{2,1},{3,2},{4,7},{5,4},{6,5},{7,6},{8,11},{9,8},{10,9... | collective-permute-start | bytes 1474568 | tf_op jit(solution)/shard_map/ppermute | solution.py:13
  27.6 3.4 %collective-permute-start.7 = (bf16[15,128,128]{2,1,0:T(8,128)(2,1)S(1)}, bf16[15,128,128]{2,1,0:T(8,128)(2,1)}, u32[]{:S(2)}, u32[]{:S(2)}) collective-permute-start(bf16[15,128,128]{2,1,0:T(8,128)(2,1)S(1)} %bitcast_multiply_fusion), channel_id=1, source_target_pairs={{0,2},{1,3},{2,0},{3,1},{4,6},{5,7},{6,4},{7,5},{8,10},{9,11},{10,... | collective-permute-start | bytes 1474568 | tf_op jit(solution)/shard_map/ppermute | solution.py:13
  30.9 1.9 %collective-permute-start.9 = (bf16[15,128,128]{2,1,0:T(8,128)(2,1)S(1)}, bf16[15,128,128]{2,1,0:T(8,128)(2,1)}, u32[]{:S(2)}, u32[]{:S(2)}) collective-permute-start(bf16[15,128,128]{2,1,0:T(8,128)(2,1)S(1)} %bitcast_multiply_fusion), channel_id=1, source_target_pairs={{0,1},{1,2},{2,3},{3,0},{4,5},{5,6},{6,7},{7,4},{8,9},{9,10},{10,1... | collective-permute-start | bytes 1474568 | tf_op jit(solution)/shard_map/ppermute | solution.py:13
  32.9 2.0 %collective-permute-start.2 = (bf16[4,128,256]{1,2,0:T(8,128)(2,1)S(1)}, bf16[4,128,256]{1,2,0:T(8,128)(2,1)S(1)}, u32[]{:S(2)}, u32[]{:S(2)}) collective-permute-start(bf16[4,128,256]{1,2,0:T(8,128)(2,1)S(1)} %all-to-all-done), channel_id=1, source_target_pairs={{0,60},{4,0},{8,4},{12,8},{16,12},{20,16},{24,20},{28,24},{32,28},... | collective-permute-start | bytes 786440 | tf_op jit(solution)/shard_map/ppermute | solution.py:13
  35.1 1.9 %collective-permute-start.4 = (bf16[15,128,128]{2,1,0:T(8,128)(2,1)S(1)}, bf16[15,128,128]{2,1,0:T(8,128)(2,1)S(1)}, u32[]{:S(2)}, u32[]{:S(2)}) collective-permute-start(bf16[15,128,128]{2,1,0:T(8,128)(2,1)S(1)} %bitcast_multiply_fusion), channel_id=1, source_target_pairs={{0,64},{64,0},{1,65},{65,1},{2,66},{66,2},{3,67},{67,3},{4,68},{68... | collective-permute-start | bytes 1474568 | tf_op jit(solution)/shard_map/ppermute | solution.py:13
  37.1 5.3 %collective-permute-done.2 = bf16[4,128,256]{1,2,0:T(8,128)(2,1)S(1)} collective-permute-done((bf16[4,128,256]{1,2,0:T(8,128)(2,1)S(1)}, bf16[4,128,256]{1,2,0:T(8,128)(2,1)S(1)}, u32[]{:S(2)}, u32[]{:S(2)}) %collective-permute-start.2) | collective-permute-done | bytes 262176 | tf_op jit(solution)/shard_map/ppermute | solution.py:13
  42.4 1.9 %collective-permute-start.3 = (bf16[3,128,256]{1,2,0:T(8,128)(2,1)S(1)}, bf16[3,128,256]{1,2,0:T(8,128)(2,1)S(1)}, u32[]{:S(2)}, u32[]{:S(2)}) collective-permute-start(bf16[3,128,256]{1,2,0:T(8,128)(2,1)S(1)} %get-tuple-element.5), channel_id=1, source_target_pairs={{0,56},{4,60},{8,0},{12,4},{16,8},{20,12},{24,16},{28,20},{32,24},... | collective-permute-start | bytes 589832 | tf_op jit(solution)/shard_map/ppermute | solution.py:13
  44.3 1.9 %collective-permute-start.6 = (bf16[15,128,128]{2,1,0:T(8,128)(2,1)}, bf16[15,128,128]{2,1,0:T(8,128)(2,1)}, u32[]{:S(2)}, u32[]{:S(2)}) collective-permute-start(bf16[15,128,128]{2,1,0:T(8,128)(2,1)} %collective-permute-done.5), channel_id=1, source_target_pairs={{0,64},{64,0},{1,65},{65,1},{2,66},{66,2},{3,67},{67,3},{4,68},{68... | collective-permute-start | bytes 1474568 | tf_op jit(solution)/shard_map/ppermute | solution.py:13
  46.3 2.4 %collective-permute-start.8 = (bf16[15,128,128]{2,1,0:T(8,128)(2,1)}, bf16[15,128,128]{2,1,0:T(8,128)(2,1)}, u32[]{:S(2)}, u32[]{:S(2)}) collective-permute-start(bf16[15,128,128]{2,1,0:T(8,128)(2,1)} %collective-permute-done.7), channel_id=1, source_target_pairs={{0,64},{64,0},{1,65},{65,1},{2,66},{66,2},{3,67},{67,3},{4,68},{68... | collective-permute-start | bytes 1474568 | tf_op jit(solution)/shard_map/ppermute | solution.py:13
  48.7 3.6 %collective-permute-done.9 = bf16[15,128,128]{2,1,0:T(8,128)(2,1)} collective-permute-done((bf16[15,128,128]{2,1,0:T(8,128)(2,1)S(1)}, bf16[15,128,128]{2,1,0:T(8,128)(2,1)}, u32[]{:S(2)}, u32[]{:S(2)}) %collective-permute-start.9) | collective-permute-done | bytes 491552 | tf_op jit(solution)/shard_map/ppermute | solution.py:13
  52.3 1.9 %collective-permute-start.10 = (bf16[15,128,128]{2,1,0:T(8,128)(2,1)}, bf16[15,128,128]{2,1,0:T(8,128)(2,1)}, u32[]{:S(2)}, u32[]{:S(2)}) collective-permute-start(bf16[15,128,128]{2,1,0:T(8,128)(2,1)} %collective-permute-done.9), channel_id=1, source_target_pairs={{0,64},{64,0},{1,65},{65,1},{2,66},{66,2},{3,67},{67,3},{4,68},{68... | collective-permute-start | bytes 1474568 | tf_op jit(solution)/shard_map/ppermute | solution.py:13
  55.8 1.9 %fusion.2 = bf16[256,2,128]{2,0,1:T(8,128)(2,1)S(1)} fusion(bf16[1,15,128,128]{3,2,1,0:T(8,128)(2,1)} %bitcast.13, bf16[1,15,128,128]{3,2,1,0:T(8,128)(2,1)} %bitcast.12, bf16[18,128,256]{1,2,0:T(8,128)(2,1)} %copy-done.1, s32[]{:T(128)S(6)} %select_n.51), kind=kOutput, calls=%fused_computation.11 | convolution fusion | flops 253689856 | bytes 2097156 | tf_op jit(solution)/shard_map/pomn,onk->mpk/dot_general | solution.py:41
  57.9 2.0 %fusion.3 = bf16[256,2,128]{2,0,1:T(8,128)(2,1)S(1)} fusion(bf16[1,15,128,128]{3,2,1,0:T(8,128)(2,1)} %bitcast.20, bf16[1,15,128,128]{3,2,1,0:T(8,128)(2,1)} %bitcast.19, bf16[18,128,256]{1,2,0:T(8,128)(2,1)} %copy-done.1, s32[]{:T(128)S(6)} %select_n.53), kind=kOutput, calls=%fused_computation.12 | convolution fusion | flops 253689856 | bytes 2097156 | tf_op jit(solution)/shard_map/pomn,onk->mpk/dot_general | solution.py:41
  60.0 1.9 %fusion.4 = bf16[256,2,128]{2,0,1:T(8,128)(2,1)S(1)} fusion(bf16[1,15,128,128]{3,2,1,0:T(8,128)(2,1)} %bitcast.27, bf16[1,15,128,128]{3,2,1,0:T(8,128)(2,1)} %bitcast.26, bf16[18,128,256]{1,2,0:T(8,128)(2,1)} %copy-done.1, s32[]{:T(128)S(6)} %select_n.55), kind=kOutput, calls=%fused_computation.13 | convolution fusion | flops 253689856 | bytes 2097156 | tf_op jit(solution)/shard_map/pomn,onk->mpk/dot_general | solution.py:41
  62.3 1.9 %collective-permute-start.12 = (bf16[4,128,512]{2,1,0:T(8,128)(2,1)S(1)}, bf16[4,128,512]{2,1,0:T(8,128)(2,1)S(1)}, u32[]{:S(2)}, u32[]{:S(2)}) collective-permute-start(bf16[4,128,512]{2,1,0:T(8,128)(2,1)S(1)} %constant_dynamic-slice_fusion.1), channel_id=1, source_target_pairs={{0,60},{4,0},{8,4},{12,8},{16,12},{20,16},{24,20},{28,24},{32,28},... | collective-permute-start | bytes 1572872 | tf_op jit(solution)/shard_map/ppermute | solution.py:13
  64.2 5.1 %collective-permute-start.11 = (bf16[4,128,512]{2,1,0:T(8,128)(2,1)S(1)}, bf16[4,128,512]{2,1,0:T(8,128)(2,1)S(1)}, u32[]{:S(2)}, u32[]{:S(2)}) collective-permute-start(bf16[4,128,512]{2,1,0:T(8,128)(2,1)S(1)} %constant_dynamic-slice_fusion.1), channel_id=1, source_target_pairs={{0,4},{4,8},{8,12},{12,16},{16,20},{20,24},{24,28},{28,32},{32,36}... | collective-permute-start | bytes 1572872 | tf_op jit(solution)/shard_map/ppermute | solution.py:13
  69.4 9.9 %collective-permute-done.12 = bf16[4,128,512]{2,1,0:T(8,128)(2,1)S(1)} collective-permute-done((bf16[4,128,512]{2,1,0:T(8,128)(2,1)S(1)}, bf16[4,128,512]{2,1,0:T(8,128)(2,1)S(1)}, u32[]{:S(2)}, u32[]{:S(2)}) %collective-permute-start.12) | collective-permute-done | bytes 524320 | tf_op jit(solution)/shard_map/ppermute | solution.py:13
  79.3 1.2 collective-permute-done.11
  80.7 1.9 %collective-permute-start.13 = (bf16[3,4,128,512]{3,2,1,0:T(8,128)(2,1)S(1)}, bf16[3,4,128,512]{3,2,1,0:T(8,128)(2,1)}, u32[]{:S(2)}, u32[]{:S(2)}) collective-permute-start(bf16[3,4,128,512]{3,2,1,0:T(8,128)(2,1)S(1)} %pad_maximum_fusion.1), channel_id=1, source_target_pairs={{0,64},{64,0},{1,65},{65,1},{2,66},{66,2},{3,67},{67,3},{4,68},{68... | collective-permute-start | bytes 4718600 | tf_op jit(solution)/shard_map/ppermute | solution.py:13
  82.6 3.5 %collective-permute-done.13 = bf16[3,4,128,512]{3,2,1,0:T(8,128)(2,1)} collective-permute-done((bf16[3,4,128,512]{3,2,1,0:T(8,128)(2,1)S(1)}, bf16[3,4,128,512]{3,2,1,0:T(8,128)(2,1)}, u32[]{:S(2)}, u32[]{:S(2)}) %collective-permute-start.13) | collective-permute-done | bytes 1572896 | tf_op jit(solution)/shard_map/ppermute | solution.py:13
  86.1 1.6 %pad_maximum_fusion = bf16[3,4,128,1024]{3,2,1,0:T(8,128)(2,1)S(1)} fusion(bf16[3,4,128,512]{3,2,1,0:T(8,128)(2,1)} %collective-permute-done.13, bf16[1,4,128,512]{3,2,1,0:T(8,128)(2,1)S(1)} %bitcast.121, bf16[1,4,128,512]{3,2,1,0:T(8,128)(2,1)S(1)} %fusion.43, bf16[1,4,128,512]{3,2,1,0:T(8,128)(2,1)S(1)} %bitcast.123), kind=kLoop, calls=%fused_computation | loop fusion | flops 12582912 | bytes 6291456 | tf_op jit(solution)/shard_map/concatenate | solution.py:50
  88.7 1.0 convolution_convert_fusion
  89.8 22.0 %all_to_all.10 = bf16[16,16,15,128]{3,1,2,0:T(8,128)(2,1)S(1)} all-to-all(bf16[16,16,15,128]{3,1,2,0:T(8,128)(2,1)S(1)} %pad_maximum_fusion.2), channel_id=1, replica_groups=mesh['y'=4,'core'=2,'z'=16,'x'=4] {'x','y'}, dimensions={0} | all-to-all | bytes 1966080 | tf_op jit(solution)/shard_map/all_to_all | solution.py:66
  112.0 5.6 %collective-permute-start.14 = (f32[3,16,128]{2,1,0:T(8,128)S(1)}, f32[3,16,128]{2,1,0:T(8,128)S(1)}, u32[]{:S(2)}, u32[]{:S(2)}) collective-permute-start(f32[3,16,128]{2,1,0:T(8,128)S(1)} %slice.43), channel_id=1, source_target_pairs={{0,4},{4,8},{8,12},{12,16},{16,20},{20,24},{24,28},{28,32},{32,36}... | collective-permute-start | bytes 73736 | tf_op jit(solution)/shard_map/ppermute | solution.py:13
  117.6 1.9 %collective-permute-start.15 = (f32[3,16,128]{2,1,0:T(8,128)S(1)}, f32[3,16,128]{2,1,0:T(8,128)S(1)}, u32[]{:S(2)}, u32[]{:S(2)}) collective-permute-start(f32[3,16,128]{2,1,0:T(8,128)S(1)} %slice.43), channel_id=1, source_target_pairs={{0,60},{4,0},{8,4},{12,8},{16,12},{20,16},{24,20},{28,24},{32,28},... | collective-permute-start | bytes 73736 | tf_op jit(solution)/shard_map/ppermute | solution.py:13
  119.6 5.0 %collective-permute-done.15 = f32[3,16,128]{2,1,0:T(8,128)S(1)} collective-permute-done((f32[3,16,128]{2,1,0:T(8,128)S(1)}, f32[3,16,128]{2,1,0:T(8,128)S(1)}, u32[]{:S(2)}, u32[]{:S(2)}) %collective-permute-start.15) | collective-permute-done | bytes 24608 | tf_op jit(solution)/shard_map/ppermute | solution.py:13
  (51 shorter events, 5.1 us)
Async XLA Ops:
  0.0 7.4 %copy-start.2 = (s32[1,15]{1,0:T(1,128)S(1)}, s32[1,15]{1,0:T(1,128)}, u32[]{:S(2)}) copy-start(s32[1,15]{1,0:T(1,128)} %param.5) | copy-start | bytes 184
  0.0 24.4 %copy-start = (bf16[1,1,15,128,128]{4,3,2,1,0:T(8,128)(2,1)S(1)}, bf16[1,1,15,128,128]{4,3,2,1,0:T(8,128)(2,1)}, u32[]{:S(2)}) copy-start(bf16[1,1,15,128,128]{4,3,2,1,0:T(8,128)(2,1)} %param.4) | copy-start | bytes 1474564
  3.1 11.0 %all-to-all-start = ((bf16[4,128,256]{1,2,0:T(8,128)(2,1)}), bf16[4,128,256]{1,2,0:T(8,128)(2,1)S(1)}, u32[]{:S(2)}, u32[]{:S(2)}) async-start(bf16[4,128,256]{1,2,0:T(8,128)(2,1)} %bitcast.1), calls=%async_computation | async-start | bytes 524288 | tf_op jit(solution)/shard_map/all_to_all | solution.py:30
  14.1 18.7 %collective-permute-start = (bf16[3,128,256]{1,2,0:T(8,128)(2,1)S(1)}, bf16[3,128,256]{1,2,0:T(8,128)(2,1)S(1)}, u32[]{:S(2)}, u32[]{:S(2)}) collective-permute-start(bf16[3,128,256]{1,2,0:T(8,128)(2,1)S(1)} %get-tuple-element.6), channel_id=1, source_target_pairs={{0,8},{4,12},{8,16},{12,20},{16,24},{20,28},{24,32},{28,36},{32,40... | collective-permute-start | bytes 589832 | tf_op jit(solution)/shard_map/ppermute | solution.py:13
  20.5 14.6 %collective-permute-start.1 = (bf16[4,128,256]{1,2,0:T(8,128)(2,1)S(1)}, bf16[4,128,256]{1,2,0:T(8,128)(2,1)S(1)}, u32[]{:S(2)}, u32[]{:S(2)}) collective-permute-start(bf16[4,128,256]{1,2,0:T(8,128)(2,1)S(1)} %all-to-all-done), channel_id=1, source_target_pairs={{0,4},{4,8},{8,12},{12,16},{16,20},{20,24},{24,28},{28,32},{32,36}... | collective-permute-start | bytes 786440 | tf_op jit(solution)/shard_map/ppermute | solution.py:13
  24.5 19.8 %collective-permute-start.5 = (bf16[15,128,128]{2,1,0:T(8,128)(2,1)S(1)}, bf16[15,128,128]{2,1,0:T(8,128)(2,1)}, u32[]{:S(2)}, u32[]{:S(2)}) collective-permute-start(bf16[15,128,128]{2,1,0:T(8,128)(2,1)S(1)} %bitcast_multiply_fusion), channel_id=1, source_target_pairs={{0,3},{1,0},{2,1},{3,2},{4,7},{5,4},{6,5},{7,6},{8,11},{9,8},{10,9... | collective-permute-start | bytes 1474568 | tf_op jit(solution)/shard_map/ppermute | solution.py:13
  27.6 18.7 %collective-permute-start.7 = (bf16[15,128,128]{2,1,0:T(8,128)(2,1)S(1)}, bf16[15,128,128]{2,1,0:T(8,128)(2,1)}, u32[]{:S(2)}, u32[]{:S(2)}) collective-permute-start(bf16[15,128,128]{2,1,0:T(8,128)(2,1)S(1)} %bitcast_multiply_fusion), channel_id=1, source_target_pairs={{0,2},{1,3},{2,0},{3,1},{4,6},{5,7},{6,4},{7,5},{8,10},{9,11},{10,... | collective-permute-start | bytes 1474568 | tf_op jit(solution)/shard_map/ppermute | solution.py:13
  30.9 21.3 %collective-permute-start.9 = (bf16[15,128,128]{2,1,0:T(8,128)(2,1)S(1)}, bf16[15,128,128]{2,1,0:T(8,128)(2,1)}, u32[]{:S(2)}, u32[]{:S(2)}) collective-permute-start(bf16[15,128,128]{2,1,0:T(8,128)(2,1)S(1)} %bitcast_multiply_fusion), channel_id=1, source_target_pairs={{0,1},{1,2},{2,3},{3,0},{4,5},{5,6},{6,7},{7,4},{8,9},{9,10},{10,1... | collective-permute-start | bytes 1474568 | tf_op jit(solution)/shard_map/ppermute | solution.py:13
  32.9 9.5 %collective-permute-start.2 = (bf16[4,128,256]{1,2,0:T(8,128)(2,1)S(1)}, bf16[4,128,256]{1,2,0:T(8,128)(2,1)S(1)}, u32[]{:S(2)}, u32[]{:S(2)}) collective-permute-start(bf16[4,128,256]{1,2,0:T(8,128)(2,1)S(1)} %all-to-all-done), channel_id=1, source_target_pairs={{0,60},{4,0},{8,4},{12,8},{16,12},{20,16},{24,20},{28,24},{32,28},... | collective-permute-start | bytes 786440 | tf_op jit(solution)/shard_map/ppermute | solution.py:13
  35.1 19.6 %collective-permute-start.4 = (bf16[15,128,128]{2,1,0:T(8,128)(2,1)S(1)}, bf16[15,128,128]{2,1,0:T(8,128)(2,1)S(1)}, u32[]{:S(2)}, u32[]{:S(2)}) collective-permute-start(bf16[15,128,128]{2,1,0:T(8,128)(2,1)S(1)} %bitcast_multiply_fusion), channel_id=1, source_target_pairs={{0,64},{64,0},{1,65},{65,1},{2,66},{66,2},{3,67},{67,3},{4,68},{68... | collective-permute-start | bytes 1474568 | tf_op jit(solution)/shard_map/ppermute | solution.py:13
  42.4 12.2 %collective-permute-start.3 = (bf16[3,128,256]{1,2,0:T(8,128)(2,1)S(1)}, bf16[3,128,256]{1,2,0:T(8,128)(2,1)S(1)}, u32[]{:S(2)}, u32[]{:S(2)}) collective-permute-start(bf16[3,128,256]{1,2,0:T(8,128)(2,1)S(1)} %get-tuple-element.5), channel_id=1, source_target_pairs={{0,56},{4,60},{8,0},{12,4},{16,8},{20,12},{24,16},{28,20},{32,24},... | collective-permute-start | bytes 589832 | tf_op jit(solution)/shard_map/ppermute | solution.py:13
  44.3 11.5 %collective-permute-start.6 = (bf16[15,128,128]{2,1,0:T(8,128)(2,1)}, bf16[15,128,128]{2,1,0:T(8,128)(2,1)}, u32[]{:S(2)}, u32[]{:S(2)}) collective-permute-start(bf16[15,128,128]{2,1,0:T(8,128)(2,1)} %collective-permute-done.5), channel_id=1, source_target_pairs={{0,64},{64,0},{1,65},{65,1},{2,66},{66,2},{3,67},{67,3},{4,68},{68... | collective-permute-start | bytes 1474568 | tf_op jit(solution)/shard_map/ppermute | solution.py:13
  46.3 11.6 %collective-permute-start.8 = (bf16[15,128,128]{2,1,0:T(8,128)(2,1)}, bf16[15,128,128]{2,1,0:T(8,128)(2,1)}, u32[]{:S(2)}, u32[]{:S(2)}) collective-permute-start(bf16[15,128,128]{2,1,0:T(8,128)(2,1)} %collective-permute-done.7), channel_id=1, source_target_pairs={{0,64},{64,0},{1,65},{65,1},{2,66},{66,2},{3,67},{67,3},{4,68},{68... | collective-permute-start | bytes 1474568 | tf_op jit(solution)/shard_map/ppermute | solution.py:13
  52.3 7.7 %collective-permute-start.10 = (bf16[15,128,128]{2,1,0:T(8,128)(2,1)}, bf16[15,128,128]{2,1,0:T(8,128)(2,1)}, u32[]{:S(2)}, u32[]{:S(2)}) collective-permute-start(bf16[15,128,128]{2,1,0:T(8,128)(2,1)} %collective-permute-done.9), channel_id=1, source_target_pairs={{0,64},{64,0},{1,65},{65,1},{2,66},{66,2},{3,67},{67,3},{4,68},{68... | collective-permute-start | bytes 1474568 | tf_op jit(solution)/shard_map/ppermute | solution.py:13
  54.6 1.0 copy-start.1
  62.3 17.1 %collective-permute-start.12 = (bf16[4,128,512]{2,1,0:T(8,128)(2,1)S(1)}, bf16[4,128,512]{2,1,0:T(8,128)(2,1)S(1)}, u32[]{:S(2)}, u32[]{:S(2)}) collective-permute-start(bf16[4,128,512]{2,1,0:T(8,128)(2,1)S(1)} %constant_dynamic-slice_fusion.1), channel_id=1, source_target_pairs={{0,60},{4,0},{8,4},{12,8},{16,12},{20,16},{24,20},{28,24},{32,28},... | collective-permute-start | bytes 1572872 | tf_op jit(solution)/shard_map/ppermute | solution.py:13
  64.2 16.3 %collective-permute-start.11 = (bf16[4,128,512]{2,1,0:T(8,128)(2,1)S(1)}, bf16[4,128,512]{2,1,0:T(8,128)(2,1)S(1)}, u32[]{:S(2)}, u32[]{:S(2)}) collective-permute-start(bf16[4,128,512]{2,1,0:T(8,128)(2,1)S(1)} %constant_dynamic-slice_fusion.1), channel_id=1, source_target_pairs={{0,4},{4,8},{8,12},{12,16},{16,20},{20,24},{24,28},{28,32},{32,36}... | collective-permute-start | bytes 1572872 | tf_op jit(solution)/shard_map/ppermute | solution.py:13
  80.7 5.4 %collective-permute-start.13 = (bf16[3,4,128,512]{3,2,1,0:T(8,128)(2,1)S(1)}, bf16[3,4,128,512]{3,2,1,0:T(8,128)(2,1)}, u32[]{:S(2)}, u32[]{:S(2)}) collective-permute-start(bf16[3,4,128,512]{3,2,1,0:T(8,128)(2,1)S(1)} %pad_maximum_fusion.1), channel_id=1, source_target_pairs={{0,64},{64,0},{1,65},{65,1},{2,66},{66,2},{3,67},{67,3},{4,68},{68... | collective-permute-start | bytes 4718600 | tf_op jit(solution)/shard_map/ppermute | solution.py:13
  112.0 7.6 %collective-permute-start.14 = (f32[3,16,128]{2,1,0:T(8,128)S(1)}, f32[3,16,128]{2,1,0:T(8,128)S(1)}, u32[]{:S(2)}, u32[]{:S(2)}) collective-permute-start(f32[3,16,128]{2,1,0:T(8,128)S(1)} %slice.43), channel_id=1, source_target_pairs={{0,4},{4,8},{8,12},{12,16},{16,20},{20,24},{24,28},{28,32},{32,36}... | collective-permute-start | bytes 73736 | tf_op jit(solution)/shard_map/ppermute | solution.py:13
  117.6 6.9 %collective-permute-start.15 = (f32[3,16,128]{2,1,0:T(8,128)S(1)}, f32[3,16,128]{2,1,0:T(8,128)S(1)}, u32[]{:S(2)}, u32[]{:S(2)}) collective-permute-start(f32[3,16,128]{2,1,0:T(8,128)S(1)} %slice.43), channel_id=1, source_target_pairs={{0,60},{4,0},{8,4},{12,8},{16,12},{20,16},{24,20},{28,24},{32,28},... | collective-permute-start | bytes 73736 | tf_op jit(solution)/shard_map/ppermute | solution.py:13

commit v2 on v1

v2 whole, which is shorter than its diff:
```python
import jax
import jax.numpy as jnp
from jax import lax
from jax.experimental import pallas as pl
from jax.experimental.pallas import tpu as pltpu
from jax.sharding import Mesh, PartitionSpec as P

ROWS = 128
WIDE = 256
SPAN = 15
PLANE = 512
F32 = jnp.float32
BF16 = jnp.bfloat16


def moved(x, axis, by):
    n = lax.axis_size(axis)
    return lax.ppermute(x, axis, [(i, (i + by) % n) for i in range(n)])


def half_kernel(tiles, below2, below, plane, above, above2, half, window):
    @pl.when(pl.program_id(0) == 0)
    def _():
        at = 0
        for part in (below2, below, plane, above, above2):
            n = part.shape[0] * ROWS
            window[pl.ds(at, n), :] = part[...].reshape(n, WIDE)
            at += n

    a = pl.program_id(0)
    near = window[pl.ds(pl.multiple_of(a * ROWS, ROWS), SPAN * ROWS), :]
    for p in range(2):
        wide = jnp.concatenate([tiles[0, p, s] for s in range(SPAN)], 1)
        made = jnp.dot(wide, near, preferred_element_type=F32)
        half[:, p * WIDE : (p + 1) * WIDE] = made.astype(BF16)


def make_half(tiles, parts):
    whole = [pl.BlockSpec(p.shape, lambda a: (0, 0, 0)) for p in parts]
    return pl.pallas_call(
        half_kernel,
        grid=(4,),
        in_specs=[pl.BlockSpec((1, 2, SPAN, ROWS, ROWS), lambda a: (a, 0, 0, 0, 0))] + whole,
        out_specs=pl.BlockSpec((ROWS, 2 * WIDE), lambda a: (a, 0)),
        out_shape=jax.ShapeDtypeStruct((PLANE, 2 * WIDE), BF16),
        scratch_shapes=[pltpu.VMEM((18 * ROWS, WIDE), BF16)],
        compiler_params=pltpu.CompilerParams(vmem_limit_bytes=32 * 2**20),
        name="make_half",
    )(tiles, *parts)


def dot_t(a, b):
    return lax.dot_general(a, b, (((1,), (1,)), ((), ())), preferred_element_type=F32)


def tile_kernel(core, own, own2, up, up2, down, down2, out, mine, lower, upper):
    shift = core[0] * 16
    for k in range(16):
        at = pl.ds(pl.multiple_of(k * 32 + shift, 16), 16)
        to = pl.ds(k * 16, 16)
        for rows, first, second in ((mine, own, own2), (lower, up, up2), (upper, down, down2)):
            rows[to, :PLANE] = first[at, :]
            rows[to, PLANE:] = second[at, :]

    def put(rows, r, n, first, second, b, m, at):
        pair = dot_t(rows[r : r + n, :PLANE], first[b : b + m, :])
        pair += dot_t(rows[r : r + n, PLANE:], second[b : b + m, :])
        out[r : r + n, at : at + m] = pair.astype(BF16)

    for i, (first, second) in enumerate(((up, up2), (own, own2), (down, down2))):
        put(mine, 0, 256, first, second, 0, PLANE, i * PLANE)
    for x in range(4):
        if x > 0:
            put(lower, x * 64, 64, down, down2, 0, x * ROWS, 3 * PLANE)
        if x < 3:
            put(upper, x * 64, 64, up, up2, (x + 1) * ROWS, (3 - x) * ROWS, 3 * PLANE + x * ROWS)


def make_tiles(core, *halves):
    vmem = pl.BlockSpec(memory_space=pltpu.VMEM)
    return pl.pallas_call(
        tile_kernel,
        in_specs=[pl.BlockSpec(memory_space=pltpu.SMEM)] + [vmem] * 6,
        out_specs=vmem,
        out_shape=jax.ShapeDtypeStruct((256, SPAN * ROWS), BF16),
        scratch_shapes=[pltpu.VMEM((256, 2 * PLANE), BF16)] * 3,
        compiler_params=pltpu.CompilerParams(vmem_limit_bytes=32 * 2**20),
        name="make_tiles",
    )(core, *halves)


def per_device(occupied, integrals, pair_mask):
    x = lax.axis_index("x")
    core = lax.axis_index("core")
    mask_row = pair_mask[0]
    tiles = integrals[0, 0] * mask_row.astype(BF16)[:, None, None]
    gathered = lax.all_gather(tiles, ("x", "core")).reshape(4, 2, SPAN, ROWS, ROWS)

    rows = lax.dynamic_slice_in_dim(occupied, core * 64, 64, 0).reshape(64, 8, WIDE)
    plane = lax.all_to_all(rows.transpose(1, 0, 2), ("x", "core"), 0, 0)
    plane = plane.reshape(4, ROWS, WIDE)
    below2 = moved(plane[1:], "z", 2)
    above2 = moved(plane[:3], "z", -2)
    below = moved(plane, "z", 1)
    above = moved(plane, "z", -1)

    own = make_half(gathered, (below2, below, plane, above, above2))
    up = moved(own, "z", 1)
    down = moved(own, "z", -1)
    own2 = moved(own, "core", 1)
    up2 = moved(up, "core", 1)
    down2 = moved(down, "core", 1)
    partial = make_tiles(core[None], own, own2, up, up2, down, down2)
    partial = lax.all_to_all(partial.reshape(16, 16, SPAN * ROWS), ("x", "y"), 0, 0)
    total = partial.astype(F32).sum(0).reshape(16, SPAN, ROWS).transpose(1, 0, 2)
    far = total[12:]
    line = jnp.concatenate([moved(far, "z", 1), total[:12], moved(far, "z", -1)], 0)
    out = lax.dynamic_slice_in_dim(line, x, SPAN, 0)
    return (out * mask_row.astype(F32)[:, None, None])[None]


def solution(mesh):
    split = Mesh(mesh.devices.reshape(4, 2, 16, 4), ("y", "core", "z", "x"))
    aux, orb = ("y", "core"), ("z", "x")
    return jax.shard_map(
        per_device,
        mesh=split,
        in_specs=(P(orb, None), P(aux, orb, None, None, None), P(orb, None)),
        out_specs=P(orb, None, aux, None),
        check_vma=False,
    )
```

time: 126 us -> 124 us (0.984)
  the two profiles are of different devices: /device:TPU:96 before, /device:TPU:8 now
where the time goes in v2:
time: 124 us
  starting transfers between devices  40.7 us (33%)
  blocking collectives  32.7 us (26%)
  waiting for transfers between devices  27 us (22%)
  between operations  13.6 us (11%)
  Pallas kernels  3.85 us (3%)
  local copies, waits for them, and re-layouts  3 us (2%)
  other arithmetic  2.85 us (2%)
    ppermute x11, starting transfers between devices, moved(): return lax.ppermute(x, axis, [(i, (i + by) % n) for i in range(n)])  40.7 us
    ppermute x11, waiting for transfers between devices, moved(): return lax.ppermute(x, axis, [(i, (i + by) % n) for i in range(n)])  24.2 us
    all_to_all x1, blocking collectives, per_device(): lax.all_to_all(partial.reshape(16, 16, SPAN * ROWS), ('x', 'y'), 0, 0)  21.1 us
    all_to_all x1, blocking collectives, per_device(): plane = lax.all_to_all(rows.transpose(1, 0, 2), ('x', 'core'), 0, 0)  11.6 us
    all_gather x1, waiting for transfers between devices, per_device(): lax.all_gather(tiles, ('x', 'core')).reshape(4, 2, SPAN, ROWS, ROWS)  2.77 us
  transfers between devices with their start and end apart: 12, of which 7 were waited for; matrix products, arithmetic and copies ran while one was open for 0% of the time, Pallas kernels for 0%

profile of v2, /device:TPU:8, one launch (start us, length us, event | category | flops | bytes accessed | tf_op | source)
XLA Modules:
  0.0 123.7 jit_solution(15846597292627030414)
XLA Ops:
  6.5 0.7 convert_bitcast_fusion
  7.3 1.9 %bitcast_multiply_fusion = bf16[1,15,128,128]{3,2,1,0:T(8,128)(2,1)} fusion(bf16[1,1,15,128,128]{4,3,2,1,0:T(8,128)(2,1)} %param.4, bf16[15]{0:T(256)(128)(2,1)S(1)} %get-tuple-element.8), kind=kLoop, calls=%fused_computation.1 | loop fusion | flops 245760 | bytes 983070 | tf_op jit(solution)/shard_map/mul | solution.py:96
  9.2 0.0 all-gather.2.cloned.1.call-update
  9.3 0.1 copy.10
  9.4 11.6 %all_to_all.10 = bf16[8,64,256]{2,1,0:T(8,128)(2,1)S(1)} all-to-all(bf16[8,64,256]{2,1,0:T(8,128)(2,1)S(1)} %copy.8), channel_id=1, replica_groups=mesh['y'=4,'core'=2,'z'=16,'x'=4] {'x','core'}, dimensions={0} | all-to-all | bytes 524288 | tf_op jit(solution)/shard_map/all_to_all | solution.py:100
  21.0 11.4 %collective-permute-start.2 = (bf16[4,128,256]{2,1,0:T(8,128)(2,1)S(1)}, bf16[4,128,256]{2,1,0:T(8,128)(2,1)S(1)}, u32[]{:S(2)}, u32[]{:S(2)}) collective-permute-start(bf16[4,128,256]{2,1,0:T(8,128)(2,1)S(1)} %bitcast.22), channel_id=1, source_target_pairs={{0,60},{4,0},{8,4},{12,8},{16,12},{20,16},{24,20},{28,24},{32,28},... | collective-permute-start | bytes 786440 | tf_op jit(solution)/shard_map/ppermute | solution.py:18
  32.4 1.9 %collective-permute-start.1 = (bf16[4,128,256]{2,1,0:T(8,128)(2,1)S(1)}, bf16[4,128,256]{2,1,0:T(8,128)(2,1)S(1)}, u32[]{:S(2)}, u32[]{:S(2)}) collective-permute-start(bf16[4,128,256]{2,1,0:T(8,128)(2,1)S(1)} %bitcast.23), channel_id=1, source_target_pairs={{0,4},{4,8},{8,12},{12,16},{16,20},{20,24},{24,28},{28,32},{32,36}... | collective-permute-start | bytes 786440 | tf_op jit(solution)/shard_map/ppermute | solution.py:18
  34.4 1.9 %collective-permute-start = (bf16[3,128,256]{2,1,0:T(8,128)(2,1)S(1)}, bf16[3,128,256]{2,1,0:T(8,128)(2,1)S(1)}, u32[]{:S(2)}, u32[]{:S(2)}) collective-permute-start(bf16[3,128,256]{2,1,0:T(8,128)(2,1)S(1)} %bitcast.30), channel_id=1, source_target_pairs={{0,8},{4,12},{8,16},{12,20},{16,24},{20,28},{24,32},{28,36},{32,40... | collective-permute-start | bytes 589832 | tf_op jit(solution)/shard_map/ppermute | solution.py:18
  36.3 6.0 %collective-permute-start.3 = (bf16[3,128,256]{2,1,0:T(8,128)(2,1)S(1)}, bf16[3,128,256]{2,1,0:T(8,128)(2,1)S(1)}, u32[]{:S(2)}, u32[]{:S(2)}) collective-permute-start(bf16[3,128,256]{2,1,0:T(8,128)(2,1)S(1)} %bitcast.29), channel_id=1, source_target_pairs={{0,56},{4,60},{8,0},{12,4},{16,8},{20,12},{24,16},{28,20},{32,24},... | collective-permute-start | bytes 589832 | tf_op jit(solution)/shard_map/ppermute | solution.py:18
  42.3 6.2 %collective-permute-done.below2 = bf16[3,128,256]{2,1,0:T(8,128)(2,1)S(1)} collective-permute-done((bf16[3,128,256]{2,1,0:T(8,128)(2,1)S(1)}, bf16[3,128,256]{2,1,0:T(8,128)(2,1)S(1)}, u32[]{:S(2)}, u32[]{:S(2)}) %collective-permute-start) | collective-permute-done | bytes 196640 | tf_op jit(solution)/shard_map/ppermute | solution.py:18
  48.6 1.2 %collective-permute-done.3.above2 = bf16[3,128,256]{2,1,0:T(8,128)(2,1)S(1)} collective-permute-done((bf16[3,128,256]{2,1,0:T(8,128)(2,1)S(1)}, bf16[3,128,256]{2,1,0:T(8,128)(2,1)S(1)}, u32[]{:S(2)}, u32[]{:S(2)}) %collective-permute-start.3) | collective-permute-done | bytes 196640 | tf_op jit(solution)/shard_map/ppermute | solution.py:18
  49.8 0.0 collective-permute-done.1.below
  49.8 2.8 %all-gather.2.cloned.1.call-done = bf16[8,15,128,128]{3,2,1,0:T(8,128)(2,1)} async-done(((bf16[1,15,128,128]{3,2,1,0:T(8,128)(2,1)}), bf16[8,15,128,128]{3,2,1,0:T(8,128)(2,1)}) %all-gather.2.cloned.1.call-update) | async-done | bytes 3932176 | tf_op jit(solution)/shard_map/all_gather | solution.py:97
  52.6 2.1 %copy-done.1 = bf16[8,15,128,128]{3,2,1,0:T(8,128)(2,1)S(1)} copy-done((bf16[8,15,128,128]{3,2,1,0:T(8,128)(2,1)S(1)}, bf16[8,15,128,128]{3,2,1,0:T(8,128)(2,1)}, u32[]{:S(2)}) %copy-start.1) | copy-done | bytes 3932184
  54.7 1.9 %make_half.1.own = bf16[512,512]{1,0:T(8,128)(2,1)S(1)} custom-call(bf16[4,2,15,128,128]{4,3,2,1,0:T(8,128)(2,1)S(1)} %bitcast.20, bf16[3,128,256]{2,1,0:T(8,128)(2,1)S(1)} %collective-permute-done.below2, bf16[4,128,256]{2,1,0:T(8,128)(2,1)S(1)} %collective-permute-done.1.below, bf16[4,128,256]{2,1,0:T(8,128)(2,1)S(1)} %bitcast.24, ...), custom_call_target="tpu_custom_call" | custom-call | tf_op jit(solution)/shard_map/make_half/pallas_call | solution.py:40
  56.6 5.9 %collective-permute-start.7 = (bf16[512,512]{1,0:T(8,128)(2,1)S(1)}, bf16[512,512]{1,0:T(8,128)(2,1)S(1)}, u32[]{:S(2)}, u32[]{:S(2)}) collective-permute-start(bf16[512,512]{1,0:T(8,128)(2,1)S(1)} %make_half.1.own), channel_id=1, source_target_pairs={{0,60},{4,0},{8,4},{12,8},{16,12},{20,16},{24,20},{28,24},{32,28},... | collective-permute-start | bytes 1572872 | tf_op jit(solution)/shard_map/ppermute | solution.py:18
  62.6 1.9 %collective-permute-start.5 = (bf16[512,512]{1,0:T(8,128)(2,1)S(1)}, bf16[512,512]{1,0:T(8,128)(2,1)S(1)}, u32[]{:S(2)}, u32[]{:S(2)}) collective-permute-start(bf16[512,512]{1,0:T(8,128)(2,1)S(1)} %make_half.1.own), channel_id=1, source_target_pairs={{0,4},{4,8},{8,12},{12,16},{16,20},{20,24},{24,28},{28,32},{32,36}... | collective-permute-start | bytes 1572872 | tf_op jit(solution)/shard_map/ppermute | solution.py:18
  64.5 1.9 %collective-permute-start.4 = (bf16[512,512]{1,0:T(8,128)(2,1)S(1)}, bf16[512,512]{1,0:T(8,128)(2,1)S(1)}, u32[]{:S(2)}, u32[]{:S(2)}) collective-permute-start(bf16[512,512]{1,0:T(8,128)(2,1)S(1)} %make_half.1.own), channel_id=1, source_target_pairs={{0,64},{64,0},{1,65},{65,1},{2,66},{66,2},{3,67},{67,3},{4,68},{68... | collective-permute-start | bytes 1572872 | tf_op jit(solution)/shard_map/ppermute | solution.py:18
  66.4 7.7 %collective-permute-done.7.down = bf16[512,512]{1,0:T(8,128)(2,1)S(1)} collective-permute-done((bf16[512,512]{1,0:T(8,128)(2,1)S(1)}, bf16[512,512]{1,0:T(8,128)(2,1)S(1)}, u32[]{:S(2)}, u32[]{:S(2)}) %collective-permute-start.7) | collective-permute-done | bytes 524320 | tf_op jit(solution)/shard_map/ppermute | solution.py:18
  74.1 1.9 %collective-permute-start.8 = (bf16[512,512]{1,0:T(8,128)(2,1)S(1)}, bf16[512,512]{1,0:T(8,128)(2,1)S(1)}, u32[]{:S(2)}, u32[]{:S(2)}) collective-permute-start(bf16[512,512]{1,0:T(8,128)(2,1)S(1)} %collective-permute-done.7.down), channel_id=1, source_target_pairs={{0,64},{64,0},{1,65},{65,1},{2,66},{66,2},{3,67},{67,3},{4,68},{68... | collective-permute-start | bytes 1572872 | tf_op jit(solution)/shard_map/ppermute | solution.py:18
  76.1 3.4 %collective-permute-done.5.up = bf16[512,512]{1,0:T(8,128)(2,1)S(1)} collective-permute-done((bf16[512,512]{1,0:T(8,128)(2,1)S(1)}, bf16[512,512]{1,0:T(8,128)(2,1)S(1)}, u32[]{:S(2)}, u32[]{:S(2)}) %collective-permute-start.5) | collective-permute-done | bytes 524320 | tf_op jit(solution)/shard_map/ppermute | solution.py:18
  79.5 1.9 %collective-permute-start.6 = (bf16[512,512]{1,0:T(8,128)(2,1)S(1)}, bf16[512,512]{1,0:T(8,128)(2,1)S(1)}, u32[]{:S(2)}, u32[]{:S(2)}) collective-permute-start(bf16[512,512]{1,0:T(8,128)(2,1)S(1)} %collective-permute-done.5.up), channel_id=1, source_target_pairs={{0,64},{64,0},{1,65},{65,1},{2,66},{66,2},{3,67},{67,3},{4,68},{68... | collective-permute-start | bytes 1572872 | tf_op jit(solution)/shard_map/ppermute | solution.py:18
  81.4 0.0 collective-permute-done.4.own2
  81.4 1.9 %collective-permute-done.6.up2 = bf16[512,512]{1,0:T(8,128)(2,1)S(1)} collective-permute-done((bf16[512,512]{1,0:T(8,128)(2,1)S(1)}, bf16[512,512]{1,0:T(8,128)(2,1)S(1)}, u32[]{:S(2)}, u32[]{:S(2)}) %collective-permute-start.6) | collective-permute-done | bytes 524320 | tf_op jit(solution)/shard_map/ppermute | solution.py:18
  83.3 1.9 %make_tiles.1 = bf16[256,1920]{1,0:T(8,128)(2,1)S(1)} custom-call(s32[1]{0:T(128)} %bitcast.core, bf16[512,512]{1,0:T(8,128)(2,1)S(1)} %make_half.1.own, bf16[512,512]{1,0:T(8,128)(2,1)S(1)} %collective-permute-done.4.own2, bf16[512,512]{1,0:T(8,128)(2,1)S(1)} %collective-permute-done.5.up, bf16[512,512]{1,0:T(8,128)(2,1)S(1)} %collective-permute-done.6.up2, ...), custom_call_target="tpu_custom_call" | custom-call | tf_op jit(solution)/shard_map/make_tiles/pallas_call | solution.py:81
  85.2 21.1 %all_to_all.11 = bf16[16,16,1920]{2,1,0:T(8,128)(2,1)S(1)} all-to-all(bf16[16,16,1920]{2,1,0:T(8,128)(2,1)S(1)} %bitcast.21), channel_id=1, replica_groups=mesh['y'=4,'core'=2,'z'=16,'x'=4] {'x','y'}, dimensions={0} | all-to-all | bytes 1966080 | tf_op jit(solution)/shard_map/all_to_all | solution.py:114
  106.3 0.1 convert_reduce_fusion
  106.5 2.6 %collective-permute-start.10 = (f32[3,16,128]{2,0,1:T(4,128)S(1)}, f32[3,16,128]{2,0,1:T(4,128)S(1)}, u32[]{:S(2)}, u32[]{:S(2)}) collective-permute-start(f32[3,16,128]{2,0,1:T(4,128)S(1)} %slice.26), channel_id=1, source_target_pairs={{0,60},{4,0},{8,4},{12,8},{16,12},{20,16},{24,20},{28,24},{32,28},... | collective-permute-start | bytes 73736 | tf_op jit(solution)/shard_map/ppermute | solution.py:18
  109.0 3.3 %collective-permute-start.9 = (f32[3,16,128]{2,0,1:T(4,128)S(1)}, f32[3,16,128]{2,0,1:T(4,128)S(1)}, u32[]{:S(2)}, u32[]{:S(2)}) collective-permute-start(f32[3,16,128]{2,0,1:T(4,128)S(1)} %slice.26), channel_id=1, source_target_pairs={{0,4},{4,8},{8,12},{12,16},{16,20},{20,24},{24,28},{28,32},{32,36}... | collective-permute-start | bytes 73736 | tf_op jit(solution)/shard_map/ppermute | solution.py:18
  112.3 3.7 %collective-permute-done.9 = f32[3,16,128]{2,0,1:T(4,128)S(1)} collective-permute-done((f32[3,16,128]{2,0,1:T(4,128)S(1)}, f32[3,16,128]{2,0,1:T(4,128)S(1)}, u32[]{:S(2)}, u32[]{:S(2)}) %collective-permute-start.9) | collective-permute-done | bytes 24608 | tf_op jit(solution)/shard_map/ppermute | solution.py:18
  116.1 0.1 fusion.3
  116.1 0.7 copy.9
  (12 shorter events, 0.2 us)
Async XLA Ops:
  6.5 2.7 %copy-start = (bf16[128,2048]{1,0:T(8,128)(2,1)S(1)}, bf16[128,2048]{1,0:T(8,128)(2,1)}, u32[]{:S(2)}) copy-start(bf16[128,2048]{1,0:T(8,128)(2,1)} %param.3) | copy-start | bytes 1572868
  6.5 46.0 %all-gather.2.cloned.1.call-start = ((), (), s32[]{:S(2)}) async-start(), calls=%async_computation.2 | async-start | bytes 4423680 | tf_op jit(solution)/shard_map/all_gather | solution.py:97
  21.0 28.8 %collective-permute-start.2 = (bf16[4,128,256]{2,1,0:T(8,128)(2,1)S(1)}, bf16[4,128,256]{2,1,0:T(8,128)(2,1)S(1)}, u32[]{:S(2)}, u32[]{:S(2)}) collective-permute-start(bf16[4,128,256]{2,1,0:T(8,128)(2,1)S(1)} %bitcast.22), channel_id=1, source_target_pairs={{0,60},{4,0},{8,4},{12,8},{16,12},{20,16},{24,20},{28,24},{32,28},... | collective-permute-start | bytes 786440 | tf_op jit(solution)/shard_map/ppermute | solution.py:18
  32.4 17.4 %collective-permute-start.1 = (bf16[4,128,256]{2,1,0:T(8,128)(2,1)S(1)}, bf16[4,128,256]{2,1,0:T(8,128)(2,1)S(1)}, u32[]{:S(2)}, u32[]{:S(2)}) collective-permute-start(bf16[4,128,256]{2,1,0:T(8,128)(2,1)S(1)} %bitcast.23), channel_id=1, source_target_pairs={{0,4},{4,8},{8,12},{12,16},{16,20},{20,24},{24,28},{28,32},{32,36}... | collective-permute-start | bytes 786440 | tf_op jit(solution)/shard_map/ppermute | solution.py:18
  34.4 14.2 %collective-permute-start = (bf16[3,128,256]{2,1,0:T(8,128)(2,1)S(1)}, bf16[3,128,256]{2,1,0:T(8,128)(2,1)S(1)}, u32[]{:S(2)}, u32[]{:S(2)}) collective-permute-start(bf16[3,128,256]{2,1,0:T(8,128)(2,1)S(1)} %bitcast.30), channel_id=1, source_target_pairs={{0,8},{4,12},{8,16},{12,20},{16,24},{20,28},{24,32},{28,36},{32,40... | collective-permute-start | bytes 589832 | tf_op jit(solution)/shard_map/ppermute | solution.py:18
  36.3 13.5 %collective-permute-start.3 = (bf16[3,128,256]{2,1,0:T(8,128)(2,1)S(1)}, bf16[3,128,256]{2,1,0:T(8,128)(2,1)S(1)}, u32[]{:S(2)}, u32[]{:S(2)}) collective-permute-start(bf16[3,128,256]{2,1,0:T(8,128)(2,1)S(1)} %bitcast.29), channel_id=1, source_target_pairs={{0,56},{4,60},{8,0},{12,4},{16,8},{20,12},{24,16},{28,20},{32,24},... | collective-permute-start | bytes 589832 | tf_op jit(solution)/shard_map/ppermute | solution.py:18
  52.6 2.1 %copy-start.1 = (bf16[8,15,128,128]{3,2,1,0:T(8,128)(2,1)S(1)}, bf16[8,15,128,128]{3,2,1,0:T(8,128)(2,1)}, u32[]{:S(2)}) copy-start(bf16[8,15,128,128]{3,2,1,0:T(8,128)(2,1)} %all-gather.2.cloned.1.call-done) | copy-start | bytes 11796484
  56.6 17.5 %collective-permute-start.7 = (bf16[512,512]{1,0:T(8,128)(2,1)S(1)}, bf16[512,512]{1,0:T(8,128)(2,1)S(1)}, u32[]{:S(2)}, u32[]{:S(2)}) collective-permute-start(bf16[512,512]{1,0:T(8,128)(2,1)S(1)} %make_half.1.own), channel_id=1, source_target_pairs={{0,60},{4,0},{8,4},{12,8},{16,12},{20,16},{24,20},{28,24},{32,28},... | collective-permute-start | bytes 1572872 | tf_op jit(solution)/shard_map/ppermute | solution.py:18
  62.6 16.9 %collective-permute-start.5 = (bf16[512,512]{1,0:T(8,128)(2,1)S(1)}, bf16[512,512]{1,0:T(8,128)(2,1)S(1)}, u32[]{:S(2)}, u32[]{:S(2)}) collective-permute-start(bf16[512,512]{1,0:T(8,128)(2,1)S(1)} %make_half.1.own), channel_id=1, source_target_pairs={{0,4},{4,8},{8,12},{12,16},{16,20},{20,24},{24,28},{28,32},{32,36}... | collective-permute-start | bytes 1572872 | tf_op jit(solution)/shard_map/ppermute | solution.py:18
  64.5 16.9 %collective-permute-start.4 = (bf16[512,512]{1,0:T(8,128)(2,1)S(1)}, bf16[512,512]{1,0:T(8,128)(2,1)S(1)}, u32[]{:S(2)}, u32[]{:S(2)}) collective-permute-start(bf16[512,512]{1,0:T(8,128)(2,1)S(1)} %make_half.1.own), channel_id=1, source_target_pairs={{0,64},{64,0},{1,65},{65,1},{2,66},{66,2},{3,67},{67,3},{4,68},{68... | collective-permute-start | bytes 1572872 | tf_op jit(solution)/shard_map/ppermute | solution.py:18
  74.1 7.3 %collective-permute-start.8 = (bf16[512,512]{1,0:T(8,128)(2,1)S(1)}, bf16[512,512]{1,0:T(8,128)(2,1)S(1)}, u32[]{:S(2)}, u32[]{:S(2)}) collective-permute-start(bf16[512,512]{1,0:T(8,128)(2,1)S(1)} %collective-permute-done.7.down), channel_id=1, source_target_pairs={{0,64},{64,0},{1,65},{65,1},{2,66},{66,2},{3,67},{67,3},{4,68},{68... | collective-permute-start | bytes 1572872 | tf_op jit(solution)/shard_map/ppermute | solution.py:18
  79.5 3.8 %collective-permute-start.6 = (bf16[512,512]{1,0:T(8,128)(2,1)S(1)}, bf16[512,512]{1,0:T(8,128)(2,1)S(1)}, u32[]{:S(2)}, u32[]{:S(2)}) collective-permute-start(bf16[512,512]{1,0:T(8,128)(2,1)S(1)} %collective-permute-done.5.up), channel_id=1, source_target_pairs={{0,64},{64,0},{1,65},{65,1},{2,66},{66,2},{3,67},{67,3},{4,68},{68... | collective-permute-start | bytes 1572872 | tf_op jit(solution)/shard_map/ppermute | solution.py:18
  106.5 5.9 %collective-permute-start.10 = (f32[3,16,128]{2,0,1:T(4,128)S(1)}, f32[3,16,128]{2,0,1:T(4,128)S(1)}, u32[]{:S(2)}, u32[]{:S(2)}) collective-permute-start(f32[3,16,128]{2,0,1:T(4,128)S(1)} %slice.26), channel_id=1, source_target_pairs={{0,60},{4,0},{8,4},{12,8},{16,12},{20,16},{24,20},{28,24},{32,28},... | collective-permute-start | bytes 73736 | tf_op jit(solution)/shard_map/ppermute | solution.py:18
  109.0 7.0 %collective-permute-start.9 = (f32[3,16,128]{2,0,1:T(4,128)S(1)}, f32[3,16,128]{2,0,1:T(4,128)S(1)}, u32[]{:S(2)}, u32[]{:S(2)}) collective-permute-start(f32[3,16,128]{2,0,1:T(4,128)S(1)} %slice.26), channel_id=1, source_target_pairs={{0,4},{4,8},{8,12},{12,16},{16,20},{20,24},{24,28},{28,32},{32,36}... | collective-permute-start | bytes 73736 | tf_op jit(solution)/shard_map/ppermute | solution.py:18
Sparse Core Ops, SparseCore 0:
  9.5 43.0 all-gather.1

commit v3 on v1

v3 whole, which is shorter than its diff:
```python
import jax
import jax.numpy as jnp
from jax import lax
from jax.experimental import pallas as pl
from jax.experimental.pallas import tpu as pltpu
from jax.sharding import Mesh, PartitionSpec as P

ROWS = 128
HALF = 64
COLS = 512
SPAN = 15
F32 = jnp.float32
BF16 = jnp.bfloat16
VMEM = pl.BlockSpec(memory_space=pltpu.VMEM)
SMEM = pl.BlockSpec(memory_space=pltpu.SMEM)
ROOM = pltpu.CompilerParams(vmem_limit_bytes=12 * 2**20)


def moved(x, axis, by):
    n = lax.axis_size(axis)
    return lax.ppermute(x, axis, [(i, (i + by) % n) for i in range(n)])


def orbital_kernel(core, occupied, out):
    rows = occupied[pl.ds(pl.multiple_of(core[0] * HALF, HALF), HALF), :]
    for x in range(4):
        out[x] = rows[:, x * COLS : (x + 1) * COLS]


def integral_kernel(mask, integrals, out):
    for s in range(SPAN):
        tile = integrals[s]
        tile = jnp.where(mask[0, s] != 0, tile, jnp.zeros_like(tile))
        for core in range(2):
            for y in range(4):
                at = (2 * y + core) * 16
                for x in range(4):
                    out[x, core, s, y * 16 : y * 16 + 16, :] = tile[at : at + 16]


def half_kernel(core, tiles, below2, below, plane, above, above2, first, second, half, window):
    c = core[0]

    def place(part, blocks, at, where):
        for b in range(blocks.shape[0]):
            to = pl.multiple_of(at * ROWS + b * ROWS + where * HALF, HALF)
            window[pl.ds(to, HALF), :] = part[b]

    at = 0
    others = (first.at[4:7], second.at[0:4], first.at[0:4], second.at[4:8], first.at[7:10])
    for mine, other in zip((below2, below, plane, above, above2), others):
        place(mine, mine, at, c)
        place(other, mine, at, 1 - c)
        at += mine.shape[0]
    for a in range(4):
        near = window[a * ROWS : (a + SPAN) * ROWS, :]
        wide = jnp.concatenate(
            [tiles[2 * a : 2 * a + 2, s].reshape(2 * HALF, ROWS) for s in range(SPAN)], 1
        )
        made = jnp.dot(wide, near, preferred_element_type=F32).astype(BF16)
        half[a * HALF : (a + 1) * HALF, :COLS] = made[:HALF]
        half[a * HALF : (a + 1) * HALF, COLS:] = made[HALF:]


def dot_t(a, b):
    return lax.dot_general(a, b, (((1,), (1,)), ((), ())), preferred_element_type=F32)


def tile_kernel(core, up, own, down, up2, own2, down2, out, wide):
    c = core[0]
    for i, (mine, other) in enumerate(((up, up2), (own, own2), (down, down2))):
        for k in range(16):
            to = i * 512 + k * 32
            wide[pl.ds(pl.multiple_of(to + c * 16, 16), 16), :] = mine[k * 16 : k * 16 + 16, :]
            wide[pl.ds(pl.multiple_of(to + 16 - c * 16, 16), 16), :] = other[k * 16 : k * 16 + 16, :]
    for i in range(3):
        out[:, i * 512 : (i + 1) * 512] = dot_t(own[...], wide[i * 512 : (i + 1) * 512, :]).astype(BF16)
    for x in range(4):
        rows = slice(x * HALF, (x + 1) * HALF)
        cut = 1536 + x * ROWS
        if x > 0:
            out[rows, 1536:cut] = dot_t(up[rows, :], wide[1024 : 1024 + x * ROWS, :]).astype(BF16)
        if x < 3:
            out[rows, cut:] = dot_t(down[rows, :], wide[(x + 1) * ROWS : 512, :]).astype(BF16)


def per_device(occupied, integrals, pair_mask):
    x = lax.axis_index("x")
    core = lax.axis_index("core")[None]

    pieces = pl.pallas_call(
        orbital_kernel,
        in_specs=[SMEM, VMEM],
        out_specs=VMEM,
        out_shape=jax.ShapeDtypeStruct((4, HALF, COLS), BF16),
        compiler_params=ROOM,
        name="cut_orbitals",
    )(core, occupied)
    plane = lax.all_to_all(pieces, "x", 0, 0)

    tiles = pl.pallas_call(
        integral_kernel,
        in_specs=[SMEM, VMEM],
        out_specs=VMEM,
        out_shape=jax.ShapeDtypeStruct((4, 2, SPAN, HALF, ROWS), BF16),
        compiler_params=ROOM,
        name="cut_integrals",
    )(pair_mask, integrals[0, 0])
    tiles = lax.all_to_all(tiles.reshape(8, SPAN, HALF, ROWS), ("x", "core"), 0, 0)

    below2 = moved(plane[1:], "z", 2)
    above2 = moved(plane[:3], "z", -2)
    below = moved(plane, "z", 1)
    above = moved(plane, "z", -1)
    first = moved(jnp.concatenate([plane, below2, above2]), "core", 1)
    second = moved(jnp.concatenate([below, above]), "core", 1)

    own = pl.pallas_call(
        half_kernel,
        in_specs=[SMEM] + [VMEM] * 8,
        out_specs=VMEM,
        out_shape=jax.ShapeDtypeStruct((4 * HALF, 2 * COLS), BF16),
        scratch_shapes=[pltpu.VMEM((18 * ROWS, COLS), BF16)],
        compiler_params=ROOM,
        name="make_half",
    )(core, tiles, below2, below, plane, above, above2, first, second)

    up = moved(own, "z", 1)
    down = moved(own, "z", -1)
    own2 = moved(own, "core", 1)
    up2 = moved(up, "core", 1)
    down2 = moved(down, "core", 1)
    partial = pl.pallas_call(
        tile_kernel,
        in_specs=[SMEM] + [VMEM] * 6,
        out_specs=VMEM,
        out_shape=jax.ShapeDtypeStruct((256, SPAN * ROWS), BF16),
        scratch_shapes=[pltpu.VMEM((12 * ROWS, 2 * COLS), BF16)],
        compiler_params=ROOM,
        name="make_tiles",
    )(core, up, own, down, up2, own2, down2)
    partial = lax.all_to_all(partial.reshape(16, 16, SPAN * ROWS), ("x", "y"), 0, 0)
    total = partial.astype(F32).sum(0).reshape(16, SPAN, ROWS).transpose(1, 0, 2)
    far = total[12:]
    line = jnp.concatenate([moved(far, "z", 1), total[:12], moved(far, "z", -1)], 0)
    out = lax.dynamic_slice_in_dim(line, x, SPAN, 0)
    return (out * pair_mask[0].astype(F32)[:, None, None])[None]


def solution(mesh):
    split = Mesh(mesh.devices.reshape(4, 2, 16, 4), ("y", "core", "z", "x"))
    aux, orb = ("y", "core"), ("z", "x")
    return jax.shard_map(
        per_device,
        mesh=split,
        in_specs=(P(orb, None), P(aux, orb, None, None, None), P(orb, None)),
        out_specs=P(orb, None, aux, None),
        check_vma=False,
    )
```

time: 126 us -> 114 us (0.905)
  matrix products: 8.25 us -> 0 us
  starting transfers between devices: 51.5 us -> 44.7 us
  waiting for transfers between devices: 35.5 us -> 30.2 us
  Pallas kernels: 0 us -> 5.08 us
  local copies, waits for them, and re-layouts: 4.53 us -> 8.53 us
  other arithmetic: 2.91 us -> 0.34 us
  blocking collectives: 22 us -> 23.7 us
    ppermute x16 -> x13, starting transfers between devices: 47.2 us -> 36.8 us  [moved(): return lax.ppermute(x, axis, [(i, (i + by) % n) for i in range(n)])]
    dot_general x7 -> x0, matrix products: 8.25 us -> none  [the longest x4 6.32 us: per_device(): jnp.einsum('pomn,onk->mpk', both, near, preferred_element_type=jnp.float32)]
    unnamed x18, local copies, waits for them, and re-layouts: 1.82 us -> 7.78 us
    pallas_call x0 -> x4, Pallas kernels: none -> 5.08 us  [the longest x1 2.14 us: per_device(): pl.pallas_call(tile_kernel, in_specs=[SMEM] + [VMEM] * 6, out_specs=VMEM,...]
    all_to_all x1 -> x2, waiting for transfers between devices: 6.67 us -> 2.9 us  [the longest x1 2.89 us: per_device(): plane = lax.all_to_all(pieces, 'x', 0, 0)]
    all_to_all x1 -> x2, starting transfers between devices: 4.29 us -> 7.89 us  [the longest x1 4.29 us: per_device(): plane = lax.all_to_all(pieces, 'x', 0, 0)]
    all_to_all x1, blocking collectives: 22 us -> 23.7 us  [per_device(): lax.all_to_all(partial.reshape(16, 16, SPAN * ROWS), ('x', 'y'), 0, 0)]
    concatenate x2, other arithmetic: 1.66 us -> 0.12 us  [the longest x1 0.07 us: per_device(): first = moved(jnp.concatenate([plane, below2, above2]), 'core', 1)]
  transfers between devices with their start and end apart: 17 -> 15, of which waited for: 8 -> 9; matrix products, arithmetic and copies ran while one was open for 4% -> 0% of each run, Pallas kernels for 0% -> 1%
where the time goes in v3:
time: 114 us; the launch traced here: 113 us
  starting transfers between devices  44.7 us (39%)
  waiting for transfers between devices  30.2 us (26%)
  blocking collectives  23.7 us (21%)
  local copies, waits for them, and re-layouts  8.53 us (7%)
  Pallas kernels  5.08 us (4%)
    ppermute x13, starting transfers between devices, moved(): return lax.ppermute(x, axis, [(i, (i + by) % n) for i in range(n)])  36.8 us
    ppermute x13, waiting for transfers between devices, moved(): return lax.ppermute(x, axis, [(i, (i + by) % n) for i in range(n)])  27.3 us
    all_to_all x1, blocking collectives, per_device(): lax.all_to_all(partial.reshape(16, 16, SPAN * ROWS), ('x', 'y'), 0, 0)  23.7 us
    unnamed x18, local copies, waits for them, and re-layouts  7.78 us
    all_to_all x1, starting transfers between devices, per_device(): plane = lax.all_to_all(pieces, 'x', 0, 0)  4.29 us
    all_to_all x1, starting transfers between devices, per_device(): lax.all_to_all(tiles.reshape(8, SPAN, HALF, ROWS), ('x', 'core'), 0, 0)  3.6 us
    all_to_all x1, waiting for transfers between devices, per_device(): plane = lax.all_to_all(pieces, 'x', 0, 0)  2.89 us
  transfers between devices with their start and end apart: 15, of which 9 were waited for; matrix products, arithmetic and copies ran while one was open for 0% of the time, Pallas kernels for 1%

profile of v3, /device:TPU:96, one launch (start us, length us, event | category | flops | bytes accessed | tf_op | source)
XLA Modules:
  0.0 112.8 jit_solution(251150889972602627)
XLA Ops:
  0.0 1.0 copy-done.5
  1.8 4.3 %all-to-all-start.1 = ((bf16[4,64,512]{2,1,0:T(8,128)(2,1)}), bf16[4,64,512]{2,1,0:T(8,128)(2,1)S(1)}, u32[]{:S(2)}, u32[]{:S(2)}) async-start(bf16[4,64,512]{2,1,0:T(8,128)(2,1)} %cut_orbitals.1), calls=%async_computation.1 | async-start | bytes 524288 | tf_op jit(solution)/shard_map/all_to_all | solution.py:99
  6.1 1.0 copy-done.6
  8.6 1.3 %copy-done = bf16[4,2,15,64,128]{4,3,2,1,0:T(8,128)(2,1)} copy-done((bf16[4,2,15,64,128]{4,3,2,1,0:T(8,128)(2,1)}, bf16[4,2,15,64,128]{4,3,2,1,0:T(8,128)(2,1)S(1)}, u32[]{:S(2)}) %copy-start) | copy-done | bytes 1966104
  9.9 2.9 %all-to-all-done.1.plane = bf16[4,64,512]{2,1,0:T(8,128)(2,1)S(1)} async-done(((bf16[4,64,512]{2,1,0:T(8,128)(2,1)}), bf16[4,64,512]{2,1,0:T(8,128)(2,1)S(1)}, u32[]{:S(2)}, u32[]{:S(2)}) %all-to-all-start.1) | async-done | bytes 262176 | tf_op jit(solution)/shard_map/all_to_all | solution.py:99
  12.7 3.6 %all-to-all-start = ((bf16[8,15,64,128]{3,2,1,0:T(8,128)(2,1)}), bf16[8,15,64,128]{3,2,1,0:T(8,128)(2,1)S(1)}, u32[]{:S(2)}, u32[]{:S(2)}) async-start(bf16[8,15,64,128]{3,2,1,0:T(8,128)(2,1)} %bitcast.10), calls=%async_computation | async-start | bytes 3932160 | tf_op jit(solution)/shard_map/all_to_all | solution.py:109
  16.4 6.4 %collective-permute-start = (bf16[3,64,512]{2,1,0:T(8,128)(2,1)S(1)}, bf16[3,64,512]{2,1,0:T(8,128)(2,1)S(1)}, u32[]{:S(2)}, u32[]{:S(2)}) collective-permute-start(bf16[3,64,512]{2,1,0:T(8,128)(2,1)S(1)} %get-tuple-element.6), channel_id=1, source_target_pairs={{0,8},{4,12},{8,16},{12,20},{16,24},{20,28},{24,32},{28,36},{32,40... | collective-permute-start | bytes 589832 | tf_op jit(solution)/shard_map/ppermute | solution.py:21
  22.8 1.9 %collective-permute-start.3 = (bf16[3,64,512]{2,1,0:T(8,128)(2,1)S(1)}, bf16[3,64,512]{2,1,0:T(8,128)(2,1)S(1)}, u32[]{:S(2)}, u32[]{:S(2)}) collective-permute-start(bf16[3,64,512]{2,1,0:T(8,128)(2,1)S(1)} %get-tuple-element.5), channel_id=1, source_target_pairs={{0,56},{4,60},{8,0},{12,4},{16,8},{20,12},{24,16},{28,20},{32,24},... | collective-permute-start | bytes 589832 | tf_op jit(solution)/shard_map/ppermute | solution.py:21
  24.7 4.7 %collective-permute-start.1 = (bf16[4,64,512]{2,1,0:T(8,128)(2,1)S(1)}, bf16[4,64,512]{2,1,0:T(8,128)(2,1)S(1)}, u32[]{:S(2)}, u32[]{:S(2)}) collective-permute-start(bf16[4,64,512]{2,1,0:T(8,128)(2,1)S(1)} %all-to-all-done.1.plane), channel_id=1, source_target_pairs={{0,4},{4,8},{8,12},{12,16},{16,20},{20,24},{24,28},{28,32},{32,36}... | collective-permute-start | bytes 786440 | tf_op jit(solution)/shard_map/ppermute | solution.py:21
  29.4 1.9 %collective-permute-start.2 = (bf16[4,64,512]{2,1,0:T(8,128)(2,1)S(1)}, bf16[4,64,512]{2,1,0:T(8,128)(2,1)S(1)}, u32[]{:S(2)}, u32[]{:S(2)}) collective-permute-start(bf16[4,64,512]{2,1,0:T(8,128)(2,1)S(1)} %all-to-all-done.1.plane), channel_id=1, source_target_pairs={{0,60},{4,0},{8,4},{12,8},{16,12},{20,16},{24,20},{28,24},{32,28},... | collective-permute-start | bytes 786440 | tf_op jit(solution)/shard_map/ppermute | solution.py:21
  31.4 3.0 %collective-permute-done.3.above2 = bf16[3,64,512]{2,1,0:T(8,128)(2,1)S(1)} collective-permute-done((bf16[3,64,512]{2,1,0:T(8,128)(2,1)S(1)}, bf16[3,64,512]{2,1,0:T(8,128)(2,1)S(1)}, u32[]{:S(2)}, u32[]{:S(2)}) %collective-permute-start.3) | collective-permute-done | bytes 196640 | tf_op jit(solution)/shard_map/ppermute | solution.py:21
  34.4 1.9 %collective-permute-start.4 = (bf16[10,64,512]{2,1,0:T(8,128)(2,1)S(1)}, bf16[10,64,512]{2,1,0:T(8,128)(2,1)S(1)}, u32[]{:S(2)}, u32[]{:S(2)}) collective-permute-start(bf16[10,64,512]{2,1,0:T(8,128)(2,1)S(1)} %pad_maximum_fusion), channel_id=1, source_target_pairs={{0,64},{64,0},{1,65},{65,1},{2,66},{66,2},{3,67},{67,3},{4,68},{68... | collective-permute-start | bytes 1966088 | tf_op jit(solution)/shard_map/ppermute | solution.py:21
  37.0 5.3 %collective-permute-done.2.above = bf16[4,64,512]{2,1,0:T(8,128)(2,1)S(1)} collective-permute-done((bf16[4,64,512]{2,1,0:T(8,128)(2,1)S(1)}, bf16[4,64,512]{2,1,0:T(8,128)(2,1)S(1)}, u32[]{:S(2)}, u32[]{:S(2)}) %collective-permute-start.2) | collective-permute-done | bytes 262176 | tf_op jit(solution)/shard_map/ppermute | solution.py:21
  42.3 1.9 %collective-permute-start.5 = (bf16[8,64,512]{2,1,0:T(8,128)(2,1)S(1)}, bf16[8,64,512]{2,1,0:T(8,128)(2,1)S(1)}, u32[]{:S(2)}, u32[]{:S(2)}) collective-permute-start(bf16[8,64,512]{2,1,0:T(8,128)(2,1)S(1)} %pad_maximum_fusion.1), channel_id=1, source_target_pairs={{0,64},{64,0},{1,65},{65,1},{2,66},{66,2},{3,67},{67,3},{4,68},{68... | collective-permute-start | bytes 1572872 | tf_op jit(solution)/shard_map/ppermute | solution.py:21
  44.2 1.9 %collective-permute-done.5.second = bf16[8,64,512]{2,1,0:T(8,128)(2,1)S(1)} collective-permute-done((bf16[8,64,512]{2,1,0:T(8,128)(2,1)S(1)}, bf16[8,64,512]{2,1,0:T(8,128)(2,1)S(1)}, u32[]{:S(2)}, u32[]{:S(2)}) %collective-permute-start.5) | collective-permute-done | bytes 524320 | tf_op jit(solution)/shard_map/ppermute | solution.py:21
  46.9 0.8 copy-done.1
  47.7 1.1 copy-done.2
  48.8 1.0 copy-done.4
  49.9 1.4 %make_half.1.own = bf16[256,1024]{1,0:T(8,128)(2,1)S(1)} custom-call(s32[1]{0:T(128)} %bitcast.core, bf16[8,15,64,128]{3,2,1,0:T(8,128)(2,1)S(1)} %all-to-all-done.tiles, bf16[3,64,512]{2,1,0:T(8,128)(2,1)S(1)} %collective-permute-done.below2, bf16[4,64,512]{2,1,0:T(8,128)(2,1)S(1)} %collective-permute-done.1.below, ...), custom_call_target="tpu_custom_call" | custom-call | tf_op jit(solution)/shard_map/make_half/pallas_call | solution.py:118
  51.3 4.6 %collective-permute-start.6 = (bf16[256,1024]{1,0:T(8,128)(2,1)S(1)}, bf16[256,1024]{1,0:T(8,128)(2,1)S(1)}, u32[]{:S(2)}, u32[]{:S(2)}) collective-permute-start(bf16[256,1024]{1,0:T(8,128)(2,1)S(1)} %make_half.1.own), channel_id=1, source_target_pairs={{0,4},{4,8},{8,12},{12,16},{16,20},{20,24},{24,28},{28,32},{32,36}... | collective-permute-start | bytes 1572872 | tf_op jit(solution)/shard_map/ppermute | solution.py:21
  55.9 1.9 %collective-permute-start.7 = (bf16[256,1024]{1,0:T(8,128)(2,1)S(1)}, bf16[256,1024]{1,0:T(8,128)(2,1)S(1)}, u32[]{:S(2)}, u32[]{:S(2)}) collective-permute-start(bf16[256,1024]{1,0:T(8,128)(2,1)S(1)} %make_half.1.own), channel_id=1, source_target_pairs={{0,60},{4,0},{8,4},{12,8},{16,12},{20,16},{24,20},{28,24},{32,28},... | collective-permute-start | bytes 1572872 | tf_op jit(solution)/shard_map/ppermute | solution.py:21
  57.8 1.9 %collective-permute-start.9 = (bf16[256,1024]{1,0:T(8,128)(2,1)S(1)}, bf16[256,1024]{1,0:T(8,128)(2,1)S(1)}, u32[]{:S(2)}, u32[]{:S(2)}) collective-permute-start(bf16[256,1024]{1,0:T(8,128)(2,1)S(1)} %make_half.1.own), channel_id=1, source_target_pairs={{0,64},{64,0},{1,65},{65,1},{2,66},{66,2},{3,67},{67,3},{4,68},{68... | collective-permute-start | bytes 1572872 | tf_op jit(solution)/shard_map/ppermute | solution.py:21
  59.7 7.6 %collective-permute-done.6.up = bf16[256,1024]{1,0:T(8,128)(2,1)S(1)} collective-permute-done((bf16[256,1024]{1,0:T(8,128)(2,1)S(1)}, bf16[256,1024]{1,0:T(8,128)(2,1)S(1)}, u32[]{:S(2)}, u32[]{:S(2)}) %collective-permute-start.6) | collective-permute-done | bytes 524320 | tf_op jit(solution)/shard_map/ppermute | solution.py:21
  67.3 1.9 %collective-permute-start.8 = (bf16[256,1024]{1,0:T(8,128)(2,1)S(1)}, bf16[256,1024]{1,0:T(8,128)(2,1)S(1)}, u32[]{:S(2)}, u32[]{:S(2)}) collective-permute-start(bf16[256,1024]{1,0:T(8,128)(2,1)S(1)} %collective-permute-done.6.up), channel_id=1, source_target_pairs={{0,64},{64,0},{1,65},{65,1},{2,66},{66,2},{3,67},{67,3},{4,68},{68... | collective-permute-start | bytes 1572872 | tf_op jit(solution)/shard_map/ppermute | solution.py:21
  69.2 3.4 %collective-permute-done.7.down = bf16[256,1024]{1,0:T(8,128)(2,1)S(1)} collective-permute-done((bf16[256,1024]{1,0:T(8,128)(2,1)S(1)}, bf16[256,1024]{1,0:T(8,128)(2,1)S(1)}, u32[]{:S(2)}, u32[]{:S(2)}) %collective-permute-start.7) | collective-permute-done | bytes 524320 | tf_op jit(solution)/shard_map/ppermute | solution.py:21
  72.6 1.9 %collective-permute-start.10 = (bf16[256,1024]{1,0:T(8,128)(2,1)S(1)}, bf16[256,1024]{1,0:T(8,128)(2,1)S(1)}, u32[]{:S(2)}, u32[]{:S(2)}) collective-permute-start(bf16[256,1024]{1,0:T(8,128)(2,1)S(1)} %collective-permute-done.7.down), channel_id=1, source_target_pairs={{0,64},{64,0},{1,65},{65,1},{2,66},{66,2},{3,67},{67,3},{4,68},{68... | collective-permute-start | bytes 1572872 | tf_op jit(solution)/shard_map/ppermute | solution.py:21
  74.6 1.9 %collective-permute-done.10.down2 = bf16[256,1024]{1,0:T(8,128)(2,1)S(1)} collective-permute-done((bf16[256,1024]{1,0:T(8,128)(2,1)S(1)}, bf16[256,1024]{1,0:T(8,128)(2,1)S(1)}, u32[]{:S(2)}, u32[]{:S(2)}) %collective-permute-start.10) | collective-permute-done | bytes 524320 | tf_op jit(solution)/shard_map/ppermute | solution.py:21
  76.4 2.1 %make_tiles.1 = bf16[256,1920]{1,0:T(8,128)(2,1)S(1)} custom-call(s32[1]{0:T(128)} %bitcast.core, bf16[256,1024]{1,0:T(8,128)(2,1)S(1)} %collective-permute-done.6.up, bf16[256,1024]{1,0:T(8,128)(2,1)S(1)} %make_half.1.own, bf16[256,1024]{1,0:T(8,128)(2,1)S(1)} %collective-permute-done.7.down, bf16[256,1024]{1,0:T(8,128)(2,1)S(1)} %collective-permute-done.8.up2, ...), custom_call_target="tpu_custom_call" | custom-call | tf_op jit(solution)/shard_map/make_tiles/pallas_call | solution.py:133
  78.6 23.7 %all_to_all.15 = bf16[16,16,1920]{2,1,0:T(8,128)(2,1)S(1)} all-to-all(bf16[16,16,1920]{2,1,0:T(8,128)(2,1)S(1)} %bitcast.11), channel_id=1, replica_groups=mesh['y'=4,'core'=2,'z'=16,'x'=4] {'x','y'}, dimensions={0} | all-to-all | bytes 1966080 | tf_op jit(solution)/shard_map/all_to_all | solution.py:142
  102.5 2.6 %collective-permute-start.11 = (f32[3,16,128]{2,0,1:T(4,128)S(1)}, f32[3,16,128]{2,0,1:T(4,128)S(1)}, u32[]{:S(2)}, u32[]{:S(2)}) collective-permute-start(f32[3,16,128]{2,0,1:T(4,128)S(1)} %slice.18), channel_id=1, source_target_pairs={{0,4},{4,8},{8,12},{12,16},{16,20},{20,24},{24,28},{28,32},{32,36}... | collective-permute-start | bytes 73736 | tf_op jit(solution)/shard_map/ppermute | solution.py:21
  105.0 3.3 %collective-permute-start.12 = (f32[3,16,128]{2,0,1:T(4,128)S(1)}, f32[3,16,128]{2,0,1:T(4,128)S(1)}, u32[]{:S(2)}, u32[]{:S(2)}) collective-permute-start(f32[3,16,128]{2,0,1:T(4,128)S(1)} %slice.18), channel_id=1, source_target_pairs={{0,60},{4,0},{8,4},{12,8},{16,12},{20,16},{24,20},{28,24},{32,28},... | collective-permute-start | bytes 73736 | tf_op jit(solution)/shard_map/ppermute | solution.py:21
  108.4 3.7 %collective-permute-done.12 = f32[3,16,128]{2,0,1:T(4,128)S(1)} collective-permute-done((f32[3,16,128]{2,0,1:T(4,128)S(1)}, f32[3,16,128]{2,0,1:T(4,128)S(1)}, u32[]{:S(2)}, u32[]{:S(2)}) %collective-permute-start.12) | collective-permute-done | bytes 24608 | tf_op jit(solution)/shard_map/ppermute | solution.py:21
  (30 shorter events, 4.7 us)
Async XLA Ops:
  0.0 1.0 copy-start.5
  1.8 11.0 %all-to-all-start.1 = ((bf16[4,64,512]{2,1,0:T(8,128)(2,1)}), bf16[4,64,512]{2,1,0:T(8,128)(2,1)S(1)}, u32[]{:S(2)}, u32[]{:S(2)}) async-start(bf16[4,64,512]{2,1,0:T(8,128)(2,1)} %cut_orbitals.1), calls=%async_computation.1 | async-start | bytes 524288 | tf_op jit(solution)/shard_map/all_to_all | solution.py:99
  6.1 1.0 copy-start.6
  7.1 0.7 copy-start.7
  8.6 1.3 %copy-start = (bf16[4,2,15,64,128]{4,3,2,1,0:T(8,128)(2,1)}, bf16[4,2,15,64,128]{4,3,2,1,0:T(8,128)(2,1)S(1)}, u32[]{:S(2)}) copy-start(bf16[4,2,15,64,128]{4,3,2,1,0:T(8,128)(2,1)S(1)} %cut_integrals.1) | copy-start | bytes 5898244
  12.7 35.0 %all-to-all-start = ((bf16[8,15,64,128]{3,2,1,0:T(8,128)(2,1)}), bf16[8,15,64,128]{3,2,1,0:T(8,128)(2,1)S(1)}, u32[]{:S(2)}, u32[]{:S(2)}) async-start(bf16[8,15,64,128]{3,2,1,0:T(8,128)(2,1)} %bitcast.10), calls=%async_computation | async-start | bytes 3932160 | tf_op jit(solution)/shard_map/all_to_all | solution.py:109
  16.4 15.0 %collective-permute-start = (bf16[3,64,512]{2,1,0:T(8,128)(2,1)S(1)}, bf16[3,64,512]{2,1,0:T(8,128)(2,1)S(1)}, u32[]{:S(2)}, u32[]{:S(2)}) collective-permute-start(bf16[3,64,512]{2,1,0:T(8,128)(2,1)S(1)} %get-tuple-element.6), channel_id=1, source_target_pairs={{0,8},{4,12},{8,16},{12,20},{16,24},{20,28},{24,32},{28,36},{32,40... | collective-permute-start | bytes 589832 | tf_op jit(solution)/shard_map/ppermute | solution.py:21
  22.8 11.6 %collective-permute-start.3 = (bf16[3,64,512]{2,1,0:T(8,128)(2,1)S(1)}, bf16[3,64,512]{2,1,0:T(8,128)(2,1)S(1)}, u32[]{:S(2)}, u32[]{:S(2)}) collective-permute-start(bf16[3,64,512]{2,1,0:T(8,128)(2,1)S(1)} %get-tuple-element.5), channel_id=1, source_target_pairs={{0,56},{4,60},{8,0},{12,4},{16,8},{20,12},{24,16},{28,20},{32,24},... | collective-permute-start | bytes 589832 | tf_op jit(solution)/shard_map/ppermute | solution.py:21
  24.7 12.2 %collective-permute-start.1 = (bf16[4,64,512]{2,1,0:T(8,128)(2,1)S(1)}, bf16[4,64,512]{2,1,0:T(8,128)(2,1)S(1)}, u32[]{:S(2)}, u32[]{:S(2)}) collective-permute-start(bf16[4,64,512]{2,1,0:T(8,128)(2,1)S(1)} %all-to-all-done.1.plane), channel_id=1, source_target_pairs={{0,4},{4,8},{8,12},{12,16},{16,20},{20,24},{24,28},{28,32},{32,36}... | collective-permute-start | bytes 786440 | tf_op jit(solution)/shard_map/ppermute | solution.py:21
  29.4 12.8 %collective-permute-start.2 = (bf16[4,64,512]{2,1,0:T(8,128)(2,1)S(1)}, bf16[4,64,512]{2,1,0:T(8,128)(2,1)S(1)}, u32[]{:S(2)}, u32[]{:S(2)}) collective-permute-start(bf16[4,64,512]{2,1,0:T(8,128)(2,1)S(1)} %all-to-all-done.1.plane), channel_id=1, source_target_pairs={{0,60},{4,0},{8,4},{12,8},{16,12},{20,16},{24,20},{28,24},{32,28},... | collective-permute-start | bytes 786440 | tf_op jit(solution)/shard_map/ppermute | solution.py:21
  34.4 12.5 %collective-permute-start.4 = (bf16[10,64,512]{2,1,0:T(8,128)(2,1)S(1)}, bf16[10,64,512]{2,1,0:T(8,128)(2,1)S(1)}, u32[]{:S(2)}, u32[]{:S(2)}) collective-permute-start(bf16[10,64,512]{2,1,0:T(8,128)(2,1)S(1)} %pad_maximum_fusion), channel_id=1, source_target_pairs={{0,64},{64,0},{1,65},{65,1},{2,66},{66,2},{3,67},{67,3},{4,68},{68... | collective-permute-start | bytes 1966088 | tf_op jit(solution)/shard_map/ppermute | solution.py:21
  42.3 3.8 %collective-permute-start.5 = (bf16[8,64,512]{2,1,0:T(8,128)(2,1)S(1)}, bf16[8,64,512]{2,1,0:T(8,128)(2,1)S(1)}, u32[]{:S(2)}, u32[]{:S(2)}) collective-permute-start(bf16[8,64,512]{2,1,0:T(8,128)(2,1)S(1)} %pad_maximum_fusion.1), channel_id=1, source_target_pairs={{0,64},{64,0},{1,65},{65,1},{2,66},{66,2},{3,67},{67,3},{4,68},{68... | collective-permute-start | bytes 1572872 | tf_op jit(solution)/shard_map/ppermute | solution.py:21
  46.1 0.8 copy-start.3
  46.9 0.8 copy-start.1
  47.7 1.1 copy-start.2
  48.8 1.0 copy-start.4
  51.3 16.0 %collective-permute-start.6 = (bf16[256,1024]{1,0:T(8,128)(2,1)S(1)}, bf16[256,1024]{1,0:T(8,128)(2,1)S(1)}, u32[]{:S(2)}, u32[]{:S(2)}) collective-permute-start(bf16[256,1024]{1,0:T(8,128)(2,1)S(1)} %make_half.1.own), channel_id=1, source_target_pairs={{0,4},{4,8},{8,12},{12,16},{16,20},{20,24},{24,28},{28,32},{32,36}... | collective-permute-start | bytes 1572872 | tf_op jit(solution)/shard_map/ppermute | solution.py:21
  55.9 16.8 %collective-permute-start.7 = (bf16[256,1024]{1,0:T(8,128)(2,1)S(1)}, bf16[256,1024]{1,0:T(8,128)(2,1)S(1)}, u32[]{:S(2)}, u32[]{:S(2)}) collective-permute-start(bf16[256,1024]{1,0:T(8,128)(2,1)S(1)} %make_half.1.own), channel_id=1, source_target_pairs={{0,60},{4,0},{8,4},{12,8},{16,12},{20,16},{24,20},{28,24},{32,28},... | collective-permute-start | bytes 1572872 | tf_op jit(solution)/shard_map/ppermute | solution.py:21
  57.8 16.8 %collective-permute-start.9 = (bf16[256,1024]{1,0:T(8,128)(2,1)S(1)}, bf16[256,1024]{1,0:T(8,128)(2,1)S(1)}, u32[]{:S(2)}, u32[]{:S(2)}) collective-permute-start(bf16[256,1024]{1,0:T(8,128)(2,1)S(1)} %make_half.1.own), channel_id=1, source_target_pairs={{0,64},{64,0},{1,65},{65,1},{2,66},{66,2},{3,67},{67,3},{4,68},{68... | collective-permute-start | bytes 1572872 | tf_op jit(solution)/shard_map/ppermute | solution.py:21
  67.3 7.3 %collective-permute-start.8 = (bf16[256,1024]{1,0:T(8,128)(2,1)S(1)}, bf16[256,1024]{1,0:T(8,128)(2,1)S(1)}, u32[]{:S(2)}, u32[]{:S(2)}) collective-permute-start(bf16[256,1024]{1,0:T(8,128)(2,1)S(1)} %collective-permute-done.6.up), channel_id=1, source_target_pairs={{0,64},{64,0},{1,65},{65,1},{2,66},{66,2},{3,67},{67,3},{4,68},{68... | collective-permute-start | bytes 1572872 | tf_op jit(solution)/shard_map/ppermute | solution.py:21
  72.6 3.8 %collective-permute-start.10 = (bf16[256,1024]{1,0:T(8,128)(2,1)S(1)}, bf16[256,1024]{1,0:T(8,128)(2,1)S(1)}, u32[]{:S(2)}, u32[]{:S(2)}) collective-permute-start(bf16[256,1024]{1,0:T(8,128)(2,1)S(1)} %collective-permute-done.7.down), channel_id=1, source_target_pairs={{0,64},{64,0},{1,65},{65,1},{2,66},{66,2},{3,67},{67,3},{4,68},{68... | collective-permute-start | bytes 1572872 | tf_op jit(solution)/shard_map/ppermute | solution.py:21
  78.6 29.7 %copy-start.8 = (s32[1,15]{1,0:T(1,128)S(1)}, s32[1,15]{1,0:T(1,128)}, u32[]{:S(2)}) copy-start(s32[1,15]{1,0:T(1,128)} %mask.1) | copy-start | bytes 184
  102.5 5.9 %collective-permute-start.11 = (f32[3,16,128]{2,0,1:T(4,128)S(1)}, f32[3,16,128]{2,0,1:T(4,128)S(1)}, u32[]{:S(2)}, u32[]{:S(2)}) collective-permute-start(f32[3,16,128]{2,0,1:T(4,128)S(1)} %slice.18), channel_id=1, source_target_pairs={{0,4},{4,8},{8,12},{12,16},{16,20},{20,24},{24,28},{28,32},{32,36}... | collective-permute-start | bytes 73736 | tf_op jit(solution)/shard_map/ppermute | solution.py:21
  105.0 7.0 %collective-permute-start.12 = (f32[3,16,128]{2,0,1:T(4,128)S(1)}, f32[3,16,128]{2,0,1:T(4,128)S(1)}, u32[]{:S(2)}, u32[]{:S(2)}) collective-permute-start(f32[3,16,128]{2,0,1:T(4,128)S(1)} %slice.18), channel_id=1, source_target_pairs={{0,60},{4,0},{8,4},{12,8},{16,12},{20,16},{24,20},{28,24},{32,28},... | collective-permute-start | bytes 73736 | tf_op jit(solution)/shard_map/ppermute | solution.py:21

commit v4 on v0

v4 whole, which is shorter than its diff:
```python
import jax
import jax.numpy as jnp
from jax import lax
from jax.experimental import pallas as pl
from jax.experimental.pallas import tpu as pltpu
from jax.sharding import Mesh, PartitionSpec as P

ROWS = 128
HALF = 64
COLS = 512
SPAN = 15
F32 = jnp.float32
BF16 = jnp.bfloat16
VMEM = pl.BlockSpec(memory_space=pltpu.VMEM)
SMEM = pl.BlockSpec(memory_space=pltpu.SMEM)


def call(kernel, name, specs, shape, dtype, *args, scratch=()):
    return pl.pallas_call(
        kernel,
        in_specs=specs,
        out_specs=VMEM,
        out_shape=jax.ShapeDtypeStruct(shape, dtype),
        scratch_shapes=scratch,
        compiler_params=pltpu.CompilerParams(vmem_limit_bytes=12 * 2**20),
        name=name,
    )(*args)


def swapped(x):
    return lax.ppermute(x, "core", [(0, 1), (1, 0)])


def moved(x, by):
    n = lax.axis_size("z")
    return lax.ppermute(x, "z", [(i, (i + by) % n) for i in range(n)])


def sided(x, by):
    n = lax.axis_size("z")
    pairs = [(i, (i + by) % n) for i in range(n)]
    pairs += [(n + i, n + (i - by) % n) for i in range(n)]
    return lax.ppermute(x, ("core", "z"), pairs)


def orbital_kernel(occupied, out):
    for x in range(4):
        out[x] = occupied[:, x * COLS : (x + 1) * COLS]


def integral_kernel(mask, integrals, out):
    for s in range(SPAN):
        tile = integrals[s]
        tile = jnp.where(mask[0, s] != 0, tile, jnp.zeros_like(tile))
        for x in range(4):
            out[x, 0, s] = tile[:HALF]
            out[x, 1, s] = tile[HALF:]


def half_kernel(core, tiles, plane, mine, other, half, window):
    c = core[0]

    def place(part, first, n, at):
        window[pl.ds(pl.multiple_of(at * ROWS, ROWS), n * ROWS), :] = part[
            first : first + n
        ].reshape(n * ROWS, COLS)

    place(plane, 0, 4, 7)
    place(mine, 0, 3, c * 15)
    place(mine, 3, 4, 3 + c * 8)
    place(other, 0, 3, 15 - c * 15)
    place(other, 3, 4, 11 - c * 8)
    for a in range(4):
        near = window[a * ROWS : (a + SPAN) * ROWS, :]
        wide = jnp.concatenate(
            [tiles[2 * a : 2 * a + 2, s].reshape(2 * HALF, ROWS) for s in range(SPAN)], 1
        )
        made = jnp.dot(wide, near, preferred_element_type=F32).astype(BF16)
        half[a * HALF : (a + 1) * HALF, :COLS] = made[:HALF]
        half[a * HALF : (a + 1) * HALF, COLS:] = made[HALF:]


def dot_t(a, b):
    return lax.dot_general(a, b, (((1,), (1,)), ((), ())), preferred_element_type=F32)


def interleave(core, mine, other, wide, at):
    for b in range(4):
        to = at + b * ROWS
        rows = slice(b * HALF, (b + 1) * HALF)
        wide[pl.ds(pl.multiple_of(to + core * HALF, HALF), HALF), :] = mine[rows, :]
        wide[pl.ds(pl.multiple_of(to + HALF - core * HALF, HALF), HALF), :] = other[rows, :]


def home_kernel(core, own, own2, side, side2, out, wide):
    c = core[0]
    interleave(c, side, side2, wide, 0)
    interleave(c, own, own2, wide, 512)
    inner = wide[pl.ds(pl.multiple_of(512 + c * 256, 256), 256), :]
    for k, rows in ((c, own), (1 - c, own2)):
        left = rows[...]
        outer = dot_t(left, wide[0:512, :]).astype(BF16)
        within = dot_t(left, inner).astype(BF16)
        for x in range(4):
            for j in range(4):
                at = slice(x * HALF + j * 16, x * HALF + j * 16 + 16)
                out[x * 8 + k * 4 + j, :, :512] = outer[at]
                out[x * 8 + k * 4 + j, :, 512:] = within[at]


def far_kernel(core, side, side2, other, other2, out, low, high, below, above):
    c = core[0]

    @pl.when(c == 0)
    def _():
        interleave(0, side, side2, low, 0)
        interleave(0, other2, other, high, 0)

    @pl.when(c == 1)
    def _():
        interleave(0, other, other2, low, 0)
        interleave(0, side2, side, high, 0)

    for k in range(16):
        at = pl.ds(pl.multiple_of(k * 32 + c * 16, 16), 16)
        below[k * 16 : k * 16 + 16, :] = low[at, :]
        above[k * 16 : k * 16 + 16, :] = high[at, :]
    for x in range(4):
        rows = slice(x * HALF, (x + 1) * HALF)
        cut = x * ROWS
        made = []
        if x > 0:
            made.append(dot_t(below[rows, :], high[0:cut, :]).astype(BF16))
        if x < 3:
            made.append(dot_t(above[rows, :], low[cut + ROWS : 512, :]).astype(BF16))
        out[rows, :] = jnp.concatenate(made, 1)


def last_kernel(place, mask, home, low, high, out, line):
    for e in range(3):
        line[e] = low[:, e * ROWS : (e + 1) * ROWS]
        line[15 + e] = high[:, e * ROWS : (e + 1) * ROWS]
    for b in range(4):
        line[3 + b] = home[0, :, b * ROWS : (b + 1) * ROWS]
        line[11 + b] = home[1, :, b * ROWS : (b + 1) * ROWS]
        at = 512 + (b % 2) * ROWS
        line[7 + b] = home[b // 2, :, at : at + ROWS]
    x = place[0]
    for s in range(SPAN):
        out[s] = line[x + s] * mask[0, s].astype(F32)


def per_device(occupied, integrals, pair_mask):
    x = lax.axis_index("x")[None]
    c = lax.axis_index("core")
    core = c[None]

    pieces = call(orbital_kernel, "cut_orbitals", [VMEM], (4, ROWS, COLS), BF16, occupied)
    plane = lax.all_to_all(pieces, "x", 0, 0)

    tiles = call(
        integral_kernel, "cut_integrals", [SMEM, VMEM], (4, 2, SPAN, HALF, ROWS), BF16,
        pair_mask, integrals[0, 0],
    )
    tiles = lax.all_to_all(tiles.reshape(8, SPAN, HALF, ROWS), ("x", "core"), 0, 0)

    near2 = sided(lax.dynamic_slice_in_dim(plane, 1 - c, 3, 0), 2)
    near = sided(plane, 1)
    mine = jnp.concatenate([near2, near])
    other = swapped(mine)

    own = call(
        half_kernel, "make_half", [SMEM] + [VMEM] * 4, (4 * HALF, 2 * COLS), BF16,
        core, tiles, plane, mine, other,
        scratch=[pltpu.VMEM((18 * ROWS, COLS), BF16)],
    )

    side = sided(own, 1)
    own2 = swapped(own)
    side2 = sided(own2, 1)
    home = call(
        home_kernel, "make_home", [SMEM] + [VMEM] * 4, (32, 16, 768), BF16,
        core, own, own2, side, side2,
        scratch=[pltpu.VMEM((1024, 2 * COLS), BF16)],
    )
    home = lax.all_to_all(home, ("x", "y", "core"), 0, 0)
    home = home.reshape(16, 2, 16, 768).astype(F32).sum(0)

    far = call(
        far_kernel, "make_far", [SMEM] + [VMEM] * 4, (256, 384), BF16,
        core, side, side2, swapped(side), swapped(side2),
        scratch=[pltpu.VMEM((512, 2 * COLS), BF16)] * 2 + [pltpu.VMEM((256, 2 * COLS), BF16)] * 2,
    )
    far = lax.all_to_all(far.reshape(16, 16, 384), ("x", "y"), 0, 0)
    far = far.astype(F32).sum(0)
    out = call(
        last_kernel, "join", [SMEM, SMEM] + [VMEM] * 3, (SPAN, 16, ROWS), F32,
        x, pair_mask, home, moved(far, 1), moved(far, -1),
        scratch=[pltpu.VMEM((18, 16, ROWS), F32)],
    )
    return out[None]


def solution(mesh):
    split = Mesh(mesh.devices.reshape(4, 2, 16, 4), ("y", "core", "z", "x"))
    aux, orb = ("y", "core"), ("z", "x")
    return jax.shard_map(
        per_device,
        mesh=split,
        in_specs=(P(orb, None), P(aux, orb, None, None, None), P(orb, None)),
        out_specs=P(orb, None, aux, None),
        check_vma=False,
    )
```

time: 452 us -> 117 us (0.26)
  the two profiles are of different devices: /device:TPU:6 before, /device:TPU:1 now
where the time goes in v4:
time: 117 us; the launch traced here: 116 us
  starting transfers between devices  63.9 us (55%)
  waiting for transfers between devices  37.8 us (32%)
  Pallas kernels  9.39 us (8%)
  local copies, waits for them, and re-layouts  4.53 us (4%)
    ppermute x4, starting transfers between devices, sided(): return lax.ppermute(x, ('core', 'z'), pairs)  20.3 us
    ppermute x4, waiting for transfers between devices, sided(): return lax.ppermute(x, ('core', 'z'), pairs)  17.2 us
    ppermute x4, starting transfers between devices, swapped(): return lax.ppermute(x, 'core', [(0, 1), (1, 0)])  10.6 us
    all_to_all x1, starting transfers between devices, per_device(): lax.all_to_all(tiles.reshape(8, SPAN, HALF, ROWS), ('x', 'core'), 0, 0)  10.1 us
    pallas_call x6, Pallas kernels, call(): pl.pallas_call(kernel, in_specs=specs, out_specs=VMEM, out_shape=jax.Shap...  9.39 us
    all_to_all x1, waiting for transfers between devices, per_device(): home = lax.all_to_all(home, ('x', 'y', 'core'), 0, 0)  7.72 us
    ppermute x2, starting transfers between devices, moved(): return lax.ppermute(x, 'z', [(i, (i + by) % n) for i in range(n)])  6.49 us
    all_to_all x1, starting transfers between devices, per_device(): far = lax.all_to_all(far.reshape(16, 16, 384), ('x', 'y'), 0, 0)  6.1 us
  transfers between devices with their start and end apart: 14, of which 8 were waited for; matrix products, arithmetic and copies ran while one was open for 0% of the time, Pallas kernels for 2%

profile of v4, /device:TPU:1, one launch (start us, length us, event | category | flops | bytes accessed | tf_op | source)
XLA Modules:
  0.0 115.9 jit_solution(9471750321209140054)
XLA Ops:
  0.0 1.0 copy-done.3
  1.0 0.8 cut_orbitals.1
  1.9 4.8 %all-to-all-start.1 = ((bf16[4,128,512]{2,1,0:T(8,128)(2,1)}), bf16[4,128,512]{2,1,0:T(8,128)(2,1)S(1)}, u32[]{:S(2)}, u32[]{:S(2)}) async-start(bf16[4,128,512]{2,1,0:T(8,128)(2,1)} %cut_orbitals.1), calls=%async_computation.1 | async-start | bytes 1048576 | tf_op jit(solution)/shard_map/all_to_all | solution.py:159
  6.7 0.8 cut_integrals.1
  7.6 1.3 %copy-done = bf16[4,2,15,64,128]{4,3,2,1,0:T(8,128)(2,1)} copy-done((bf16[4,2,15,64,128]{4,3,2,1,0:T(8,128)(2,1)}, bf16[4,2,15,64,128]{4,3,2,1,0:T(8,128)(2,1)S(1)}, u32[]{:S(2)}) %copy-start) | copy-done | bytes 1966104
  8.8 4.8 %all-to-all-done.1.plane = bf16[4,128,512]{2,1,0:T(8,128)(2,1)S(1)} async-done(((bf16[4,128,512]{2,1,0:T(8,128)(2,1)}), bf16[4,128,512]{2,1,0:T(8,128)(2,1)S(1)}, u32[]{:S(2)}, u32[]{:S(2)}) %all-to-all-start.1) | async-done | bytes 524320 | tf_op jit(solution)/shard_map/all_to_all | solution.py:159
  13.7 10.1 %all-to-all-start = ((bf16[8,15,64,128]{3,2,1,0:T(8,128)(2,1)}), bf16[8,15,64,128]{3,2,1,0:T(8,128)(2,1)S(1)}, u32[]{:S(2)}, u32[]{:S(2)}) async-start(bf16[8,15,64,128]{3,2,1,0:T(8,128)(2,1)} %bitcast.8), calls=%async_computation | async-start | bytes 3932160 | tf_op jit(solution)/shard_map/all_to_all | solution.py:165
  23.8 8.0 %collective-permute-start.1 = (bf16[4,128,512]{2,1,0:T(8,128)(2,1)S(1)}, bf16[4,128,512]{2,1,0:T(8,128)(2,1)S(1)}, u32[]{:S(2)}, u32[]{:S(2)}) collective-permute-start(bf16[4,128,512]{2,1,0:T(8,128)(2,1)S(1)} %all-to-all-done.1.plane), channel_id=1, source_target_pairs={{0,4},{4,8},{8,12},{12,16},{16,20},{20,24},{24,28},{28,32},{32,36}... | collective-permute-start | bytes 1572872 | tf_op jit(solution)/shard_map/ppermute | solution.py:43
  31.8 3.1 %collective-permute-start = (bf16[3,128,512]{2,1,0:T(8,128)(2,1)S(1)}, bf16[3,128,512]{2,1,0:T(8,128)(2,1)S(1)}, u32[]{:S(2)}, u32[]{:S(2)}) collective-permute-start(bf16[3,128,512]{2,1,0:T(8,128)(2,1)S(1)} %constant_dynamic-slice_fusion), channel_id=1, source_target_pairs={{0,8},{4,12},{8,16},{12,20},{16,24},{20,28},{24,32},{28,36},{32,40... | collective-permute-start | bytes 1179656 | tf_op jit(solution)/shard_map/ppermute | solution.py:43
  34.9 11.4 %collective-permute-done = bf16[3,128,512]{2,1,0:T(8,128)(2,1)S(1)} collective-permute-done((bf16[3,128,512]{2,1,0:T(8,128)(2,1)S(1)}, bf16[3,128,512]{2,1,0:T(8,128)(2,1)S(1)}, u32[]{:S(2)}, u32[]{:S(2)}) %collective-permute-start) | collective-permute-done | bytes 393248 | tf_op jit(solution)/shard_map/ppermute | solution.py:43
  46.4 2.1 %collective-permute-start.2 = (bf16[7,128,512]{2,1,0:T(8,128)(2,1)S(1)}, bf16[7,128,512]{2,1,0:T(8,128)(2,1)}, u32[]{:S(2)}, u32[]{:S(2)}) collective-permute-start(bf16[7,128,512]{2,1,0:T(8,128)(2,1)S(1)} %constant_dynamic-update-slice_fusion.mine), channel_id=1, source_target_pairs={{0,64},{64,0},{1,65},{65,1},{2,66},{66,2},{3,67},{67,3},{4,68},{68... | collective-permute-start | bytes 2752520 | tf_op jit(solution)/shard_map/ppermute | solution.py:31
  48.5 0.9 copy-done.1
  49.4 1.5 %collective-permute-done.2.other = bf16[7,128,512]{2,1,0:T(8,128)(2,1)} collective-permute-done((bf16[7,128,512]{2,1,0:T(8,128)(2,1)S(1)}, bf16[7,128,512]{2,1,0:T(8,128)(2,1)}, u32[]{:S(2)}, u32[]{:S(2)}) %collective-permute-start.2) | collective-permute-done | bytes 917536 | tf_op jit(solution)/shard_map/ppermute | solution.py:31
  50.9 1.2 %copy-done.2 = bf16[7,128,512]{2,1,0:T(8,128)(2,1)S(1)} copy-done((bf16[7,128,512]{2,1,0:T(8,128)(2,1)S(1)}, bf16[7,128,512]{2,1,0:T(8,128)(2,1)}, u32[]{:S(2)}) %copy-start.2) | copy-done | bytes 917528
  52.1 2.6 %make_half.1.own = bf16[256,1024]{1,0:T(8,128)(2,1)S(1)} custom-call(s32[1]{0:T(128)} %bitcast.1.core, bf16[8,15,64,128]{3,2,1,0:T(8,128)(2,1)S(1)} %all-to-all-done.tiles, bf16[4,128,512]{2,1,0:T(8,128)(2,1)S(1)} %all-to-all-done.1.plane, bf16[7,128,512]{2,1,0:T(8,128)(2,1)S(1)} %copy-done.2, bf16[7,128,512]{2,1,0:T(8,128)(2,1)} %collective-permute-done.2.other), custom_call_target="tpu_custom_call" | custom-call | tf_op jit(solution)/shard_map/make_half/pallas_call | solution.py:19
  54.7 2.1 %collective-permute-start.3 = (bf16[256,1024]{1,0:T(8,128)(2,1)S(1)}, bf16[256,1024]{1,0:T(8,128)(2,1)S(1)}, u32[]{:S(2)}, u32[]{:S(2)}) collective-permute-start(bf16[256,1024]{1,0:T(8,128)(2,1)S(1)} %make_half.1.own), channel_id=1, source_target_pairs={{0,64},{64,0},{1,65},{65,1},{2,66},{66,2},{3,67},{67,3},{4,68},{68... | collective-permute-start | bytes 1572872 | tf_op jit(solution)/shard_map/ppermute | solution.py:31
  56.7 6.6 %collective-permute-start.4 = (bf16[256,1024]{1,0:T(8,128)(2,1)S(1)}, bf16[256,1024]{1,0:T(8,128)(2,1)S(1)}, u32[]{:S(2)}, u32[]{:S(2)}) collective-permute-start(bf16[256,1024]{1,0:T(8,128)(2,1)S(1)} %make_half.1.own), channel_id=1, source_target_pairs={{0,4},{4,8},{8,12},{12,16},{16,20},{20,24},{24,28},{28,32},{32,36}... | collective-permute-start | bytes 1572872 | tf_op jit(solution)/shard_map/ppermute | solution.py:43
  63.3 2.6 %collective-permute-start.5 = (bf16[256,1024]{1,0:T(8,128)(2,1)S(1)}, bf16[256,1024]{1,0:T(8,128)(2,1)S(1)}, u32[]{:S(2)}, u32[]{:S(2)}) collective-permute-start(bf16[256,1024]{1,0:T(8,128)(2,1)S(1)} %collective-permute-done.3.own2), channel_id=1, source_target_pairs={{0,4},{4,8},{8,12},{12,16},{16,20},{20,24},{24,28},{28,32},{32,36}... | collective-permute-start | bytes 1572872 | tf_op jit(solution)/shard_map/ppermute | solution.py:43
  66.0 3.5 %collective-permute-done.4.side = bf16[256,1024]{1,0:T(8,128)(2,1)S(1)} collective-permute-done((bf16[256,1024]{1,0:T(8,128)(2,1)S(1)}, bf16[256,1024]{1,0:T(8,128)(2,1)S(1)}, u32[]{:S(2)}, u32[]{:S(2)}) %collective-permute-start.4) | collective-permute-done | bytes 524320 | tf_op jit(solution)/shard_map/ppermute | solution.py:43
  69.4 3.2 %collective-permute-start.6 = (bf16[256,1024]{1,0:T(8,128)(2,1)S(1)}, bf16[256,1024]{1,0:T(8,128)(2,1)S(1)}, u32[]{:S(2)}, u32[]{:S(2)}) collective-permute-start(bf16[256,1024]{1,0:T(8,128)(2,1)S(1)} %collective-permute-done.4.side), channel_id=1, source_target_pairs={{0,64},{64,0},{1,65},{65,1},{2,66},{66,2},{3,67},{67,3},{4,68},{68... | collective-permute-start | bytes 1572872 | tf_op jit(solution)/shard_map/ppermute | solution.py:31
  72.7 2.4 %collective-permute-done.5.side2 = bf16[256,1024]{1,0:T(8,128)(2,1)S(1)} collective-permute-done((bf16[256,1024]{1,0:T(8,128)(2,1)S(1)}, bf16[256,1024]{1,0:T(8,128)(2,1)S(1)}, u32[]{:S(2)}, u32[]{:S(2)}) %collective-permute-start.5) | collective-permute-done | bytes 524320 | tf_op jit(solution)/shard_map/ppermute | solution.py:43
  75.0 3.2 %collective-permute-start.7 = (bf16[256,1024]{1,0:T(8,128)(2,1)S(1)}, bf16[256,1024]{1,0:T(8,128)(2,1)S(1)}, u32[]{:S(2)}, u32[]{:S(2)}) collective-permute-start(bf16[256,1024]{1,0:T(8,128)(2,1)S(1)} %collective-permute-done.5.side2), channel_id=1, source_target_pairs={{0,64},{64,0},{1,65},{65,1},{2,66},{66,2},{3,67},{67,3},{4,68},{68... | collective-permute-start | bytes 1572872 | tf_op jit(solution)/shard_map/ppermute | solution.py:31
  78.3 1.5 %collective-permute-done.7.other2 = bf16[256,1024]{1,0:T(8,128)(2,1)S(1)} collective-permute-done((bf16[256,1024]{1,0:T(8,128)(2,1)S(1)}, bf16[256,1024]{1,0:T(8,128)(2,1)S(1)}, u32[]{:S(2)}, u32[]{:S(2)}) %collective-permute-start.7) | collective-permute-done | bytes 524320 | tf_op jit(solution)/shard_map/ppermute | solution.py:31
  79.8 1.9 %make_far.1 = bf16[256,384]{1,0:T(8,128)(2,1)} custom-call(s32[1]{0:T(128)} %bitcast.1.core, bf16[256,1024]{1,0:T(8,128)(2,1)S(1)} %collective-permute-done.4.side, bf16[256,1024]{1,0:T(8,128)(2,1)S(1)} %collective-permute-done.5.side2, bf16[256,1024]{1,0:T(8,128)(2,1)S(1)} %collective-permute-done.6.other, bf16[256,1024]{1,0:T(8,128)(2,1)S(1)} %collective-permute-done.7.other2), custom_call_target="tpu_custom_call" | custom-call | tf_op jit(solution)/shard_map/make_far/pallas_call | solution.py:19
  81.7 6.1 %all-to-all-start.3 = ((bf16[16,16,384]{2,1,0:T(8,128)(2,1)}), bf16[16,16,384]{2,1,0:T(8,128)(2,1)S(1)}, u32[]{:S(2)}, u32[]{:S(2)}) async-start(bf16[16,16,384]{2,1,0:T(8,128)(2,1)} %bitcast.5), calls=%async_computation.3 | async-start | bytes 393216 | tf_op jit(solution)/shard_map/all_to_all | solution.py:194
  87.8 2.1 %make_home.1 = bf16[32,16,768]{2,1,0:T(8,128)(2,1)} custom-call(s32[1]{0:T(128)} %bitcast.1.core, bf16[256,1024]{1,0:T(8,128)(2,1)S(1)} %make_half.1.own, bf16[256,1024]{1,0:T(8,128)(2,1)S(1)} %collective-permute-done.3.own2, bf16[256,1024]{1,0:T(8,128)(2,1)S(1)} %collective-permute-done.4.side, bf16[256,1024]{1,0:T(8,128)(2,1)S(1)} %collective-permute-done.5.side2), custom_call_target="tpu_custom_call" | custom-call | tf_op jit(solution)/shard_map/make_home/pallas_call | solution.py:19
  89.8 5.0 %all-to-all-done.3 = bf16[16,16,384]{2,1,0:T(8,128)(2,1)S(1)} async-done(((bf16[16,16,384]{2,1,0:T(8,128)(2,1)}), bf16[16,16,384]{2,1,0:T(8,128)(2,1)S(1)}, u32[]{:S(2)}, u32[]{:S(2)}) %all-to-all-start.3) | async-done | bytes 196640 | tf_op jit(solution)/shard_map/all_to_all | solution.py:194
  94.9 5.4 %all-to-all-start.2 = ((bf16[32,16,768]{2,1,0:T(8,128)(2,1)}), bf16[32,16,768]{2,1,0:T(8,128)(2,1)S(1)}, u32[]{:S(2)}, u32[]{:S(2)}) async-start(bf16[32,16,768]{2,1,0:T(8,128)(2,1)} %make_home.1), calls=%async_computation.2 | async-start | bytes 1572864 | tf_op jit(solution)/shard_map/all_to_all | solution.py:186
  100.3 2.6 %collective-permute-start.8 = (f32[16,384]{1,0:T(8,128)S(1)}, f32[16,384]{1,0:T(8,128)S(1)}, u32[]{:S(2)}, u32[]{:S(2)}) collective-permute-start(f32[16,384]{1,0:T(8,128)S(1)} %convert_reduce_fusion.1), channel_id=1, source_target_pairs={{0,4},{4,8},{8,12},{12,16},{16,20},{20,24},{24,28},{28,32},{32,36}... | collective-permute-start | bytes 73736 | tf_op jit(solution)/shard_map/ppermute | solution.py:36
  103.0 3.9 %collective-permute-start.9 = (f32[16,384]{1,0:T(8,128)S(1)}, f32[16,384]{1,0:T(8,128)S(1)}, u32[]{:S(2)}, u32[]{:S(2)}) collective-permute-start(f32[16,384]{1,0:T(8,128)S(1)} %convert_reduce_fusion.1), channel_id=1, source_target_pairs={{0,60},{4,0},{8,4},{12,8},{16,12},{20,16},{24,20},{28,24},{32,28},... | collective-permute-start | bytes 73736 | tf_op jit(solution)/shard_map/ppermute | solution.py:36
  106.8 7.7 %all-to-all-done.2 = bf16[32,16,768]{2,1,0:T(8,128)(2,1)S(1)} async-done(((bf16[32,16,768]{2,1,0:T(8,128)(2,1)}), bf16[32,16,768]{2,1,0:T(8,128)(2,1)S(1)}, u32[]{:S(2)}, u32[]{:S(2)}) %all-to-all-start.2) | async-done | bytes 786464 | tf_op jit(solution)/shard_map/all_to_all | solution.py:186
  114.7 1.2 %join.1 = f32[15,16,128]{2,1,0:T(8,128)} custom-call(s32[1]{0:T(128)} %bitcast.place, s32[1,15]{1,0:T(1,128)S(1)} %copy-done.5, f32[2,16,768]{2,1,0:T(8,128)S(1)} %convert_reduce_fusion.home, f32[16,384]{1,0:T(8,128)S(1)} %collective-permute-done.8.low, f32[16,384]{1,0:T(8,128)S(1)} %collective-permute-done.9.high), custom_call_target="tpu_custom_call" | custom-call | tf_op jit(solution)/shard_map/join/pallas_call | solution.py:19
  (19 shorter events, 0.3 us)
Async XLA Ops:
  0.0 1.0 copy-start.3
  1.0 5.7 %copy-start.4 = (bf16[1,1,15,128,128]{4,3,2,1,0:T(8,128)(2,1)S(1)}, bf16[1,1,15,128,128]{4,3,2,1,0:T(8,128)(2,1)}, u32[]{:S(2)}) copy-start(bf16[1,1,15,128,128]{4,3,2,1,0:T(8,128)(2,1)} %param.4) | copy-start | bytes 1474564
  1.0 5.7 %copy-start.5 = (s32[1,15]{1,0:T(1,128)S(1)}, s32[1,15]{1,0:T(1,128)}, u32[]{:S(2)}) copy-start(s32[1,15]{1,0:T(1,128)} %mask.3) | copy-start | bytes 184
  1.9 11.8 %all-to-all-start.1 = ((bf16[4,128,512]{2,1,0:T(8,128)(2,1)}), bf16[4,128,512]{2,1,0:T(8,128)(2,1)S(1)}, u32[]{:S(2)}, u32[]{:S(2)}) async-start(bf16[4,128,512]{2,1,0:T(8,128)(2,1)} %cut_orbitals.1), calls=%async_computation.1 | async-start | bytes 1048576 | tf_op jit(solution)/shard_map/all_to_all | solution.py:159
  7.5 1.3 %copy-start = (bf16[4,2,15,64,128]{4,3,2,1,0:T(8,128)(2,1)}, bf16[4,2,15,64,128]{4,3,2,1,0:T(8,128)(2,1)S(1)}, u32[]{:S(2)}) copy-start(bf16[4,2,15,64,128]{4,3,2,1,0:T(8,128)(2,1)S(1)} %cut_integrals.1) | copy-start | bytes 5898244
  13.7 35.7 %all-to-all-start = ((bf16[8,15,64,128]{3,2,1,0:T(8,128)(2,1)}), bf16[8,15,64,128]{3,2,1,0:T(8,128)(2,1)S(1)}, u32[]{:S(2)}, u32[]{:S(2)}) async-start(bf16[8,15,64,128]{3,2,1,0:T(8,128)(2,1)} %bitcast.8), calls=%async_computation | async-start | bytes 3932160 | tf_op jit(solution)/shard_map/all_to_all | solution.py:165
  23.8 22.6 %collective-permute-start.1 = (bf16[4,128,512]{2,1,0:T(8,128)(2,1)S(1)}, bf16[4,128,512]{2,1,0:T(8,128)(2,1)S(1)}, u32[]{:S(2)}, u32[]{:S(2)}) collective-permute-start(bf16[4,128,512]{2,1,0:T(8,128)(2,1)S(1)} %all-to-all-done.1.plane), channel_id=1, source_target_pairs={{0,4},{4,8},{8,12},{12,16},{16,20},{20,24},{24,28},{28,32},{32,36}... | collective-permute-start | bytes 1572872 | tf_op jit(solution)/shard_map/ppermute | solution.py:43
  31.8 14.5 %collective-permute-start = (bf16[3,128,512]{2,1,0:T(8,128)(2,1)S(1)}, bf16[3,128,512]{2,1,0:T(8,128)(2,1)S(1)}, u32[]{:S(2)}, u32[]{:S(2)}) collective-permute-start(bf16[3,128,512]{2,1,0:T(8,128)(2,1)S(1)} %constant_dynamic-slice_fusion), channel_id=1, source_target_pairs={{0,8},{4,12},{8,16},{12,20},{16,24},{20,28},{24,32},{28,36},{32,40... | collective-permute-start | bytes 1179656 | tf_op jit(solution)/shard_map/ppermute | solution.py:43
  46.4 4.5 %collective-permute-start.2 = (bf16[7,128,512]{2,1,0:T(8,128)(2,1)S(1)}, bf16[7,128,512]{2,1,0:T(8,128)(2,1)}, u32[]{:S(2)}, u32[]{:S(2)}) collective-permute-start(bf16[7,128,512]{2,1,0:T(8,128)(2,1)S(1)} %constant_dynamic-update-slice_fusion.mine), channel_id=1, source_target_pairs={{0,64},{64,0},{1,65},{65,1},{2,66},{66,2},{3,67},{67,3},{4,68},{68... | collective-permute-start | bytes 2752520 | tf_op jit(solution)/shard_map/ppermute | solution.py:31
  48.5 0.9 copy-start.1
  50.9 1.2 %copy-start.2 = (bf16[7,128,512]{2,1,0:T(8,128)(2,1)S(1)}, bf16[7,128,512]{2,1,0:T(8,128)(2,1)}, u32[]{:S(2)}) copy-start(bf16[7,128,512]{2,1,0:T(8,128)(2,1)} %copy-done.1) | copy-start | bytes 2752516
  54.7 8.6 %collective-permute-start.3 = (bf16[256,1024]{1,0:T(8,128)(2,1)S(1)}, bf16[256,1024]{1,0:T(8,128)(2,1)S(1)}, u32[]{:S(2)}, u32[]{:S(2)}) collective-permute-start(bf16[256,1024]{1,0:T(8,128)(2,1)S(1)} %make_half.1.own), channel_id=1, source_target_pairs={{0,64},{64,0},{1,65},{65,1},{2,66},{66,2},{3,67},{67,3},{4,68},{68... | collective-permute-start | bytes 1572872 | tf_op jit(solution)/shard_map/ppermute | solution.py:31
  56.7 12.7 %collective-permute-start.4 = (bf16[256,1024]{1,0:T(8,128)(2,1)S(1)}, bf16[256,1024]{1,0:T(8,128)(2,1)S(1)}, u32[]{:S(2)}, u32[]{:S(2)}) collective-permute-start(bf16[256,1024]{1,0:T(8,128)(2,1)S(1)} %make_half.1.own), channel_id=1, source_target_pairs={{0,4},{4,8},{8,12},{12,16},{16,20},{20,24},{24,28},{28,32},{32,36}... | collective-permute-start | bytes 1572872 | tf_op jit(solution)/shard_map/ppermute | solution.py:43
  63.3 11.7 %collective-permute-start.5 = (bf16[256,1024]{1,0:T(8,128)(2,1)S(1)}, bf16[256,1024]{1,0:T(8,128)(2,1)S(1)}, u32[]{:S(2)}, u32[]{:S(2)}) collective-permute-start(bf16[256,1024]{1,0:T(8,128)(2,1)S(1)} %collective-permute-done.3.own2), channel_id=1, source_target_pairs={{0,4},{4,8},{8,12},{12,16},{16,20},{20,24},{24,28},{28,32},{32,36}... | collective-permute-start | bytes 1572872 | tf_op jit(solution)/shard_map/ppermute | solution.py:43
  69.4 8.9 %collective-permute-start.6 = (bf16[256,1024]{1,0:T(8,128)(2,1)S(1)}, bf16[256,1024]{1,0:T(8,128)(2,1)S(1)}, u32[]{:S(2)}, u32[]{:S(2)}) collective-permute-start(bf16[256,1024]{1,0:T(8,128)(2,1)S(1)} %collective-permute-done.4.side), channel_id=1, source_target_pairs={{0,64},{64,0},{1,65},{65,1},{2,66},{66,2},{3,67},{67,3},{4,68},{68... | collective-permute-start | bytes 1572872 | tf_op jit(solution)/shard_map/ppermute | solution.py:31
  75.0 4.8 %collective-permute-start.7 = (bf16[256,1024]{1,0:T(8,128)(2,1)S(1)}, bf16[256,1024]{1,0:T(8,128)(2,1)S(1)}, u32[]{:S(2)}, u32[]{:S(2)}) collective-permute-start(bf16[256,1024]{1,0:T(8,128)(2,1)S(1)} %collective-permute-done.5.side2), channel_id=1, source_target_pairs={{0,64},{64,0},{1,65},{65,1},{2,66},{66,2},{3,67},{67,3},{4,68},{68... | collective-permute-start | bytes 1572872 | tf_op jit(solution)/shard_map/ppermute | solution.py:31
  81.7 13.2 %all-to-all-start.3 = ((bf16[16,16,384]{2,1,0:T(8,128)(2,1)}), bf16[16,16,384]{2,1,0:T(8,128)(2,1)S(1)}, u32[]{:S(2)}, u32[]{:S(2)}) async-start(bf16[16,16,384]{2,1,0:T(8,128)(2,1)} %bitcast.5), calls=%async_computation.3 | async-start | bytes 393216 | tf_op jit(solution)/shard_map/all_to_all | solution.py:194
  94.9 19.7 %all-to-all-start.2 = ((bf16[32,16,768]{2,1,0:T(8,128)(2,1)}), bf16[32,16,768]{2,1,0:T(8,128)(2,1)S(1)}, u32[]{:S(2)}, u32[]{:S(2)}) async-start(bf16[32,16,768]{2,1,0:T(8,128)(2,1)} %make_home.1), calls=%async_computation.2 | async-start | bytes 1572864 | tf_op jit(solution)/shard_map/all_to_all | solution.py:186
  100.3 14.3 %collective-permute-start.8 = (f32[16,384]{1,0:T(8,128)S(1)}, f32[16,384]{1,0:T(8,128)S(1)}, u32[]{:S(2)}, u32[]{:S(2)}) collective-permute-start(f32[16,384]{1,0:T(8,128)S(1)} %convert_reduce_fusion.1), channel_id=1, source_target_pairs={{0,4},{4,8},{8,12},{12,16},{16,20},{20,24},{24,28},{28,32},{32,36}... | collective-permute-start | bytes 73736 | tf_op jit(solution)/shard_map/ppermute | solution.py:36
  103.0 11.7 %collective-permute-start.9 = (f32[16,384]{1,0:T(8,128)S(1)}, f32[16,384]{1,0:T(8,128)S(1)}, u32[]{:S(2)}, u32[]{:S(2)}) collective-permute-start(f32[16,384]{1,0:T(8,128)S(1)} %convert_reduce_fusion.1), channel_id=1, source_target_pairs={{0,60},{4,0},{8,4},{12,8},{16,12},{20,16},{24,20},{28,24},{32,28},... | collective-permute-start | bytes 73736 | tf_op jit(solution)/shard_map/ppermute | solution.py:36

commit v5 on v3

v5 whole, which is shorter than its diff:
```python
import jax
import jax.numpy as jnp
from jax import lax
from jax.experimental import pallas as pl
from jax.experimental.pallas import tpu as pltpu
from jax.sharding import Mesh, PartitionSpec as P

ROWS = 128
HALF = 64
COLS = 512
SPAN = 15
F32 = jnp.float32
BF16 = jnp.bfloat16
VMEM = pl.BlockSpec(memory_space=pltpu.VMEM)
SMEM = pl.BlockSpec(memory_space=pltpu.SMEM)
ANY = pl.BlockSpec(memory_space=pl.ANY)


def call(kernel, name, specs, shape, dtype, *args, scratch=(), out=VMEM):
    return pl.pallas_call(
        kernel,
        in_specs=specs,
        out_specs=out,
        out_shape=jax.ShapeDtypeStruct(shape, dtype),
        scratch_shapes=scratch,
        compiler_params=pltpu.CompilerParams(vmem_limit_bytes=12 * 2**20),
        name=name,
    )(*args)


def moved(x, axis, by):
    n = lax.axis_size(axis)
    return lax.ppermute(x, axis, [(i, (i + by) % n) for i in range(n)])


def swapped(x):
    return moved(x, "core", 1)


def sided(x, by):
    n = lax.axis_size("z")
    pairs = [(i, (i + by) % n) for i in range(n)]
    pairs += [(n + i, n + (i - by) % n) for i in range(n)]
    return lax.ppermute(x, ("core", "z"), pairs)


def orbital_kernel(occupied, out, sems):
    copies = [
        pltpu.make_async_copy(occupied.at[:, pl.ds(x * COLS, COLS)], out.at[x], sems.at[x])
        for x in range(4)
    ]
    for copy in copies:
        copy.start()
    for copy in copies:
        copy.wait()


def integral_kernel(mask, integrals, out):
    for s in range(SPAN):
        tile = integrals[s]
        tile = jnp.where(mask[0, s] != 0, tile, jnp.zeros_like(tile))
        for core in range(2):
            for k in range(4):
                at = k * 32 + core * 16
                for x in range(4):
                    out[x, core, s, k * 16 : k * 16 + 16, :] = tile[at : at + 16]


def half_kernel(core, tiles, plane, mine, other, half, window, sems):
    c = core[0]
    moves = (
        (plane, 0, 4, 7),
        (mine, 0, 3, c * 15),
        (mine, 3, 4, 3 + c * 8),
        (other, 0, 3, 15 - c * 15),
        (other, 3, 4, 11 - c * 8),
    )
    copies = [
        pltpu.make_async_copy(part.at[pl.ds(first, n)], window.at[pl.ds(at, n)], sems.at[i])
        for i, (part, first, n, at) in enumerate(moves)
    ]
    for copy in copies:
        copy.start()
    for copy in copies:
        copy.wait()
    for a in range(4):
        near = window[a : a + SPAN].reshape(SPAN * ROWS, COLS)
        wide = jnp.concatenate(
            [tiles[2 * a : 2 * a + 2, s].reshape(2 * HALF, ROWS) for s in range(SPAN)], 1
        )
        made = jnp.dot(wide, near, preferred_element_type=F32).astype(BF16)
        half[a * HALF : (a + 1) * HALF, :COLS] = made[:HALF]
        half[a * HALF : (a + 1) * HALF, COLS:] = made[HALF:]


def dot_t(a, b):
    return lax.dot_general(a, b, (((1,), (1,)), ((), ())), preferred_element_type=F32)


def interleave(c, mine, other, wide, at):
    for k in range(16):
        to = at + k * 32
        rows = slice(k * 16, k * 16 + 16)
        wide[pl.ds(pl.multiple_of(to + c * 16, 16), 16), :] = mine[rows, :]
        wide[pl.ds(pl.multiple_of(to + 16 - c * 16, 16), 16), :] = other[rows, :]


def inner_kernel(core, own, own2, out, wide):
    interleave(core[0], own, own2, wide, 0)
    out[...] = dot_t(own[...], wide[...]).astype(BF16)


def tile_kernel(core, inner, own, up, down, up2, down2, out, wide):
    interleave(core[0], up, up2, wide, 0)
    interleave(core[0], down, down2, wide, 512)
    out[:, 0:512] = dot_t(own[...], wide[0:512, :]).astype(BF16)
    out[:, 512:1024] = inner[...]
    out[:, 1024:1536] = dot_t(own[...], wide[512:1024, :]).astype(BF16)
    for x in range(4):
        rows = slice(x * HALF, (x + 1) * HALF)
        cut = 1536 + x * ROWS
        if x > 0:
            out[rows, 1536:cut] = dot_t(up[rows, :], wide[512 : 512 + x * ROWS, :]).astype(BF16)
        if x < 3:
            out[rows, cut:] = dot_t(down[rows, :], wide[(x + 1) * ROWS : 512, :]).astype(BF16)


def sum_kernel(parts, out):
    for t in range(SPAN):
        total = parts[0, :, t * ROWS : (t + 1) * ROWS].astype(F32)
        for k in range(1, 16):
            total += parts[k, :, t * ROWS : (t + 1) * ROWS].astype(F32)
        out[t] = total


def per_device(occupied, integrals, pair_mask):
    x = lax.axis_index("x")
    c = lax.axis_index("core")
    core = c[None]

    pieces = call(
        orbital_kernel, "cut_orbitals", [ANY], (4, ROWS, COLS), BF16, occupied,
        scratch=[pltpu.SemaphoreType.DMA((4,))], out=ANY,
    )
    plane = lax.all_to_all(pieces, "x", 0, 0)

    tiles = call(
        integral_kernel, "cut_integrals", [SMEM, VMEM], (4, 2, SPAN, HALF, ROWS), BF16,
        pair_mask, integrals[0, 0],
    )
    tiles = lax.all_to_all(tiles.reshape(8, SPAN, HALF, ROWS), ("x", "core"), 0, 0)

    two_away = sided(lax.dynamic_slice_in_dim(plane, 1 - c, 3, 0), 2)
    one_away = sided(plane, 1)
    mine = jnp.concatenate([two_away, one_away])
    other = swapped(mine)

    own = call(
        half_kernel, "make_half", [SMEM, VMEM] + [ANY] * 3, (4 * HALF, 2 * COLS), BF16,
        core, tiles, plane, mine, other,
        scratch=[pltpu.VMEM((18, ROWS, COLS), BF16), pltpu.SemaphoreType.DMA((5,))],
    )

    up = moved(own, "z", 1)
    down = moved(own, "z", -1)
    own2 = swapped(own)
    inner = call(
        inner_kernel, "make_inner", [SMEM] + [VMEM] * 2, (256, 512), BF16, core, own, own2,
        scratch=[pltpu.VMEM((512, 2 * COLS), BF16)],
    )
    inner, up, down = lax.optimization_barrier((inner, up, down))
    partial = call(
        tile_kernel, "make_tiles", [SMEM] + [VMEM] * 6, (256, SPAN * ROWS), BF16,
        core, inner, own, up, down, swapped(up), swapped(down),
        scratch=[pltpu.VMEM((1024, 2 * COLS), BF16)],
    )
    partial = lax.all_to_all(partial.reshape(16, 16, SPAN * ROWS), ("x", "y"), 0, 0)
    total = call(sum_kernel, "sum_parts", [VMEM], (SPAN, 16, ROWS), F32, partial)
    far = total[12:]
    line = jnp.concatenate([moved(far, "z", 1), total[:12], moved(far, "z", -1)], 0)
    out = lax.dynamic_slice_in_dim(line, x, SPAN, 0)
    return (out * pair_mask[0].astype(F32)[:, None, None])[None]


def solution(mesh):
    split = Mesh(mesh.devices.reshape(4, 2, 16, 4), ("y", "core", "z", "x"))
    aux, orb = ("y", "core"), ("z", "x")
    return jax.shard_map(
        per_device,
        mesh=split,
        in_specs=(P(orb, None), P(aux, orb, None, None, None), P(orb, None)),
        out_specs=P(orb, None, aux, None),
        check_vma=False,
    )
```

time: 114 us -> 116 us (1.018)
  the two profiles are of different devices: /device:TPU:96 before, /device:TPU:8 now
where the time goes in v5:
time: 116 us; the launch traced here: 115 us
  starting transfers between devices  41.2 us (36%)
  waiting for transfers between devices  40.5 us (35%)
  blocking collectives  23.2 us (20%)
  Pallas kernels  6.85 us (6%)
  local copies, waits for them, and re-layouts  2.45 us (2%)
    ppermute x8, starting transfers between devices, moved(): return lax.ppermute(x, axis, [(i, (i + by) % n) for i in range(n)])  24.3 us
    all_to_all x1, blocking collectives, per_device(): lax.all_to_all(partial.reshape(16, 16, SPAN * ROWS), ('x', 'y'), 0, 0)  23.2 us
    ppermute x2, waiting for transfers between devices, sided(): return lax.ppermute(x, ('core', 'z'), pairs)  16.6 us
    ppermute x8, waiting for transfers between devices, moved(): return lax.ppermute(x, axis, [(i, (i + by) % n) for i in range(n)])  16.5 us
    ppermute x2, starting transfers between devices, sided(): return lax.ppermute(x, ('core', 'z'), pairs)  9.01 us
    all_to_all x1, waiting for transfers between devices, per_device(): plane = lax.all_to_all(pieces, 'x', 0, 0)  7.36 us
    pallas_call x6, Pallas kernels, call(): pl.pallas_call(kernel, in_specs=specs, out_specs=out, out_shape=jax.Shape...  6.85 us
    all_to_all x1, starting transfers between devices, per_device(): plane = lax.all_to_all(pieces, 'x', 0, 0)  4.3 us
  transfers between devices with their start and end apart: 12, of which 7 were waited for; matrix products, arithmetic and copies ran while one was open for 0% of the time, Pallas kernels for 1%

profile of v5, /device:TPU:8, one launch (start us, length us, event | category | flops | bytes accessed | tf_op | source)
XLA Modules:
  0.0 115.1 jit_solution(16372929715319895113)
XLA Ops:
  0.0 1.0 copy-done.1
  1.0 0.8 cut_orbitals.1
  1.9 4.3 %all-to-all-start.1 = ((bf16[4,128,512]{2,1,0:T(8,128)(2,1)}), bf16[4,128,512]{2,1,0:T(8,128)(2,1)S(1)}, u32[]{:S(2)}, u32[]{:S(2)}) async-start(bf16[4,128,512]{2,1,0:T(8,128)(2,1)} %cut_orbitals.1), calls=%async_computation.1 | async-start | bytes 1048576 | tf_op jit(solution)/shard_map/all_to_all | solution.py:145
  6.2 0.8 cut_integrals.1
  7.0 1.3 %copy-done = bf16[4,2,15,64,128]{4,3,2,1,0:T(8,128)(2,1)} copy-done((bf16[4,2,15,64,128]{4,3,2,1,0:T(8,128)(2,1)}, bf16[4,2,15,64,128]{4,3,2,1,0:T(8,128)(2,1)S(1)}, u32[]{:S(2)}) %copy-start) | copy-done | bytes 1966104
  8.3 7.4 %all-to-all-done.1.plane = bf16[4,128,512]{2,1,0:T(8,128)(2,1)S(1)} async-done(((bf16[4,128,512]{2,1,0:T(8,128)(2,1)}), bf16[4,128,512]{2,1,0:T(8,128)(2,1)S(1)}, u32[]{:S(2)}, u32[]{:S(2)}) %all-to-all-start.1) | async-done | bytes 524320 | tf_op jit(solution)/shard_map/all_to_all | solution.py:145
  15.7 3.6 %all-to-all-start = ((bf16[8,15,64,128]{3,2,1,0:T(8,128)(2,1)}), bf16[8,15,64,128]{3,2,1,0:T(8,128)(2,1)S(1)}, u32[]{:S(2)}, u32[]{:S(2)}) async-start(bf16[8,15,64,128]{3,2,1,0:T(8,128)(2,1)} %bitcast.8), calls=%async_computation | async-start | bytes 3932160 | tf_op jit(solution)/shard_map/all_to_all | solution.py:151
  19.3 3.8 %collective-permute-start.1 = (bf16[4,128,512]{2,1,0:T(8,128)(2,1)S(1)}, bf16[4,128,512]{2,1,0:T(8,128)(2,1)S(1)}, u32[]{:S(2)}, u32[]{:S(2)}) collective-permute-start(bf16[4,128,512]{2,1,0:T(8,128)(2,1)S(1)} %all-to-all-done.1.plane), channel_id=1, source_target_pairs={{0,4},{4,8},{8,12},{12,16},{16,20},{20,24},{24,28},{28,32},{32,36}... | collective-permute-start | bytes 1572872 | tf_op jit(solution)/shard_map/ppermute | solution.py:44
  23.2 5.2 %collective-permute-start = (bf16[3,128,512]{2,1,0:T(8,128)(2,1)S(1)}, bf16[3,128,512]{2,1,0:T(8,128)(2,1)S(1)}, u32[]{:S(2)}, u32[]{:S(2)}) collective-permute-start(bf16[3,128,512]{2,1,0:T(8,128)(2,1)S(1)} %constant_dynamic-slice_fusion), channel_id=1, source_target_pairs={{0,8},{4,12},{8,16},{12,20},{16,24},{20,28},{24,32},{28,36},{32,40... | collective-permute-start | bytes 1179656 | tf_op jit(solution)/shard_map/ppermute | solution.py:44
  28.4 16.6 %collective-permute-done = bf16[3,128,512]{2,1,0:T(8,128)(2,1)S(1)} collective-permute-done((bf16[3,128,512]{2,1,0:T(8,128)(2,1)S(1)}, bf16[3,128,512]{2,1,0:T(8,128)(2,1)S(1)}, u32[]{:S(2)}, u32[]{:S(2)}) %collective-permute-start) | collective-permute-done | bytes 393248 | tf_op jit(solution)/shard_map/ppermute | solution.py:44
  45.0 0.0 collective-permute-done.1
  45.1 2.3 %collective-permute-start.2 = (bf16[7,128,512]{2,1,0:T(8,128)(2,1)S(1)}, bf16[7,128,512]{2,1,0:T(8,128)(2,1)}, u32[]{:S(2)}, u32[]{:S(2)}) collective-permute-start(bf16[7,128,512]{2,1,0:T(8,128)(2,1)S(1)} %constant_dynamic-update-slice_fusion.mine), channel_id=1, source_target_pairs={{0,64},{64,0},{1,65},{65,1},{2,66},{66,2},{3,67},{67,3},{4,68},{68... | collective-permute-start | bytes 2752520 | tf_op jit(solution)/shard_map/ppermute | solution.py:33
  47.3 0.0 all-to-all-done.tiles
  47.4 2.2 %collective-permute-done.2.other = bf16[7,128,512]{2,1,0:T(8,128)(2,1)} collective-permute-done((bf16[7,128,512]{2,1,0:T(8,128)(2,1)S(1)}, bf16[7,128,512]{2,1,0:T(8,128)(2,1)}, u32[]{:S(2)}, u32[]{:S(2)}) %collective-permute-start.2) | collective-permute-done | bytes 917536 | tf_op jit(solution)/shard_map/ppermute | solution.py:33
  49.6 2.7 %make_half.1.own = bf16[256,1024]{1,0:T(8,128)(2,1)S(1)} custom-call(s32[1]{0:T(128)} %bitcast.core, bf16[8,15,64,128]{3,2,1,0:T(8,128)(2,1)S(1)} %all-to-all-done.tiles, bf16[4,128,512]{2,1,0:T(8,128)(2,1)S(1)} %all-to-all-done.1.plane, bf16[7,128,512]{2,1,0:T(8,128)(2,1)S(1)} %constant_dynamic-update-slice_fusion.mine, ...), custom_call_target="tpu_custom_call" | custom-call | tf_op jit(solution)/shard_map/make_half/pallas_call | solution.py:20
  52.3 2.3 %collective-permute-start.3 = (bf16[256,1024]{1,0:T(8,128)(2,1)S(1)}, bf16[256,1024]{1,0:T(8,128)(2,1)S(1)}, u32[]{:S(2)}, u32[]{:S(2)}) collective-permute-start(bf16[256,1024]{1,0:T(8,128)(2,1)S(1)} %make_half.1.own), channel_id=1, source_target_pairs={{0,64},{64,0},{1,65},{65,1},{2,66},{66,2},{3,67},{67,3},{4,68},{68... | collective-permute-start | bytes 1572872 | tf_op jit(solution)/shard_map/ppermute | solution.py:33
  54.6 4.5 %collective-permute-start.4 = (bf16[256,1024]{1,0:T(8,128)(2,1)S(1)}, bf16[256,1024]{1,0:T(8,128)(2,1)S(1)}, u32[]{:S(2)}, u32[]{:S(2)}) collective-permute-start(bf16[256,1024]{1,0:T(8,128)(2,1)S(1)} %make_half.1.own), channel_id=1, source_target_pairs={{0,4},{4,8},{8,12},{12,16},{16,20},{20,24},{24,28},{28,32},{32,36}... | collective-permute-start | bytes 1572872 | tf_op jit(solution)/shard_map/ppermute | solution.py:33
  59.0 4.0 %collective-permute-start.5 = (bf16[256,1024]{1,0:T(8,128)(2,1)S(1)}, bf16[256,1024]{1,0:T(8,128)(2,1)S(1)}, u32[]{:S(2)}, u32[]{:S(2)}) collective-permute-start(bf16[256,1024]{1,0:T(8,128)(2,1)S(1)} %make_half.1.own), channel_id=1, source_target_pairs={{0,60},{4,0},{8,4},{12,8},{16,12},{20,16},{24,20},{28,24},{32,28},... | collective-permute-start | bytes 1572872 | tf_op jit(solution)/shard_map/ppermute | solution.py:33
  63.0 0.0 collective-permute-done.3.own2
  63.0 0.5 make_inner.1.inner
  63.6 10.1 %collective-permute-done.4.up = bf16[256,1024]{1,0:T(8,128)(2,1)S(1)} collective-permute-done((bf16[256,1024]{1,0:T(8,128)(2,1)S(1)}, bf16[256,1024]{1,0:T(8,128)(2,1)S(1)}, u32[]{:S(2)}, u32[]{:S(2)}) %collective-permute-start.4) | collective-permute-done | bytes 524320 | tf_op jit(solution)/shard_map/ppermute | solution.py:33
  73.6 1.2 %collective-permute-done.5.down = bf16[256,1024]{1,0:T(8,128)(2,1)S(1)} collective-permute-done((bf16[256,1024]{1,0:T(8,128)(2,1)S(1)}, bf16[256,1024]{1,0:T(8,128)(2,1)S(1)}, u32[]{:S(2)}, u32[]{:S(2)}) %collective-permute-start.5) | collective-permute-done | bytes 524320 | tf_op jit(solution)/shard_map/ppermute | solution.py:33
  74.8 1.9 %collective-permute-start.6 = (bf16[256,1024]{1,0:T(8,128)(2,1)S(1)}, bf16[256,1024]{1,0:T(8,128)(2,1)S(1)}, u32[]{:S(2)}, u32[]{:S(2)}) collective-permute-start(bf16[256,1024]{1,0:T(8,128)(2,1)S(1)} %collective-permute-done.4.up), channel_id=1, source_target_pairs={{0,64},{64,0},{1,65},{65,1},{2,66},{66,2},{3,67},{67,3},{4,68},{68... | collective-permute-start | bytes 1572872 | tf_op jit(solution)/shard_map/ppermute | solution.py:33
  76.7 2.4 %collective-permute-start.7 = (bf16[256,1024]{1,0:T(8,128)(2,1)S(1)}, bf16[256,1024]{1,0:T(8,128)(2,1)S(1)}, u32[]{:S(2)}, u32[]{:S(2)}) collective-permute-start(bf16[256,1024]{1,0:T(8,128)(2,1)S(1)} %collective-permute-done.5.down), channel_id=1, source_target_pairs={{0,64},{64,0},{1,65},{65,1},{2,66},{66,2},{3,67},{67,3},{4,68},{68... | collective-permute-start | bytes 1572872 | tf_op jit(solution)/shard_map/ppermute | solution.py:33
  79.2 1.5 %collective-permute-done.7.down2 = bf16[256,1024]{1,0:T(8,128)(2,1)S(1)} collective-permute-done((bf16[256,1024]{1,0:T(8,128)(2,1)S(1)}, bf16[256,1024]{1,0:T(8,128)(2,1)S(1)}, u32[]{:S(2)}, u32[]{:S(2)}) %collective-permute-start.7) | collective-permute-done | bytes 524320 | tf_op jit(solution)/shard_map/ppermute | solution.py:33
  80.7 1.8 %make_tiles.1 = bf16[256,1920]{1,0:T(8,128)(2,1)S(1)} custom-call(s32[1]{0:T(128)} %bitcast.core, bf16[256,512]{1,0:T(8,128)(2,1)S(1)} %make_inner.1.inner, bf16[256,1024]{1,0:T(8,128)(2,1)S(1)} %make_half.1.own, bf16[256,1024]{1,0:T(8,128)(2,1)S(1)} %collective-permute-done.4.up, bf16[256,1024]{1,0:T(8,128)(2,1)S(1)} %collective-permute-done.5.down, ...), custom_call_target="tpu_custom_call" | custom-call | tf_op jit(solution)/shard_map/make_tiles/pallas_call | solution.py:20
  82.5 23.2 %all_to_all.15.parts = bf16[16,16,1920]{2,1,0:T(8,128)(2,1)S(1)} all-to-all(bf16[16,16,1920]{2,1,0:T(8,128)(2,1)S(1)} %bitcast.9), channel_id=1, replica_groups=mesh['y'=4,'core'=2,'z'=16,'x'=4] {'x','y'}, dimensions={0} | all-to-all | bytes 1966080 | tf_op jit(solution)/shard_map/all_to_all | solution.py:177
  105.7 0.1 sum_parts.1
  105.8 2.2 %collective-permute-start.8 = (f32[3,16,128]{2,1,0:T(8,128)S(1)}, f32[3,16,128]{2,1,0:T(8,128)S(1)}, u32[]{:S(2)}, u32[]{:S(2)}) collective-permute-start(f32[3,16,128]{2,1,0:T(8,128)S(1)} %slice.8), channel_id=1, source_target_pairs={{0,4},{4,8},{8,12},{12,16},{16,20},{20,24},{24,28},{28,32},{32,36}... | collective-permute-start | bytes 73736 | tf_op jit(solution)/shard_map/ppermute | solution.py:33
  108.0 4.8 %collective-permute-start.9 = (f32[3,16,128]{2,1,0:T(8,128)S(1)}, f32[3,16,128]{2,1,0:T(8,128)S(1)}, u32[]{:S(2)}, u32[]{:S(2)}) collective-permute-start(f32[3,16,128]{2,1,0:T(8,128)S(1)} %slice.8), channel_id=1, source_target_pairs={{0,60},{4,0},{8,4},{12,8},{16,12},{20,16},{24,20},{28,24},{32,28},... | collective-permute-start | bytes 73736 | tf_op jit(solution)/shard_map/ppermute | solution.py:33
  112.9 1.5 %collective-permute-done.9 = f32[3,16,128]{2,1,0:T(8,128)S(1)} collective-permute-done((f32[3,16,128]{2,1,0:T(8,128)S(1)}, f32[3,16,128]{2,1,0:T(8,128)S(1)}, u32[]{:S(2)}, u32[]{:S(2)}) %collective-permute-start.9) | collective-permute-done | bytes 24608 | tf_op jit(solution)/shard_map/ppermute | solution.py:33
  114.4 0.7 fusion.3
  (14 shorter events, 0.1 us)
Async XLA Ops:
  0.0 1.0 copy-start.1
  1.0 5.2 %copy-start.2 = (bf16[1,1,15,128,128]{4,3,2,1,0:T(8,128)(2,1)S(1)}, bf16[1,1,15,128,128]{4,3,2,1,0:T(8,128)(2,1)}, u32[]{:S(2)}) copy-start(bf16[1,1,15,128,128]{4,3,2,1,0:T(8,128)(2,1)} %param.4) | copy-start | bytes 1474564
  1.0 5.2 %copy-start.3 = (s32[1,15]{1,0:T(1,128)S(1)}, s32[1,15]{1,0:T(1,128)}, u32[]{:S(2)}) copy-start(s32[1,15]{1,0:T(1,128)} %mask.1) | copy-start | bytes 184
  1.9 13.8 %all-to-all-start.1 = ((bf16[4,128,512]{2,1,0:T(8,128)(2,1)}), bf16[4,128,512]{2,1,0:T(8,128)(2,1)S(1)}, u32[]{:S(2)}, u32[]{:S(2)}) async-start(bf16[4,128,512]{2,1,0:T(8,128)(2,1)} %cut_orbitals.1), calls=%async_computation.1 | async-start | bytes 1048576 | tf_op jit(solution)/shard_map/all_to_all | solution.py:145
  7.0 1.3 %copy-start = (bf16[4,2,15,64,128]{4,3,2,1,0:T(8,128)(2,1)}, bf16[4,2,15,64,128]{4,3,2,1,0:T(8,128)(2,1)S(1)}, u32[]{:S(2)}) copy-start(bf16[4,2,15,64,128]{4,3,2,1,0:T(8,128)(2,1)S(1)} %cut_integrals.1) | copy-start | bytes 5898244
  15.7 31.7 %all-to-all-start = ((bf16[8,15,64,128]{3,2,1,0:T(8,128)(2,1)}), bf16[8,15,64,128]{3,2,1,0:T(8,128)(2,1)S(1)}, u32[]{:S(2)}, u32[]{:S(2)}) async-start(bf16[8,15,64,128]{3,2,1,0:T(8,128)(2,1)} %bitcast.8), calls=%async_computation | async-start | bytes 3932160 | tf_op jit(solution)/shard_map/all_to_all | solution.py:151
  19.3 25.7 %collective-permute-start.1 = (bf16[4,128,512]{2,1,0:T(8,128)(2,1)S(1)}, bf16[4,128,512]{2,1,0:T(8,128)(2,1)S(1)}, u32[]{:S(2)}, u32[]{:S(2)}) collective-permute-start(bf16[4,128,512]{2,1,0:T(8,128)(2,1)S(1)} %all-to-all-done.1.plane), channel_id=1, source_target_pairs={{0,4},{4,8},{8,12},{12,16},{16,20},{20,24},{24,28},{28,32},{32,36}... | collective-permute-start | bytes 1572872 | tf_op jit(solution)/shard_map/ppermute | solution.py:44
  23.2 21.8 %collective-permute-start = (bf16[3,128,512]{2,1,0:T(8,128)(2,1)S(1)}, bf16[3,128,512]{2,1,0:T(8,128)(2,1)S(1)}, u32[]{:S(2)}, u32[]{:S(2)}) collective-permute-start(bf16[3,128,512]{2,1,0:T(8,128)(2,1)S(1)} %constant_dynamic-slice_fusion), channel_id=1, source_target_pairs={{0,8},{4,12},{8,16},{12,20},{16,24},{20,28},{24,32},{28,36},{32,40... | collective-permute-start | bytes 1179656 | tf_op jit(solution)/shard_map/ppermute | solution.py:44
  45.1 4.5 %collective-permute-start.2 = (bf16[7,128,512]{2,1,0:T(8,128)(2,1)S(1)}, bf16[7,128,512]{2,1,0:T(8,128)(2,1)}, u32[]{:S(2)}, u32[]{:S(2)}) collective-permute-start(bf16[7,128,512]{2,1,0:T(8,128)(2,1)S(1)} %constant_dynamic-update-slice_fusion.mine), channel_id=1, source_target_pairs={{0,64},{64,0},{1,65},{65,1},{2,66},{66,2},{3,67},{67,3},{4,68},{68... | collective-permute-start | bytes 2752520 | tf_op jit(solution)/shard_map/ppermute | solution.py:33
  52.3 10.7 %collective-permute-start.3 = (bf16[256,1024]{1,0:T(8,128)(2,1)S(1)}, bf16[256,1024]{1,0:T(8,128)(2,1)S(1)}, u32[]{:S(2)}, u32[]{:S(2)}) collective-permute-start(bf16[256,1024]{1,0:T(8,128)(2,1)S(1)} %make_half.1.own), channel_id=1, source_target_pairs={{0,64},{64,0},{1,65},{65,1},{2,66},{66,2},{3,67},{67,3},{4,68},{68... | collective-permute-start | bytes 1572872 | tf_op jit(solution)/shard_map/ppermute | solution.py:33
  54.6 19.1 %collective-permute-start.4 = (bf16[256,1024]{1,0:T(8,128)(2,1)S(1)}, bf16[256,1024]{1,0:T(8,128)(2,1)S(1)}, u32[]{:S(2)}, u32[]{:S(2)}) collective-permute-start(bf16[256,1024]{1,0:T(8,128)(2,1)S(1)} %make_half.1.own), channel_id=1, source_target_pairs={{0,4},{4,8},{8,12},{12,16},{16,20},{20,24},{24,28},{28,32},{32,36}... | collective-permute-start | bytes 1572872 | tf_op jit(solution)/shard_map/ppermute | solution.py:33
  59.0 15.8 %collective-permute-start.5 = (bf16[256,1024]{1,0:T(8,128)(2,1)S(1)}, bf16[256,1024]{1,0:T(8,128)(2,1)S(1)}, u32[]{:S(2)}, u32[]{:S(2)}) collective-permute-start(bf16[256,1024]{1,0:T(8,128)(2,1)S(1)} %make_half.1.own), channel_id=1, source_target_pairs={{0,60},{4,0},{8,4},{12,8},{16,12},{20,16},{24,20},{28,24},{32,28},... | collective-permute-start | bytes 1572872 | tf_op jit(solution)/shard_map/ppermute | solution.py:33
  74.8 4.3 %collective-permute-start.6 = (bf16[256,1024]{1,0:T(8,128)(2,1)S(1)}, bf16[256,1024]{1,0:T(8,128)(2,1)S(1)}, u32[]{:S(2)}, u32[]{:S(2)}) collective-permute-start(bf16[256,1024]{1,0:T(8,128)(2,1)S(1)} %collective-permute-done.4.up), channel_id=1, source_target_pairs={{0,64},{64,0},{1,65},{65,1},{2,66},{66,2},{3,67},{67,3},{4,68},{68... | collective-permute-start | bytes 1572872 | tf_op jit(solution)/shard_map/ppermute | solution.py:33
  76.7 3.9 %collective-permute-start.7 = (bf16[256,1024]{1,0:T(8,128)(2,1)S(1)}, bf16[256,1024]{1,0:T(8,128)(2,1)S(1)}, u32[]{:S(2)}, u32[]{:S(2)}) collective-permute-start(bf16[256,1024]{1,0:T(8,128)(2,1)S(1)} %collective-permute-done.5.down), channel_id=1, source_target_pairs={{0,64},{64,0},{1,65},{65,1},{2,66},{66,2},{3,67},{67,3},{4,68},{68... | collective-permute-start | bytes 1572872 | tf_op jit(solution)/shard_map/ppermute | solution.py:33
  105.8 7.1 %collective-permute-start.8 = (f32[3,16,128]{2,1,0:T(8,128)S(1)}, f32[3,16,128]{2,1,0:T(8,128)S(1)}, u32[]{:S(2)}, u32[]{:S(2)}) collective-permute-start(f32[3,16,128]{2,1,0:T(8,128)S(1)} %slice.8), channel_id=1, source_target_pairs={{0,4},{4,8},{8,12},{12,16},{16,20},{20,24},{24,28},{28,32},{32,36}... | collective-permute-start | bytes 73736 | tf_op jit(solution)/shard_map/ppermute | solution.py:33
  108.0 6.4 %collective-permute-start.9 = (f32[3,16,128]{2,1,0:T(8,128)S(1)}, f32[3,16,128]{2,1,0:T(8,128)S(1)}, u32[]{:S(2)}, u32[]{:S(2)}) collective-permute-start(f32[3,16,128]{2,1,0:T(8,128)S(1)} %slice.8), channel_id=1, source_target_pairs={{0,60},{4,0},{8,4},{12,8},{16,12},{20,16},{24,20},{28,24},{32,28},... | collective-permute-start | bytes 73736 | tf_op jit(solution)/shard_map/ppermute | solution.py:33

commit v6 on v5

--- a/solution.py
+++ b/solution.py
@@ -13,6 +13,7 @@
 BF16 = jnp.bfloat16
 VMEM = pl.BlockSpec(memory_space=pltpu.VMEM)
 SMEM = pl.BlockSpec(memory_space=pltpu.SMEM)
+HBM = pl.BlockSpec(memory_space=pltpu.HBM)
 ANY = pl.BlockSpec(memory_space=pl.ANY)
 
 
@@ -37,16 +38,10 @@
     return moved(x, "core", 1)
 
 
-def sided(x, by):
-    n = lax.axis_size("z")
-    pairs = [(i, (i + by) % n) for i in range(n)]
-    pairs += [(n + i, n + (i - by) % n) for i in range(n)]
-    return lax.ppermute(x, ("core", "z"), pairs)
-
-
-def orbital_kernel(occupied, out, sems):
+def orbital_kernel(core, occupied, out, sems):
+    rows = pl.ds(pl.multiple_of(core[0] * HALF, HALF), HALF)
     copies = [
-        pltpu.make_async_copy(occupied.at[:, pl.ds(x * COLS, COLS)], out.at[x], sems.at[x])
+        pltpu.make_async_copy(occupied.at[rows, pl.ds(x * COLS, COLS)], out.at[x], sems.at[x])
         for x in range(4)
     ]
     for copy in copies:
@@ -66,21 +61,20 @@
                     out[x, core, s, k * 16 : k * 16 + 16, :] = tile[at : at + 16]
 
 
-def half_kernel(core, tiles, plane, mine, other, half, window, sems):
+def half_kernel(core, tiles, below2, below, plane, above, above2, first, second, half, window, sems):
     c = core[0]
-    moves = (
-        (plane, 0, 4, 7),
-        (mine, 0, 3, c * 15),
-        (mine, 3, 4, 3 + c * 8),
-        (other, 0, 3, 15 - c * 15),
-        (other, 3, 4, 11 - c * 8),
-    )
+    moves = ((first, 4, 3, 0), (second, 0, 4, 3), (first, 0, 4, 7), (second, 4, 4, 11), (first, 7, 3, 15))
     copies = [
-        pltpu.make_async_copy(part.at[pl.ds(first, n)], window.at[pl.ds(at, n)], sems.at[i])
-        for i, (part, first, n, at) in enumerate(moves)
+        pltpu.make_async_copy(part.at[pl.ds(at, n)], window.at[pl.ds(to, n), 1 - c], sems.at[i])
+        for i, (part, at, n, to) in enumerate(moves)
     ]
     for copy in copies:
         copy.start()
+    at = 0
+    for part in (below2, below, plane, above, above2):
+        for b in range(part.shape[0]):
+            window[at, c] = part[b]
+            at += 1
     for copy in copies:
         copy.wait()
     for a in range(4):
@@ -105,22 +99,16 @@
         wide[pl.ds(pl.multiple_of(to + 16 - c * 16, 16), 16), :] = other[rows, :]
 
 
-def inner_kernel(core, own, own2, out, wide):
-    interleave(core[0], own, own2, wide, 0)
-    out[...] = dot_t(own[...], wide[...]).astype(BF16)
-
-
-def tile_kernel(core, inner, own, up, down, up2, down2, out, wide):
-    interleave(core[0], up, up2, wide, 0)
-    interleave(core[0], down, down2, wide, 512)
-    out[:, 0:512] = dot_t(own[...], wide[0:512, :]).astype(BF16)
-    out[:, 512:1024] = inner[...]
-    out[:, 1024:1536] = dot_t(own[...], wide[512:1024, :]).astype(BF16)
+def tile_kernel(core, up, own, down, up2, own2, down2, out, wide):
+    for i, (mine, other) in enumerate(((up, up2), (own, own2), (down, down2))):
+        interleave(core[0], mine, other, wide, i * 512)
+    for i in range(3):
+        out[:, i * 512 : (i + 1) * 512] = dot_t(own[...], wide[i * 512 : (i + 1) * 512, :]).astype(BF16)
     for x in range(4):
         rows = slice(x * HALF, (x + 1) * HALF)
         cut = 1536 + x * ROWS
         if x > 0:
-            out[rows, 1536:cut] = dot_t(up[rows, :], wide[512 : 512 + x * ROWS, :]).astype(BF16)
+            out[rows, 1536:cut] = dot_t(up[rows, :], wide[1024 : 1024 + x * ROWS, :]).astype(BF16)
         if x < 3:
             out[rows, cut:] = dot_t(down[rows, :], wide[(x + 1) * ROWS : 512, :]).astype(BF16)
 
@@ -139,8 +127,8 @@
     core = c[None]
 
     pieces = call(
-        orbital_kernel, "cut_orbitals", [ANY], (4, ROWS, COLS), BF16, occupied,
-        scratch=[pltpu.SemaphoreType.DMA((4,))], out=ANY,
+        orbital_kernel, "cut_orbitals", [SMEM, HBM], (4, HALF, COLS), BF16, core, occupied,
+        scratch=[pltpu.SemaphoreType.DMA((4,))], out=HBM,
     )
     plane = lax.all_to_all(pieces, "x", 0, 0)
 
@@ -150,29 +138,27 @@
     )
     tiles = lax.all_to_all(tiles.reshape(8, SPAN, HALF, ROWS), ("x", "core"), 0, 0)
 
-    two_away = sided(lax.dynamic_slice_in_dim(plane, 1 - c, 3, 0), 2)
-    one_away = sided(plane, 1)
-    mine = jnp.concatenate([two_away, one_away])
-    other = swapped(mine)
+    below2 = moved(plane[1:], "z", 2)
+    above2 = moved(plane[:3], "z", -2)
+    below = moved(plane, "z", 1)
+    above = moved(plane, "z", -1)
+    first = swapped(jnp.concatenate([plane, below2, above2]))
+    tiles, above = lax.optimization_barrier((tiles, above))
+    second = swapped(jnp.concatenate([below, above]))
 
     own = call(
-        half_kernel, "make_half", [SMEM, VMEM] + [ANY] * 3, (4 * HALF, 2 * COLS), BF16,
-        core, tiles, plane, mine, other,
-        scratch=[pltpu.VMEM((18, ROWS, COLS), BF16), pltpu.SemaphoreType.DMA((5,))],
+        half_kernel, "make_half", [SMEM] + [VMEM] * 6 + [ANY] * 2, (4 * HALF, 2 * COLS), BF16,
+        core, tiles, below2, below, plane, above, above2, first, second,
+        scratch=[pltpu.VMEM((18, 2, HALF, COLS), BF16), pltpu.SemaphoreType.DMA((5,))],
     )
 
     up = moved(own, "z", 1)
     down = moved(own, "z", -1)
     own2 = swapped(own)
-    inner = call(
-        inner_kernel, "make_inner", [SMEM] + [VMEM] * 2, (256, 512), BF16, core, own, own2,
-        scratch=[pltpu.VMEM((512, 2 * COLS), BF16)],
-    )
-    inner, up, down = lax.optimization_barrier((inner, up, down))
     partial = call(
         tile_kernel, "make_tiles", [SMEM] + [VMEM] * 6, (256, SPAN * ROWS), BF16,
-        core, inner, own, up, down, swapped(up), swapped(down),
-        scratch=[pltpu.VMEM((1024, 2 * COLS), BF16)],
+        core, up, own, down, swapped(up), own2, swapped(down),
+        scratch=[pltpu.VMEM((1536, 2 * COLS), BF16)],
     )
     partial = lax.all_to_all(partial.reshape(16, 16, SPAN * ROWS), ("x", "y"), 0, 0)
     total = call(sum_kernel, "sum_parts", [VMEM], (SPAN, 16, ROWS), F32, partial)

time: 116 us -> 111 us (0.957)
  waiting for transfers between devices: 40.5 us -> 22.2 us
  starting transfers between devices: 41.2 us -> 55 us
  blocking collectives: 23.2 us -> 20.9 us
  local copies, waits for them, and re-layouts: 2.45 us -> 4.07 us
    ppermute x8 -> x13, starting transfers between devices: 24.3 us -> 47.1 us  [moved(): return lax.ppermute(x, axis, [(i, (i + by) % n) for i in range(n)])]
    ppermute x2 -> x0, waiting for transfers between devices: 16.6 us -> none  [sided(): return lax.ppermute(x, ('core', 'z'), pairs)]
    ppermute x2 -> x0, starting transfers between devices: 9.01 us -> none  [sided(): return lax.ppermute(x, ('core', 'z'), pairs)]
    all_to_all x1, waiting for transfers between devices: 7.36 us -> 2.88 us  [per_device(): plane = lax.all_to_all(pieces, 'x', 0, 0)]
    ppermute x8 -> x13, waiting for transfers between devices: 16.5 us -> 19.3 us  [moved(): return lax.ppermute(x, axis, [(i, (i + by) % n) for i in range(n)])]
    all_to_all x1, blocking collectives: 23.2 us -> 20.9 us  [per_device(): lax.all_to_all(partial.reshape(16, 16, SPAN * ROWS), ('x', 'y'), 0, 0)]
    unnamed x9 -> x10, local copies, waits for them, and re-layouts: 2.37 us -> 4.02 us
    pallas_call x6 -> x5, Pallas kernels: 6.85 us -> 6.22 us  [call(): pl.pallas_call(kernel, in_specs=specs, out_specs=out, out_shape=jax.Shape...]
  transfers between devices with their start and end apart: 12 -> 15, of which waited for: 7 -> 8; matrix products, arithmetic and copies ran while one was open for 0% -> 1% of each run, Pallas kernels for 1% -> 1%
where the time goes in v6:
time: 111 us; the launch traced here: 110 us
  starting transfers between devices  55 us (50%)
  waiting for transfers between devices  22.2 us (20%)
  blocking collectives  20.9 us (19%)
  Pallas kernels  6.22 us (6%)
  local copies, waits for them, and re-layouts  4.07 us (4%)
  other arithmetic  1.69 us (2%)
    ppermute x13, starting transfers between devices, moved(): return lax.ppermute(x, axis, [(i, (i + by) % n) for i in range(n)])  47.1 us
    all_to_all x1, blocking collectives, per_device(): lax.all_to_all(partial.reshape(16, 16, SPAN * ROWS), ('x', 'y'), 0, 0)  20.9 us
    ppermute x13, waiting for transfers between devices, moved(): return lax.ppermute(x, axis, [(i, (i + by) % n) for i in range(n)])  19.3 us
    pallas_call x5, Pallas kernels, call(): pl.pallas_call(kernel, in_specs=specs, out_specs=out, out_shape=jax.Shape...  6.22 us
    all_to_all x1, starting transfers between devices, per_device(): plane = lax.all_to_all(pieces, 'x', 0, 0)  4.3 us
    unnamed x10, local copies, waits for them, and re-layouts  4.02 us
    all_to_all x1, starting transfers between devices, per_device(): lax.all_to_all(tiles.reshape(8, SPAN, HALF, ROWS), ('x', 'core'), 0, 0)  3.6 us
    all_to_all x1, waiting for transfers between devices, per_device(): plane = lax.all_to_all(pieces, 'x', 0, 0)  2.88 us
  transfers between devices with their start and end apart: 15, of which 8 were waited for; matrix products, arithmetic and copies ran while one was open for 1% of the time, Pallas kernels for 1%

profile of v6, /device:TPU:8, one launch (start us, length us, event | category | flops | bytes accessed | tf_op | source)
XLA Modules:
  0.0 110.4 jit_solution(7518527384433767946)
XLA Ops:
  0.0 1.0 copy-done.1
  1.0 0.7 cut_orbitals.1
  1.8 4.3 %all-to-all-start.1 = ((bf16[4,64,512]{2,1,0:T(8,128)(2,1)}), bf16[4,64,512]{2,1,0:T(8,128)(2,1)S(1)}, u32[]{:S(2)}, u32[]{:S(2)}) async-start(bf16[4,64,512]{2,1,0:T(8,128)(2,1)} %cut_orbitals.1), calls=%async_computation.1 | async-start | bytes 524288 | tf_op jit(solution)/shard_map/all_to_all | solution.py:133
  6.1 1.0 copy-done.2
  7.8 0.8 cut_integrals.1
  8.6 1.3 %copy-done = bf16[4,2,15,64,128]{4,3,2,1,0:T(8,128)(2,1)} copy-done((bf16[4,2,15,64,128]{4,3,2,1,0:T(8,128)(2,1)}, bf16[4,2,15,64,128]{4,3,2,1,0:T(8,128)(2,1)S(1)}, u32[]{:S(2)}) %copy-start) | copy-done | bytes 1966104
  9.9 2.9 %all-to-all-done.1.plane = bf16[4,64,512]{2,1,0:T(8,128)(2,1)S(1)} async-done(((bf16[4,64,512]{2,1,0:T(8,128)(2,1)}), bf16[4,64,512]{2,1,0:T(8,128)(2,1)S(1)}, u32[]{:S(2)}, u32[]{:S(2)}) %all-to-all-start.1) | async-done | bytes 262176 | tf_op jit(solution)/shard_map/all_to_all | solution.py:133
  12.8 3.6 %all-to-all-start = ((bf16[8,15,64,128]{3,2,1,0:T(8,128)(2,1)}), bf16[8,15,64,128]{3,2,1,0:T(8,128)(2,1)S(1)}, u32[]{:S(2)}, u32[]{:S(2)}) async-start(bf16[8,15,64,128]{3,2,1,0:T(8,128)(2,1)} %bitcast.8), calls=%async_computation | async-start | bytes 3932160 | tf_op jit(solution)/shard_map/all_to_all | solution.py:139
  16.4 5.2 %collective-permute-start.1 = (bf16[3,64,512]{2,1,0:T(8,128)(2,1)S(1)}, bf16[3,64,512]{2,1,0:T(8,128)(2,1)S(1)}, u32[]{:S(2)}, u32[]{:S(2)}) collective-permute-start(bf16[3,64,512]{2,1,0:T(8,128)(2,1)S(1)} %get-tuple-element.10), channel_id=1, source_target_pairs={{0,8},{4,12},{8,16},{12,20},{16,24},{20,28},{24,32},{28,36},{32,40... | collective-permute-start | bytes 589832 | tf_op jit(solution)/shard_map/ppermute | solution.py:34
  21.6 8.6 %collective-permute-start.3 = (bf16[3,64,512]{2,1,0:T(8,128)(2,1)S(1)}, bf16[3,64,512]{2,1,0:T(8,128)(2,1)S(1)}, u32[]{:S(2)}, u32[]{:S(2)}) collective-permute-start(bf16[3,64,512]{2,1,0:T(8,128)(2,1)S(1)} %get-tuple-element.9), channel_id=1, source_target_pairs={{0,56},{4,60},{8,0},{12,4},{16,8},{20,12},{24,16},{28,20},{32,24},... | collective-permute-start | bytes 589832 | tf_op jit(solution)/shard_map/ppermute | solution.py:34
  30.2 4.4 %collective-permute-start = (bf16[4,64,512]{2,1,0:T(8,128)(2,1)S(1)}, bf16[4,64,512]{2,1,0:T(8,128)(2,1)S(1)}, u32[]{:S(2)}, u32[]{:S(2)}) collective-permute-start(bf16[4,64,512]{2,1,0:T(8,128)(2,1)S(1)} %all-to-all-done.1.plane), channel_id=1, source_target_pairs={{0,60},{4,0},{8,4},{12,8},{16,12},{20,16},{24,20},{28,24},{32,28},... | collective-permute-start | bytes 786440 | tf_op jit(solution)/shard_map/ppermute | solution.py:34
  34.6 1.9 %collective-permute-start.2 = (bf16[4,64,512]{2,1,0:T(8,128)(2,1)S(1)}, bf16[4,64,512]{2,1,0:T(8,128)(2,1)S(1)}, u32[]{:S(2)}, u32[]{:S(2)}) collective-permute-start(bf16[4,64,512]{2,1,0:T(8,128)(2,1)S(1)} %all-to-all-done.1.plane), channel_id=1, source_target_pairs={{0,4},{4,8},{8,12},{12,16},{16,20},{20,24},{24,28},{28,32},{32,36}... | collective-permute-start | bytes 786440 | tf_op jit(solution)/shard_map/ppermute | solution.py:34
  36.5 2.9 %collective-permute-done.3.above2 = bf16[3,64,512]{2,1,0:T(8,128)(2,1)S(1)} collective-permute-done((bf16[3,64,512]{2,1,0:T(8,128)(2,1)S(1)}, bf16[3,64,512]{2,1,0:T(8,128)(2,1)S(1)}, u32[]{:S(2)}, u32[]{:S(2)}) %collective-permute-start.3) | collective-permute-done | bytes 196640 | tf_op jit(solution)/shard_map/ppermute | solution.py:34
  39.5 0.9 pad_maximum_fusion
  40.4 1.9 %collective-permute-start.4 = (bf16[10,64,512]{2,1,0:T(8,128)(2,1)}, bf16[10,64,512]{2,1,0:T(8,128)(2,1)}, u32[]{:S(2)}, u32[]{:S(2)}) collective-permute-start(bf16[10,64,512]{2,1,0:T(8,128)(2,1)} %pad_maximum_fusion), channel_id=1, source_target_pairs={{0,64},{64,0},{1,65},{65,1},{2,66},{66,2},{3,67},{67,3},{4,68},{68... | collective-permute-start | bytes 1966088 | tf_op jit(solution)/shard_map/ppermute | solution.py:34
  42.3 2.5 %collective-permute-done.above = bf16[4,64,512]{2,1,0:T(8,128)(2,1)S(1)} collective-permute-done((bf16[4,64,512]{2,1,0:T(8,128)(2,1)S(1)}, bf16[4,64,512]{2,1,0:T(8,128)(2,1)S(1)}, u32[]{:S(2)}, u32[]{:S(2)}) %collective-permute-start) | collective-permute-done | bytes 262176 | tf_op jit(solution)/shard_map/ppermute | solution.py:34
  45.5 1.9 %collective-permute-start.5 = (bf16[8,64,512]{2,1,0:T(8,128)(2,1)S(1)}, bf16[8,64,512]{2,1,0:T(8,128)(2,1)S(1)}, u32[]{:S(2)}, u32[]{:S(2)}) collective-permute-start(bf16[8,64,512]{2,1,0:T(8,128)(2,1)S(1)} %pad_maximum_fusion.1), channel_id=1, source_target_pairs={{0,64},{64,0},{1,65},{65,1},{2,66},{66,2},{3,67},{67,3},{4,68},{68... | collective-permute-start | bytes 1572872 | tf_op jit(solution)/shard_map/ppermute | solution.py:34
  47.5 1.9 %collective-permute-done.5.second = bf16[8,64,512]{2,1,0:T(8,128)(2,1)S(1)} collective-permute-done((bf16[8,64,512]{2,1,0:T(8,128)(2,1)S(1)}, bf16[8,64,512]{2,1,0:T(8,128)(2,1)S(1)}, u32[]{:S(2)}, u32[]{:S(2)}) %collective-permute-start.5) | collective-permute-done | bytes 524320 | tf_op jit(solution)/shard_map/ppermute | solution.py:34
  49.3 2.4 %make_half.1.own = bf16[256,1024]{1,0:T(8,128)(2,1)S(1)} custom-call(s32[1]{0:T(128)} %bitcast.core, bf16[8,15,64,128]{3,2,1,0:T(8,128)(2,1)S(1)} %all-to-all-done.tiles, bf16[3,64,512]{2,1,0:T(8,128)(2,1)S(1)} %collective-permute-done.1.below2, bf16[4,64,512]{2,1,0:T(8,128)(2,1)S(1)} %collective-permute-done.2.below, ...), custom_call_target="tpu_custom_call" | custom-call | tf_op jit(solution)/shard_map/make_half/pallas_call | solution.py:21
  51.8 1.9 %collective-permute-start.6 = (bf16[256,1024]{1,0:T(8,128)(2,1)S(1)}, bf16[256,1024]{1,0:T(8,128)(2,1)S(1)}, u32[]{:S(2)}, u32[]{:S(2)}) collective-permute-start(bf16[256,1024]{1,0:T(8,128)(2,1)S(1)} %make_half.1.own), channel_id=1, source_target_pairs={{0,4},{4,8},{8,12},{12,16},{16,20},{20,24},{24,28},{28,32},{32,36}... | collective-permute-start | bytes 1572872 | tf_op jit(solution)/shard_map/ppermute | solution.py:34
  53.7 8.0 %collective-permute-start.7 = (bf16[256,1024]{1,0:T(8,128)(2,1)S(1)}, bf16[256,1024]{1,0:T(8,128)(2,1)S(1)}, u32[]{:S(2)}, u32[]{:S(2)}) collective-permute-start(bf16[256,1024]{1,0:T(8,128)(2,1)S(1)} %make_half.1.own), channel_id=1, source_target_pairs={{0,60},{4,0},{8,4},{12,8},{16,12},{20,16},{24,20},{28,24},{32,28},... | collective-permute-start | bytes 1572872 | tf_op jit(solution)/shard_map/ppermute | solution.py:34
  61.7 1.9 %collective-permute-start.9 = (bf16[256,1024]{1,0:T(8,128)(2,1)S(1)}, bf16[256,1024]{1,0:T(8,128)(2,1)S(1)}, u32[]{:S(2)}, u32[]{:S(2)}) collective-permute-start(bf16[256,1024]{1,0:T(8,128)(2,1)S(1)} %make_half.1.own), channel_id=1, source_target_pairs={{0,64},{64,0},{1,65},{65,1},{2,66},{66,2},{3,67},{67,3},{4,68},{68... | collective-permute-start | bytes 1572872 | tf_op jit(solution)/shard_map/ppermute | solution.py:34
  63.7 8.3 %collective-permute-done.6.up = bf16[256,1024]{1,0:T(8,128)(2,1)S(1)} collective-permute-done((bf16[256,1024]{1,0:T(8,128)(2,1)S(1)}, bf16[256,1024]{1,0:T(8,128)(2,1)S(1)}, u32[]{:S(2)}, u32[]{:S(2)}) %collective-permute-start.6) | collective-permute-done | bytes 524320 | tf_op jit(solution)/shard_map/ppermute | solution.py:34
  72.0 1.9 %collective-permute-start.8 = (bf16[256,1024]{1,0:T(8,128)(2,1)S(1)}, bf16[256,1024]{1,0:T(8,128)(2,1)S(1)}, u32[]{:S(2)}, u32[]{:S(2)}) collective-permute-start(bf16[256,1024]{1,0:T(8,128)(2,1)S(1)} %collective-permute-done.6.up), channel_id=1, source_target_pairs={{0,64},{64,0},{1,65},{65,1},{2,66},{66,2},{3,67},{67,3},{4,68},{68... | collective-permute-start | bytes 1572872 | tf_op jit(solution)/shard_map/ppermute | solution.py:34
  73.9 2.4 %collective-permute-start.10 = (bf16[256,1024]{1,0:T(8,128)(2,1)S(1)}, bf16[256,1024]{1,0:T(8,128)(2,1)S(1)}, u32[]{:S(2)}, u32[]{:S(2)}) collective-permute-start(bf16[256,1024]{1,0:T(8,128)(2,1)S(1)} %collective-permute-done.7.down), channel_id=1, source_target_pairs={{0,64},{64,0},{1,65},{65,1},{2,66},{66,2},{3,67},{67,3},{4,68},{68... | collective-permute-start | bytes 1572872 | tf_op jit(solution)/shard_map/ppermute | solution.py:34
  76.4 1.5 %collective-permute-done.10.down2 = bf16[256,1024]{1,0:T(8,128)(2,1)S(1)} collective-permute-done((bf16[256,1024]{1,0:T(8,128)(2,1)S(1)}, bf16[256,1024]{1,0:T(8,128)(2,1)S(1)}, u32[]{:S(2)}, u32[]{:S(2)}) %collective-permute-start.10) | collective-permute-done | bytes 524320 | tf_op jit(solution)/shard_map/ppermute | solution.py:34
  77.9 2.1 %make_tiles.1 = bf16[256,1920]{1,0:T(8,128)(2,1)S(1)} custom-call(s32[1]{0:T(128)} %bitcast.core, bf16[256,1024]{1,0:T(8,128)(2,1)S(1)} %collective-permute-done.6.up, bf16[256,1024]{1,0:T(8,128)(2,1)S(1)} %make_half.1.own, bf16[256,1024]{1,0:T(8,128)(2,1)S(1)} %collective-permute-done.7.down, bf16[256,1024]{1,0:T(8,128)(2,1)S(1)} %collective-permute-done.8.up2, ...), custom_call_target="tpu_custom_call" | custom-call | tf_op jit(solution)/shard_map/make_tiles/pallas_call | solution.py:21
  80.0 20.9 %all_to_all.15.parts = bf16[16,16,1920]{2,1,0:T(8,128)(2,1)S(1)} all-to-all(bf16[16,16,1920]{2,1,0:T(8,128)(2,1)S(1)} %bitcast.9), channel_id=1, replica_groups=mesh['y'=4,'core'=2,'z'=16,'x'=4] {'x','y'}, dimensions={0} | all-to-all | bytes 1966080 | tf_op jit(solution)/shard_map/all_to_all | solution.py:163
  101.1 1.9 %collective-permute-start.11 = (f32[3,16,128]{2,1,0:T(8,128)S(1)}, f32[3,16,128]{2,1,0:T(8,128)S(1)}, u32[]{:S(2)}, u32[]{:S(2)}) collective-permute-start(f32[3,16,128]{2,1,0:T(8,128)S(1)} %slice.18), channel_id=1, source_target_pairs={{0,4},{4,8},{8,12},{12,16},{16,20},{20,24},{24,28},{28,32},{32,36}... | collective-permute-start | bytes 73736 | tf_op jit(solution)/shard_map/ppermute | solution.py:34
  103.0 5.1 %collective-permute-start.12 = (f32[3,16,128]{2,1,0:T(8,128)S(1)}, f32[3,16,128]{2,1,0:T(8,128)S(1)}, u32[]{:S(2)}, u32[]{:S(2)}) collective-permute-start(f32[3,16,128]{2,1,0:T(8,128)S(1)} %slice.18), channel_id=1, source_target_pairs={{0,60},{4,0},{8,4},{12,8},{16,12},{20,16},{24,20},{28,24},{32,28},... | collective-permute-start | bytes 73736 | tf_op jit(solution)/shard_map/ppermute | solution.py:34
  108.2 1.5 %collective-permute-done.12 = f32[3,16,128]{2,1,0:T(8,128)S(1)} collective-permute-done((f32[3,16,128]{2,1,0:T(8,128)S(1)}, f32[3,16,128]{2,1,0:T(8,128)S(1)}, u32[]{:S(2)}, u32[]{:S(2)}) %collective-permute-start.12) | collective-permute-done | bytes 24608 | tf_op jit(solution)/shard_map/ppermute | solution.py:34
  109.6 0.7 fusion.3
  (21 shorter events, 1.6 us)
Async XLA Ops:
  0.0 1.0 copy-start.1
  1.8 11.0 %all-to-all-start.1 = ((bf16[4,64,512]{2,1,0:T(8,128)(2,1)}), bf16[4,64,512]{2,1,0:T(8,128)(2,1)S(1)}, u32[]{:S(2)}, u32[]{:S(2)}) async-start(bf16[4,64,512]{2,1,0:T(8,128)(2,1)} %cut_orbitals.1), calls=%async_computation.1 | async-start | bytes 524288 | tf_op jit(solution)/shard_map/all_to_all | solution.py:133
  6.1 1.0 copy-start.2
  7.1 0.7 copy-start.3
  8.6 1.3 %copy-start = (bf16[4,2,15,64,128]{4,3,2,1,0:T(8,128)(2,1)}, bf16[4,2,15,64,128]{4,3,2,1,0:T(8,128)(2,1)S(1)}, u32[]{:S(2)}) copy-start(bf16[4,2,15,64,128]{4,3,2,1,0:T(8,128)(2,1)S(1)} %cut_integrals.1) | copy-start | bytes 5898244
  12.8 32.1 %all-to-all-start = ((bf16[8,15,64,128]{3,2,1,0:T(8,128)(2,1)}), bf16[8,15,64,128]{3,2,1,0:T(8,128)(2,1)S(1)}, u32[]{:S(2)}, u32[]{:S(2)}) async-start(bf16[8,15,64,128]{3,2,1,0:T(8,128)(2,1)} %bitcast.8), calls=%async_computation | async-start | bytes 3932160 | tf_op jit(solution)/shard_map/all_to_all | solution.py:139
  16.4 20.1 %collective-permute-start.1 = (bf16[3,64,512]{2,1,0:T(8,128)(2,1)S(1)}, bf16[3,64,512]{2,1,0:T(8,128)(2,1)S(1)}, u32[]{:S(2)}, u32[]{:S(2)}) collective-permute-start(bf16[3,64,512]{2,1,0:T(8,128)(2,1)S(1)} %get-tuple-element.10), channel_id=1, source_target_pairs={{0,8},{4,12},{8,16},{12,20},{16,24},{20,28},{24,32},{28,36},{32,40... | collective-permute-start | bytes 589832 | tf_op jit(solution)/shard_map/ppermute | solution.py:34
  21.6 17.9 %collective-permute-start.3 = (bf16[3,64,512]{2,1,0:T(8,128)(2,1)S(1)}, bf16[3,64,512]{2,1,0:T(8,128)(2,1)S(1)}, u32[]{:S(2)}, u32[]{:S(2)}) collective-permute-start(bf16[3,64,512]{2,1,0:T(8,128)(2,1)S(1)} %get-tuple-element.9), channel_id=1, source_target_pairs={{0,56},{4,60},{8,0},{12,4},{16,8},{20,12},{24,16},{28,20},{32,24},... | collective-permute-start | bytes 589832 | tf_op jit(solution)/shard_map/ppermute | solution.py:34
  30.2 14.6 %collective-permute-start = (bf16[4,64,512]{2,1,0:T(8,128)(2,1)S(1)}, bf16[4,64,512]{2,1,0:T(8,128)(2,1)S(1)}, u32[]{:S(2)}, u32[]{:S(2)}) collective-permute-start(bf16[4,64,512]{2,1,0:T(8,128)(2,1)S(1)} %all-to-all-done.1.plane), channel_id=1, source_target_pairs={{0,60},{4,0},{8,4},{12,8},{16,12},{20,16},{24,20},{28,24},{32,28},... | collective-permute-start | bytes 786440 | tf_op jit(solution)/shard_map/ppermute | solution.py:34
  34.6 10.9 %collective-permute-start.2 = (bf16[4,64,512]{2,1,0:T(8,128)(2,1)S(1)}, bf16[4,64,512]{2,1,0:T(8,128)(2,1)S(1)}, u32[]{:S(2)}, u32[]{:S(2)}) collective-permute-start(bf16[4,64,512]{2,1,0:T(8,128)(2,1)S(1)} %all-to-all-done.1.plane), channel_id=1, source_target_pairs={{0,4},{4,8},{8,12},{12,16},{16,20},{20,24},{24,28},{28,32},{32,36}... | collective-permute-start | bytes 786440 | tf_op jit(solution)/shard_map/ppermute | solution.py:34
  40.4 7.1 %collective-permute-start.4 = (bf16[10,64,512]{2,1,0:T(8,128)(2,1)}, bf16[10,64,512]{2,1,0:T(8,128)(2,1)}, u32[]{:S(2)}, u32[]{:S(2)}) collective-permute-start(bf16[10,64,512]{2,1,0:T(8,128)(2,1)} %pad_maximum_fusion), channel_id=1, source_target_pairs={{0,64},{64,0},{1,65},{65,1},{2,66},{66,2},{3,67},{67,3},{4,68},{68... | collective-permute-start | bytes 1966088 | tf_op jit(solution)/shard_map/ppermute | solution.py:34
  45.5 3.8 %collective-permute-start.5 = (bf16[8,64,512]{2,1,0:T(8,128)(2,1)S(1)}, bf16[8,64,512]{2,1,0:T(8,128)(2,1)S(1)}, u32[]{:S(2)}, u32[]{:S(2)}) collective-permute-start(bf16[8,64,512]{2,1,0:T(8,128)(2,1)S(1)} %pad_maximum_fusion.1), channel_id=1, source_target_pairs={{0,64},{64,0},{1,65},{65,1},{2,66},{66,2},{3,67},{67,3},{4,68},{68... | collective-permute-start | bytes 1572872 | tf_op jit(solution)/shard_map/ppermute | solution.py:34
  51.8 20.2 %collective-permute-start.6 = (bf16[256,1024]{1,0:T(8,128)(2,1)S(1)}, bf16[256,1024]{1,0:T(8,128)(2,1)S(1)}, u32[]{:S(2)}, u32[]{:S(2)}) collective-permute-start(bf16[256,1024]{1,0:T(8,128)(2,1)S(1)} %make_half.1.own), channel_id=1, source_target_pairs={{0,4},{4,8},{8,12},{12,16},{16,20},{20,24},{24,28},{28,32},{32,36}... | collective-permute-start | bytes 1572872 | tf_op jit(solution)/shard_map/ppermute | solution.py:34
  53.7 20.2 %collective-permute-start.7 = (bf16[256,1024]{1,0:T(8,128)(2,1)S(1)}, bf16[256,1024]{1,0:T(8,128)(2,1)S(1)}, u32[]{:S(2)}, u32[]{:S(2)}) collective-permute-start(bf16[256,1024]{1,0:T(8,128)(2,1)S(1)} %make_half.1.own), channel_id=1, source_target_pairs={{0,60},{4,0},{8,4},{12,8},{16,12},{20,16},{24,20},{28,24},{32,28},... | collective-permute-start | bytes 1572872 | tf_op jit(solution)/shard_map/ppermute | solution.py:34
  61.7 14.6 %collective-permute-start.9 = (bf16[256,1024]{1,0:T(8,128)(2,1)S(1)}, bf16[256,1024]{1,0:T(8,128)(2,1)S(1)}, u32[]{:S(2)}, u32[]{:S(2)}) collective-permute-start(bf16[256,1024]{1,0:T(8,128)(2,1)S(1)} %make_half.1.own), channel_id=1, source_target_pairs={{0,64},{64,0},{1,65},{65,1},{2,66},{66,2},{3,67},{67,3},{4,68},{68... | collective-permute-start | bytes 1572872 | tf_op jit(solution)/shard_map/ppermute | solution.py:34
  72.0 4.4 %collective-permute-start.8 = (bf16[256,1024]{1,0:T(8,128)(2,1)S(1)}, bf16[256,1024]{1,0:T(8,128)(2,1)S(1)}, u32[]{:S(2)}, u32[]{:S(2)}) collective-permute-start(bf16[256,1024]{1,0:T(8,128)(2,1)S(1)} %collective-permute-done.6.up), channel_id=1, source_target_pairs={{0,64},{64,0},{1,65},{65,1},{2,66},{66,2},{3,67},{67,3},{4,68},{68... | collective-permute-start | bytes 1572872 | tf_op jit(solution)/shard_map/ppermute | solution.py:34
  73.9 3.9 %collective-permute-start.10 = (bf16[256,1024]{1,0:T(8,128)(2,1)S(1)}, bf16[256,1024]{1,0:T(8,128)(2,1)S(1)}, u32[]{:S(2)}, u32[]{:S(2)}) collective-permute-start(bf16[256,1024]{1,0:T(8,128)(2,1)S(1)} %collective-permute-done.7.down), channel_id=1, source_target_pairs={{0,64},{64,0},{1,65},{65,1},{2,66},{66,2},{3,67},{67,3},{4,68},{68... | collective-permute-start | bytes 1572872 | tf_op jit(solution)/shard_map/ppermute | solution.py:34
  80.0 28.1 %copy-start.4 = (s32[1,15]{1,0:T(1,128)S(1)}, s32[1,15]{1,0:T(1,128)}, u32[]{:S(2)}) copy-start(s32[1,15]{1,0:T(1,128)} %mask.1) | copy-start | bytes 184
  101.1 7.1 %collective-permute-start.11 = (f32[3,16,128]{2,1,0:T(8,128)S(1)}, f32[3,16,128]{2,1,0:T(8,128)S(1)}, u32[]{:S(2)}, u32[]{:S(2)}) collective-permute-start(f32[3,16,128]{2,1,0:T(8,128)S(1)} %slice.18), channel_id=1, source_target_pairs={{0,4},{4,8},{8,12},{12,16},{16,20},{20,24},{24,28},{28,32},{32,36}... | collective-permute-start | bytes 73736 | tf_op jit(solution)/shard_map/ppermute | solution.py:34
  103.0 6.6 %collective-permute-start.12 = (f32[3,16,128]{2,1,0:T(8,128)S(1)}, f32[3,16,128]{2,1,0:T(8,128)S(1)}, u32[]{:S(2)}, u32[]{:S(2)}) collective-permute-start(f32[3,16,128]{2,1,0:T(8,128)S(1)} %slice.18), channel_id=1, source_target_pairs={{0,60},{4,0},{8,4},{12,8},{16,12},{20,16},{24,20},{28,24},{32,28},... | collective-permute-start | bytes 73736 | tf_op jit(solution)/shard_map/ppermute | solution.py:34

commit v7 on v6

--- a/solution.py
+++ b/solution.py
@@ -29,13 +29,13 @@
     )(*args)
 
 
-def moved(x, axis, by):
-    n = lax.axis_size(axis)
-    return lax.ppermute(x, axis, [(i, (i + by) % n) for i in range(n)])
+def moved(x, by):
+    n = lax.axis_size("z")
+    return lax.ppermute(x, "z", [(i, i + by) for i in range(n) if 0 <= i + by < n])
 
 
 def swapped(x):
-    return moved(x, "core", 1)
+    return lax.ppermute(x, "core", [(0, 1), (1, 0)])
 
 
 def orbital_kernel(core, occupied, out, sems):
@@ -138,10 +138,10 @@
     )
     tiles = lax.all_to_all(tiles.reshape(8, SPAN, HALF, ROWS), ("x", "core"), 0, 0)
 
-    below2 = moved(plane[1:], "z", 2)
-    above2 = moved(plane[:3], "z", -2)
-    below = moved(plane, "z", 1)
-    above = moved(plane, "z", -1)
+    below2 = moved(plane[1:], 2)
+    above2 = moved(plane[:3], -2)
+    below = moved(plane, 1)
+    above = moved(plane, -1)
     first = swapped(jnp.concatenate([plane, below2, above2]))
     tiles, above = lax.optimization_barrier((tiles, above))
     second = swapped(jnp.concatenate([below, above]))
@@ -152,8 +152,8 @@
         scratch=[pltpu.VMEM((18, 2, HALF, COLS), BF16), pltpu.SemaphoreType.DMA((5,))],
     )
 
-    up = moved(own, "z", 1)
-    down = moved(own, "z", -1)
+    up = moved(own, 1)
+    down = moved(own, -1)
     own2 = swapped(own)
     partial = call(
         tile_kernel, "make_tiles", [SMEM] + [VMEM] * 6, (256, SPAN * ROWS), BF16,
@@ -163,7 +163,7 @@
     partial = lax.all_to_all(partial.reshape(16, 16, SPAN * ROWS), ("x", "y"), 0, 0)
     total = call(sum_kernel, "sum_parts", [VMEM], (SPAN, 16, ROWS), F32, partial)
     far = total[12:]
-    line = jnp.concatenate([moved(far, "z", 1), total[:12], moved(far, "z", -1)], 0)
+    line = jnp.concatenate([moved(far, 1), total[:12], moved(far, -1)], 0)
     out = lax.dynamic_slice_in_dim(line, x, SPAN, 0)
     return (out * pair_mask[0].astype(F32)[:, None, None])[None]
 

time: 111 us -> 111 us (level)
  the two profiles are of different devices: /device:TPU:8 before, /device:TPU:96 now
where the time goes in v7:
time: 111 us; the launch traced here: 110 us
  starting transfers between devices  45.5 us (41%)
  waiting for transfers between devices  29.4 us (26%)
  blocking collectives  22.8 us (21%)
  Pallas kernels  6.22 us (6%)
  local copies, waits for them, and re-layouts  4.07 us (4%)
  other arithmetic  1.69 us (2%)
    ppermute x8, starting transfers between devices, moved(): lax.ppermute(x, 'z', [(i, i + by) for i in range(n) if 0 <= i + by < n])  28 us
    ppermute x8, waiting for transfers between devices, moved(): lax.ppermute(x, 'z', [(i, i + by) for i in range(n) if 0 <= i + by < n])  22.8 us
    all_to_all x1, blocking collectives, per_device(): lax.all_to_all(partial.reshape(16, 16, SPAN * ROWS), ('x', 'y'), 0, 0)  22.8 us
    ppermute x5, starting transfers between devices, swapped(): return lax.ppermute(x, 'core', [(0, 1), (1, 0)])  9.57 us
    pallas_call x5, Pallas kernels, call(): pl.pallas_call(kernel, in_specs=specs, out_specs=out, out_shape=jax.Shape...  6.22 us
    all_to_all x1, starting transfers between devices, per_device(): plane = lax.all_to_all(pieces, 'x', 0, 0)  4.3 us
    unnamed x10, local copies, waits for them, and re-layouts  4.02 us
    ppermute x5, waiting for transfers between devices, swapped(): return lax.ppermute(x, 'core', [(0, 1), (1, 0)])  3.73 us
  transfers between devices with their start and end apart: 15, of which 8 were waited for; matrix products, arithmetic and copies ran while one was open for 1% of the time, Pallas kernels for 1%

profile of v7, /device:TPU:96, one launch (start us, length us, event | category | flops | bytes accessed | tf_op | source)
XLA Modules:
  0.0 109.9 jit_solution(12095012555349078546)
XLA Ops:
  0.0 1.0 copy-done.1
  1.0 0.7 cut_orbitals.1
  1.8 4.3 %all-to-all-start.1 = ((bf16[4,64,512]{2,1,0:T(8,128)(2,1)}), bf16[4,64,512]{2,1,0:T(8,128)(2,1)S(1)}, u32[]{:S(2)}, u32[]{:S(2)}) async-start(bf16[4,64,512]{2,1,0:T(8,128)(2,1)} %cut_orbitals.1), calls=%async_computation.1 | async-start | bytes 524288 | tf_op jit(solution)/shard_map/all_to_all | solution.py:133
  6.1 1.0 copy-done.2
  7.8 0.8 cut_integrals.1
  8.6 1.3 %copy-done = bf16[4,2,15,64,128]{4,3,2,1,0:T(8,128)(2,1)} copy-done((bf16[4,2,15,64,128]{4,3,2,1,0:T(8,128)(2,1)}, bf16[4,2,15,64,128]{4,3,2,1,0:T(8,128)(2,1)S(1)}, u32[]{:S(2)}) %copy-start) | copy-done | bytes 1966104
  9.9 2.9 %all-to-all-done.1.plane = bf16[4,64,512]{2,1,0:T(8,128)(2,1)S(1)} async-done(((bf16[4,64,512]{2,1,0:T(8,128)(2,1)}), bf16[4,64,512]{2,1,0:T(8,128)(2,1)S(1)}, u32[]{:S(2)}, u32[]{:S(2)}) %all-to-all-start.1) | async-done | bytes 262176 | tf_op jit(solution)/shard_map/all_to_all | solution.py:133
  12.8 3.6 %all-to-all-start = ((bf16[8,15,64,128]{3,2,1,0:T(8,128)(2,1)}), bf16[8,15,64,128]{3,2,1,0:T(8,128)(2,1)S(1)}, u32[]{:S(2)}, u32[]{:S(2)}) async-start(bf16[8,15,64,128]{3,2,1,0:T(8,128)(2,1)} %bitcast.8), calls=%async_computation | async-start | bytes 3932160 | tf_op jit(solution)/shard_map/all_to_all | solution.py:139
  16.4 6.4 %collective-permute-start.1 = (bf16[3,64,512]{2,1,0:T(8,128)(2,1)S(1)}, bf16[3,64,512]{2,1,0:T(8,128)(2,1)S(1)}, u32[]{:S(2)}, u32[]{:S(2)}) collective-permute-start(bf16[3,64,512]{2,1,0:T(8,128)(2,1)S(1)} %get-tuple-element.10), channel_id=1, source_target_pairs={{0,8},{4,12},{8,16},{12,20},{16,24},{20,28},{24,32},{28,36},{32,40... | collective-permute-start | bytes 589832 | tf_op jit(solution)/shard_map/ppermute | solution.py:34
  22.8 1.9 %collective-permute-start.3 = (bf16[3,64,512]{2,1,0:T(8,128)(2,1)S(1)}, bf16[3,64,512]{2,1,0:T(8,128)(2,1)S(1)}, u32[]{:S(2)}, u32[]{:S(2)}) collective-permute-start(bf16[3,64,512]{2,1,0:T(8,128)(2,1)S(1)} %get-tuple-element.9), channel_id=1, source_target_pairs={{8,0},{12,4},{16,8},{20,12},{24,16},{28,20},{32,24},{36,28},{40,32... | collective-permute-start | bytes 589832 | tf_op jit(solution)/shard_map/ppermute | solution.py:34
  24.7 2.0 %collective-permute-start = (bf16[4,64,512]{2,1,0:T(8,128)(2,1)S(1)}, bf16[4,64,512]{2,1,0:T(8,128)(2,1)S(1)}, u32[]{:S(2)}, u32[]{:S(2)}) collective-permute-start(bf16[4,64,512]{2,1,0:T(8,128)(2,1)S(1)} %all-to-all-done.1.plane), channel_id=1, source_target_pairs={{4,0},{8,4},{12,8},{16,12},{20,16},{24,20},{28,24},{32,28},{36,32}... | collective-permute-start | bytes 786440 | tf_op jit(solution)/shard_map/ppermute | solution.py:34
  26.8 5.0 %collective-permute-start.2 = (bf16[4,64,512]{2,1,0:T(8,128)(2,1)S(1)}, bf16[4,64,512]{2,1,0:T(8,128)(2,1)S(1)}, u32[]{:S(2)}, u32[]{:S(2)}) collective-permute-start(bf16[4,64,512]{2,1,0:T(8,128)(2,1)S(1)} %all-to-all-done.1.plane), channel_id=1, source_target_pairs={{0,4},{4,8},{8,12},{12,16},{16,20},{20,24},{24,28},{28,32},{32,36}... | collective-permute-start | bytes 786440 | tf_op jit(solution)/shard_map/ppermute | solution.py:34
  31.8 3.9 %collective-permute-done.3.above2 = bf16[3,64,512]{2,1,0:T(8,128)(2,1)S(1)} collective-permute-done((bf16[3,64,512]{2,1,0:T(8,128)(2,1)S(1)}, bf16[3,64,512]{2,1,0:T(8,128)(2,1)S(1)}, u32[]{:S(2)}, u32[]{:S(2)}) %collective-permute-start.3) | collective-permute-done | bytes 196640 | tf_op jit(solution)/shard_map/ppermute | solution.py:34
  35.8 0.9 pad_maximum_fusion
  36.7 1.9 %collective-permute-start.4 = (bf16[10,64,512]{2,1,0:T(8,128)(2,1)}, bf16[10,64,512]{2,1,0:T(8,128)(2,1)}, u32[]{:S(2)}, u32[]{:S(2)}) collective-permute-start(bf16[10,64,512]{2,1,0:T(8,128)(2,1)} %pad_maximum_fusion), channel_id=1, source_target_pairs={{0,64},{64,0},{1,65},{65,1},{2,66},{66,2},{3,67},{67,3},{4,68},{68... | collective-permute-start | bytes 1966088 | tf_op jit(solution)/shard_map/ppermute | solution.py:38
  38.6 3.7 %collective-permute-done.above = bf16[4,64,512]{2,1,0:T(8,128)(2,1)S(1)} collective-permute-done((bf16[4,64,512]{2,1,0:T(8,128)(2,1)S(1)}, bf16[4,64,512]{2,1,0:T(8,128)(2,1)S(1)}, u32[]{:S(2)}, u32[]{:S(2)}) %collective-permute-start) | collective-permute-done | bytes 262176 | tf_op jit(solution)/shard_map/ppermute | solution.py:34
  42.3 1.9 %collective-permute-start.5 = (bf16[8,64,512]{2,1,0:T(8,128)(2,1)S(1)}, bf16[8,64,512]{2,1,0:T(8,128)(2,1)S(1)}, u32[]{:S(2)}, u32[]{:S(2)}) collective-permute-start(bf16[8,64,512]{2,1,0:T(8,128)(2,1)S(1)} %pad_maximum_fusion.1), channel_id=1, source_target_pairs={{0,64},{64,0},{1,65},{65,1},{2,66},{66,2},{3,67},{67,3},{4,68},{68... | collective-permute-start | bytes 1572872 | tf_op jit(solution)/shard_map/ppermute | solution.py:38
  44.3 1.9 %collective-permute-done.5.second = bf16[8,64,512]{2,1,0:T(8,128)(2,1)S(1)} collective-permute-done((bf16[8,64,512]{2,1,0:T(8,128)(2,1)S(1)}, bf16[8,64,512]{2,1,0:T(8,128)(2,1)S(1)}, u32[]{:S(2)}, u32[]{:S(2)}) %collective-permute-start.5) | collective-permute-done | bytes 524320 | tf_op jit(solution)/shard_map/ppermute | solution.py:38
  46.1 2.4 %make_half.1.own = bf16[256,1024]{1,0:T(8,128)(2,1)S(1)} custom-call(s32[1]{0:T(128)} %bitcast.core, bf16[8,15,64,128]{3,2,1,0:T(8,128)(2,1)S(1)} %all-to-all-done.tiles, bf16[3,64,512]{2,1,0:T(8,128)(2,1)S(1)} %collective-permute-done.1.below2, bf16[4,64,512]{2,1,0:T(8,128)(2,1)S(1)} %collective-permute-done.2.below, ...), custom_call_target="tpu_custom_call" | custom-call | tf_op jit(solution)/shard_map/make_half/pallas_call | solution.py:21
  48.5 4.9 %collective-permute-start.6 = (bf16[256,1024]{1,0:T(8,128)(2,1)S(1)}, bf16[256,1024]{1,0:T(8,128)(2,1)S(1)}, u32[]{:S(2)}, u32[]{:S(2)}) collective-permute-start(bf16[256,1024]{1,0:T(8,128)(2,1)S(1)} %make_half.1.own), channel_id=1, source_target_pairs={{0,4},{4,8},{8,12},{12,16},{16,20},{20,24},{24,28},{28,32},{32,36}... | collective-permute-start | bytes 1572872 | tf_op jit(solution)/shard_map/ppermute | solution.py:34
  53.4 1.9 %collective-permute-start.7 = (bf16[256,1024]{1,0:T(8,128)(2,1)S(1)}, bf16[256,1024]{1,0:T(8,128)(2,1)S(1)}, u32[]{:S(2)}, u32[]{:S(2)}) collective-permute-start(bf16[256,1024]{1,0:T(8,128)(2,1)S(1)} %make_half.1.own), channel_id=1, source_target_pairs={{4,0},{8,4},{12,8},{16,12},{20,16},{24,20},{28,24},{32,28},{36,32}... | collective-permute-start | bytes 1572872 | tf_op jit(solution)/shard_map/ppermute | solution.py:34
  55.3 1.9 %collective-permute-start.9 = (bf16[256,1024]{1,0:T(8,128)(2,1)S(1)}, bf16[256,1024]{1,0:T(8,128)(2,1)S(1)}, u32[]{:S(2)}, u32[]{:S(2)}) collective-permute-start(bf16[256,1024]{1,0:T(8,128)(2,1)S(1)} %make_half.1.own), channel_id=1, source_target_pairs={{0,64},{64,0},{1,65},{65,1},{2,66},{66,2},{3,67},{67,3},{4,68},{68... | collective-permute-start | bytes 1572872 | tf_op jit(solution)/shard_map/ppermute | solution.py:38
  57.3 7.6 %collective-permute-done.6.up = bf16[256,1024]{1,0:T(8,128)(2,1)S(1)} collective-permute-done((bf16[256,1024]{1,0:T(8,128)(2,1)S(1)}, bf16[256,1024]{1,0:T(8,128)(2,1)S(1)}, u32[]{:S(2)}, u32[]{:S(2)}) %collective-permute-start.6) | collective-permute-done | bytes 524320 | tf_op jit(solution)/shard_map/ppermute | solution.py:34
  64.9 1.9 %collective-permute-start.8 = (bf16[256,1024]{1,0:T(8,128)(2,1)S(1)}, bf16[256,1024]{1,0:T(8,128)(2,1)S(1)}, u32[]{:S(2)}, u32[]{:S(2)}) collective-permute-start(bf16[256,1024]{1,0:T(8,128)(2,1)S(1)} %collective-permute-done.6.up), channel_id=1, source_target_pairs={{0,64},{64,0},{1,65},{65,1},{2,66},{66,2},{3,67},{67,3},{4,68},{68... | collective-permute-start | bytes 1572872 | tf_op jit(solution)/shard_map/ppermute | solution.py:38
  66.8 3.4 %collective-permute-done.7.down = bf16[256,1024]{1,0:T(8,128)(2,1)S(1)} collective-permute-done((bf16[256,1024]{1,0:T(8,128)(2,1)S(1)}, bf16[256,1024]{1,0:T(8,128)(2,1)S(1)}, u32[]{:S(2)}, u32[]{:S(2)}) %collective-permute-start.7) | collective-permute-done | bytes 524320 | tf_op jit(solution)/shard_map/ppermute | solution.py:34
  70.2 1.9 %collective-permute-start.10 = (bf16[256,1024]{1,0:T(8,128)(2,1)S(1)}, bf16[256,1024]{1,0:T(8,128)(2,1)S(1)}, u32[]{:S(2)}, u32[]{:S(2)}) collective-permute-start(bf16[256,1024]{1,0:T(8,128)(2,1)S(1)} %collective-permute-done.7.down), channel_id=1, source_target_pairs={{0,64},{64,0},{1,65},{65,1},{2,66},{66,2},{3,67},{67,3},{4,68},{68... | collective-permute-start | bytes 1572872 | tf_op jit(solution)/shard_map/ppermute | solution.py:38
  72.1 1.9 %collective-permute-done.10.down2 = bf16[256,1024]{1,0:T(8,128)(2,1)S(1)} collective-permute-done((bf16[256,1024]{1,0:T(8,128)(2,1)S(1)}, bf16[256,1024]{1,0:T(8,128)(2,1)S(1)}, u32[]{:S(2)}, u32[]{:S(2)}) %collective-permute-start.10) | collective-permute-done | bytes 524320 | tf_op jit(solution)/shard_map/ppermute | solution.py:38
  74.0 2.1 %make_tiles.1 = bf16[256,1920]{1,0:T(8,128)(2,1)S(1)} custom-call(s32[1]{0:T(128)} %bitcast.core, bf16[256,1024]{1,0:T(8,128)(2,1)S(1)} %collective-permute-done.6.up, bf16[256,1024]{1,0:T(8,128)(2,1)S(1)} %make_half.1.own, bf16[256,1024]{1,0:T(8,128)(2,1)S(1)} %collective-permute-done.7.down, bf16[256,1024]{1,0:T(8,128)(2,1)S(1)} %collective-permute-done.8.up2, ...), custom_call_target="tpu_custom_call" | custom-call | tf_op jit(solution)/shard_map/make_tiles/pallas_call | solution.py:21
  76.2 22.8 %all_to_all.15.parts = bf16[16,16,1920]{2,1,0:T(8,128)(2,1)S(1)} all-to-all(bf16[16,16,1920]{2,1,0:T(8,128)(2,1)S(1)} %bitcast.9), channel_id=1, replica_groups=mesh['y'=4,'core'=2,'z'=16,'x'=4] {'x','y'}, dimensions={0} | all-to-all | bytes 1966080 | tf_op jit(solution)/shard_map/all_to_all | solution.py:163
  99.1 3.1 %collective-permute-start.11 = (f32[3,16,128]{2,1,0:T(8,128)S(1)}, f32[3,16,128]{2,1,0:T(8,128)S(1)}, u32[]{:S(2)}, u32[]{:S(2)}) collective-permute-start(f32[3,16,128]{2,1,0:T(8,128)S(1)} %slice.18), channel_id=1, source_target_pairs={{0,4},{4,8},{8,12},{12,16},{16,20},{20,24},{24,28},{28,32},{32,36}... | collective-permute-start | bytes 73736 | tf_op jit(solution)/shard_map/ppermute | solution.py:34
  102.2 2.7 %collective-permute-start.12 = (f32[3,16,128]{2,1,0:T(8,128)S(1)}, f32[3,16,128]{2,1,0:T(8,128)S(1)}, u32[]{:S(2)}, u32[]{:S(2)}) collective-permute-start(f32[3,16,128]{2,1,0:T(8,128)S(1)} %slice.18), channel_id=1, source_target_pairs={{4,0},{8,4},{12,8},{16,12},{20,16},{24,20},{28,24},{32,28},{36,32}... | collective-permute-start | bytes 73736 | tf_op jit(solution)/shard_map/ppermute | solution.py:34
  105.0 4.2 %collective-permute-done.12 = f32[3,16,128]{2,1,0:T(8,128)S(1)} collective-permute-done((f32[3,16,128]{2,1,0:T(8,128)S(1)}, f32[3,16,128]{2,1,0:T(8,128)S(1)}, u32[]{:S(2)}, u32[]{:S(2)}) %collective-permute-start.12) | collective-permute-done | bytes 24608 | tf_op jit(solution)/shard_map/ppermute | solution.py:34
  (21 shorter events, 1.6 us)
Async XLA Ops:
  0.0 1.0 copy-start.1
  1.8 11.0 %all-to-all-start.1 = ((bf16[4,64,512]{2,1,0:T(8,128)(2,1)}), bf16[4,64,512]{2,1,0:T(8,128)(2,1)S(1)}, u32[]{:S(2)}, u32[]{:S(2)}) async-start(bf16[4,64,512]{2,1,0:T(8,128)(2,1)} %cut_orbitals.1), calls=%async_computation.1 | async-start | bytes 524288 | tf_op jit(solution)/shard_map/all_to_all | solution.py:133
  6.1 1.0 copy-start.2
  7.1 0.7 copy-start.3
  8.6 1.3 %copy-start = (bf16[4,2,15,64,128]{4,3,2,1,0:T(8,128)(2,1)}, bf16[4,2,15,64,128]{4,3,2,1,0:T(8,128)(2,1)S(1)}, u32[]{:S(2)}) copy-start(bf16[4,2,15,64,128]{4,3,2,1,0:T(8,128)(2,1)S(1)} %cut_integrals.1) | copy-start | bytes 5898244
  12.8 29.5 %all-to-all-start = ((bf16[8,15,64,128]{3,2,1,0:T(8,128)(2,1)}), bf16[8,15,64,128]{3,2,1,0:T(8,128)(2,1)S(1)}, u32[]{:S(2)}, u32[]{:S(2)}) async-start(bf16[8,15,64,128]{3,2,1,0:T(8,128)(2,1)} %bitcast.8), calls=%async_computation | async-start | bytes 3932160 | tf_op jit(solution)/shard_map/all_to_all | solution.py:139
  16.4 15.4 %collective-permute-start.1 = (bf16[3,64,512]{2,1,0:T(8,128)(2,1)S(1)}, bf16[3,64,512]{2,1,0:T(8,128)(2,1)S(1)}, u32[]{:S(2)}, u32[]{:S(2)}) collective-permute-start(bf16[3,64,512]{2,1,0:T(8,128)(2,1)S(1)} %get-tuple-element.10), channel_id=1, source_target_pairs={{0,8},{4,12},{8,16},{12,20},{16,24},{20,28},{24,32},{28,36},{32,40... | collective-permute-start | bytes 589832 | tf_op jit(solution)/shard_map/ppermute | solution.py:34
  22.8 12.9 %collective-permute-start.3 = (bf16[3,64,512]{2,1,0:T(8,128)(2,1)S(1)}, bf16[3,64,512]{2,1,0:T(8,128)(2,1)S(1)}, u32[]{:S(2)}, u32[]{:S(2)}) collective-permute-start(bf16[3,64,512]{2,1,0:T(8,128)(2,1)S(1)} %get-tuple-element.9), channel_id=1, source_target_pairs={{8,0},{12,4},{16,8},{20,12},{24,16},{28,20},{32,24},{36,28},{40,32... | collective-permute-start | bytes 589832 | tf_op jit(solution)/shard_map/ppermute | solution.py:34
  24.7 17.5 %collective-permute-start = (bf16[4,64,512]{2,1,0:T(8,128)(2,1)S(1)}, bf16[4,64,512]{2,1,0:T(8,128)(2,1)S(1)}, u32[]{:S(2)}, u32[]{:S(2)}) collective-permute-start(bf16[4,64,512]{2,1,0:T(8,128)(2,1)S(1)} %all-to-all-done.1.plane), channel_id=1, source_target_pairs={{4,0},{8,4},{12,8},{16,12},{20,16},{24,20},{28,24},{32,28},{36,32}... | collective-permute-start | bytes 786440 | tf_op jit(solution)/shard_map/ppermute | solution.py:34
  26.8 15.5 %collective-permute-start.2 = (bf16[4,64,512]{2,1,0:T(8,128)(2,1)S(1)}, bf16[4,64,512]{2,1,0:T(8,128)(2,1)S(1)}, u32[]{:S(2)}, u32[]{:S(2)}) collective-permute-start(bf16[4,64,512]{2,1,0:T(8,128)(2,1)S(1)} %all-to-all-done.1.plane), channel_id=1, source_target_pairs={{0,4},{4,8},{8,12},{12,16},{16,20},{20,24},{24,28},{28,32},{32,36}... | collective-permute-start | bytes 786440 | tf_op jit(solution)/shard_map/ppermute | solution.py:34
  36.7 7.6 %collective-permute-start.4 = (bf16[10,64,512]{2,1,0:T(8,128)(2,1)}, bf16[10,64,512]{2,1,0:T(8,128)(2,1)}, u32[]{:S(2)}, u32[]{:S(2)}) collective-permute-start(bf16[10,64,512]{2,1,0:T(8,128)(2,1)} %pad_maximum_fusion), channel_id=1, source_target_pairs={{0,64},{64,0},{1,65},{65,1},{2,66},{66,2},{3,67},{67,3},{4,68},{68... | collective-permute-start | bytes 1966088 | tf_op jit(solution)/shard_map/ppermute | solution.py:38
  42.3 3.8 %collective-permute-start.5 = (bf16[8,64,512]{2,1,0:T(8,128)(2,1)S(1)}, bf16[8,64,512]{2,1,0:T(8,128)(2,1)S(1)}, u32[]{:S(2)}, u32[]{:S(2)}) collective-permute-start(bf16[8,64,512]{2,1,0:T(8,128)(2,1)S(1)} %pad_maximum_fusion.1), channel_id=1, source_target_pairs={{0,64},{64,0},{1,65},{65,1},{2,66},{66,2},{3,67},{67,3},{4,68},{68... | collective-permute-start | bytes 1572872 | tf_op jit(solution)/shard_map/ppermute | solution.py:38
  48.5 16.3 %collective-permute-start.6 = (bf16[256,1024]{1,0:T(8,128)(2,1)S(1)}, bf16[256,1024]{1,0:T(8,128)(2,1)S(1)}, u32[]{:S(2)}, u32[]{:S(2)}) collective-permute-start(bf16[256,1024]{1,0:T(8,128)(2,1)S(1)} %make_half.1.own), channel_id=1, source_target_pairs={{0,4},{4,8},{8,12},{12,16},{16,20},{20,24},{24,28},{28,32},{32,36}... | collective-permute-start | bytes 1572872 | tf_op jit(solution)/shard_map/ppermute | solution.py:34
  53.4 16.8 %collective-permute-start.7 = (bf16[256,1024]{1,0:T(8,128)(2,1)S(1)}, bf16[256,1024]{1,0:T(8,128)(2,1)S(1)}, u32[]{:S(2)}, u32[]{:S(2)}) collective-permute-start(bf16[256,1024]{1,0:T(8,128)(2,1)S(1)} %make_half.1.own), channel_id=1, source_target_pairs={{4,0},{8,4},{12,8},{16,12},{20,16},{24,20},{28,24},{32,28},{36,32}... | collective-permute-start | bytes 1572872 | tf_op jit(solution)/shard_map/ppermute | solution.py:34
  55.3 16.8 %collective-permute-start.9 = (bf16[256,1024]{1,0:T(8,128)(2,1)S(1)}, bf16[256,1024]{1,0:T(8,128)(2,1)S(1)}, u32[]{:S(2)}, u32[]{:S(2)}) collective-permute-start(bf16[256,1024]{1,0:T(8,128)(2,1)S(1)} %make_half.1.own), channel_id=1, source_target_pairs={{0,64},{64,0},{1,65},{65,1},{2,66},{66,2},{3,67},{67,3},{4,68},{68... | collective-permute-start | bytes 1572872 | tf_op jit(solution)/shard_map/ppermute | solution.py:38
  64.9 7.3 %collective-permute-start.8 = (bf16[256,1024]{1,0:T(8,128)(2,1)S(1)}, bf16[256,1024]{1,0:T(8,128)(2,1)S(1)}, u32[]{:S(2)}, u32[]{:S(2)}) collective-permute-start(bf16[256,1024]{1,0:T(8,128)(2,1)S(1)} %collective-permute-done.6.up), channel_id=1, source_target_pairs={{0,64},{64,0},{1,65},{65,1},{2,66},{66,2},{3,67},{67,3},{4,68},{68... | collective-permute-start | bytes 1572872 | tf_op jit(solution)/shard_map/ppermute | solution.py:38
  70.2 3.8 %collective-permute-start.10 = (bf16[256,1024]{1,0:T(8,128)(2,1)S(1)}, bf16[256,1024]{1,0:T(8,128)(2,1)S(1)}, u32[]{:S(2)}, u32[]{:S(2)}) collective-permute-start(bf16[256,1024]{1,0:T(8,128)(2,1)S(1)} %collective-permute-done.7.down), channel_id=1, source_target_pairs={{0,64},{64,0},{1,65},{65,1},{2,66},{66,2},{3,67},{67,3},{4,68},{68... | collective-permute-start | bytes 1572872 | tf_op jit(solution)/shard_map/ppermute | solution.py:38
  76.1 28.8 %copy-start.4 = (s32[1,15]{1,0:T(1,128)S(1)}, s32[1,15]{1,0:T(1,128)}, u32[]{:S(2)}) copy-start(s32[1,15]{1,0:T(1,128)} %mask.1) | copy-start | bytes 184
  99.1 5.9 %collective-permute-start.11 = (f32[3,16,128]{2,1,0:T(8,128)S(1)}, f32[3,16,128]{2,1,0:T(8,128)S(1)}, u32[]{:S(2)}, u32[]{:S(2)}) collective-permute-start(f32[3,16,128]{2,1,0:T(8,128)S(1)} %slice.18), channel_id=1, source_target_pairs={{0,4},{4,8},{8,12},{12,16},{16,20},{20,24},{24,28},{28,32},{32,36}... | collective-permute-start | bytes 73736 | tf_op jit(solution)/shard_map/ppermute | solution.py:34
  102.2 6.9 %collective-permute-start.12 = (f32[3,16,128]{2,1,0:T(8,128)S(1)}, f32[3,16,128]{2,1,0:T(8,128)S(1)}, u32[]{:S(2)}, u32[]{:S(2)}) collective-permute-start(f32[3,16,128]{2,1,0:T(8,128)S(1)} %slice.18), channel_id=1, source_target_pairs={{4,0},{8,4},{12,8},{16,12},{20,16},{24,20},{28,24},{32,28},{36,32}... | collective-permute-start | bytes 73736 | tf_op jit(solution)/shard_map/ppermute | solution.py:34

commit v8 on v7

--- a/solution.py
+++ b/solution.py
@@ -34,16 +34,20 @@
     return lax.ppermute(x, "z", [(i, i + by) for i in range(n) if 0 <= i + by < n])
 
 
+def turned(x, by):
+    return lax.ppermute(x, "x", [(i, (i + by) % 4) for i in range(4)])
+
+
 def swapped(x):
     return lax.ppermute(x, "core", [(0, 1), (1, 0)])
 
 
-def orbital_kernel(core, occupied, out, sems):
-    rows = pl.ds(pl.multiple_of(core[0] * HALF, HALF), HALF)
-    copies = [
-        pltpu.make_async_copy(occupied.at[rows, pl.ds(x * COLS, COLS)], out.at[x], sems.at[x])
-        for x in range(4)
-    ]
+def orbital_kernel(place, occupied, own, right, far, left, sems):
+    rows = pl.ds(pl.multiple_of(place[0] * HALF, HALF), HALF)
+    copies = []
+    for turn, out in enumerate((own, right, far, left)):
+        columns = pl.ds(pl.multiple_of(lax.rem(place[1] + turn, 4) * COLS, COLS), COLS)
+        copies.append(pltpu.make_async_copy(occupied.at[rows, columns], out, sems.at[turn]))
     for copy in copies:
         copy.start()
     for copy in copies:
@@ -126,24 +130,34 @@
     c = lax.axis_index("core")
     core = c[None]
 
-    pieces = call(
-        orbital_kernel, "cut_orbitals", [SMEM, HBM], (4, HALF, COLS), BF16, core, occupied,
-        scratch=[pltpu.SemaphoreType.DMA((4,))], out=HBM,
-    )
-    plane = lax.all_to_all(pieces, "x", 0, 0)
-
     tiles = call(
         integral_kernel, "cut_integrals", [SMEM, VMEM], (4, 2, SPAN, HALF, ROWS), BF16,
         pair_mask, integrals[0, 0],
     )
+    tiles, occupied = lax.optimization_barrier((tiles, occupied))
     tiles = lax.all_to_all(tiles.reshape(8, SPAN, HALF, ROWS), ("x", "core"), 0, 0)
+
+    piece = jax.ShapeDtypeStruct((HALF, COLS), BF16)
+    mine, right, far, left = pl.pallas_call(
+        orbital_kernel,
+        in_specs=[SMEM, ANY],
+        out_specs=[ANY] * 4,
+        out_shape=[piece] * 4,
+        scratch_shapes=[pltpu.SemaphoreType.DMA((4,))],
+        name="cut_orbitals",
+    )(jnp.stack([c, x]), occupied)
+    from_left = turned(right, 1)
+    from_right = turned(left, -1)
+    from_far = turned(far, 2)
+    by_turn = jnp.stack([mine, from_right, from_far, from_left] * 2)
+    plane = lax.dynamic_slice_in_dim(by_turn, 4 - x, 4, 0)
 
     below2 = moved(plane[1:], 2)
     above2 = moved(plane[:3], -2)
     below = moved(plane, 1)
     above = moved(plane, -1)
+    tiles, above2 = lax.optimization_barrier((tiles, above2))
     first = swapped(jnp.concatenate([plane, below2, above2]))
-    tiles, above = lax.optimization_barrier((tiles, above))
     second = swapped(jnp.concatenate([below, above]))
 
     own = call(

time: 111 us -> 126 us (1.14)
  the two profiles are of different devices: /device:TPU:96 before, /device:TPU:64 now
where the time goes in v8:
time: 126 us; the launch traced here: 125 us
  starting transfers between devices  52.2 us (41%)
  waiting for transfers between devices  31.2 us (25%)
  blocking collectives  21 us (17%)
  Pallas kernels  14.4 us (11%)
  local copies, waits for them, and re-layouts  4.78 us (4%)
  other arithmetic  1.43 us (1%)
    ppermute x8, starting transfers between devices, moved(): lax.ppermute(x, 'z', [(i, i + by) for i in range(n) if 0 <= i + by < n])  27.7 us
    all_to_all x1, blocking collectives, per_device(): lax.all_to_all(partial.reshape(16, 16, SPAN * ROWS), ('x', 'y'), 0, 0)  21 us
    ppermute x8, waiting for transfers between devices, moved(): lax.ppermute(x, 'z', [(i, i + by) for i in range(n) if 0 <= i + by < n])  20.7 us
    ppermute x3, starting transfers between devices, turned(): return lax.ppermute(x, 'x', [(i, (i + by) % 4) for i in range(4)])  10.7 us
    pallas_call x1, Pallas kernels, per_device(): pl.pallas_call(orbital_kernel, in_specs=[SMEM, ANY], out_specs=[ANY] * 4,...  9.75 us
    ppermute x5, starting transfers between devices, swapped(): return lax.ppermute(x, 'core', [(0, 1), (1, 0)])  9.58 us
    ppermute x3, waiting for transfers between devices, turned(): return lax.ppermute(x, 'x', [(i, (i + by) % 4) for i in range(4)])  6.72 us
    unnamed x15, local copies, waits for them, and re-layouts  4.7 us
  transfers between devices with their start and end apart: 17, of which 12 were waited for; matrix products, arithmetic and copies ran while one was open for 2% of the time, Pallas kernels for 8%

profile of v8, /device:TPU:64, one launch (start us, length us, event | category | flops | bytes accessed | tf_op | source)
XLA Modules:
  0.0 125.3 jit_solution(14837272651461534913)
XLA Ops:
  2.5 1.3 %copy-done = bf16[4,2,15,64,128]{4,3,2,1,0:T(8,128)(2,1)} copy-done((bf16[4,2,15,64,128]{4,3,2,1,0:T(8,128)(2,1)}, bf16[4,2,15,64,128]{4,3,2,1,0:T(8,128)(2,1)S(1)}, u32[]{:S(2)}) %copy-start) | copy-done | bytes 1966104
  3.8 4.3 %all-to-all-start = ((bf16[8,15,64,128]{3,2,1,0:T(8,128)(2,1)}), bf16[8,15,64,128]{3,2,1,0:T(8,128)(2,1)S(1)}, u32[]{:S(2)}, u32[]{:S(2)}) async-start(bf16[8,15,64,128]{3,2,1,0:T(8,128)(2,1)} %bitcast.21), calls=%async_computation | async-start | bytes 3932160 | tf_op jit(solution)/shard_map/all_to_all | solution.py:138
  8.7 9.7 %cut_orbitals.1 = (bf16[64,512]{1,0:T(8,128)(2,1)}, bf16[64,512]{1,0:T(8,128)(2,1)}, bf16[64,512]{1,0:T(8,128)(2,1)}, bf16[64,512]{1,0:T(8,128)(2,1)}) custom-call(s32[2]{0:T(128)} %pad_add_fusion.place, bf16[128,2048]{1,0:T(8,128)(2,1)} %occupied), custom_call_target="tpu_custom_call" | custom-call | tf_op jit(solution)/shard_map/cut_orbitals/pallas_call | solution.py:141
  18.4 5.1 %collective-permute-start = (bf16[64,512]{1,0:T(8,128)(2,1)}, bf16[64,512]{1,0:T(8,128)(2,1)S(1)}, u32[]{:S(2)}, u32[]{:S(2)}) collective-permute-start(bf16[64,512]{1,0:T(8,128)(2,1)} %get-tuple-element.16), channel_id=1, source_target_pairs={{0,3},{1,0},{2,1},{3,2},{4,7},{5,4},{6,5},{7,6},{8,11},{9,8},{10,9... | collective-permute-start | bytes 196616 | tf_op jit(solution)/shard_map/ppermute | solution.py:38
  23.6 2.8 %collective-permute-start.1 = (bf16[64,512]{1,0:T(8,128)(2,1)}, bf16[64,512]{1,0:T(8,128)(2,1)S(1)}, u32[]{:S(2)}, u32[]{:S(2)}) collective-permute-start(bf16[64,512]{1,0:T(8,128)(2,1)} %get-tuple-element.17), channel_id=1, source_target_pairs={{0,2},{1,3},{2,0},{3,1},{4,6},{5,7},{6,4},{7,5},{8,10},{9,11},{10,... | collective-permute-start | bytes 196616 | tf_op jit(solution)/shard_map/ppermute | solution.py:38
  26.3 2.8 %collective-permute-start.2 = (bf16[64,512]{1,0:T(8,128)(2,1)}, bf16[64,512]{1,0:T(8,128)(2,1)S(1)}, u32[]{:S(2)}, u32[]{:S(2)}) collective-permute-start(bf16[64,512]{1,0:T(8,128)(2,1)} %get-tuple-element.18), channel_id=1, source_target_pairs={{0,1},{1,2},{2,3},{3,0},{4,5},{5,6},{6,7},{7,4},{8,9},{9,10},{10,1... | collective-permute-start | bytes 196616 | tf_op jit(solution)/shard_map/ppermute | solution.py:38
  30.0 4.3 %collective-permute-done = bf16[64,512]{1,0:T(8,128)(2,1)S(1)} collective-permute-done((bf16[64,512]{1,0:T(8,128)(2,1)}, bf16[64,512]{1,0:T(8,128)(2,1)S(1)}, u32[]{:S(2)}, u32[]{:S(2)}) %collective-permute-start) | collective-permute-done | bytes 65568 | tf_op jit(solution)/shard_map/ppermute | solution.py:38
  34.3 1.5 %collective-permute-done.1 = bf16[64,512]{1,0:T(8,128)(2,1)S(1)} collective-permute-done((bf16[64,512]{1,0:T(8,128)(2,1)}, bf16[64,512]{1,0:T(8,128)(2,1)S(1)}, u32[]{:S(2)}, u32[]{:S(2)}) %collective-permute-start.1) | collective-permute-done | bytes 65568 | tf_op jit(solution)/shard_map/ppermute | solution.py:38
  37.6 6.2 %collective-permute-start.3 = (bf16[3,64,512]{2,1,0:T(8,128)(2,1)S(1)}, bf16[3,64,512]{2,1,0:T(8,128)(2,1)S(1)}, u32[]{:S(2)}, u32[]{:S(2)}) collective-permute-start(bf16[3,64,512]{2,1,0:T(8,128)(2,1)S(1)} %get-tuple-element.22), channel_id=1, source_target_pairs={{8,0},{12,4},{16,8},{20,12},{24,16},{28,20},{32,24},{36,28},{40,32... | collective-permute-start | bytes 589832 | tf_op jit(solution)/shard_map/ppermute | solution.py:34
  43.8 2.2 %collective-permute-start.4 = (bf16[3,64,512]{2,1,0:T(8,128)(2,1)S(1)}, bf16[3,64,512]{2,1,0:T(8,128)(2,1)S(1)}, u32[]{:S(2)}, u32[]{:S(2)}) collective-permute-start(bf16[3,64,512]{2,1,0:T(8,128)(2,1)S(1)} %get-tuple-element.21), channel_id=1, source_target_pairs={{0,8},{4,12},{8,16},{12,20},{16,24},{20,28},{24,32},{28,36},{32,40... | collective-permute-start | bytes 589832 | tf_op jit(solution)/shard_map/ppermute | solution.py:34
  46.0 3.8 %collective-permute-start.5 = (bf16[4,64,512]{2,1,0:T(8,128)(2,1)S(1)}, bf16[4,64,512]{2,1,0:T(8,128)(2,1)S(1)}, u32[]{:S(2)}, u32[]{:S(2)}) collective-permute-start(bf16[4,64,512]{2,1,0:T(8,128)(2,1)S(1)} %constant_dynamic-slice_fusion.2.plane), channel_id=1, source_target_pairs={{0,4},{4,8},{8,12},{12,16},{16,20},{20,24},{24,28},{28,32},{32,36}... | collective-permute-start | bytes 786440 | tf_op jit(solution)/shard_map/ppermute | solution.py:34
  49.8 2.0 %collective-permute-start.6 = (bf16[4,64,512]{2,1,0:T(8,128)(2,1)S(1)}, bf16[4,64,512]{2,1,0:T(8,128)(2,1)S(1)}, u32[]{:S(2)}, u32[]{:S(2)}) collective-permute-start(bf16[4,64,512]{2,1,0:T(8,128)(2,1)S(1)} %constant_dynamic-slice_fusion.2.plane), channel_id=1, source_target_pairs={{4,0},{8,4},{12,8},{16,12},{20,16},{24,20},{28,24},{32,28},{36,32}... | collective-permute-start | bytes 786440 | tf_op jit(solution)/shard_map/ppermute | solution.py:34
  51.8 1.5 %collective-permute-done.3.above2 = bf16[3,64,512]{2,1,0:T(8,128)(2,1)S(1)} collective-permute-done((bf16[3,64,512]{2,1,0:T(8,128)(2,1)S(1)}, bf16[3,64,512]{2,1,0:T(8,128)(2,1)S(1)}, u32[]{:S(2)}, u32[]{:S(2)}) %collective-permute-start.3) | collective-permute-done | bytes 196640 | tf_op jit(solution)/shard_map/ppermute | solution.py:34
  53.3 1.1 collective-permute-done.4.below2
  54.5 1.9 %collective-permute-start.7 = (bf16[10,64,512]{2,1,0:T(8,128)(2,1)S(1)}, bf16[10,64,512]{2,1,0:T(8,128)(2,1)S(1)}, u32[]{:S(2)}, u32[]{:S(2)}) collective-permute-start(bf16[10,64,512]{2,1,0:T(8,128)(2,1)S(1)} %pad_maximum_fusion), channel_id=1, source_target_pairs={{0,64},{64,0},{1,65},{65,1},{2,66},{66,2},{3,67},{67,3},{4,68},{68... | collective-permute-start | bytes 1966088 | tf_op jit(solution)/shard_map/ppermute | solution.py:42
  56.4 3.1 %collective-permute-done.5.below = bf16[4,64,512]{2,1,0:T(8,128)(2,1)S(1)} collective-permute-done((bf16[4,64,512]{2,1,0:T(8,128)(2,1)S(1)}, bf16[4,64,512]{2,1,0:T(8,128)(2,1)S(1)}, u32[]{:S(2)}, u32[]{:S(2)}) %collective-permute-start.5) | collective-permute-done | bytes 262176 | tf_op jit(solution)/shard_map/ppermute | solution.py:34
  59.6 1.9 %collective-permute-start.8 = (bf16[8,64,512]{2,1,0:T(8,128)(2,1)S(1)}, bf16[8,64,512]{2,1,0:T(8,128)(2,1)S(1)}, u32[]{:S(2)}, u32[]{:S(2)}) collective-permute-start(bf16[8,64,512]{2,1,0:T(8,128)(2,1)S(1)} %pad_maximum_fusion.1), channel_id=1, source_target_pairs={{0,64},{64,0},{1,65},{65,1},{2,66},{66,2},{3,67},{67,3},{4,68},{68... | collective-permute-start | bytes 1572872 | tf_op jit(solution)/shard_map/ppermute | solution.py:42
  61.5 1.9 %collective-permute-done.8.second = bf16[8,64,512]{2,1,0:T(8,128)(2,1)S(1)} collective-permute-done((bf16[8,64,512]{2,1,0:T(8,128)(2,1)S(1)}, bf16[8,64,512]{2,1,0:T(8,128)(2,1)S(1)}, u32[]{:S(2)}, u32[]{:S(2)}) %collective-permute-start.8) | collective-permute-done | bytes 524320 | tf_op jit(solution)/shard_map/ppermute | solution.py:42
  63.4 1.6 %make_half.1.own = bf16[256,1024]{1,0:T(8,128)(2,1)S(1)} custom-call(s32[1]{0:T(128)} %bitcast.core, bf16[8,15,64,128]{3,2,1,0:T(8,128)(2,1)S(1)} %all-to-all-done.tiles, bf16[3,64,512]{2,1,0:T(8,128)(2,1)S(1)} %collective-permute-done.4.below2, bf16[4,64,512]{2,1,0:T(8,128)(2,1)S(1)} %collective-permute-done.5.below, ...), custom_call_target="tpu_custom_call" | custom-call | tf_op jit(solution)/shard_map/make_half/pallas_call | solution.py:21
  65.0 4.8 %collective-permute-start.9 = (bf16[256,1024]{1,0:T(8,128)(2,1)S(1)}, bf16[256,1024]{1,0:T(8,128)(2,1)S(1)}, u32[]{:S(2)}, u32[]{:S(2)}) collective-permute-start(bf16[256,1024]{1,0:T(8,128)(2,1)S(1)} %make_half.1.own), channel_id=1, source_target_pairs={{0,4},{4,8},{8,12},{12,16},{16,20},{20,24},{24,28},{28,32},{32,36}... | collective-permute-start | bytes 1572872 | tf_op jit(solution)/shard_map/ppermute | solution.py:34
  69.9 1.9 %collective-permute-start.10 = (bf16[256,1024]{1,0:T(8,128)(2,1)S(1)}, bf16[256,1024]{1,0:T(8,128)(2,1)S(1)}, u32[]{:S(2)}, u32[]{:S(2)}) collective-permute-start(bf16[256,1024]{1,0:T(8,128)(2,1)S(1)} %make_half.1.own), channel_id=1, source_target_pairs={{4,0},{8,4},{12,8},{16,12},{20,16},{24,20},{28,24},{32,28},{36,32}... | collective-permute-start | bytes 1572872 | tf_op jit(solution)/shard_map/ppermute | solution.py:34
  71.8 1.9 %collective-permute-start.12 = (bf16[256,1024]{1,0:T(8,128)(2,1)S(1)}, bf16[256,1024]{1,0:T(8,128)(2,1)S(1)}, u32[]{:S(2)}, u32[]{:S(2)}) collective-permute-start(bf16[256,1024]{1,0:T(8,128)(2,1)S(1)} %make_half.1.own), channel_id=1, source_target_pairs={{0,64},{64,0},{1,65},{65,1},{2,66},{66,2},{3,67},{67,3},{4,68},{68... | collective-permute-start | bytes 1572872 | tf_op jit(solution)/shard_map/ppermute | solution.py:42
  73.8 7.6 %collective-permute-done.9.up = bf16[256,1024]{1,0:T(8,128)(2,1)S(1)} collective-permute-done((bf16[256,1024]{1,0:T(8,128)(2,1)S(1)}, bf16[256,1024]{1,0:T(8,128)(2,1)S(1)}, u32[]{:S(2)}, u32[]{:S(2)}) %collective-permute-start.9) | collective-permute-done | bytes 524320 | tf_op jit(solution)/shard_map/ppermute | solution.py:34
  81.4 1.9 %collective-permute-start.11 = (bf16[256,1024]{1,0:T(8,128)(2,1)S(1)}, bf16[256,1024]{1,0:T(8,128)(2,1)S(1)}, u32[]{:S(2)}, u32[]{:S(2)}) collective-permute-start(bf16[256,1024]{1,0:T(8,128)(2,1)S(1)} %collective-permute-done.9.up), channel_id=1, source_target_pairs={{0,64},{64,0},{1,65},{65,1},{2,66},{66,2},{3,67},{67,3},{4,68},{68... | collective-permute-start | bytes 1572872 | tf_op jit(solution)/shard_map/ppermute | solution.py:42
  83.3 3.6 %collective-permute-done.10.down = bf16[256,1024]{1,0:T(8,128)(2,1)S(1)} collective-permute-done((bf16[256,1024]{1,0:T(8,128)(2,1)S(1)}, bf16[256,1024]{1,0:T(8,128)(2,1)S(1)}, u32[]{:S(2)}, u32[]{:S(2)}) %collective-permute-start.10) | collective-permute-done | bytes 524320 | tf_op jit(solution)/shard_map/ppermute | solution.py:34
  86.9 1.9 %collective-permute-start.13 = (bf16[256,1024]{1,0:T(8,128)(2,1)S(1)}, bf16[256,1024]{1,0:T(8,128)(2,1)S(1)}, u32[]{:S(2)}, u32[]{:S(2)}) collective-permute-start(bf16[256,1024]{1,0:T(8,128)(2,1)S(1)} %collective-permute-done.10.down), channel_id=1, source_target_pairs={{0,64},{64,0},{1,65},{65,1},{2,66},{66,2},{3,67},{67,3},{4,68},{68... | collective-permute-start | bytes 1572872 | tf_op jit(solution)/shard_map/ppermute | solution.py:42
  88.8 1.9 %collective-permute-done.13.down2 = bf16[256,1024]{1,0:T(8,128)(2,1)S(1)} collective-permute-done((bf16[256,1024]{1,0:T(8,128)(2,1)S(1)}, bf16[256,1024]{1,0:T(8,128)(2,1)S(1)}, u32[]{:S(2)}, u32[]{:S(2)}) %collective-permute-start.13) | collective-permute-done | bytes 524320 | tf_op jit(solution)/shard_map/ppermute | solution.py:42
  90.7 2.1 %make_tiles.1 = bf16[256,1920]{1,0:T(8,128)(2,1)S(1)} custom-call(s32[1]{0:T(128)} %bitcast.core, bf16[256,1024]{1,0:T(8,128)(2,1)S(1)} %collective-permute-done.9.up, bf16[256,1024]{1,0:T(8,128)(2,1)S(1)} %make_half.1.own, bf16[256,1024]{1,0:T(8,128)(2,1)S(1)} %collective-permute-done.10.down, bf16[256,1024]{1,0:T(8,128)(2,1)S(1)} %collective-permute-done.11.up2, ...), custom_call_target="tpu_custom_call" | custom-call | tf_op jit(solution)/shard_map/make_tiles/pallas_call | solution.py:21
  92.9 21.0 %all_to_all.10.parts = bf16[16,16,1920]{2,1,0:T(8,128)(2,1)S(1)} all-to-all(bf16[16,16,1920]{2,1,0:T(8,128)(2,1)S(1)} %bitcast.22), channel_id=1, replica_groups=mesh['y'=4,'core'=2,'z'=16,'x'=4] {'x','y'}, dimensions={0} | all-to-all | bytes 1966080 | tf_op jit(solution)/shard_map/all_to_all | solution.py:177
  114.0 4.8 %collective-permute-start.14 = (f32[3,16,128]{2,1,0:T(8,128)S(1)}, f32[3,16,128]{2,1,0:T(8,128)S(1)}, u32[]{:S(2)}, u32[]{:S(2)}) collective-permute-start(f32[3,16,128]{2,1,0:T(8,128)S(1)} %slice.16), channel_id=1, source_target_pairs={{0,4},{4,8},{8,12},{12,16},{16,20},{20,24},{24,28},{28,32},{32,36}... | collective-permute-start | bytes 73736 | tf_op jit(solution)/shard_map/ppermute | solution.py:34
  118.8 1.9 %collective-permute-start.15 = (f32[3,16,128]{2,1,0:T(8,128)S(1)}, f32[3,16,128]{2,1,0:T(8,128)S(1)}, u32[]{:S(2)}, u32[]{:S(2)}) collective-permute-start(f32[3,16,128]{2,1,0:T(8,128)S(1)} %slice.16), channel_id=1, source_target_pairs={{4,0},{8,4},{12,8},{16,12},{20,16},{24,20},{28,24},{32,28},{36,32}... | collective-permute-start | bytes 73736 | tf_op jit(solution)/shard_map/ppermute | solution.py:34
  120.8 3.7 %collective-permute-done.15 = f32[3,16,128]{2,1,0:T(8,128)S(1)} collective-permute-done((f32[3,16,128]{2,1,0:T(8,128)S(1)}, f32[3,16,128]{2,1,0:T(8,128)S(1)}, u32[]{:S(2)}, u32[]{:S(2)}) %collective-permute-start.15) | collective-permute-done | bytes 24608 | tf_op jit(solution)/shard_map/ppermute | solution.py:34
  (33 shorter events, 6.8 us)
Async XLA Ops:
  0.0 1.0 copy-start.1
  1.0 0.7 copy-start.2
  2.5 1.3 %copy-start = (bf16[4,2,15,64,128]{4,3,2,1,0:T(8,128)(2,1)}, bf16[4,2,15,64,128]{4,3,2,1,0:T(8,128)(2,1)S(1)}, u32[]{:S(2)}) copy-start(bf16[4,2,15,64,128]{4,3,2,1,0:T(8,128)(2,1)S(1)} %cut_integrals.1) | copy-start | bytes 5898244
  3.8 49.5 %all-to-all-start = ((bf16[8,15,64,128]{3,2,1,0:T(8,128)(2,1)}), bf16[8,15,64,128]{3,2,1,0:T(8,128)(2,1)S(1)}, u32[]{:S(2)}, u32[]{:S(2)}) async-start(bf16[8,15,64,128]{3,2,1,0:T(8,128)(2,1)} %bitcast.21), calls=%async_computation | async-start | bytes 3932160 | tf_op jit(solution)/shard_map/all_to_all | solution.py:138
  18.4 15.9 %collective-permute-start = (bf16[64,512]{1,0:T(8,128)(2,1)}, bf16[64,512]{1,0:T(8,128)(2,1)S(1)}, u32[]{:S(2)}, u32[]{:S(2)}) collective-permute-start(bf16[64,512]{1,0:T(8,128)(2,1)} %get-tuple-element.16), channel_id=1, source_target_pairs={{0,3},{1,0},{2,1},{3,2},{4,7},{5,4},{6,5},{7,6},{8,11},{9,8},{10,9... | collective-permute-start | bytes 196616 | tf_op jit(solution)/shard_map/ppermute | solution.py:38
  23.6 12.2 %collective-permute-start.1 = (bf16[64,512]{1,0:T(8,128)(2,1)}, bf16[64,512]{1,0:T(8,128)(2,1)S(1)}, u32[]{:S(2)}, u32[]{:S(2)}) collective-permute-start(bf16[64,512]{1,0:T(8,128)(2,1)} %get-tuple-element.17), channel_id=1, source_target_pairs={{0,2},{1,3},{2,0},{3,1},{4,6},{5,7},{6,4},{7,5},{8,10},{9,11},{10,... | collective-permute-start | bytes 196616 | tf_op jit(solution)/shard_map/ppermute | solution.py:38
  26.3 10.4 %collective-permute-start.2 = (bf16[64,512]{1,0:T(8,128)(2,1)}, bf16[64,512]{1,0:T(8,128)(2,1)S(1)}, u32[]{:S(2)}, u32[]{:S(2)}) collective-permute-start(bf16[64,512]{1,0:T(8,128)(2,1)} %get-tuple-element.18), channel_id=1, source_target_pairs={{0,1},{1,2},{2,3},{3,0},{4,5},{5,6},{6,7},{7,4},{8,9},{9,10},{10,1... | collective-permute-start | bytes 196616 | tf_op jit(solution)/shard_map/ppermute | solution.py:38
  37.6 15.7 %collective-permute-start.3 = (bf16[3,64,512]{2,1,0:T(8,128)(2,1)S(1)}, bf16[3,64,512]{2,1,0:T(8,128)(2,1)S(1)}, u32[]{:S(2)}, u32[]{:S(2)}) collective-permute-start(bf16[3,64,512]{2,1,0:T(8,128)(2,1)S(1)} %get-tuple-element.22), channel_id=1, source_target_pairs={{8,0},{12,4},{16,8},{20,12},{24,16},{28,20},{32,24},{36,28},{40,32... | collective-permute-start | bytes 589832 | tf_op jit(solution)/shard_map/ppermute | solution.py:34
  43.8 10.6 %collective-permute-start.4 = (bf16[3,64,512]{2,1,0:T(8,128)(2,1)S(1)}, bf16[3,64,512]{2,1,0:T(8,128)(2,1)S(1)}, u32[]{:S(2)}, u32[]{:S(2)}) collective-permute-start(bf16[3,64,512]{2,1,0:T(8,128)(2,1)S(1)} %get-tuple-element.21), channel_id=1, source_target_pairs={{0,8},{4,12},{8,16},{12,20},{16,24},{20,28},{24,32},{28,36},{32,40... | collective-permute-start | bytes 589832 | tf_op jit(solution)/shard_map/ppermute | solution.py:34
  46.0 13.5 %collective-permute-start.5 = (bf16[4,64,512]{2,1,0:T(8,128)(2,1)S(1)}, bf16[4,64,512]{2,1,0:T(8,128)(2,1)S(1)}, u32[]{:S(2)}, u32[]{:S(2)}) collective-permute-start(bf16[4,64,512]{2,1,0:T(8,128)(2,1)S(1)} %constant_dynamic-slice_fusion.2.plane), channel_id=1, source_target_pairs={{0,4},{4,8},{8,12},{12,16},{16,20},{20,24},{24,28},{28,32},{32,36}... | collective-permute-start | bytes 786440 | tf_op jit(solution)/shard_map/ppermute | solution.py:34
  49.8 9.7 %collective-permute-start.6 = (bf16[4,64,512]{2,1,0:T(8,128)(2,1)S(1)}, bf16[4,64,512]{2,1,0:T(8,128)(2,1)S(1)}, u32[]{:S(2)}, u32[]{:S(2)}) collective-permute-start(bf16[4,64,512]{2,1,0:T(8,128)(2,1)S(1)} %constant_dynamic-slice_fusion.2.plane), channel_id=1, source_target_pairs={{4,0},{8,4},{12,8},{16,12},{20,16},{24,20},{28,24},{32,28},{36,32}... | collective-permute-start | bytes 786440 | tf_op jit(solution)/shard_map/ppermute | solution.py:34
  54.5 9.0 %collective-permute-start.7 = (bf16[10,64,512]{2,1,0:T(8,128)(2,1)S(1)}, bf16[10,64,512]{2,1,0:T(8,128)(2,1)S(1)}, u32[]{:S(2)}, u32[]{:S(2)}) collective-permute-start(bf16[10,64,512]{2,1,0:T(8,128)(2,1)S(1)} %pad_maximum_fusion), channel_id=1, source_target_pairs={{0,64},{64,0},{1,65},{65,1},{2,66},{66,2},{3,67},{67,3},{4,68},{68... | collective-permute-start | bytes 1966088 | tf_op jit(solution)/shard_map/ppermute | solution.py:42
  59.6 3.8 %collective-permute-start.8 = (bf16[8,64,512]{2,1,0:T(8,128)(2,1)S(1)}, bf16[8,64,512]{2,1,0:T(8,128)(2,1)S(1)}, u32[]{:S(2)}, u32[]{:S(2)}) collective-permute-start(bf16[8,64,512]{2,1,0:T(8,128)(2,1)S(1)} %pad_maximum_fusion.1), channel_id=1, source_target_pairs={{0,64},{64,0},{1,65},{65,1},{2,66},{66,2},{3,67},{67,3},{4,68},{68... | collective-permute-start | bytes 1572872 | tf_op jit(solution)/shard_map/ppermute | solution.py:42
  65.0 16.3 %collective-permute-start.9 = (bf16[256,1024]{1,0:T(8,128)(2,1)S(1)}, bf16[256,1024]{1,0:T(8,128)(2,1)S(1)}, u32[]{:S(2)}, u32[]{:S(2)}) collective-permute-start(bf16[256,1024]{1,0:T(8,128)(2,1)S(1)} %make_half.1.own), channel_id=1, source_target_pairs={{0,4},{4,8},{8,12},{12,16},{16,20},{20,24},{24,28},{28,32},{32,36}... | collective-permute-start | bytes 1572872 | tf_op jit(solution)/shard_map/ppermute | solution.py:34
  69.9 17.0 %collective-permute-start.10 = (bf16[256,1024]{1,0:T(8,128)(2,1)S(1)}, bf16[256,1024]{1,0:T(8,128)(2,1)S(1)}, u32[]{:S(2)}, u32[]{:S(2)}) collective-permute-start(bf16[256,1024]{1,0:T(8,128)(2,1)S(1)} %make_half.1.own), channel_id=1, source_target_pairs={{4,0},{8,4},{12,8},{16,12},{20,16},{24,20},{28,24},{32,28},{36,32}... | collective-permute-start | bytes 1572872 | tf_op jit(solution)/shard_map/ppermute | solution.py:34
  71.8 17.0 %collective-permute-start.12 = (bf16[256,1024]{1,0:T(8,128)(2,1)S(1)}, bf16[256,1024]{1,0:T(8,128)(2,1)S(1)}, u32[]{:S(2)}, u32[]{:S(2)}) collective-permute-start(bf16[256,1024]{1,0:T(8,128)(2,1)S(1)} %make_half.1.own), channel_id=1, source_target_pairs={{0,64},{64,0},{1,65},{65,1},{2,66},{66,2},{3,67},{67,3},{4,68},{68... | collective-permute-start | bytes 1572872 | tf_op jit(solution)/shard_map/ppermute | solution.py:42
  81.4 7.5 %collective-permute-start.11 = (bf16[256,1024]{1,0:T(8,128)(2,1)S(1)}, bf16[256,1024]{1,0:T(8,128)(2,1)S(1)}, u32[]{:S(2)}, u32[]{:S(2)}) collective-permute-start(bf16[256,1024]{1,0:T(8,128)(2,1)S(1)} %collective-permute-done.9.up), channel_id=1, source_target_pairs={{0,64},{64,0},{1,65},{65,1},{2,66},{66,2},{3,67},{67,3},{4,68},{68... | collective-permute-start | bytes 1572872 | tf_op jit(solution)/shard_map/ppermute | solution.py:42
  86.9 3.8 %collective-permute-start.13 = (bf16[256,1024]{1,0:T(8,128)(2,1)S(1)}, bf16[256,1024]{1,0:T(8,128)(2,1)S(1)}, u32[]{:S(2)}, u32[]{:S(2)}) collective-permute-start(bf16[256,1024]{1,0:T(8,128)(2,1)S(1)} %collective-permute-done.10.down), channel_id=1, source_target_pairs={{0,64},{64,0},{1,65},{65,1},{2,66},{66,2},{3,67},{67,3},{4,68},{68... | collective-permute-start | bytes 1572872 | tf_op jit(solution)/shard_map/ppermute | solution.py:42
  92.8 27.9 %copy-start.3 = (s32[1,15]{1,0:T(1,128)S(1)}, s32[1,15]{1,0:T(1,128)}, u32[]{:S(2)}) copy-start(s32[1,15]{1,0:T(1,128)} %mask.1) | copy-start | bytes 184
  114.0 6.8 %collective-permute-start.14 = (f32[3,16,128]{2,1,0:T(8,128)S(1)}, f32[3,16,128]{2,1,0:T(8,128)S(1)}, u32[]{:S(2)}, u32[]{:S(2)}) collective-permute-start(f32[3,16,128]{2,1,0:T(8,128)S(1)} %slice.16), channel_id=1, source_target_pairs={{0,4},{4,8},{8,12},{12,16},{16,20},{20,24},{24,28},{28,32},{32,36}... | collective-permute-start | bytes 73736 | tf_op jit(solution)/shard_map/ppermute | solution.py:34
  118.8 5.7 %collective-permute-start.15 = (f32[3,16,128]{2,1,0:T(8,128)S(1)}, f32[3,16,128]{2,1,0:T(8,128)S(1)}, u32[]{:S(2)}, u32[]{:S(2)}) collective-permute-start(f32[3,16,128]{2,1,0:T(8,128)S(1)} %slice.16), channel_id=1, source_target_pairs={{4,0},{8,4},{12,8},{16,12},{20,16},{24,20},{28,24},{32,28},{36,32}... | collective-permute-start | bytes 73736 | tf_op jit(solution)/shard_map/ppermute | solution.py:34

commit v9 on v7

--- a/solution.py
+++ b/solution.py
@@ -143,7 +143,6 @@
     below = moved(plane, 1)
     above = moved(plane, -1)
     first = swapped(jnp.concatenate([plane, below2, above2]))
-    tiles, above = lax.optimization_barrier((tiles, above))
     second = swapped(jnp.concatenate([below, above]))
 
     own = call(

time: 111 us -> 115 us (1.036)
  local copies, waits for them, and re-layouts: 4.07 us -> 7.83 us
  waiting for transfers between devices: 29.4 us -> 31 us
    unnamed x10 -> x18, local copies, waits for them, and re-layouts: 4.02 us -> 7.79 us
    ppermute x8, waiting for transfers between devices: 22.8 us -> 24.4 us  [moved(): lax.ppermute(x, 'z', [(i, i + by) for i in range(n) if 0 <= i + by < n])]
  transfers between devices with their start and end apart: 15 -> 15, of which waited for: 8 -> 9; matrix products, arithmetic and copies ran while one was open for 1% -> 0% of each run, Pallas kernels for 1% -> 1%
where the time goes in v9:
time: 115 us; the launch traced here: 114 us
  starting transfers between devices  44.7 us (39%)
  waiting for transfers between devices  31 us (27%)
  blocking collectives  23.7 us (21%)
  local copies, waits for them, and re-layouts  7.83 us (7%)
  Pallas kernels  5.41 us (5%)
    ppermute x8, starting transfers between devices, moved(): lax.ppermute(x, 'z', [(i, i + by) for i in range(n) if 0 <= i + by < n])  27.3 us
    ppermute x8, waiting for transfers between devices, moved(): lax.ppermute(x, 'z', [(i, i + by) for i in range(n) if 0 <= i + by < n])  24.4 us
    all_to_all x1, blocking collectives, per_device(): lax.all_to_all(partial.reshape(16, 16, SPAN * ROWS), ('x', 'y'), 0, 0)  23.7 us
    ppermute x5, starting transfers between devices, swapped(): return lax.ppermute(x, 'core', [(0, 1), (1, 0)])  9.58 us
    unnamed x18, local copies, waits for them, and re-layouts  7.79 us
    pallas_call x5, Pallas kernels, call(): pl.pallas_call(kernel, in_specs=specs, out_specs=out, out_shape=jax.Shape...  5.41 us
    all_to_all x1, starting transfers between devices, per_device(): plane = lax.all_to_all(pieces, 'x', 0, 0)  4.3 us
    ppermute x5, waiting for transfers between devices, swapped(): return lax.ppermute(x, 'core', [(0, 1), (1, 0)])  3.74 us
  transfers between devices with their start and end apart: 15, of which 9 were waited for; matrix products, arithmetic and copies ran while one was open for 0% of the time, Pallas kernels for 1%

profile of v9, /device:TPU:96, one launch (start us, length us, event | category | flops | bytes accessed | tf_op | source)
XLA Modules:
  0.0 113.7 jit_solution(17613452608813513532)
XLA Ops:
  0.0 1.0 copy-done.5
  1.8 4.3 %all-to-all-start.1 = ((bf16[4,64,512]{2,1,0:T(8,128)(2,1)}), bf16[4,64,512]{2,1,0:T(8,128)(2,1)S(1)}, u32[]{:S(2)}, u32[]{:S(2)}) async-start(bf16[4,64,512]{2,1,0:T(8,128)(2,1)} %cut_orbitals.1), calls=%async_computation.1 | async-start | bytes 524288 | tf_op jit(solution)/shard_map/all_to_all | solution.py:133
  6.1 1.0 copy-done.6
  8.6 1.3 %copy-done = bf16[4,2,15,64,128]{4,3,2,1,0:T(8,128)(2,1)} copy-done((bf16[4,2,15,64,128]{4,3,2,1,0:T(8,128)(2,1)}, bf16[4,2,15,64,128]{4,3,2,1,0:T(8,128)(2,1)S(1)}, u32[]{:S(2)}) %copy-start) | copy-done | bytes 1966104
  9.9 2.9 %all-to-all-done.1.plane = bf16[4,64,512]{2,1,0:T(8,128)(2,1)S(1)} async-done(((bf16[4,64,512]{2,1,0:T(8,128)(2,1)}), bf16[4,64,512]{2,1,0:T(8,128)(2,1)S(1)}, u32[]{:S(2)}, u32[]{:S(2)}) %all-to-all-start.1) | async-done | bytes 262176 | tf_op jit(solution)/shard_map/all_to_all | solution.py:133
  12.8 3.6 %all-to-all-start = ((bf16[8,15,64,128]{3,2,1,0:T(8,128)(2,1)}), bf16[8,15,64,128]{3,2,1,0:T(8,128)(2,1)S(1)}, u32[]{:S(2)}, u32[]{:S(2)}) async-start(bf16[8,15,64,128]{3,2,1,0:T(8,128)(2,1)} %bitcast.8), calls=%async_computation | async-start | bytes 3932160 | tf_op jit(solution)/shard_map/all_to_all | solution.py:139
  16.4 6.4 %collective-permute-start = (bf16[3,64,512]{2,1,0:T(8,128)(2,1)S(1)}, bf16[3,64,512]{2,1,0:T(8,128)(2,1)S(1)}, u32[]{:S(2)}, u32[]{:S(2)}) collective-permute-start(bf16[3,64,512]{2,1,0:T(8,128)(2,1)S(1)} %get-tuple-element.6), channel_id=1, source_target_pairs={{0,8},{4,12},{8,16},{12,20},{16,24},{20,28},{24,32},{28,36},{32,40... | collective-permute-start | bytes 589832 | tf_op jit(solution)/shard_map/ppermute | solution.py:34
  22.8 1.9 %collective-permute-start.3 = (bf16[3,64,512]{2,1,0:T(8,128)(2,1)S(1)}, bf16[3,64,512]{2,1,0:T(8,128)(2,1)S(1)}, u32[]{:S(2)}, u32[]{:S(2)}) collective-permute-start(bf16[3,64,512]{2,1,0:T(8,128)(2,1)S(1)} %get-tuple-element.5), channel_id=1, source_target_pairs={{8,0},{12,4},{16,8},{20,12},{24,16},{28,20},{32,24},{36,28},{40,32... | collective-permute-start | bytes 589832 | tf_op jit(solution)/shard_map/ppermute | solution.py:34
  24.7 4.7 %collective-permute-start.1 = (bf16[4,64,512]{2,1,0:T(8,128)(2,1)S(1)}, bf16[4,64,512]{2,1,0:T(8,128)(2,1)S(1)}, u32[]{:S(2)}, u32[]{:S(2)}) collective-permute-start(bf16[4,64,512]{2,1,0:T(8,128)(2,1)S(1)} %all-to-all-done.1.plane), channel_id=1, source_target_pairs={{0,4},{4,8},{8,12},{12,16},{16,20},{20,24},{24,28},{28,32},{32,36}... | collective-permute-start | bytes 786440 | tf_op jit(solution)/shard_map/ppermute | solution.py:34
  29.4 1.9 %collective-permute-start.2 = (bf16[4,64,512]{2,1,0:T(8,128)(2,1)S(1)}, bf16[4,64,512]{2,1,0:T(8,128)(2,1)S(1)}, u32[]{:S(2)}, u32[]{:S(2)}) collective-permute-start(bf16[4,64,512]{2,1,0:T(8,128)(2,1)S(1)} %all-to-all-done.1.plane), channel_id=1, source_target_pairs={{4,0},{8,4},{12,8},{16,12},{20,16},{24,20},{28,24},{32,28},{36,32}... | collective-permute-start | bytes 786440 | tf_op jit(solution)/shard_map/ppermute | solution.py:34
  31.4 3.0 %collective-permute-done.3.above2 = bf16[3,64,512]{2,1,0:T(8,128)(2,1)S(1)} collective-permute-done((bf16[3,64,512]{2,1,0:T(8,128)(2,1)S(1)}, bf16[3,64,512]{2,1,0:T(8,128)(2,1)S(1)}, u32[]{:S(2)}, u32[]{:S(2)}) %collective-permute-start.3) | collective-permute-done | bytes 196640 | tf_op jit(solution)/shard_map/ppermute | solution.py:34
  34.5 1.9 %collective-permute-start.4 = (bf16[10,64,512]{2,1,0:T(8,128)(2,1)S(1)}, bf16[10,64,512]{2,1,0:T(8,128)(2,1)S(1)}, u32[]{:S(2)}, u32[]{:S(2)}) collective-permute-start(bf16[10,64,512]{2,1,0:T(8,128)(2,1)S(1)} %pad_maximum_fusion), channel_id=1, source_target_pairs={{0,64},{64,0},{1,65},{65,1},{2,66},{66,2},{3,67},{67,3},{4,68},{68... | collective-permute-start | bytes 1966088 | tf_op jit(solution)/shard_map/ppermute | solution.py:38
  36.4 1.1 collective-permute-done.1.below
  37.5 4.7 %collective-permute-done.2.above = bf16[4,64,512]{2,1,0:T(8,128)(2,1)S(1)} collective-permute-done((bf16[4,64,512]{2,1,0:T(8,128)(2,1)S(1)}, bf16[4,64,512]{2,1,0:T(8,128)(2,1)S(1)}, u32[]{:S(2)}, u32[]{:S(2)}) %collective-permute-start.2) | collective-permute-done | bytes 262176 | tf_op jit(solution)/shard_map/ppermute | solution.py:34
  42.3 1.9 %collective-permute-start.5 = (bf16[8,64,512]{2,1,0:T(8,128)(2,1)S(1)}, bf16[8,64,512]{2,1,0:T(8,128)(2,1)S(1)}, u32[]{:S(2)}, u32[]{:S(2)}) collective-permute-start(bf16[8,64,512]{2,1,0:T(8,128)(2,1)S(1)} %pad_maximum_fusion.1), channel_id=1, source_target_pairs={{0,64},{64,0},{1,65},{65,1},{2,66},{66,2},{3,67},{67,3},{4,68},{68... | collective-permute-start | bytes 1572872 | tf_op jit(solution)/shard_map/ppermute | solution.py:38
  44.2 1.9 %collective-permute-done.5.second = bf16[8,64,512]{2,1,0:T(8,128)(2,1)S(1)} collective-permute-done((bf16[8,64,512]{2,1,0:T(8,128)(2,1)S(1)}, bf16[8,64,512]{2,1,0:T(8,128)(2,1)S(1)}, u32[]{:S(2)}, u32[]{:S(2)}) %collective-permute-start.5) | collective-permute-done | bytes 524320 | tf_op jit(solution)/shard_map/ppermute | solution.py:38
  47.8 1.1 copy-done.2
  48.9 1.0 copy-done.4
  49.9 1.6 %make_half.1.own = bf16[256,1024]{1,0:T(8,128)(2,1)S(1)} custom-call(s32[1]{0:T(128)} %bitcast.core, bf16[8,15,64,128]{3,2,1,0:T(8,128)(2,1)S(1)} %all-to-all-done.tiles, bf16[3,64,512]{2,1,0:T(8,128)(2,1)S(1)} %collective-permute-done.below2, bf16[4,64,512]{2,1,0:T(8,128)(2,1)S(1)} %collective-permute-done.1.below, ...), custom_call_target="tpu_custom_call" | custom-call | tf_op jit(solution)/shard_map/make_half/pallas_call | solution.py:21
  51.5 4.6 %collective-permute-start.6 = (bf16[256,1024]{1,0:T(8,128)(2,1)S(1)}, bf16[256,1024]{1,0:T(8,128)(2,1)S(1)}, u32[]{:S(2)}, u32[]{:S(2)}) collective-permute-start(bf16[256,1024]{1,0:T(8,128)(2,1)S(1)} %make_half.1.own), channel_id=1, source_target_pairs={{0,4},{4,8},{8,12},{12,16},{16,20},{20,24},{24,28},{28,32},{32,36}... | collective-permute-start | bytes 1572872 | tf_op jit(solution)/shard_map/ppermute | solution.py:34
  56.1 1.9 %collective-permute-start.7 = (bf16[256,1024]{1,0:T(8,128)(2,1)S(1)}, bf16[256,1024]{1,0:T(8,128)(2,1)S(1)}, u32[]{:S(2)}, u32[]{:S(2)}) collective-permute-start(bf16[256,1024]{1,0:T(8,128)(2,1)S(1)} %make_half.1.own), channel_id=1, source_target_pairs={{4,0},{8,4},{12,8},{16,12},{20,16},{24,20},{28,24},{32,28},{36,32}... | collective-permute-start | bytes 1572872 | tf_op jit(solution)/shard_map/ppermute | solution.py:34
  58.0 1.9 %collective-permute-start.9 = (bf16[256,1024]{1,0:T(8,128)(2,1)S(1)}, bf16[256,1024]{1,0:T(8,128)(2,1)S(1)}, u32[]{:S(2)}, u32[]{:S(2)}) collective-permute-start(bf16[256,1024]{1,0:T(8,128)(2,1)S(1)} %make_half.1.own), channel_id=1, source_target_pairs={{0,64},{64,0},{1,65},{65,1},{2,66},{66,2},{3,67},{67,3},{4,68},{68... | collective-permute-start | bytes 1572872 | tf_op jit(solution)/shard_map/ppermute | solution.py:38
  59.9 7.6 %collective-permute-done.6.up = bf16[256,1024]{1,0:T(8,128)(2,1)S(1)} collective-permute-done((bf16[256,1024]{1,0:T(8,128)(2,1)S(1)}, bf16[256,1024]{1,0:T(8,128)(2,1)S(1)}, u32[]{:S(2)}, u32[]{:S(2)}) %collective-permute-start.6) | collective-permute-done | bytes 524320 | tf_op jit(solution)/shard_map/ppermute | solution.py:34
  67.6 1.9 %collective-permute-start.8 = (bf16[256,1024]{1,0:T(8,128)(2,1)S(1)}, bf16[256,1024]{1,0:T(8,128)(2,1)S(1)}, u32[]{:S(2)}, u32[]{:S(2)}) collective-permute-start(bf16[256,1024]{1,0:T(8,128)(2,1)S(1)} %collective-permute-done.6.up), channel_id=1, source_target_pairs={{0,64},{64,0},{1,65},{65,1},{2,66},{66,2},{3,67},{67,3},{4,68},{68... | collective-permute-start | bytes 1572872 | tf_op jit(solution)/shard_map/ppermute | solution.py:38
  69.5 3.4 %collective-permute-done.7.down = bf16[256,1024]{1,0:T(8,128)(2,1)S(1)} collective-permute-done((bf16[256,1024]{1,0:T(8,128)(2,1)S(1)}, bf16[256,1024]{1,0:T(8,128)(2,1)S(1)}, u32[]{:S(2)}, u32[]{:S(2)}) %collective-permute-start.7) | collective-permute-done | bytes 524320 | tf_op jit(solution)/shard_map/ppermute | solution.py:34
  72.9 1.9 %collective-permute-start.10 = (bf16[256,1024]{1,0:T(8,128)(2,1)S(1)}, bf16[256,1024]{1,0:T(8,128)(2,1)S(1)}, u32[]{:S(2)}, u32[]{:S(2)}) collective-permute-start(bf16[256,1024]{1,0:T(8,128)(2,1)S(1)} %collective-permute-done.7.down), channel_id=1, source_target_pairs={{0,64},{64,0},{1,65},{65,1},{2,66},{66,2},{3,67},{67,3},{4,68},{68... | collective-permute-start | bytes 1572872 | tf_op jit(solution)/shard_map/ppermute | solution.py:38
  74.8 1.9 %collective-permute-done.10.down2 = bf16[256,1024]{1,0:T(8,128)(2,1)S(1)} collective-permute-done((bf16[256,1024]{1,0:T(8,128)(2,1)S(1)}, bf16[256,1024]{1,0:T(8,128)(2,1)S(1)}, u32[]{:S(2)}, u32[]{:S(2)}) %collective-permute-start.10) | collective-permute-done | bytes 524320 | tf_op jit(solution)/shard_map/ppermute | solution.py:38
  76.7 2.1 %make_tiles.1 = bf16[256,1920]{1,0:T(8,128)(2,1)S(1)} custom-call(s32[1]{0:T(128)} %bitcast.core, bf16[256,1024]{1,0:T(8,128)(2,1)S(1)} %collective-permute-done.6.up, bf16[256,1024]{1,0:T(8,128)(2,1)S(1)} %make_half.1.own, bf16[256,1024]{1,0:T(8,128)(2,1)S(1)} %collective-permute-done.7.down, bf16[256,1024]{1,0:T(8,128)(2,1)S(1)} %collective-permute-done.8.up2, ...), custom_call_target="tpu_custom_call" | custom-call | tf_op jit(solution)/shard_map/make_tiles/pallas_call | solution.py:21
  78.8 23.7 %all_to_all.15.parts = bf16[16,16,1920]{2,1,0:T(8,128)(2,1)S(1)} all-to-all(bf16[16,16,1920]{2,1,0:T(8,128)(2,1)S(1)} %bitcast.9), channel_id=1, replica_groups=mesh['y'=4,'core'=2,'z'=16,'x'=4] {'x','y'}, dimensions={0} | all-to-all | bytes 1966080 | tf_op jit(solution)/shard_map/all_to_all | solution.py:162
  102.6 3.4 %collective-permute-start.11 = (f32[3,16,128]{2,1,0:T(8,128)S(1)}, f32[3,16,128]{2,1,0:T(8,128)S(1)}, u32[]{:S(2)}, u32[]{:S(2)}) collective-permute-start(f32[3,16,128]{2,1,0:T(8,128)S(1)} %slice.18), channel_id=1, source_target_pairs={{0,4},{4,8},{8,12},{12,16},{16,20},{20,24},{24,28},{28,32},{32,36}... | collective-permute-start | bytes 73736 | tf_op jit(solution)/shard_map/ppermute | solution.py:34
  106.1 2.4 %collective-permute-start.12 = (f32[3,16,128]{2,1,0:T(8,128)S(1)}, f32[3,16,128]{2,1,0:T(8,128)S(1)}, u32[]{:S(2)}, u32[]{:S(2)}) collective-permute-start(f32[3,16,128]{2,1,0:T(8,128)S(1)} %slice.18), channel_id=1, source_target_pairs={{4,0},{8,4},{12,8},{16,12},{20,16},{24,20},{28,24},{32,28},{36,32}... | collective-permute-start | bytes 73736 | tf_op jit(solution)/shard_map/ppermute | solution.py:34
  108.5 4.5 %collective-permute-done.12 = f32[3,16,128]{2,1,0:T(8,128)S(1)} collective-permute-done((f32[3,16,128]{2,1,0:T(8,128)S(1)}, f32[3,16,128]{2,1,0:T(8,128)S(1)}, u32[]{:S(2)}, u32[]{:S(2)}) %collective-permute-start.12) | collective-permute-done | bytes 24608 | tf_op jit(solution)/shard_map/ppermute | solution.py:34
  (29 shorter events, 4.9 us)
Async XLA Ops:
  0.0 1.0 copy-start.5
  1.8 11.0 %all-to-all-start.1 = ((bf16[4,64,512]{2,1,0:T(8,128)(2,1)}), bf16[4,64,512]{2,1,0:T(8,128)(2,1)S(1)}, u32[]{:S(2)}, u32[]{:S(2)}) async-start(bf16[4,64,512]{2,1,0:T(8,128)(2,1)} %cut_orbitals.1), calls=%async_computation.1 | async-start | bytes 524288 | tf_op jit(solution)/shard_map/all_to_all | solution.py:133
  6.1 1.0 copy-start.6
  7.1 0.7 copy-start.7
  8.6 1.3 %copy-start = (bf16[4,2,15,64,128]{4,3,2,1,0:T(8,128)(2,1)}, bf16[4,2,15,64,128]{4,3,2,1,0:T(8,128)(2,1)S(1)}, u32[]{:S(2)}) copy-start(bf16[4,2,15,64,128]{4,3,2,1,0:T(8,128)(2,1)S(1)} %cut_integrals.1) | copy-start | bytes 5898244
  12.8 35.0 %all-to-all-start = ((bf16[8,15,64,128]{3,2,1,0:T(8,128)(2,1)}), bf16[8,15,64,128]{3,2,1,0:T(8,128)(2,1)S(1)}, u32[]{:S(2)}, u32[]{:S(2)}) async-start(bf16[8,15,64,128]{3,2,1,0:T(8,128)(2,1)} %bitcast.8), calls=%async_computation | async-start | bytes 3932160 | tf_op jit(solution)/shard_map/all_to_all | solution.py:139
  16.4 14.9 %collective-permute-start = (bf16[3,64,512]{2,1,0:T(8,128)(2,1)S(1)}, bf16[3,64,512]{2,1,0:T(8,128)(2,1)S(1)}, u32[]{:S(2)}, u32[]{:S(2)}) collective-permute-start(bf16[3,64,512]{2,1,0:T(8,128)(2,1)S(1)} %get-tuple-element.6), channel_id=1, source_target_pairs={{0,8},{4,12},{8,16},{12,20},{16,24},{20,28},{24,32},{28,36},{32,40... | collective-permute-start | bytes 589832 | tf_op jit(solution)/shard_map/ppermute | solution.py:34
  22.8 11.6 %collective-permute-start.3 = (bf16[3,64,512]{2,1,0:T(8,128)(2,1)S(1)}, bf16[3,64,512]{2,1,0:T(8,128)(2,1)S(1)}, u32[]{:S(2)}, u32[]{:S(2)}) collective-permute-start(bf16[3,64,512]{2,1,0:T(8,128)(2,1)S(1)} %get-tuple-element.5), channel_id=1, source_target_pairs={{8,0},{12,4},{16,8},{20,12},{24,16},{28,20},{32,24},{36,28},{40,32... | collective-permute-start | bytes 589832 | tf_op jit(solution)/shard_map/ppermute | solution.py:34
  24.7 12.8 %collective-permute-start.1 = (bf16[4,64,512]{2,1,0:T(8,128)(2,1)S(1)}, bf16[4,64,512]{2,1,0:T(8,128)(2,1)S(1)}, u32[]{:S(2)}, u32[]{:S(2)}) collective-permute-start(bf16[4,64,512]{2,1,0:T(8,128)(2,1)S(1)} %all-to-all-done.1.plane), channel_id=1, source_target_pairs={{0,4},{4,8},{8,12},{12,16},{16,20},{20,24},{24,28},{28,32},{32,36}... | collective-permute-start | bytes 786440 | tf_op jit(solution)/shard_map/ppermute | solution.py:34
  29.4 12.8 %collective-permute-start.2 = (bf16[4,64,512]{2,1,0:T(8,128)(2,1)S(1)}, bf16[4,64,512]{2,1,0:T(8,128)(2,1)S(1)}, u32[]{:S(2)}, u32[]{:S(2)}) collective-permute-start(bf16[4,64,512]{2,1,0:T(8,128)(2,1)S(1)} %all-to-all-done.1.plane), channel_id=1, source_target_pairs={{4,0},{8,4},{12,8},{16,12},{20,16},{24,20},{28,24},{32,28},{36,32}... | collective-permute-start | bytes 786440 | tf_op jit(solution)/shard_map/ppermute | solution.py:34
  34.5 12.5 %collective-permute-start.4 = (bf16[10,64,512]{2,1,0:T(8,128)(2,1)S(1)}, bf16[10,64,512]{2,1,0:T(8,128)(2,1)S(1)}, u32[]{:S(2)}, u32[]{:S(2)}) collective-permute-start(bf16[10,64,512]{2,1,0:T(8,128)(2,1)S(1)} %pad_maximum_fusion), channel_id=1, source_target_pairs={{0,64},{64,0},{1,65},{65,1},{2,66},{66,2},{3,67},{67,3},{4,68},{68... | collective-permute-start | bytes 1966088 | tf_op jit(solution)/shard_map/ppermute | solution.py:38
  42.3 3.8 %collective-permute-start.5 = (bf16[8,64,512]{2,1,0:T(8,128)(2,1)S(1)}, bf16[8,64,512]{2,1,0:T(8,128)(2,1)S(1)}, u32[]{:S(2)}, u32[]{:S(2)}) collective-permute-start(bf16[8,64,512]{2,1,0:T(8,128)(2,1)S(1)} %pad_maximum_fusion.1), channel_id=1, source_target_pairs={{0,64},{64,0},{1,65},{65,1},{2,66},{66,2},{3,67},{67,3},{4,68},{68... | collective-permute-start | bytes 1572872 | tf_op jit(solution)/shard_map/ppermute | solution.py:38
  46.1 0.8 copy-start.3
  46.9 0.8 copy-start.1
  47.8 1.1 copy-start.2
  48.8 1.0 copy-start.4
  51.5 16.1 %collective-permute-start.6 = (bf16[256,1024]{1,0:T(8,128)(2,1)S(1)}, bf16[256,1024]{1,0:T(8,128)(2,1)S(1)}, u32[]{:S(2)}, u32[]{:S(2)}) collective-permute-start(bf16[256,1024]{1,0:T(8,128)(2,1)S(1)} %make_half.1.own), channel_id=1, source_target_pairs={{0,4},{4,8},{8,12},{12,16},{16,20},{20,24},{24,28},{28,32},{32,36}... | collective-permute-start | bytes 1572872 | tf_op jit(solution)/shard_map/ppermute | solution.py:34
  56.1 16.8 %collective-permute-start.7 = (bf16[256,1024]{1,0:T(8,128)(2,1)S(1)}, bf16[256,1024]{1,0:T(8,128)(2,1)S(1)}, u32[]{:S(2)}, u32[]{:S(2)}) collective-permute-start(bf16[256,1024]{1,0:T(8,128)(2,1)S(1)} %make_half.1.own), channel_id=1, source_target_pairs={{4,0},{8,4},{12,8},{16,12},{20,16},{24,20},{28,24},{32,28},{36,32}... | collective-permute-start | bytes 1572872 | tf_op jit(solution)/shard_map/ppermute | solution.py:34
  58.0 16.8 %collective-permute-start.9 = (bf16[256,1024]{1,0:T(8,128)(2,1)S(1)}, bf16[256,1024]{1,0:T(8,128)(2,1)S(1)}, u32[]{:S(2)}, u32[]{:S(2)}) collective-permute-start(bf16[256,1024]{1,0:T(8,128)(2,1)S(1)} %make_half.1.own), channel_id=1, source_target_pairs={{0,64},{64,0},{1,65},{65,1},{2,66},{66,2},{3,67},{67,3},{4,68},{68... | collective-permute-start | bytes 1572872 | tf_op jit(solution)/shard_map/ppermute | solution.py:38
  67.6 7.3 %collective-permute-start.8 = (bf16[256,1024]{1,0:T(8,128)(2,1)S(1)}, bf16[256,1024]{1,0:T(8,128)(2,1)S(1)}, u32[]{:S(2)}, u32[]{:S(2)}) collective-permute-start(bf16[256,1024]{1,0:T(8,128)(2,1)S(1)} %collective-permute-done.6.up), channel_id=1, source_target_pairs={{0,64},{64,0},{1,65},{65,1},{2,66},{66,2},{3,67},{67,3},{4,68},{68... | collective-permute-start | bytes 1572872 | tf_op jit(solution)/shard_map/ppermute | solution.py:38
  72.9 3.8 %collective-permute-start.10 = (bf16[256,1024]{1,0:T(8,128)(2,1)S(1)}, bf16[256,1024]{1,0:T(8,128)(2,1)S(1)}, u32[]{:S(2)}, u32[]{:S(2)}) collective-permute-start(bf16[256,1024]{1,0:T(8,128)(2,1)S(1)} %collective-permute-done.7.down), channel_id=1, source_target_pairs={{0,64},{64,0},{1,65},{65,1},{2,66},{66,2},{3,67},{67,3},{4,68},{68... | collective-permute-start | bytes 1572872 | tf_op jit(solution)/shard_map/ppermute | solution.py:38
  78.8 29.7 %copy-start.8 = (s32[1,15]{1,0:T(1,128)S(1)}, s32[1,15]{1,0:T(1,128)}, u32[]{:S(2)}) copy-start(s32[1,15]{1,0:T(1,128)} %mask.1) | copy-start | bytes 184
  102.6 5.9 %collective-permute-start.11 = (f32[3,16,128]{2,1,0:T(8,128)S(1)}, f32[3,16,128]{2,1,0:T(8,128)S(1)}, u32[]{:S(2)}, u32[]{:S(2)}) collective-permute-start(f32[3,16,128]{2,1,0:T(8,128)S(1)} %slice.18), channel_id=1, source_target_pairs={{0,4},{4,8},{8,12},{12,16},{16,20},{20,24},{24,28},{28,32},{32,36}... | collective-permute-start | bytes 73736 | tf_op jit(solution)/shard_map/ppermute | solution.py:34
  106.1 6.9 %collective-permute-start.12 = (f32[3,16,128]{2,1,0:T(8,128)S(1)}, f32[3,16,128]{2,1,0:T(8,128)S(1)}, u32[]{:S(2)}, u32[]{:S(2)}) collective-permute-start(f32[3,16,128]{2,1,0:T(8,128)S(1)} %slice.18), channel_id=1, source_target_pairs={{4,0},{8,4},{12,8},{16,12},{20,16},{24,20},{28,24},{32,28},{36,32}... | collective-permute-start | bytes 73736 | tf_op jit(solution)/shard_map/ppermute | solution.py:34

commit v10 on v9

--- a/solution.py
+++ b/solution.py
@@ -61,23 +61,26 @@
                     out[x, core, s, k * 16 : k * 16 + 16, :] = tile[at : at + 16]
 
 
-def half_kernel(core, tiles, below2, below, plane, above, above2, first, second, half, window, sems):
+def window_kernel(core, below2, below, plane, above, above2, first, second, window):
     c = core[0]
-    moves = ((first, 4, 3, 0), (second, 0, 4, 3), (first, 0, 4, 7), (second, 4, 4, 11), (first, 7, 3, 15))
+    others = ((first, 4), (second, 0), (first, 0), (second, 4), (first, 7))
+    at = 0
+    for part, (other, start) in zip((below2, below, plane, above, above2), others):
+        for b in range(part.shape[0]):
+            window[at, c] = part[b]
+            window[at, 1 - c] = other[start + b]
+            at += 1
+
+
+def half_kernel(gathered, window, half, tiles, sems):
     copies = [
-        pltpu.make_async_copy(part.at[pl.ds(at, n)], window.at[pl.ds(to, n), 1 - c], sems.at[i])
-        for i, (part, at, n, to) in enumerate(moves)
+        pltpu.make_async_copy(gathered.at[pl.ds(2 * a, 2)], tiles.at[pl.ds(2 * a, 2)], sems.at[a])
+        for a in range(4)
     ]
     for copy in copies:
         copy.start()
-    at = 0
-    for part in (below2, below, plane, above, above2):
-        for b in range(part.shape[0]):
-            window[at, c] = part[b]
-            at += 1
-    for copy in copies:
-        copy.wait()
     for a in range(4):
+        copies[a].wait()
         near = window[a : a + SPAN].reshape(SPAN * ROWS, COLS)
         wide = jnp.concatenate(
             [tiles[2 * a : 2 * a + 2, s].reshape(2 * HALF, ROWS) for s in range(SPAN)], 1
@@ -145,10 +148,13 @@
     first = swapped(jnp.concatenate([plane, below2, above2]))
     second = swapped(jnp.concatenate([below, above]))
 
+    window = call(
+        window_kernel, "place_orbitals", [SMEM] + [VMEM] * 7, (18, 2, HALF, COLS), BF16,
+        core, below2, below, plane, above, above2, first, second,
+    )
     own = call(
-        half_kernel, "make_half", [SMEM] + [VMEM] * 6 + [ANY] * 2, (4 * HALF, 2 * COLS), BF16,
-        core, tiles, below2, below, plane, above, above2, first, second,
-        scratch=[pltpu.VMEM((18, 2, HALF, COLS), BF16), pltpu.SemaphoreType.DMA((5,))],
+        half_kernel, "make_half", [ANY, VMEM], (4 * HALF, 2 * COLS), BF16, tiles, window,
+        scratch=[pltpu.VMEM((8, SPAN, HALF, ROWS), BF16), pltpu.SemaphoreType.DMA((4,))],
     )
 
     up = moved(own, 1)

time: 115 us -> 112 us (0.974)
  local copies, waits for them, and re-layouts: 7.83 us -> 2.77 us
  waiting for transfers between devices: 31 us -> 28.1 us
  Pallas kernels: 5.41 us -> 8.1 us
  starting transfers between devices: 44.7 us -> 47.1 us
    unnamed x18 -> x8, local copies, waits for them, and re-layouts: 7.79 us -> 2.73 us
    pallas_call x5 -> x6, Pallas kernels: 5.41 us -> 8.1 us  [call(): pl.pallas_call(kernel, in_specs=specs, out_specs=out, out_shape=jax.Shape...]
    ppermute x8, waiting for transfers between devices: 24.4 us -> 21.8 us  [moved(): lax.ppermute(x, 'z', [(i, i + by) for i in range(n) if 0 <= i + by < n])]
  transfers between devices with their start and end apart: 15 -> 15, of which waited for: 9 -> 8; matrix products, arithmetic and copies ran while one was open for 0% -> 0% of each run, Pallas kernels for 1% -> 2%
where the time goes in v10:
time: 112 us; the launch traced here: 111 us
  starting transfers between devices  47.1 us (42%)
  waiting for transfers between devices  28.1 us (25%)
  blocking collectives  23.9 us (21%)
  Pallas kernels  8.1 us (7%)
  local copies, waits for them, and re-layouts  2.77 us (2%)
    ppermute x8, starting transfers between devices, moved(): lax.ppermute(x, 'z', [(i, i + by) for i in range(n) if 0 <= i + by < n])  28.4 us
    all_to_all x1, blocking collectives, per_device(): lax.all_to_all(partial.reshape(16, 16, SPAN * ROWS), ('x', 'y'), 0, 0)  23.9 us
    ppermute x8, waiting for transfers between devices, moved(): lax.ppermute(x, 'z', [(i, i + by) for i in range(n) if 0 <= i + by < n])  21.8 us
    ppermute x5, starting transfers between devices, swapped(): return lax.ppermute(x, 'core', [(0, 1), (1, 0)])  10.1 us
    pallas_call x6, Pallas kernels, call(): pl.pallas_call(kernel, in_specs=specs, out_specs=out, out_shape=jax.Shape...  8.1 us
    all_to_all x1, starting transfers between devices, per_device(): lax.all_to_all(tiles.reshape(8, SPAN, HALF, ROWS), ('x', 'core'), 0, 0)  4.32 us
    all_to_all x1, starting transfers between devices, per_device(): plane = lax.all_to_all(pieces, 'x', 0, 0)  4.3 us
    ppermute x5, waiting for transfers between devices, swapped(): return lax.ppermute(x, 'core', [(0, 1), (1, 0)])  3.38 us
  transfers between devices with their start and end apart: 15, of which 8 were waited for; matrix products, arithmetic and copies ran while one was open for 0% of the time, Pallas kernels for 2%

profile of v10, /device:TPU:96, one launch (start us, length us, event | category | flops | bytes accessed | tf_op | source)
XLA Modules:
  0.0 111.1 jit_solution(8129669774515801163)
XLA Ops:
  0.0 1.0 copy-done
  1.0 0.7 cut_orbitals.1
  1.8 4.3 %all-to-all-start.1 = ((bf16[4,64,512]{2,1,0:T(8,128)(2,1)}), bf16[4,64,512]{2,1,0:T(8,128)(2,1)S(1)}, u32[]{:S(2)}, u32[]{:S(2)}) async-start(bf16[4,64,512]{2,1,0:T(8,128)(2,1)} %cut_orbitals.1), calls=%async_computation.1 | async-start | bytes 524288 | tf_op jit(solution)/shard_map/all_to_all | solution.py:136
  6.1 1.0 copy-done.1
  7.1 0.7 copy-done.2
  7.8 2.1 %cut_integrals.1 = bf16[4,2,15,64,128]{4,3,2,1,0:T(8,128)(2,1)} custom-call(s32[1,15]{1,0:T(1,128)S(1)} %copy-done.2, bf16[15,128,128]{2,1,0:T(8,128)(2,1)S(1)} %bitcast.9), custom_call_target="tpu_custom_call" | custom-call | tf_op jit(solution)/shard_map/cut_integrals/pallas_call | solution.py:21
  9.9 2.9 %all-to-all-done.1.plane = bf16[4,64,512]{2,1,0:T(8,128)(2,1)S(1)} async-done(((bf16[4,64,512]{2,1,0:T(8,128)(2,1)}), bf16[4,64,512]{2,1,0:T(8,128)(2,1)S(1)}, u32[]{:S(2)}, u32[]{:S(2)}) %all-to-all-start.1) | async-done | bytes 262176 | tf_op jit(solution)/shard_map/all_to_all | solution.py:136
  12.8 4.3 %all-to-all-start = ((bf16[8,15,64,128]{3,2,1,0:T(8,128)(2,1)}), bf16[8,15,64,128]{3,2,1,0:T(8,128)(2,1)}, u32[]{:S(2)}, u32[]{:S(2)}) async-start(bf16[8,15,64,128]{3,2,1,0:T(8,128)(2,1)} %bitcast.2), calls=%async_computation | async-start | bytes 3932160 | tf_op jit(solution)/shard_map/all_to_all | solution.py:142
  17.1 6.4 %collective-permute-start = (bf16[3,64,512]{2,1,0:T(8,128)(2,1)S(1)}, bf16[3,64,512]{2,1,0:T(8,128)(2,1)S(1)}, u32[]{:S(2)}, u32[]{:S(2)}) collective-permute-start(bf16[3,64,512]{2,1,0:T(8,128)(2,1)S(1)} %get-tuple-element.6), channel_id=1, source_target_pairs={{0,8},{4,12},{8,16},{12,20},{16,24},{20,28},{24,32},{28,36},{32,40... | collective-permute-start | bytes 589832 | tf_op jit(solution)/shard_map/ppermute | solution.py:34
  23.5 1.9 %collective-permute-start.3 = (bf16[3,64,512]{2,1,0:T(8,128)(2,1)S(1)}, bf16[3,64,512]{2,1,0:T(8,128)(2,1)S(1)}, u32[]{:S(2)}, u32[]{:S(2)}) collective-permute-start(bf16[3,64,512]{2,1,0:T(8,128)(2,1)S(1)} %get-tuple-element.5), channel_id=1, source_target_pairs={{8,0},{12,4},{16,8},{20,12},{24,16},{28,20},{32,24},{36,28},{40,32... | collective-permute-start | bytes 589832 | tf_op jit(solution)/shard_map/ppermute | solution.py:34
  25.5 4.7 %collective-permute-start.1 = (bf16[4,64,512]{2,1,0:T(8,128)(2,1)S(1)}, bf16[4,64,512]{2,1,0:T(8,128)(2,1)S(1)}, u32[]{:S(2)}, u32[]{:S(2)}) collective-permute-start(bf16[4,64,512]{2,1,0:T(8,128)(2,1)S(1)} %all-to-all-done.1.plane), channel_id=1, source_target_pairs={{0,4},{4,8},{8,12},{12,16},{16,20},{20,24},{24,28},{28,32},{32,36}... | collective-permute-start | bytes 786440 | tf_op jit(solution)/shard_map/ppermute | solution.py:34
  30.2 1.9 %collective-permute-start.2 = (bf16[4,64,512]{2,1,0:T(8,128)(2,1)S(1)}, bf16[4,64,512]{2,1,0:T(8,128)(2,1)S(1)}, u32[]{:S(2)}, u32[]{:S(2)}) collective-permute-start(bf16[4,64,512]{2,1,0:T(8,128)(2,1)S(1)} %all-to-all-done.1.plane), channel_id=1, source_target_pairs={{4,0},{8,4},{12,8},{16,12},{20,16},{24,20},{28,24},{32,28},{36,32}... | collective-permute-start | bytes 786440 | tf_op jit(solution)/shard_map/ppermute | solution.py:34
  32.1 2.9 %collective-permute-done.3.above2 = bf16[3,64,512]{2,1,0:T(8,128)(2,1)S(1)} collective-permute-done((bf16[3,64,512]{2,1,0:T(8,128)(2,1)S(1)}, bf16[3,64,512]{2,1,0:T(8,128)(2,1)S(1)}, u32[]{:S(2)}, u32[]{:S(2)}) %collective-permute-start.3) | collective-permute-done | bytes 196640 | tf_op jit(solution)/shard_map/ppermute | solution.py:34
  35.1 1.9 %collective-permute-start.4 = (bf16[10,64,512]{2,1,0:T(8,128)(2,1)S(1)}, bf16[10,64,512]{2,1,0:T(8,128)(2,1)S(1)}, u32[]{:S(2)}, u32[]{:S(2)}) collective-permute-start(bf16[10,64,512]{2,1,0:T(8,128)(2,1)S(1)} %pad_maximum_fusion), channel_id=1, source_target_pairs={{0,64},{64,0},{1,65},{65,1},{2,66},{66,2},{3,67},{67,3},{4,68},{68... | collective-permute-start | bytes 1966088 | tf_op jit(solution)/shard_map/ppermute | solution.py:38
  37.0 1.1 collective-permute-done.1.below
  38.1 4.8 %collective-permute-done.2.above = bf16[4,64,512]{2,1,0:T(8,128)(2,1)S(1)} collective-permute-done((bf16[4,64,512]{2,1,0:T(8,128)(2,1)S(1)}, bf16[4,64,512]{2,1,0:T(8,128)(2,1)S(1)}, u32[]{:S(2)}, u32[]{:S(2)}) %collective-permute-start.2) | collective-permute-done | bytes 262176 | tf_op jit(solution)/shard_map/ppermute | solution.py:34
  43.0 1.9 %collective-permute-start.5 = (bf16[8,64,512]{2,1,0:T(8,128)(2,1)S(1)}, bf16[8,64,512]{2,1,0:T(8,128)(2,1)S(1)}, u32[]{:S(2)}, u32[]{:S(2)}) collective-permute-start(bf16[8,64,512]{2,1,0:T(8,128)(2,1)S(1)} %pad_maximum_fusion.1), channel_id=1, source_target_pairs={{0,64},{64,0},{1,65},{65,1},{2,66},{66,2},{3,67},{67,3},{4,68},{68... | collective-permute-start | bytes 1572872 | tf_op jit(solution)/shard_map/ppermute | solution.py:38
  44.9 1.9 %collective-permute-done.5.second = bf16[8,64,512]{2,1,0:T(8,128)(2,1)S(1)} collective-permute-done((bf16[8,64,512]{2,1,0:T(8,128)(2,1)S(1)}, bf16[8,64,512]{2,1,0:T(8,128)(2,1)S(1)}, u32[]{:S(2)}, u32[]{:S(2)}) %collective-permute-start.5) | collective-permute-done | bytes 524320 | tf_op jit(solution)/shard_map/ppermute | solution.py:38
  46.9 2.9 %make_half.1.own = bf16[256,1024]{1,0:T(8,128)(2,1)S(1)} custom-call(bf16[8,15,64,128]{3,2,1,0:T(8,128)(2,1)} %all-to-all-done.gathered, bf16[18,2,64,512]{3,2,1,0:T(8,128)(2,1)S(1)} %place_orbitals.1.window), custom_call_target="tpu_custom_call" | custom-call | tf_op jit(solution)/shard_map/make_half/pallas_call | solution.py:21
  49.8 1.9 %collective-permute-start.7 = (bf16[256,1024]{1,0:T(8,128)(2,1)S(1)}, bf16[256,1024]{1,0:T(8,128)(2,1)S(1)}, u32[]{:S(2)}, u32[]{:S(2)}) collective-permute-start(bf16[256,1024]{1,0:T(8,128)(2,1)S(1)} %make_half.1.own), channel_id=1, source_target_pairs={{4,0},{8,4},{12,8},{16,12},{20,16},{24,20},{28,24},{32,28},{36,32}... | collective-permute-start | bytes 1572872 | tf_op jit(solution)/shard_map/ppermute | solution.py:34
  51.7 5.1 %collective-permute-start.6 = (bf16[256,1024]{1,0:T(8,128)(2,1)S(1)}, bf16[256,1024]{1,0:T(8,128)(2,1)S(1)}, u32[]{:S(2)}, u32[]{:S(2)}) collective-permute-start(bf16[256,1024]{1,0:T(8,128)(2,1)S(1)} %make_half.1.own), channel_id=1, source_target_pairs={{0,4},{4,8},{8,12},{12,16},{16,20},{20,24},{24,28},{28,32},{32,36}... | collective-permute-start | bytes 1572872 | tf_op jit(solution)/shard_map/ppermute | solution.py:34
  56.9 1.9 %collective-permute-start.9 = (bf16[256,1024]{1,0:T(8,128)(2,1)S(1)}, bf16[256,1024]{1,0:T(8,128)(2,1)S(1)}, u32[]{:S(2)}, u32[]{:S(2)}) collective-permute-start(bf16[256,1024]{1,0:T(8,128)(2,1)S(1)} %make_half.1.own), channel_id=1, source_target_pairs={{0,64},{64,0},{1,65},{65,1},{2,66},{66,2},{3,67},{67,3},{4,68},{68... | collective-permute-start | bytes 1572872 | tf_op jit(solution)/shard_map/ppermute | solution.py:38
  58.8 8.1 %collective-permute-done.7.down = bf16[256,1024]{1,0:T(8,128)(2,1)S(1)} collective-permute-done((bf16[256,1024]{1,0:T(8,128)(2,1)S(1)}, bf16[256,1024]{1,0:T(8,128)(2,1)S(1)}, u32[]{:S(2)}, u32[]{:S(2)}) %collective-permute-start.7) | collective-permute-done | bytes 524320 | tf_op jit(solution)/shard_map/ppermute | solution.py:34
  66.9 1.9 %collective-permute-start.10 = (bf16[256,1024]{1,0:T(8,128)(2,1)S(1)}, bf16[256,1024]{1,0:T(8,128)(2,1)S(1)}, u32[]{:S(2)}, u32[]{:S(2)}) collective-permute-start(bf16[256,1024]{1,0:T(8,128)(2,1)S(1)} %collective-permute-done.7.down), channel_id=1, source_target_pairs={{0,64},{64,0},{1,65},{65,1},{2,66},{66,2},{3,67},{67,3},{4,68},{68... | collective-permute-start | bytes 1572872 | tf_op jit(solution)/shard_map/ppermute | solution.py:38
  68.8 2.4 %collective-permute-start.8 = (bf16[256,1024]{1,0:T(8,128)(2,1)S(1)}, bf16[256,1024]{1,0:T(8,128)(2,1)S(1)}, u32[]{:S(2)}, u32[]{:S(2)}) collective-permute-start(bf16[256,1024]{1,0:T(8,128)(2,1)S(1)} %collective-permute-done.6.up), channel_id=1, source_target_pairs={{0,64},{64,0},{1,65},{65,1},{2,66},{66,2},{3,67},{67,3},{4,68},{68... | collective-permute-start | bytes 1572872 | tf_op jit(solution)/shard_map/ppermute | solution.py:38
  71.2 1.5 %collective-permute-done.8.up2 = bf16[256,1024]{1,0:T(8,128)(2,1)S(1)} collective-permute-done((bf16[256,1024]{1,0:T(8,128)(2,1)S(1)}, bf16[256,1024]{1,0:T(8,128)(2,1)S(1)}, u32[]{:S(2)}, u32[]{:S(2)}) %collective-permute-start.8) | collective-permute-done | bytes 524320 | tf_op jit(solution)/shard_map/ppermute | solution.py:38
  72.7 2.1 %make_tiles.1 = bf16[256,1920]{1,0:T(8,128)(2,1)S(1)} custom-call(s32[1]{0:T(128)} %bitcast.core, bf16[256,1024]{1,0:T(8,128)(2,1)S(1)} %collective-permute-done.6.up, bf16[256,1024]{1,0:T(8,128)(2,1)S(1)} %make_half.1.own, bf16[256,1024]{1,0:T(8,128)(2,1)S(1)} %collective-permute-done.7.down, bf16[256,1024]{1,0:T(8,128)(2,1)S(1)} %collective-permute-done.8.up2, ...), custom_call_target="tpu_custom_call" | custom-call | tf_op jit(solution)/shard_map/make_tiles/pallas_call | solution.py:21
  74.9 23.9 %all_to_all.15.parts = bf16[16,16,1920]{2,1,0:T(8,128)(2,1)S(1)} all-to-all(bf16[16,16,1920]{2,1,0:T(8,128)(2,1)S(1)} %bitcast.8), channel_id=1, replica_groups=mesh['y'=4,'core'=2,'z'=16,'x'=4] {'x','y'}, dimensions={0} | all-to-all | bytes 1966080 | tf_op jit(solution)/shard_map/all_to_all | solution.py:168
  99.0 4.5 %collective-permute-start.11 = (f32[3,16,128]{2,1,0:T(8,128)S(1)}, f32[3,16,128]{2,1,0:T(8,128)S(1)}, u32[]{:S(2)}, u32[]{:S(2)}) collective-permute-start(f32[3,16,128]{2,1,0:T(8,128)S(1)} %slice.18), channel_id=1, source_target_pairs={{0,4},{4,8},{8,12},{12,16},{16,20},{20,24},{24,28},{28,32},{32,36}... | collective-permute-start | bytes 73736 | tf_op jit(solution)/shard_map/ppermute | solution.py:34
  103.5 1.9 %collective-permute-start.12 = (f32[3,16,128]{2,1,0:T(8,128)S(1)}, f32[3,16,128]{2,1,0:T(8,128)S(1)}, u32[]{:S(2)}, u32[]{:S(2)}) collective-permute-start(f32[3,16,128]{2,1,0:T(8,128)S(1)} %slice.18), channel_id=1, source_target_pairs={{4,0},{8,4},{12,8},{16,12},{20,16},{24,20},{28,24},{32,28},{36,32}... | collective-permute-start | bytes 73736 | tf_op jit(solution)/shard_map/ppermute | solution.py:34
  105.5 5.0 %collective-permute-done.12 = f32[3,16,128]{2,1,0:T(8,128)S(1)} collective-permute-done((f32[3,16,128]{2,1,0:T(8,128)S(1)}, f32[3,16,128]{2,1,0:T(8,128)S(1)}, u32[]{:S(2)}, u32[]{:S(2)}) %collective-permute-start.12) | collective-permute-done | bytes 24608 | tf_op jit(solution)/shard_map/ppermute | solution.py:34
  110.4 0.7 fusion.3
  (20 shorter events, 0.5 us)
Async XLA Ops:
  0.0 1.0 copy-start
  1.8 11.0 %all-to-all-start.1 = ((bf16[4,64,512]{2,1,0:T(8,128)(2,1)}), bf16[4,64,512]{2,1,0:T(8,128)(2,1)S(1)}, u32[]{:S(2)}, u32[]{:S(2)}) async-start(bf16[4,64,512]{2,1,0:T(8,128)(2,1)} %cut_orbitals.1), calls=%async_computation.1 | async-start | bytes 524288 | tf_op jit(solution)/shard_map/all_to_all | solution.py:136
  6.1 1.0 copy-start.1
  7.1 0.7 copy-start.2
  12.8 34.2 %all-to-all-start = ((bf16[8,15,64,128]{3,2,1,0:T(8,128)(2,1)}), bf16[8,15,64,128]{3,2,1,0:T(8,128)(2,1)}, u32[]{:S(2)}, u32[]{:S(2)}) async-start(bf16[8,15,64,128]{3,2,1,0:T(8,128)(2,1)} %bitcast.2), calls=%async_computation | async-start | bytes 3932160 | tf_op jit(solution)/shard_map/all_to_all | solution.py:142
  17.1 15.0 %collective-permute-start = (bf16[3,64,512]{2,1,0:T(8,128)(2,1)S(1)}, bf16[3,64,512]{2,1,0:T(8,128)(2,1)S(1)}, u32[]{:S(2)}, u32[]{:S(2)}) collective-permute-start(bf16[3,64,512]{2,1,0:T(8,128)(2,1)S(1)} %get-tuple-element.6), channel_id=1, source_target_pairs={{0,8},{4,12},{8,16},{12,20},{16,24},{20,28},{24,32},{28,36},{32,40... | collective-permute-start | bytes 589832 | tf_op jit(solution)/shard_map/ppermute | solution.py:34
  23.5 11.5 %collective-permute-start.3 = (bf16[3,64,512]{2,1,0:T(8,128)(2,1)S(1)}, bf16[3,64,512]{2,1,0:T(8,128)(2,1)S(1)}, u32[]{:S(2)}, u32[]{:S(2)}) collective-permute-start(bf16[3,64,512]{2,1,0:T(8,128)(2,1)S(1)} %get-tuple-element.5), channel_id=1, source_target_pairs={{8,0},{12,4},{16,8},{20,12},{24,16},{28,20},{32,24},{36,28},{40,32... | collective-permute-start | bytes 589832 | tf_op jit(solution)/shard_map/ppermute | solution.py:34
  25.5 12.7 %collective-permute-start.1 = (bf16[4,64,512]{2,1,0:T(8,128)(2,1)S(1)}, bf16[4,64,512]{2,1,0:T(8,128)(2,1)S(1)}, u32[]{:S(2)}, u32[]{:S(2)}) collective-permute-start(bf16[4,64,512]{2,1,0:T(8,128)(2,1)S(1)} %all-to-all-done.1.plane), channel_id=1, source_target_pairs={{0,4},{4,8},{8,12},{12,16},{16,20},{20,24},{24,28},{28,32},{32,36}... | collective-permute-start | bytes 786440 | tf_op jit(solution)/shard_map/ppermute | solution.py:34
  30.2 12.8 %collective-permute-start.2 = (bf16[4,64,512]{2,1,0:T(8,128)(2,1)S(1)}, bf16[4,64,512]{2,1,0:T(8,128)(2,1)S(1)}, u32[]{:S(2)}, u32[]{:S(2)}) collective-permute-start(bf16[4,64,512]{2,1,0:T(8,128)(2,1)S(1)} %all-to-all-done.1.plane), channel_id=1, source_target_pairs={{4,0},{8,4},{12,8},{16,12},{20,16},{24,20},{28,24},{32,28},{36,32}... | collective-permute-start | bytes 786440 | tf_op jit(solution)/shard_map/ppermute | solution.py:34
  35.1 11.7 %collective-permute-start.4 = (bf16[10,64,512]{2,1,0:T(8,128)(2,1)S(1)}, bf16[10,64,512]{2,1,0:T(8,128)(2,1)S(1)}, u32[]{:S(2)}, u32[]{:S(2)}) collective-permute-start(bf16[10,64,512]{2,1,0:T(8,128)(2,1)S(1)} %pad_maximum_fusion), channel_id=1, source_target_pairs={{0,64},{64,0},{1,65},{65,1},{2,66},{66,2},{3,67},{67,3},{4,68},{68... | collective-permute-start | bytes 1966088 | tf_op jit(solution)/shard_map/ppermute | solution.py:38
  43.0 3.8 %collective-permute-start.5 = (bf16[8,64,512]{2,1,0:T(8,128)(2,1)S(1)}, bf16[8,64,512]{2,1,0:T(8,128)(2,1)S(1)}, u32[]{:S(2)}, u32[]{:S(2)}) collective-permute-start(bf16[8,64,512]{2,1,0:T(8,128)(2,1)S(1)} %pad_maximum_fusion.1), channel_id=1, source_target_pairs={{0,64},{64,0},{1,65},{65,1},{2,66},{66,2},{3,67},{67,3},{4,68},{68... | collective-permute-start | bytes 1572872 | tf_op jit(solution)/shard_map/ppermute | solution.py:38
  49.8 17.1 %collective-permute-start.7 = (bf16[256,1024]{1,0:T(8,128)(2,1)S(1)}, bf16[256,1024]{1,0:T(8,128)(2,1)S(1)}, u32[]{:S(2)}, u32[]{:S(2)}) collective-permute-start(bf16[256,1024]{1,0:T(8,128)(2,1)S(1)} %make_half.1.own), channel_id=1, source_target_pairs={{4,0},{8,4},{12,8},{16,12},{20,16},{24,20},{28,24},{32,28},{36,32}... | collective-permute-start | bytes 1572872 | tf_op jit(solution)/shard_map/ppermute | solution.py:34
  51.7 17.1 %collective-permute-start.6 = (bf16[256,1024]{1,0:T(8,128)(2,1)S(1)}, bf16[256,1024]{1,0:T(8,128)(2,1)S(1)}, u32[]{:S(2)}, u32[]{:S(2)}) collective-permute-start(bf16[256,1024]{1,0:T(8,128)(2,1)S(1)} %make_half.1.own), channel_id=1, source_target_pairs={{0,4},{4,8},{8,12},{12,16},{16,20},{20,24},{24,28},{28,32},{32,36}... | collective-permute-start | bytes 1572872 | tf_op jit(solution)/shard_map/ppermute | solution.py:34
  56.9 14.3 %collective-permute-start.9 = (bf16[256,1024]{1,0:T(8,128)(2,1)S(1)}, bf16[256,1024]{1,0:T(8,128)(2,1)S(1)}, u32[]{:S(2)}, u32[]{:S(2)}) collective-permute-start(bf16[256,1024]{1,0:T(8,128)(2,1)S(1)} %make_half.1.own), channel_id=1, source_target_pairs={{0,64},{64,0},{1,65},{65,1},{2,66},{66,2},{3,67},{67,3},{4,68},{68... | collective-permute-start | bytes 1572872 | tf_op jit(solution)/shard_map/ppermute | solution.py:38
  66.9 4.4 %collective-permute-start.10 = (bf16[256,1024]{1,0:T(8,128)(2,1)S(1)}, bf16[256,1024]{1,0:T(8,128)(2,1)S(1)}, u32[]{:S(2)}, u32[]{:S(2)}) collective-permute-start(bf16[256,1024]{1,0:T(8,128)(2,1)S(1)} %collective-permute-done.7.down), channel_id=1, source_target_pairs={{0,64},{64,0},{1,65},{65,1},{2,66},{66,2},{3,67},{67,3},{4,68},{68... | collective-permute-start | bytes 1572872 | tf_op jit(solution)/shard_map/ppermute | solution.py:38
  68.8 3.9 %collective-permute-start.8 = (bf16[256,1024]{1,0:T(8,128)(2,1)S(1)}, bf16[256,1024]{1,0:T(8,128)(2,1)S(1)}, u32[]{:S(2)}, u32[]{:S(2)}) collective-permute-start(bf16[256,1024]{1,0:T(8,128)(2,1)S(1)} %collective-permute-done.6.up), channel_id=1, source_target_pairs={{0,64},{64,0},{1,65},{65,1},{2,66},{66,2},{3,67},{67,3},{4,68},{68... | collective-permute-start | bytes 1572872 | tf_op jit(solution)/shard_map/ppermute | solution.py:38
  74.9 30.5 %copy-start.3 = (s32[1,15]{1,0:T(1,128)S(1)}, s32[1,15]{1,0:T(1,128)}, u32[]{:S(2)}) copy-start(s32[1,15]{1,0:T(1,128)} %mask.1) | copy-start | bytes 184
  99.0 6.5 %collective-permute-start.11 = (f32[3,16,128]{2,1,0:T(8,128)S(1)}, f32[3,16,128]{2,1,0:T(8,128)S(1)}, u32[]{:S(2)}, u32[]{:S(2)}) collective-permute-start(f32[3,16,128]{2,1,0:T(8,128)S(1)} %slice.18), channel_id=1, source_target_pairs={{0,4},{4,8},{8,12},{12,16},{16,20},{20,24},{24,28},{28,32},{32,36}... | collective-permute-start | bytes 73736 | tf_op jit(solution)/shard_map/ppermute | solution.py:34
  103.5 6.9 %collective-permute-start.12 = (f32[3,16,128]{2,1,0:T(8,128)S(1)}, f32[3,16,128]{2,1,0:T(8,128)S(1)}, u32[]{:S(2)}, u32[]{:S(2)}) collective-permute-start(f32[3,16,128]{2,1,0:T(8,128)S(1)} %slice.18), channel_id=1, source_target_pairs={{4,0},{8,4},{12,8},{16,12},{20,16},{24,20},{28,24},{32,28},{36,32}... | collective-permute-start | bytes 73736 | tf_op jit(solution)/shard_map/ppermute | solution.py:34

commit v11 on v9

--- a/solution.py
+++ b/solution.py
@@ -34,57 +34,55 @@
     return lax.ppermute(x, "z", [(i, i + by) for i in range(n) if 0 <= i + by < n])
 
 
+def turned(x, by):
+    return lax.ppermute(x, "x", [(i, (i + by) % 4) for i in range(4)])
+
+
 def swapped(x):
     return lax.ppermute(x, "core", [(0, 1), (1, 0)])
 
 
-def orbital_kernel(core, occupied, out, sems):
-    rows = pl.ds(pl.multiple_of(core[0] * HALF, HALF), HALF)
-    copies = [
-        pltpu.make_async_copy(occupied.at[rows, pl.ds(x * COLS, COLS)], out.at[x], sems.at[x])
-        for x in range(4)
-    ]
-    for copy in copies:
-        copy.start()
-    for copy in copies:
-        copy.wait()
+def sided(x, by):
+    n = lax.axis_size("z")
+    pairs = [(i, i + by) for i in range(n - by)]
+    pairs += [(n + i + by, n + i) for i in range(n - by)]
+    return lax.ppermute(x, ("core", "z"), pairs)
 
 
-def integral_kernel(mask, integrals, out):
-    for s in range(SPAN):
-        tile = integrals[s]
-        tile = jnp.where(mask[0, s] != 0, tile, jnp.zeros_like(tile))
-        for core in range(2):
-            for k in range(4):
-                at = k * 32 + core * 16
-                for x in range(4):
-                    out[x, core, s, k * 16 : k * 16 + 16, :] = tile[at : at + 16]
+def orbital_kernel(occupied, out):
+    for x in range(4):
+        out[x] = occupied[:, x * COLS : (x + 1) * COLS]
 
 
-def half_kernel(core, tiles, below2, below, plane, above, above2, first, second, half, window, sems):
+def integral_kernel(core, mask, integrals, keep, give):
     c = core[0]
-    moves = ((first, 4, 3, 0), (second, 0, 4, 3), (first, 0, 4, 7), (second, 4, 4, 11), (first, 7, 3, 15))
-    copies = [
-        pltpu.make_async_copy(part.at[pl.ds(at, n)], window.at[pl.ds(to, n), 1 - c], sems.at[i])
-        for i, (part, at, n, to) in enumerate(moves)
-    ]
-    for copy in copies:
-        copy.start()
-    at = 0
-    for part in (below2, below, plane, above, above2):
-        for b in range(part.shape[0]):
-            window[at, c] = part[b]
-            at += 1
-    for copy in copies:
-        copy.wait()
-    for a in range(4):
-        near = window[a : a + SPAN].reshape(SPAN * ROWS, COLS)
-        wide = jnp.concatenate(
-            [tiles[2 * a : 2 * a + 2, s].reshape(2 * HALF, ROWS) for s in range(SPAN)], 1
-        )
-        made = jnp.dot(wide, near, preferred_element_type=F32).astype(BF16)
-        half[a * HALF : (a + 1) * HALF, :COLS] = made[:HALF]
-        half[a * HALF : (a + 1) * HALF, COLS:] = made[HALF:]
+    for s in range(SPAN):
+        kept = mask[0, s] != 0
+        for k in range(4):
+            for out, shift in ((keep, c * 16), (give, 16 - c * 16)):
+                rows = integrals[s, pl.ds(pl.multiple_of(k * 32 + shift, 16), 16), :]
+                out[s, k * 16 : k * 16 + 16, :] = jnp.where(kept, rows, jnp.zeros_like(rows))
+
+
+def half_kernel(place, near, left, right, far, plane, mine, other, half, window):
+    c, x = place[0], place[1]
+    for b in range(4):
+        window[7 + b] = plane[b]
+        window[3 + c * 8 + b] = mine[3 + b]
+        window[11 - c * 8 + b] = other[3 + b]
+    for b in range(3):
+        window[c * 15 + b] = mine[b]
+        window[15 - c * 15 + b] = other[b]
+    own = pl.ds(pl.multiple_of(c * COLS, COLS), COLS)
+    rest = pl.ds(pl.multiple_of(COLS - c * COLS, COLS), COLS)
+    for turn, tiles in enumerate((near, right, far, left)):
+        a = lax.rem(x + turn, 4)
+        blocks = window[pl.ds(a, SPAN)].reshape(SPAN * ROWS, COLS)
+        wide = jnp.concatenate([tiles[:, s].reshape(2 * HALF, ROWS) for s in range(SPAN)], 1)
+        made = jnp.dot(wide, blocks, preferred_element_type=F32).astype(BF16)
+        to = pl.ds(pl.multiple_of(a * HALF, HALF), HALF)
+        half[to, own] = made[:HALF]
+        half[to, rest] = made[HALF:]
 
 
 def dot_t(a, b):
@@ -126,29 +124,33 @@
     c = lax.axis_index("core")
     core = c[None]
 
-    pieces = call(
-        orbital_kernel, "cut_orbitals", [SMEM, HBM], (4, HALF, COLS), BF16, core, occupied,
-        scratch=[pltpu.SemaphoreType.DMA((4,))], out=HBM,
-    )
+    pieces = call(orbital_kernel, "cut_orbitals", [VMEM], (4, ROWS, COLS), BF16, occupied)
     plane = lax.all_to_all(pieces, "x", 0, 0)
 
-    tiles = call(
-        integral_kernel, "cut_integrals", [SMEM, VMEM], (4, 2, SPAN, HALF, ROWS), BF16,
-        pair_mask, integrals[0, 0],
-    )
-    tiles = lax.all_to_all(tiles.reshape(8, SPAN, HALF, ROWS), ("x", "core"), 0, 0)
+    rows = jax.ShapeDtypeStruct((SPAN, HALF, ROWS), BF16)
+    keep, give = pl.pallas_call(
+        integral_kernel,
+        in_specs=[SMEM, SMEM, VMEM],
+        out_specs=[VMEM] * 2,
+        out_shape=[rows] * 2,
+        name="cut_integrals",
+    )(core, pair_mask, integrals[0, 0])
+    taken = swapped(give)
+    near = jnp.stack([keep, taken])
+    left = turned(near, 1)
+    right = turned(near, -1)
+    far = turned(near, 2)
 
-    below2 = moved(plane[1:], 2)
-    above2 = moved(plane[:3], -2)
-    below = moved(plane, 1)
-    above = moved(plane, -1)
-    first = swapped(jnp.concatenate([plane, below2, above2]))
-    second = swapped(jnp.concatenate([below, above]))
+    two_away = sided(lax.dynamic_slice_in_dim(plane, 1 - c, 3, 0), 2)
+    one_away = sided(plane, 1)
+    two_away, left, right, far = lax.optimization_barrier((two_away, left, right, far))
+    mine = jnp.concatenate([two_away, one_away])
+    other = swapped(mine)
 
     own = call(
-        half_kernel, "make_half", [SMEM] + [VMEM] * 6 + [ANY] * 2, (4 * HALF, 2 * COLS), BF16,
-        core, tiles, below2, below, plane, above, above2, first, second,
-        scratch=[pltpu.VMEM((18, 2, HALF, COLS), BF16), pltpu.SemaphoreType.DMA((5,))],
+        half_kernel, "make_half", [SMEM] + [VMEM] * 7, (4 * HALF, 2 * COLS), BF16,
+        jnp.stack([c, x]), near, left, right, far, plane, mine, other,
+        scratch=[pltpu.VMEM((18, ROWS, COLS), BF16)],
     )
 
     up = moved(own, 1)

time: 115 us -> 113 us (0.983)
  starting transfers between devices: 44.7 us -> 49.3 us
  waiting for transfers between devices: 31 us -> 26.9 us
  local copies, waits for them, and re-layouts: 7.83 us -> 4.79 us
  Pallas kernels: 5.41 us -> 7.04 us
  blocking collectives: 23.7 us -> 22.3 us
    ppermute x0 -> x5, starting transfers between devices: none -> 21.5 us  [the longest x3 11.3 us: turned(): return lax.ppermute(x, 'x', [(i, (i + by) % 4) for i in range(4)])]
    ppermute x8 -> x4, starting transfers between devices: 27.3 us -> 13.5 us  [moved(): lax.ppermute(x, 'z', [(i, i + by) for i in range(n) if 0 <= i + by < n])]
    ppermute x8 -> x4, waiting for transfers between devices: 24.4 us -> 13 us  [moved(): lax.ppermute(x, 'z', [(i, i + by) for i in range(n) if 0 <= i + by < n])]
    ppermute x0 -> x5, waiting for transfers between devices: none -> 8.28 us  [the longest x3 5.97 us: turned(): return lax.ppermute(x, 'x', [(i, (i + by) % 4) for i in range(4)])]
    all_to_all x1 -> x0, starting transfers between devices: 3.6 us -> none  [per_device(): lax.all_to_all(tiles.reshape(8, SPAN, HALF, ROWS), ('x', 'core'), 0, 0)]
    unnamed x18 -> x13, local copies, waits for them, and re-layouts: 7.79 us -> 4.7 us
    all_to_all x1, waiting for transfers between devices: 2.89 us -> 0.01 us  [per_device(): plane = lax.all_to_all(pieces, 'x', 0, 0)]
    pallas_call x0 -> x1, Pallas kernels: none -> 1.94 us  [per_device(): pl.pallas_call(integral_kernel, in_specs=[SMEM, SMEM, VMEM], out_specs=[V...]
  transfers between devices with their start and end apart: 15 -> 15, of which waited for: 9 -> 7; matrix products, arithmetic and copies ran while one was open for 0% -> 1% of each run, Pallas kernels for 1% -> 2%
where the time goes in v11:
time: 113 us; the launch traced here: 112 us
  starting transfers between devices  49.3 us (44%)
  waiting for transfers between devices  26.9 us (24%)
  blocking collectives  22.3 us (20%)
  Pallas kernels  7.04 us (6%)
  local copies, waits for them, and re-layouts  4.79 us (4%)
  other arithmetic  1.8 us (2%)
    all_to_all x1, blocking collectives, per_device(): lax.all_to_all(partial.reshape(16, 16, SPAN * ROWS), ('x', 'y'), 0, 0)  22.3 us
    ppermute x4, starting transfers between devices, moved(): lax.ppermute(x, 'z', [(i, i + by) for i in range(n) if 0 <= i + by < n])  13.5 us
    ppermute x4, waiting for transfers between devices, moved(): lax.ppermute(x, 'z', [(i, i + by) for i in range(n) if 0 <= i + by < n])  13 us
    ppermute x3, starting transfers between devices, turned(): return lax.ppermute(x, 'x', [(i, (i + by) % 4) for i in range(4)])  11.3 us
    ppermute x2, starting transfers between devices, sided(): return lax.ppermute(x, ('core', 'z'), pairs)  10.2 us
    ppermute x5, starting transfers between devices, swapped(): return lax.ppermute(x, 'core', [(0, 1), (1, 0)])  10.1 us
    ppermute x3, waiting for transfers between devices, turned(): return lax.ppermute(x, 'x', [(i, (i + by) % 4) for i in range(4)])  5.97 us
    ppermute x5, waiting for transfers between devices, swapped(): return lax.ppermute(x, 'core', [(0, 1), (1, 0)])  5.55 us
  transfers between devices with their start and end apart: 15, of which 7 were waited for; matrix products, arithmetic and copies ran while one was open for 1% of the time, Pallas kernels for 2%

profile of v11, /device:TPU:96, one launch (start us, length us, event | category | flops | bytes accessed | tf_op | source)
XLA Modules:
  0.0 112.4 jit_solution(5962989860253092340)
XLA Ops:
  0.0 1.0 copy-done
  1.0 0.8 cut_orbitals.1
  1.9 4.3 %all-to-all-start = ((bf16[4,128,512]{2,1,0:T(8,128)(2,1)}), bf16[4,128,512]{2,1,0:T(8,128)(2,1)S(1)}, u32[]{:S(2)}, u32[]{:S(2)}) async-start(bf16[4,128,512]{2,1,0:T(8,128)(2,1)} %cut_orbitals.1), calls=%async_computation | async-start | bytes 1048576 | tf_op jit(solution)/shard_map/all_to_all | solution.py:128
  6.2 1.9 %cut_integrals.1 = (bf16[15,64,128]{2,1,0:T(8,128)(2,1)}, bf16[15,64,128]{2,1,0:T(8,128)(2,1)}) custom-call(s32[1]{0:T(128)} %bitcast.core, s32[1,15]{1,0:T(1,128)} %mask.1, bf16[15,128,128]{2,1,0:T(8,128)(2,1)} %bitcast.11), custom_call_target="tpu_custom_call" | custom-call | tf_op jit(solution)/shard_map/cut_integrals/pallas_call | solution.py:131
  8.1 1.9 %collective-permute-start = (bf16[15,64,128]{2,1,0:T(8,128)(2,1)}, bf16[15,64,128]{2,1,0:T(8,128)(2,1)S(1)}, u32[]{:S(2)}, u32[]{:S(2)}) collective-permute-start(bf16[15,64,128]{2,1,0:T(8,128)(2,1)} %get-tuple-element.12), channel_id=1, source_target_pairs={{0,64},{64,0},{1,65},{65,1},{2,66},{66,2},{3,67},{67,3},{4,68},{68... | collective-permute-start | bytes 737288 | tf_op jit(solution)/shard_map/ppermute | solution.py:42
  10.0 1.7 %collective-permute-done = bf16[15,64,128]{2,1,0:T(8,128)(2,1)S(1)} collective-permute-done((bf16[15,64,128]{2,1,0:T(8,128)(2,1)}, bf16[15,64,128]{2,1,0:T(8,128)(2,1)S(1)}, u32[]{:S(2)}, u32[]{:S(2)}) %collective-permute-start) | collective-permute-done | bytes 245792 | tf_op jit(solution)/shard_map/ppermute | solution.py:42
  11.7 1.0 pad_maximum_fusion.near
  12.7 3.9 %collective-permute-start.2 = (bf16[2,15,64,128]{3,2,1,0:T(8,128)(2,1)S(1)}, bf16[2,15,64,128]{3,2,1,0:T(8,128)(2,1)S(1)}, u32[]{:S(2)}, u32[]{:S(2)}) collective-permute-start(bf16[2,15,64,128]{3,2,1,0:T(8,128)(2,1)S(1)} %pad_maximum_fusion.near), channel_id=1, source_target_pairs={{0,1},{1,2},{2,3},{3,0},{4,5},{5,6},{6,7},{7,4},{8,9},{9,10},{10,1... | collective-permute-start | bytes 1474568 | tf_op jit(solution)/shard_map/ppermute | solution.py:38
  16.7 3.1 %collective-permute-start.3 = (bf16[2,15,64,128]{3,2,1,0:T(8,128)(2,1)S(1)}, bf16[2,15,64,128]{3,2,1,0:T(8,128)(2,1)S(1)}, u32[]{:S(2)}, u32[]{:S(2)}) collective-permute-start(bf16[2,15,64,128]{3,2,1,0:T(8,128)(2,1)S(1)} %pad_maximum_fusion.near), channel_id=1, source_target_pairs={{0,3},{1,0},{2,1},{3,2},{4,7},{5,4},{6,5},{7,6},{8,11},{9,8},{10,9... | collective-permute-start | bytes 1474568 | tf_op jit(solution)/shard_map/ppermute | solution.py:38
  19.8 4.2 %collective-permute-start.4 = (bf16[2,15,64,128]{3,2,1,0:T(8,128)(2,1)S(1)}, bf16[2,15,64,128]{3,2,1,0:T(8,128)(2,1)S(1)}, u32[]{:S(2)}, u32[]{:S(2)}) collective-permute-start(bf16[2,15,64,128]{3,2,1,0:T(8,128)(2,1)S(1)} %pad_maximum_fusion.near), channel_id=1, source_target_pairs={{0,2},{1,3},{2,0},{3,1},{4,6},{5,7},{6,4},{7,5},{8,10},{9,11},{10,... | collective-permute-start | bytes 1474568 | tf_op jit(solution)/shard_map/ppermute | solution.py:38
  24.0 5.0 %collective-permute-start.5 = (bf16[4,128,512]{2,1,0:T(8,128)(2,1)S(1)}, bf16[4,128,512]{2,1,0:T(8,128)(2,1)S(1)}, u32[]{:S(2)}, u32[]{:S(2)}) collective-permute-start(bf16[4,128,512]{2,1,0:T(8,128)(2,1)S(1)} %all-to-all-done.plane), channel_id=1, source_target_pairs={{0,4},{4,8},{8,12},{12,16},{16,20},{20,24},{24,28},{28,32},{32,36}... | collective-permute-start | bytes 1572872 | tf_op jit(solution)/shard_map/ppermute | solution.py:49
  29.1 5.2 %collective-permute-start.1 = (bf16[3,128,512]{2,1,0:T(8,128)(2,1)S(1)}, bf16[3,128,512]{2,1,0:T(8,128)(2,1)S(1)}, u32[]{:S(2)}, u32[]{:S(2)}) collective-permute-start(bf16[3,128,512]{2,1,0:T(8,128)(2,1)S(1)} %constant_dynamic-slice_fusion), channel_id=1, source_target_pairs={{0,8},{4,12},{8,16},{12,20},{16,24},{20,28},{24,32},{28,36},{32,40... | collective-permute-start | bytes 1179656 | tf_op jit(solution)/shard_map/ppermute | solution.py:49
  35.1 6.0 %collective-permute-done.4.far = bf16[2,15,64,128]{3,2,1,0:T(8,128)(2,1)S(1)} collective-permute-done((bf16[2,15,64,128]{3,2,1,0:T(8,128)(2,1)S(1)}, bf16[2,15,64,128]{3,2,1,0:T(8,128)(2,1)S(1)}, u32[]{:S(2)}, u32[]{:S(2)}) %collective-permute-start.4) | collective-permute-done | bytes 491552 | tf_op jit(solution)/shard_map/ppermute | solution.py:38
  41.1 0.8 copy-done.3
  41.9 2.3 %collective-permute-done.1 = bf16[3,128,512]{2,1,0:T(8,128)(2,1)S(1)} collective-permute-done((bf16[3,128,512]{2,1,0:T(8,128)(2,1)S(1)}, bf16[3,128,512]{2,1,0:T(8,128)(2,1)S(1)}, u32[]{:S(2)}, u32[]{:S(2)}) %collective-permute-start.1) | collective-permute-done | bytes 393248 | tf_op jit(solution)/shard_map/ppermute | solution.py:49
  44.3 1.9 %collective-permute-start.6 = (bf16[7,128,512]{2,1,0:T(8,128)(2,1)S(1)}, bf16[7,128,512]{2,1,0:T(8,128)(2,1)S(1)}, u32[]{:S(2)}, u32[]{:S(2)}) collective-permute-start(bf16[7,128,512]{2,1,0:T(8,128)(2,1)S(1)} %constant_dynamic-update-slice_fusion.mine), channel_id=1, source_target_pairs={{0,64},{64,0},{1,65},{65,1},{2,66},{66,2},{3,67},{67,3},{4,68},{68... | collective-permute-start | bytes 2752520 | tf_op jit(solution)/shard_map/ppermute | solution.py:42
  46.3 2.4 %collective-permute-done.6.other = bf16[7,128,512]{2,1,0:T(8,128)(2,1)S(1)} collective-permute-done((bf16[7,128,512]{2,1,0:T(8,128)(2,1)S(1)}, bf16[7,128,512]{2,1,0:T(8,128)(2,1)S(1)}, u32[]{:S(2)}, u32[]{:S(2)}) %collective-permute-start.6) | collective-permute-done | bytes 917536 | tf_op jit(solution)/shard_map/ppermute | solution.py:42
  48.6 1.0 copy-done.2
  49.7 1.0 copy-done.4
  50.7 2.0 %make_half.1.own = bf16[256,1024]{1,0:T(8,128)(2,1)S(1)} custom-call(s32[2]{0:T(128)S(1)} %pad_add_fusion.place, bf16[2,15,64,128]{3,2,1,0:T(8,128)(2,1)S(1)} %pad_maximum_fusion.near, bf16[2,15,64,128]{3,2,1,0:T(8,128)(2,1)S(1)} %collective-permute-done.2.left, bf16[2,15,64,128]{3,2,1,0:T(8,128)(2,1)S(1)} %copy-done.2, ...), custom_call_target="tpu_custom_call" | custom-call | tf_op jit(solution)/shard_map/make_half/pallas_call | solution.py:21
  52.7 1.9 %collective-permute-start.8 = (bf16[256,1024]{1,0:T(8,128)(2,1)S(1)}, bf16[256,1024]{1,0:T(8,128)(2,1)S(1)}, u32[]{:S(2)}, u32[]{:S(2)}) collective-permute-start(bf16[256,1024]{1,0:T(8,128)(2,1)S(1)} %make_half.1.own), channel_id=1, source_target_pairs={{4,0},{8,4},{12,8},{16,12},{20,16},{24,20},{28,24},{32,28},{36,32}... | collective-permute-start | bytes 1572872 | tf_op jit(solution)/shard_map/ppermute | solution.py:34
  54.6 5.1 %collective-permute-start.7 = (bf16[256,1024]{1,0:T(8,128)(2,1)S(1)}, bf16[256,1024]{1,0:T(8,128)(2,1)S(1)}, u32[]{:S(2)}, u32[]{:S(2)}) collective-permute-start(bf16[256,1024]{1,0:T(8,128)(2,1)S(1)} %make_half.1.own), channel_id=1, source_target_pairs={{0,4},{4,8},{8,12},{12,16},{16,20},{20,24},{24,28},{28,32},{32,36}... | collective-permute-start | bytes 1572872 | tf_op jit(solution)/shard_map/ppermute | solution.py:34
  59.7 1.9 %collective-permute-start.10 = (bf16[256,1024]{1,0:T(8,128)(2,1)S(1)}, bf16[256,1024]{1,0:T(8,128)(2,1)S(1)}, u32[]{:S(2)}, u32[]{:S(2)}) collective-permute-start(bf16[256,1024]{1,0:T(8,128)(2,1)S(1)} %make_half.1.own), channel_id=1, source_target_pairs={{0,64},{64,0},{1,65},{65,1},{2,66},{66,2},{3,67},{67,3},{4,68},{68... | collective-permute-start | bytes 1572872 | tf_op jit(solution)/shard_map/ppermute | solution.py:42
  61.7 8.1 %collective-permute-done.8.down = bf16[256,1024]{1,0:T(8,128)(2,1)S(1)} collective-permute-done((bf16[256,1024]{1,0:T(8,128)(2,1)S(1)}, bf16[256,1024]{1,0:T(8,128)(2,1)S(1)}, u32[]{:S(2)}, u32[]{:S(2)}) %collective-permute-start.8) | collective-permute-done | bytes 524320 | tf_op jit(solution)/shard_map/ppermute | solution.py:34
  69.7 1.9 %collective-permute-start.11 = (bf16[256,1024]{1,0:T(8,128)(2,1)S(1)}, bf16[256,1024]{1,0:T(8,128)(2,1)S(1)}, u32[]{:S(2)}, u32[]{:S(2)}) collective-permute-start(bf16[256,1024]{1,0:T(8,128)(2,1)S(1)} %collective-permute-done.8.down), channel_id=1, source_target_pairs={{0,64},{64,0},{1,65},{65,1},{2,66},{66,2},{3,67},{67,3},{4,68},{68... | collective-permute-start | bytes 1572872 | tf_op jit(solution)/shard_map/ppermute | solution.py:42
  71.7 2.4 %collective-permute-start.9 = (bf16[256,1024]{1,0:T(8,128)(2,1)S(1)}, bf16[256,1024]{1,0:T(8,128)(2,1)S(1)}, u32[]{:S(2)}, u32[]{:S(2)}) collective-permute-start(bf16[256,1024]{1,0:T(8,128)(2,1)S(1)} %collective-permute-done.7.up), channel_id=1, source_target_pairs={{0,64},{64,0},{1,65},{65,1},{2,66},{66,2},{3,67},{67,3},{4,68},{68... | collective-permute-start | bytes 1572872 | tf_op jit(solution)/shard_map/ppermute | solution.py:42
  74.1 1.5 %collective-permute-done.9.up2 = bf16[256,1024]{1,0:T(8,128)(2,1)S(1)} collective-permute-done((bf16[256,1024]{1,0:T(8,128)(2,1)S(1)}, bf16[256,1024]{1,0:T(8,128)(2,1)S(1)}, u32[]{:S(2)}, u32[]{:S(2)}) %collective-permute-start.9) | collective-permute-done | bytes 524320 | tf_op jit(solution)/shard_map/ppermute | solution.py:42
  75.6 2.2 %make_tiles.1 = bf16[256,1920]{1,0:T(8,128)(2,1)S(1)} custom-call(s32[1]{0:T(128)} %bitcast.core, bf16[256,1024]{1,0:T(8,128)(2,1)S(1)} %collective-permute-done.7.up, bf16[256,1024]{1,0:T(8,128)(2,1)S(1)} %make_half.1.own, bf16[256,1024]{1,0:T(8,128)(2,1)S(1)} %collective-permute-done.8.down, bf16[256,1024]{1,0:T(8,128)(2,1)S(1)} %collective-permute-done.9.up2, ...), custom_call_target="tpu_custom_call" | custom-call | tf_op jit(solution)/shard_map/make_tiles/pallas_call | solution.py:21
  77.8 22.3 %all_to_all.10.parts = bf16[16,16,1920]{2,1,0:T(8,128)(2,1)S(1)} all-to-all(bf16[16,16,1920]{2,1,0:T(8,128)(2,1)S(1)} %bitcast.10), channel_id=1, replica_groups=mesh['y'=4,'core'=2,'z'=16,'x'=4] {'x','y'}, dimensions={0} | all-to-all | bytes 1966080 | tf_op jit(solution)/shard_map/all_to_all | solution.py:164
  100.3 4.5 %collective-permute-start.12 = (f32[3,16,128]{2,1,0:T(8,128)S(1)}, f32[3,16,128]{2,1,0:T(8,128)S(1)}, u32[]{:S(2)}, u32[]{:S(2)}) collective-permute-start(f32[3,16,128]{2,1,0:T(8,128)S(1)} %slice.8), channel_id=1, source_target_pairs={{0,4},{4,8},{8,12},{12,16},{16,20},{20,24},{24,28},{28,32},{32,36}... | collective-permute-start | bytes 73736 | tf_op jit(solution)/shard_map/ppermute | solution.py:34
  104.8 1.9 %collective-permute-start.13 = (f32[3,16,128]{2,1,0:T(8,128)S(1)}, f32[3,16,128]{2,1,0:T(8,128)S(1)}, u32[]{:S(2)}, u32[]{:S(2)}) collective-permute-start(f32[3,16,128]{2,1,0:T(8,128)S(1)} %slice.8), channel_id=1, source_target_pairs={{4,0},{8,4},{12,8},{16,12},{20,16},{24,20},{28,24},{32,28},{36,32}... | collective-permute-start | bytes 73736 | tf_op jit(solution)/shard_map/ppermute | solution.py:34
  106.7 5.0 %collective-permute-done.13 = f32[3,16,128]{2,1,0:T(8,128)S(1)} collective-permute-done((f32[3,16,128]{2,1,0:T(8,128)S(1)}, f32[3,16,128]{2,1,0:T(8,128)S(1)}, u32[]{:S(2)}, u32[]{:S(2)}) %collective-permute-start.13) | collective-permute-done | bytes 24608 | tf_op jit(solution)/shard_map/ppermute | solution.py:34
  (25 shorter events, 1.9 us)
Async XLA Ops:
  0.0 1.0 copy-start
  1.9 22.1 %all-to-all-start = ((bf16[4,128,512]{2,1,0:T(8,128)(2,1)}), bf16[4,128,512]{2,1,0:T(8,128)(2,1)S(1)}, u32[]{:S(2)}, u32[]{:S(2)}) async-start(bf16[4,128,512]{2,1,0:T(8,128)(2,1)} %cut_orbitals.1), calls=%async_computation | async-start | bytes 1048576 | tf_op jit(solution)/shard_map/all_to_all | solution.py:128
  8.1 3.6 %collective-permute-start = (bf16[15,64,128]{2,1,0:T(8,128)(2,1)}, bf16[15,64,128]{2,1,0:T(8,128)(2,1)S(1)}, u32[]{:S(2)}, u32[]{:S(2)}) collective-permute-start(bf16[15,64,128]{2,1,0:T(8,128)(2,1)} %get-tuple-element.12), channel_id=1, source_target_pairs={{0,64},{64,0},{1,65},{65,1},{2,66},{66,2},{3,67},{67,3},{4,68},{68... | collective-permute-start | bytes 737288 | tf_op jit(solution)/shard_map/ppermute | solution.py:42
  12.7 21.6 %collective-permute-start.2 = (bf16[2,15,64,128]{3,2,1,0:T(8,128)(2,1)S(1)}, bf16[2,15,64,128]{3,2,1,0:T(8,128)(2,1)S(1)}, u32[]{:S(2)}, u32[]{:S(2)}) collective-permute-start(bf16[2,15,64,128]{3,2,1,0:T(8,128)(2,1)S(1)} %pad_maximum_fusion.near), channel_id=1, source_target_pairs={{0,1},{1,2},{2,3},{3,0},{4,5},{5,6},{6,7},{7,4},{8,9},{9,10},{10,1... | collective-permute-start | bytes 1474568 | tf_op jit(solution)/shard_map/ppermute | solution.py:38
  16.7 17.7 %collective-permute-start.3 = (bf16[2,15,64,128]{3,2,1,0:T(8,128)(2,1)S(1)}, bf16[2,15,64,128]{3,2,1,0:T(8,128)(2,1)S(1)}, u32[]{:S(2)}, u32[]{:S(2)}) collective-permute-start(bf16[2,15,64,128]{3,2,1,0:T(8,128)(2,1)S(1)} %pad_maximum_fusion.near), channel_id=1, source_target_pairs={{0,3},{1,0},{2,1},{3,2},{4,7},{5,4},{6,5},{7,6},{8,11},{9,8},{10,9... | collective-permute-start | bytes 1474568 | tf_op jit(solution)/shard_map/ppermute | solution.py:38
  19.8 21.3 %collective-permute-start.4 = (bf16[2,15,64,128]{3,2,1,0:T(8,128)(2,1)S(1)}, bf16[2,15,64,128]{3,2,1,0:T(8,128)(2,1)S(1)}, u32[]{:S(2)}, u32[]{:S(2)}) collective-permute-start(bf16[2,15,64,128]{3,2,1,0:T(8,128)(2,1)S(1)} %pad_maximum_fusion.near), channel_id=1, source_target_pairs={{0,2},{1,3},{2,0},{3,1},{4,6},{5,7},{6,4},{7,5},{8,10},{9,11},{10,... | collective-permute-start | bytes 1474568 | tf_op jit(solution)/shard_map/ppermute | solution.py:38
  24.0 20.2 %collective-permute-start.5 = (bf16[4,128,512]{2,1,0:T(8,128)(2,1)S(1)}, bf16[4,128,512]{2,1,0:T(8,128)(2,1)S(1)}, u32[]{:S(2)}, u32[]{:S(2)}) collective-permute-start(bf16[4,128,512]{2,1,0:T(8,128)(2,1)S(1)} %all-to-all-done.plane), channel_id=1, source_target_pairs={{0,4},{4,8},{8,12},{12,16},{16,20},{20,24},{24,28},{28,32},{32,36}... | collective-permute-start | bytes 1572872 | tf_op jit(solution)/shard_map/ppermute | solution.py:49
  29.1 15.1 %collective-permute-start.1 = (bf16[3,128,512]{2,1,0:T(8,128)(2,1)S(1)}, bf16[3,128,512]{2,1,0:T(8,128)(2,1)S(1)}, u32[]{:S(2)}, u32[]{:S(2)}) collective-permute-start(bf16[3,128,512]{2,1,0:T(8,128)(2,1)S(1)} %constant_dynamic-slice_fusion), channel_id=1, source_target_pairs={{0,8},{4,12},{8,16},{12,20},{16,24},{20,28},{24,32},{28,36},{32,40... | collective-permute-start | bytes 1179656 | tf_op jit(solution)/shard_map/ppermute | solution.py:49
  34.3 0.8 copy-start.1
  41.1 0.8 copy-start.3
  44.3 4.4 %collective-permute-start.6 = (bf16[7,128,512]{2,1,0:T(8,128)(2,1)S(1)}, bf16[7,128,512]{2,1,0:T(8,128)(2,1)S(1)}, u32[]{:S(2)}, u32[]{:S(2)}) collective-permute-start(bf16[7,128,512]{2,1,0:T(8,128)(2,1)S(1)} %constant_dynamic-update-slice_fusion.mine), channel_id=1, source_target_pairs={{0,64},{64,0},{1,65},{65,1},{2,66},{66,2},{3,67},{67,3},{4,68},{68... | collective-permute-start | bytes 2752520 | tf_op jit(solution)/shard_map/ppermute | solution.py:42
  48.6 1.0 copy-start.2
  49.7 1.0 copy-start.4
  52.7 17.1 %collective-permute-start.8 = (bf16[256,1024]{1,0:T(8,128)(2,1)S(1)}, bf16[256,1024]{1,0:T(8,128)(2,1)S(1)}, u32[]{:S(2)}, u32[]{:S(2)}) collective-permute-start(bf16[256,1024]{1,0:T(8,128)(2,1)S(1)} %make_half.1.own), channel_id=1, source_target_pairs={{4,0},{8,4},{12,8},{16,12},{20,16},{24,20},{28,24},{32,28},{36,32}... | collective-permute-start | bytes 1572872 | tf_op jit(solution)/shard_map/ppermute | solution.py:34
  54.6 17.1 %collective-permute-start.7 = (bf16[256,1024]{1,0:T(8,128)(2,1)S(1)}, bf16[256,1024]{1,0:T(8,128)(2,1)S(1)}, u32[]{:S(2)}, u32[]{:S(2)}) collective-permute-start(bf16[256,1024]{1,0:T(8,128)(2,1)S(1)} %make_half.1.own), channel_id=1, source_target_pairs={{0,4},{4,8},{8,12},{12,16},{16,20},{20,24},{24,28},{28,32},{32,36}... | collective-permute-start | bytes 1572872 | tf_op jit(solution)/shard_map/ppermute | solution.py:34
  59.7 14.3 %collective-permute-start.10 = (bf16[256,1024]{1,0:T(8,128)(2,1)S(1)}, bf16[256,1024]{1,0:T(8,128)(2,1)S(1)}, u32[]{:S(2)}, u32[]{:S(2)}) collective-permute-start(bf16[256,1024]{1,0:T(8,128)(2,1)S(1)} %make_half.1.own), channel_id=1, source_target_pairs={{0,64},{64,0},{1,65},{65,1},{2,66},{66,2},{3,67},{67,3},{4,68},{68... | collective-permute-start | bytes 1572872 | tf_op jit(solution)/shard_map/ppermute | solution.py:42
  69.7 4.4 %collective-permute-start.11 = (bf16[256,1024]{1,0:T(8,128)(2,1)S(1)}, bf16[256,1024]{1,0:T(8,128)(2,1)S(1)}, u32[]{:S(2)}, u32[]{:S(2)}) collective-permute-start(bf16[256,1024]{1,0:T(8,128)(2,1)S(1)} %collective-permute-done.8.down), channel_id=1, source_target_pairs={{0,64},{64,0},{1,65},{65,1},{2,66},{66,2},{3,67},{67,3},{4,68},{68... | collective-permute-start | bytes 1572872 | tf_op jit(solution)/shard_map/ppermute | solution.py:42
  71.7 3.9 %collective-permute-start.9 = (bf16[256,1024]{1,0:T(8,128)(2,1)S(1)}, bf16[256,1024]{1,0:T(8,128)(2,1)S(1)}, u32[]{:S(2)}, u32[]{:S(2)}) collective-permute-start(bf16[256,1024]{1,0:T(8,128)(2,1)S(1)} %collective-permute-done.7.up), channel_id=1, source_target_pairs={{0,64},{64,0},{1,65},{65,1},{2,66},{66,2},{3,67},{67,3},{4,68},{68... | collective-permute-start | bytes 1572872 | tf_op jit(solution)/shard_map/ppermute | solution.py:42
  100.2 6.4 %copy-start.5 = (s32[1,15]{1,0:T(1,128)S(1)}, s32[1,15]{1,0:T(1,128)}, u32[]{:S(2)}) copy-start(s32[1,15]{1,0:T(1,128)} %mask.1) | copy-start | bytes 184
  100.3 6.5 %collective-permute-start.12 = (f32[3,16,128]{2,1,0:T(8,128)S(1)}, f32[3,16,128]{2,1,0:T(8,128)S(1)}, u32[]{:S(2)}, u32[]{:S(2)}) collective-permute-start(f32[3,16,128]{2,1,0:T(8,128)S(1)} %slice.8), channel_id=1, source_target_pairs={{0,4},{4,8},{8,12},{12,16},{16,20},{20,24},{24,28},{28,32},{32,36}... | collective-permute-start | bytes 73736 | tf_op jit(solution)/shard_map/ppermute | solution.py:34
  104.8 6.9 %collective-permute-start.13 = (f32[3,16,128]{2,1,0:T(8,128)S(1)}, f32[3,16,128]{2,1,0:T(8,128)S(1)}, u32[]{:S(2)}, u32[]{:S(2)}) collective-permute-start(f32[3,16,128]{2,1,0:T(8,128)S(1)} %slice.8), channel_id=1, source_target_pairs={{4,0},{8,4},{12,8},{16,12},{20,16},{24,20},{28,24},{32,28},{36,32}... | collective-permute-start | bytes 73736 | tf_op jit(solution)/shard_map/ppermute | solution.py:34

commit v12 on v10

--- a/solution.py
+++ b/solution.py
@@ -58,7 +58,7 @@
             for k in range(4):
                 at = k * 32 + core * 16
                 for x in range(4):
-                    out[x, core, s, k * 16 : k * 16 + 16, :] = tile[at : at + 16]
+                    out[core, x, s, k * 16 : k * 16 + 16, :] = tile[at : at + 16]
 
 
 def window_kernel(core, below2, below, plane, above, above2, first, second, window):
@@ -73,17 +73,15 @@
 
 
 def half_kernel(gathered, window, half, tiles, sems):
-    copies = [
-        pltpu.make_async_copy(gathered.at[pl.ds(2 * a, 2)], tiles.at[pl.ds(2 * a, 2)], sems.at[a])
-        for a in range(4)
-    ]
+    copies = [pltpu.make_async_copy(gathered.at[i], tiles.at[i], sems.at[i]) for i in (0, 4, 1, 5, 2, 6, 3, 7)]
     for copy in copies:
         copy.start()
     for a in range(4):
-        copies[a].wait()
+        copies[2 * a].wait()
+        copies[2 * a + 1].wait()
         near = window[a : a + SPAN].reshape(SPAN * ROWS, COLS)
         wide = jnp.concatenate(
-            [tiles[2 * a : 2 * a + 2, s].reshape(2 * HALF, ROWS) for s in range(SPAN)], 1
+            [jnp.concatenate([tiles[a, s], tiles[4 + a, s]], 0) for s in range(SPAN)], 1
         )
         made = jnp.dot(wide, near, preferred_element_type=F32).astype(BF16)
         half[a * HALF : (a + 1) * HALF, :COLS] = made[:HALF]
@@ -105,15 +103,21 @@
 def tile_kernel(core, up, own, down, up2, own2, down2, out, wide):
     for i, (mine, other) in enumerate(((up, up2), (own, own2), (down, down2))):
         interleave(core[0], mine, other, wide, i * 512)
+
+    def put(made, x, at):
+        for y in range(4):
+            out[y * 4 + x, :, at : at + made.shape[1]] = made[y * 16 : y * 16 + 16].astype(BF16)
+
     for i in range(3):
-        out[:, i * 512 : (i + 1) * 512] = dot_t(own[...], wide[i * 512 : (i + 1) * 512, :]).astype(BF16)
+        made = dot_t(own[...], wide[i * 512 : (i + 1) * 512, :])
+        for x in range(4):
+            put(made[x * HALF : (x + 1) * HALF], x, i * 512)
     for x in range(4):
         rows = slice(x * HALF, (x + 1) * HALF)
-        cut = 1536 + x * ROWS
         if x > 0:
-            out[rows, 1536:cut] = dot_t(up[rows, :], wide[1024 : 1024 + x * ROWS, :]).astype(BF16)
+            put(dot_t(up[rows, :], wide[1024 : 1024 + x * ROWS, :]), x, 1536)
         if x < 3:
-            out[rows, cut:] = dot_t(down[rows, :], wide[(x + 1) * ROWS : 512, :]).astype(BF16)
+            put(dot_t(down[rows, :], wide[(x + 1) * ROWS : 512, :]), x, 1536 + x * ROWS)
 
 
 def sum_kernel(parts, out):
@@ -136,10 +140,10 @@
     plane = lax.all_to_all(pieces, "x", 0, 0)
 
     tiles = call(
-        integral_kernel, "cut_integrals", [SMEM, VMEM], (4, 2, SPAN, HALF, ROWS), BF16,
+        integral_kernel, "cut_integrals", [SMEM, VMEM], (2, 4, SPAN, HALF, ROWS), BF16,
         pair_mask, integrals[0, 0],
     )
-    tiles = lax.all_to_all(tiles.reshape(8, SPAN, HALF, ROWS), ("x", "core"), 0, 0)
+    tiles = lax.all_to_all(tiles.reshape(8, SPAN, HALF, ROWS), ("core", "x"), 0, 0)
 
     below2 = moved(plane[1:], 2)
     above2 = moved(plane[:3], -2)
@@ -154,18 +158,18 @@
     )
     own = call(
         half_kernel, "make_half", [ANY, VMEM], (4 * HALF, 2 * COLS), BF16, tiles, window,
-        scratch=[pltpu.VMEM((8, SPAN, HALF, ROWS), BF16), pltpu.SemaphoreType.DMA((4,))],
+        scratch=[pltpu.VMEM((8, SPAN, HALF, ROWS), BF16), pltpu.SemaphoreType.DMA((8,))],
     )
 
     up = moved(own, 1)
     down = moved(own, -1)
     own2 = swapped(own)
     partial = call(
-        tile_kernel, "make_tiles", [SMEM] + [VMEM] * 6, (256, SPAN * ROWS), BF16,
+        tile_kernel, "make_tiles", [SMEM] + [VMEM] * 6, (16, 16, SPAN * ROWS), BF16,
         core, up, own, down, swapped(up), own2, swapped(down),
         scratch=[pltpu.VMEM((1536, 2 * COLS), BF16)],
     )
-    partial = lax.all_to_all(partial.reshape(16, 16, SPAN * ROWS), ("x", "y"), 0, 0)
+    partial = lax.all_to_all(partial, ("y", "x"), 0, 0)
     total = call(sum_kernel, "sum_parts", [VMEM], (SPAN, 16, ROWS), F32, partial)
     far = total[12:]
     line = jnp.concatenate([moved(far, 1), total[:12], moved(far, -1)], 0)

time: 112 us -> 112 us (level)
  the two profiles are of different devices: /device:TPU:96 before, /device:TPU:224 now
where the time goes in v12:
time: 112 us; the launch traced here: 111 us
  starting transfers between devices  47.1 us (42%)
  waiting for transfers between devices  28.2 us (25%)
  blocking collectives  23.9 us (21%)
  Pallas kernels  8.17 us (7%)
  local copies, waits for them, and re-layouts  2.77 us (2%)
    ppermute x8, starting transfers between devices, moved(): lax.ppermute(x, 'z', [(i, i + by) for i in range(n) if 0 <= i + by < n])  28.4 us
    all_to_all x1, blocking collectives, per_device(): partial = lax.all_to_all(partial, ('y', 'x'), 0, 0)  23.9 us
    ppermute x8, waiting for transfers between devices, moved(): lax.ppermute(x, 'z', [(i, i + by) for i in range(n) if 0 <= i + by < n])  21.9 us
    ppermute x5, starting transfers between devices, swapped(): return lax.ppermute(x, 'core', [(0, 1), (1, 0)])  10.1 us
    pallas_call x6, Pallas kernels, call(): pl.pallas_call(kernel, in_specs=specs, out_specs=out, out_shape=jax.Shape...  8.17 us
    all_to_all x1, starting transfers between devices, per_device(): lax.all_to_all(tiles.reshape(8, SPAN, HALF, ROWS), ('core', 'x'), 0, 0)  4.32 us
    all_to_all x1, starting transfers between devices, per_device(): plane = lax.all_to_all(pieces, 'x', 0, 0)  4.3 us
    ppermute x5, waiting for transfers between devices, swapped(): return lax.ppermute(x, 'core', [(0, 1), (1, 0)])  3.38 us
  transfers between devices with their start and end apart: 15, of which 7 were waited for; matrix products, arithmetic and copies ran while one was open for 0% of the time, Pallas kernels for 2%

profile of v12, /device:TPU:224, one launch (start us, length us, event | category | flops | bytes accessed | tf_op | source)
XLA Modules:
  0.0 111.2 jit_solution(11978641044089839471)
XLA Ops:
  0.0 1.0 copy-done
  1.0 0.7 cut_orbitals.1
  1.8 4.3 %all-to-all-start.1 = ((bf16[4,64,512]{2,1,0:T(8,128)(2,1)}), bf16[4,64,512]{2,1,0:T(8,128)(2,1)S(1)}, u32[]{:S(2)}, u32[]{:S(2)}) async-start(bf16[4,64,512]{2,1,0:T(8,128)(2,1)} %cut_orbitals.1), calls=%async_computation.1 | async-start | bytes 524288 | tf_op jit(solution)/shard_map/all_to_all | solution.py:140
  6.1 1.0 copy-done.1
  7.1 0.7 copy-done.2
  7.8 2.1 %cut_integrals.1 = bf16[2,4,15,64,128]{4,3,2,1,0:T(8,128)(2,1)} custom-call(s32[1,15]{1,0:T(1,128)S(1)} %copy-done.2, bf16[15,128,128]{2,1,0:T(8,128)(2,1)S(1)} %bitcast.7), custom_call_target="tpu_custom_call" | custom-call | tf_op jit(solution)/shard_map/cut_integrals/pallas_call | solution.py:21
  9.9 2.9 %all-to-all-done.1.plane = bf16[4,64,512]{2,1,0:T(8,128)(2,1)S(1)} async-done(((bf16[4,64,512]{2,1,0:T(8,128)(2,1)}), bf16[4,64,512]{2,1,0:T(8,128)(2,1)S(1)}, u32[]{:S(2)}, u32[]{:S(2)}) %all-to-all-start.1) | async-done | bytes 262176 | tf_op jit(solution)/shard_map/all_to_all | solution.py:140
  12.8 4.3 %all-to-all-start = ((bf16[8,15,64,128]{3,2,1,0:T(8,128)(2,1)}), bf16[8,15,64,128]{3,2,1,0:T(8,128)(2,1)}, u32[]{:S(2)}, u32[]{:S(2)}) async-start(bf16[8,15,64,128]{3,2,1,0:T(8,128)(2,1)} %bitcast.2), calls=%async_computation | async-start | bytes 3932160 | tf_op jit(solution)/shard_map/all_to_all | solution.py:146
  17.1 5.5 %collective-permute-start = (bf16[3,64,512]{2,1,0:T(8,128)(2,1)S(1)}, bf16[3,64,512]{2,1,0:T(8,128)(2,1)S(1)}, u32[]{:S(2)}, u32[]{:S(2)}) collective-permute-start(bf16[3,64,512]{2,1,0:T(8,128)(2,1)S(1)} %get-tuple-element.6), channel_id=1, source_target_pairs={{0,8},{4,12},{8,16},{12,20},{16,24},{20,28},{24,32},{28,36},{32,40... | collective-permute-start | bytes 589832 | tf_op jit(solution)/shard_map/ppermute | solution.py:34
  22.6 1.9 %collective-permute-start.3 = (bf16[3,64,512]{2,1,0:T(8,128)(2,1)S(1)}, bf16[3,64,512]{2,1,0:T(8,128)(2,1)S(1)}, u32[]{:S(2)}, u32[]{:S(2)}) collective-permute-start(bf16[3,64,512]{2,1,0:T(8,128)(2,1)S(1)} %get-tuple-element.5), channel_id=1, source_target_pairs={{8,0},{12,4},{16,8},{20,12},{24,16},{28,20},{32,24},{36,28},{40,32... | collective-permute-start | bytes 589832 | tf_op jit(solution)/shard_map/ppermute | solution.py:34
  24.6 5.6 %collective-permute-start.1 = (bf16[4,64,512]{2,1,0:T(8,128)(2,1)S(1)}, bf16[4,64,512]{2,1,0:T(8,128)(2,1)S(1)}, u32[]{:S(2)}, u32[]{:S(2)}) collective-permute-start(bf16[4,64,512]{2,1,0:T(8,128)(2,1)S(1)} %all-to-all-done.1.plane), channel_id=1, source_target_pairs={{0,4},{4,8},{8,12},{12,16},{16,20},{20,24},{24,28},{28,32},{32,36}... | collective-permute-start | bytes 786440 | tf_op jit(solution)/shard_map/ppermute | solution.py:34
  30.1 1.9 %collective-permute-start.2 = (bf16[4,64,512]{2,1,0:T(8,128)(2,1)S(1)}, bf16[4,64,512]{2,1,0:T(8,128)(2,1)S(1)}, u32[]{:S(2)}, u32[]{:S(2)}) collective-permute-start(bf16[4,64,512]{2,1,0:T(8,128)(2,1)S(1)} %all-to-all-done.1.plane), channel_id=1, source_target_pairs={{4,0},{8,4},{12,8},{16,12},{20,16},{24,20},{28,24},{32,28},{36,32}... | collective-permute-start | bytes 786440 | tf_op jit(solution)/shard_map/ppermute | solution.py:34
  32.1 5.0 %collective-permute-done.3.above2 = bf16[3,64,512]{2,1,0:T(8,128)(2,1)S(1)} collective-permute-done((bf16[3,64,512]{2,1,0:T(8,128)(2,1)S(1)}, bf16[3,64,512]{2,1,0:T(8,128)(2,1)S(1)}, u32[]{:S(2)}, u32[]{:S(2)}) %collective-permute-start.3) | collective-permute-done | bytes 196640 | tf_op jit(solution)/shard_map/ppermute | solution.py:34
  37.2 1.9 %collective-permute-start.4 = (bf16[10,64,512]{2,1,0:T(8,128)(2,1)S(1)}, bf16[10,64,512]{2,1,0:T(8,128)(2,1)S(1)}, u32[]{:S(2)}, u32[]{:S(2)}) collective-permute-start(bf16[10,64,512]{2,1,0:T(8,128)(2,1)S(1)} %pad_maximum_fusion), channel_id=1, source_target_pairs={{0,64},{64,0},{1,65},{65,1},{2,66},{66,2},{3,67},{67,3},{4,68},{68... | collective-permute-start | bytes 1966088 | tf_op jit(solution)/shard_map/ppermute | solution.py:38
  39.1 3.8 %collective-permute-done.2.above = bf16[4,64,512]{2,1,0:T(8,128)(2,1)S(1)} collective-permute-done((bf16[4,64,512]{2,1,0:T(8,128)(2,1)S(1)}, bf16[4,64,512]{2,1,0:T(8,128)(2,1)S(1)}, u32[]{:S(2)}, u32[]{:S(2)}) %collective-permute-start.2) | collective-permute-done | bytes 262176 | tf_op jit(solution)/shard_map/ppermute | solution.py:34
  43.0 1.9 %collective-permute-start.5 = (bf16[8,64,512]{2,1,0:T(8,128)(2,1)S(1)}, bf16[8,64,512]{2,1,0:T(8,128)(2,1)S(1)}, u32[]{:S(2)}, u32[]{:S(2)}) collective-permute-start(bf16[8,64,512]{2,1,0:T(8,128)(2,1)S(1)} %pad_maximum_fusion.1), channel_id=1, source_target_pairs={{0,64},{64,0},{1,65},{65,1},{2,66},{66,2},{3,67},{67,3},{4,68},{68... | collective-permute-start | bytes 1572872 | tf_op jit(solution)/shard_map/ppermute | solution.py:38
  44.9 1.9 %collective-permute-done.5.second = bf16[8,64,512]{2,1,0:T(8,128)(2,1)S(1)} collective-permute-done((bf16[8,64,512]{2,1,0:T(8,128)(2,1)S(1)}, bf16[8,64,512]{2,1,0:T(8,128)(2,1)S(1)}, u32[]{:S(2)}, u32[]{:S(2)}) %collective-permute-start.5) | collective-permute-done | bytes 524320 | tf_op jit(solution)/shard_map/ppermute | solution.py:38
  46.8 0.2 place_orbitals.1.window
  47.0 2.9 %make_half.1.own = bf16[256,1024]{1,0:T(8,128)(2,1)S(1)} custom-call(bf16[8,15,64,128]{3,2,1,0:T(8,128)(2,1)} %all-to-all-done.gathered, bf16[18,2,64,512]{3,2,1,0:T(8,128)(2,1)S(1)} %place_orbitals.1.window), custom_call_target="tpu_custom_call" | custom-call | tf_op jit(solution)/shard_map/make_half/pallas_call | solution.py:21
  49.9 2.2 %collective-permute-start.7 = (bf16[256,1024]{1,0:T(8,128)(2,1)S(1)}, bf16[256,1024]{1,0:T(8,128)(2,1)S(1)}, u32[]{:S(2)}, u32[]{:S(2)}) collective-permute-start(bf16[256,1024]{1,0:T(8,128)(2,1)S(1)} %make_half.1.own), channel_id=1, source_target_pairs={{4,0},{8,4},{12,8},{16,12},{20,16},{24,20},{28,24},{32,28},{36,32}... | collective-permute-start | bytes 1572872 | tf_op jit(solution)/shard_map/ppermute | solution.py:34
  52.1 4.9 %collective-permute-start.6 = (bf16[256,1024]{1,0:T(8,128)(2,1)S(1)}, bf16[256,1024]{1,0:T(8,128)(2,1)S(1)}, u32[]{:S(2)}, u32[]{:S(2)}) collective-permute-start(bf16[256,1024]{1,0:T(8,128)(2,1)S(1)} %make_half.1.own), channel_id=1, source_target_pairs={{0,4},{4,8},{8,12},{12,16},{16,20},{20,24},{24,28},{28,32},{32,36}... | collective-permute-start | bytes 1572872 | tf_op jit(solution)/shard_map/ppermute | solution.py:34
  57.0 1.9 %collective-permute-start.9 = (bf16[256,1024]{1,0:T(8,128)(2,1)S(1)}, bf16[256,1024]{1,0:T(8,128)(2,1)S(1)}, u32[]{:S(2)}, u32[]{:S(2)}) collective-permute-start(bf16[256,1024]{1,0:T(8,128)(2,1)S(1)} %make_half.1.own), channel_id=1, source_target_pairs={{0,64},{64,0},{1,65},{65,1},{2,66},{66,2},{3,67},{67,3},{4,68},{68... | collective-permute-start | bytes 1572872 | tf_op jit(solution)/shard_map/ppermute | solution.py:38
  58.9 8.1 %collective-permute-done.7.down = bf16[256,1024]{1,0:T(8,128)(2,1)S(1)} collective-permute-done((bf16[256,1024]{1,0:T(8,128)(2,1)S(1)}, bf16[256,1024]{1,0:T(8,128)(2,1)S(1)}, u32[]{:S(2)}, u32[]{:S(2)}) %collective-permute-start.7) | collective-permute-done | bytes 524320 | tf_op jit(solution)/shard_map/ppermute | solution.py:34
  67.0 1.9 %collective-permute-start.10 = (bf16[256,1024]{1,0:T(8,128)(2,1)S(1)}, bf16[256,1024]{1,0:T(8,128)(2,1)S(1)}, u32[]{:S(2)}, u32[]{:S(2)}) collective-permute-start(bf16[256,1024]{1,0:T(8,128)(2,1)S(1)} %collective-permute-done.7.down), channel_id=1, source_target_pairs={{0,64},{64,0},{1,65},{65,1},{2,66},{66,2},{3,67},{67,3},{4,68},{68... | collective-permute-start | bytes 1572872 | tf_op jit(solution)/shard_map/ppermute | solution.py:38
  68.9 2.4 %collective-permute-start.8 = (bf16[256,1024]{1,0:T(8,128)(2,1)S(1)}, bf16[256,1024]{1,0:T(8,128)(2,1)S(1)}, u32[]{:S(2)}, u32[]{:S(2)}) collective-permute-start(bf16[256,1024]{1,0:T(8,128)(2,1)S(1)} %collective-permute-done.6.up), channel_id=1, source_target_pairs={{0,64},{64,0},{1,65},{65,1},{2,66},{66,2},{3,67},{67,3},{4,68},{68... | collective-permute-start | bytes 1572872 | tf_op jit(solution)/shard_map/ppermute | solution.py:38
  71.4 1.5 %collective-permute-done.8.up2 = bf16[256,1024]{1,0:T(8,128)(2,1)S(1)} collective-permute-done((bf16[256,1024]{1,0:T(8,128)(2,1)S(1)}, bf16[256,1024]{1,0:T(8,128)(2,1)S(1)}, u32[]{:S(2)}, u32[]{:S(2)}) %collective-permute-start.8) | collective-permute-done | bytes 524320 | tf_op jit(solution)/shard_map/ppermute | solution.py:38
  72.9 2.1 %make_tiles.1 = bf16[16,16,1920]{2,1,0:T(8,128)(2,1)S(1)} custom-call(s32[1]{0:T(128)} %bitcast.core, bf16[256,1024]{1,0:T(8,128)(2,1)S(1)} %collective-permute-done.6.up, bf16[256,1024]{1,0:T(8,128)(2,1)S(1)} %make_half.1.own, bf16[256,1024]{1,0:T(8,128)(2,1)S(1)} %collective-permute-done.7.down, bf16[256,1024]{1,0:T(8,128)(2,1)S(1)} %collective-permute-done.8.up2, ...), custom_call_target="tpu_custom_call" | custom-call | tf_op jit(solution)/shard_map/make_tiles/pallas_call | solution.py:21
  75.0 23.9 %all_to_all.15.parts = bf16[16,16,1920]{2,1,0:T(8,128)(2,1)S(1)} all-to-all(bf16[16,16,1920]{2,1,0:T(8,128)(2,1)S(1)} %make_tiles.1), channel_id=1, replica_groups=mesh['y'=4,'core'=2,'z'=16,'x'=4] {'y','x'}, dimensions={0} | all-to-all | bytes 1966080 | tf_op jit(solution)/shard_map/all_to_all | solution.py:172
  99.1 4.5 %collective-permute-start.11 = (f32[3,16,128]{2,1,0:T(8,128)S(1)}, f32[3,16,128]{2,1,0:T(8,128)S(1)}, u32[]{:S(2)}, u32[]{:S(2)}) collective-permute-start(f32[3,16,128]{2,1,0:T(8,128)S(1)} %slice.18), channel_id=1, source_target_pairs={{0,4},{4,8},{8,12},{12,16},{16,20},{20,24},{24,28},{28,32},{32,36}... | collective-permute-start | bytes 73736 | tf_op jit(solution)/shard_map/ppermute | solution.py:34
  103.6 1.9 %collective-permute-start.12 = (f32[3,16,128]{2,1,0:T(8,128)S(1)}, f32[3,16,128]{2,1,0:T(8,128)S(1)}, u32[]{:S(2)}, u32[]{:S(2)}) collective-permute-start(f32[3,16,128]{2,1,0:T(8,128)S(1)} %slice.18), channel_id=1, source_target_pairs={{4,0},{8,4},{12,8},{16,12},{20,16},{24,20},{28,24},{32,28},{36,32}... | collective-permute-start | bytes 73736 | tf_op jit(solution)/shard_map/ppermute | solution.py:34
  105.5 5.0 %collective-permute-done.12 = f32[3,16,128]{2,1,0:T(8,128)S(1)} collective-permute-done((f32[3,16,128]{2,1,0:T(8,128)S(1)}, f32[3,16,128]{2,1,0:T(8,128)S(1)}, u32[]{:S(2)}, u32[]{:S(2)}) %collective-permute-start.12) | collective-permute-done | bytes 24608 | tf_op jit(solution)/shard_map/ppermute | solution.py:34
  110.5 0.7 fusion.3
  (20 shorter events, 0.3 us)
Async XLA Ops:
  0.0 1.0 copy-start
  1.8 11.0 %all-to-all-start.1 = ((bf16[4,64,512]{2,1,0:T(8,128)(2,1)}), bf16[4,64,512]{2,1,0:T(8,128)(2,1)S(1)}, u32[]{:S(2)}, u32[]{:S(2)}) async-start(bf16[4,64,512]{2,1,0:T(8,128)(2,1)} %cut_orbitals.1), calls=%async_computation.1 | async-start | bytes 524288 | tf_op jit(solution)/shard_map/all_to_all | solution.py:140
  6.1 1.0 copy-start.1
  7.1 0.7 copy-start.2
  12.8 34.2 %all-to-all-start = ((bf16[8,15,64,128]{3,2,1,0:T(8,128)(2,1)}), bf16[8,15,64,128]{3,2,1,0:T(8,128)(2,1)}, u32[]{:S(2)}, u32[]{:S(2)}) async-start(bf16[8,15,64,128]{3,2,1,0:T(8,128)(2,1)} %bitcast.2), calls=%async_computation | async-start | bytes 3932160 | tf_op jit(solution)/shard_map/all_to_all | solution.py:146
  17.1 14.9 %collective-permute-start = (bf16[3,64,512]{2,1,0:T(8,128)(2,1)S(1)}, bf16[3,64,512]{2,1,0:T(8,128)(2,1)S(1)}, u32[]{:S(2)}, u32[]{:S(2)}) collective-permute-start(bf16[3,64,512]{2,1,0:T(8,128)(2,1)S(1)} %get-tuple-element.6), channel_id=1, source_target_pairs={{0,8},{4,12},{8,16},{12,20},{16,24},{20,28},{24,32},{28,36},{32,40... | collective-permute-start | bytes 589832 | tf_op jit(solution)/shard_map/ppermute | solution.py:34
  22.6 14.5 %collective-permute-start.3 = (bf16[3,64,512]{2,1,0:T(8,128)(2,1)S(1)}, bf16[3,64,512]{2,1,0:T(8,128)(2,1)S(1)}, u32[]{:S(2)}, u32[]{:S(2)}) collective-permute-start(bf16[3,64,512]{2,1,0:T(8,128)(2,1)S(1)} %get-tuple-element.5), channel_id=1, source_target_pairs={{8,0},{12,4},{16,8},{20,12},{24,16},{28,20},{32,24},{36,28},{40,32... | collective-permute-start | bytes 589832 | tf_op jit(solution)/shard_map/ppermute | solution.py:34
  24.6 14.6 %collective-permute-start.1 = (bf16[4,64,512]{2,1,0:T(8,128)(2,1)S(1)}, bf16[4,64,512]{2,1,0:T(8,128)(2,1)S(1)}, u32[]{:S(2)}, u32[]{:S(2)}) collective-permute-start(bf16[4,64,512]{2,1,0:T(8,128)(2,1)S(1)} %all-to-all-done.1.plane), channel_id=1, source_target_pairs={{0,4},{4,8},{8,12},{12,16},{16,20},{20,24},{24,28},{28,32},{32,36}... | collective-permute-start | bytes 786440 | tf_op jit(solution)/shard_map/ppermute | solution.py:34
  30.1 12.8 %collective-permute-start.2 = (bf16[4,64,512]{2,1,0:T(8,128)(2,1)S(1)}, bf16[4,64,512]{2,1,0:T(8,128)(2,1)S(1)}, u32[]{:S(2)}, u32[]{:S(2)}) collective-permute-start(bf16[4,64,512]{2,1,0:T(8,128)(2,1)S(1)} %all-to-all-done.1.plane), channel_id=1, source_target_pairs={{4,0},{8,4},{12,8},{16,12},{20,16},{24,20},{28,24},{32,28},{36,32}... | collective-permute-start | bytes 786440 | tf_op jit(solution)/shard_map/ppermute | solution.py:34
  37.2 9.6 %collective-permute-start.4 = (bf16[10,64,512]{2,1,0:T(8,128)(2,1)S(1)}, bf16[10,64,512]{2,1,0:T(8,128)(2,1)S(1)}, u32[]{:S(2)}, u32[]{:S(2)}) collective-permute-start(bf16[10,64,512]{2,1,0:T(8,128)(2,1)S(1)} %pad_maximum_fusion), channel_id=1, source_target_pairs={{0,64},{64,0},{1,65},{65,1},{2,66},{66,2},{3,67},{67,3},{4,68},{68... | collective-permute-start | bytes 1966088 | tf_op jit(solution)/shard_map/ppermute | solution.py:38
  43.0 3.8 %collective-permute-start.5 = (bf16[8,64,512]{2,1,0:T(8,128)(2,1)S(1)}, bf16[8,64,512]{2,1,0:T(8,128)(2,1)S(1)}, u32[]{:S(2)}, u32[]{:S(2)}) collective-permute-start(bf16[8,64,512]{2,1,0:T(8,128)(2,1)S(1)} %pad_maximum_fusion.1), channel_id=1, source_target_pairs={{0,64},{64,0},{1,65},{65,1},{2,66},{66,2},{3,67},{67,3},{4,68},{68... | collective-permute-start | bytes 1572872 | tf_op jit(solution)/shard_map/ppermute | solution.py:38
  49.9 17.1 %collective-permute-start.7 = (bf16[256,1024]{1,0:T(8,128)(2,1)S(1)}, bf16[256,1024]{1,0:T(8,128)(2,1)S(1)}, u32[]{:S(2)}, u32[]{:S(2)}) collective-permute-start(bf16[256,1024]{1,0:T(8,128)(2,1)S(1)} %make_half.1.own), channel_id=1, source_target_pairs={{4,0},{8,4},{12,8},{16,12},{20,16},{24,20},{28,24},{32,28},{36,32}... | collective-permute-start | bytes 1572872 | tf_op jit(solution)/shard_map/ppermute | solution.py:34
  52.1 16.8 %collective-permute-start.6 = (bf16[256,1024]{1,0:T(8,128)(2,1)S(1)}, bf16[256,1024]{1,0:T(8,128)(2,1)S(1)}, u32[]{:S(2)}, u32[]{:S(2)}) collective-permute-start(bf16[256,1024]{1,0:T(8,128)(2,1)S(1)} %make_half.1.own), channel_id=1, source_target_pairs={{0,4},{4,8},{8,12},{12,16},{16,20},{20,24},{24,28},{28,32},{32,36}... | collective-permute-start | bytes 1572872 | tf_op jit(solution)/shard_map/ppermute | solution.py:34
  57.0 14.3 %collective-permute-start.9 = (bf16[256,1024]{1,0:T(8,128)(2,1)S(1)}, bf16[256,1024]{1,0:T(8,128)(2,1)S(1)}, u32[]{:S(2)}, u32[]{:S(2)}) collective-permute-start(bf16[256,1024]{1,0:T(8,128)(2,1)S(1)} %make_half.1.own), channel_id=1, source_target_pairs={{0,64},{64,0},{1,65},{65,1},{2,66},{66,2},{3,67},{67,3},{4,68},{68... | collective-permute-start | bytes 1572872 | tf_op jit(solution)/shard_map/ppermute | solution.py:38
  67.0 4.4 %collective-permute-start.10 = (bf16[256,1024]{1,0:T(8,128)(2,1)S(1)}, bf16[256,1024]{1,0:T(8,128)(2,1)S(1)}, u32[]{:S(2)}, u32[]{:S(2)}) collective-permute-start(bf16[256,1024]{1,0:T(8,128)(2,1)S(1)} %collective-permute-done.7.down), channel_id=1, source_target_pairs={{0,64},{64,0},{1,65},{65,1},{2,66},{66,2},{3,67},{67,3},{4,68},{68... | collective-permute-start | bytes 1572872 | tf_op jit(solution)/shard_map/ppermute | solution.py:38
  68.9 3.9 %collective-permute-start.8 = (bf16[256,1024]{1,0:T(8,128)(2,1)S(1)}, bf16[256,1024]{1,0:T(8,128)(2,1)S(1)}, u32[]{:S(2)}, u32[]{:S(2)}) collective-permute-start(bf16[256,1024]{1,0:T(8,128)(2,1)S(1)} %collective-permute-done.6.up), channel_id=1, source_target_pairs={{0,64},{64,0},{1,65},{65,1},{2,66},{66,2},{3,67},{67,3},{4,68},{68... | collective-permute-start | bytes 1572872 | tf_op jit(solution)/shard_map/ppermute | solution.py:38
  75.0 30.5 %copy-start.3 = (s32[1,15]{1,0:T(1,128)S(1)}, s32[1,15]{1,0:T(1,128)}, u32[]{:S(2)}) copy-start(s32[1,15]{1,0:T(1,128)} %mask.1) | copy-start | bytes 184
  99.1 6.5 %collective-permute-start.11 = (f32[3,16,128]{2,1,0:T(8,128)S(1)}, f32[3,16,128]{2,1,0:T(8,128)S(1)}, u32[]{:S(2)}, u32[]{:S(2)}) collective-permute-start(f32[3,16,128]{2,1,0:T(8,128)S(1)} %slice.18), channel_id=1, source_target_pairs={{0,4},{4,8},{8,12},{12,16},{16,20},{20,24},{24,28},{28,32},{32,36}... | collective-permute-start | bytes 73736 | tf_op jit(solution)/shard_map/ppermute | solution.py:34
  103.6 6.9 %collective-permute-start.12 = (f32[3,16,128]{2,1,0:T(8,128)S(1)}, f32[3,16,128]{2,1,0:T(8,128)S(1)}, u32[]{:S(2)}, u32[]{:S(2)}) collective-permute-start(f32[3,16,128]{2,1,0:T(8,128)S(1)} %slice.18), channel_id=1, source_target_pairs={{4,0},{8,4},{12,8},{16,12},{20,16},{24,20},{28,24},{32,28},{36,32}... | collective-permute-start | bytes 73736 | tf_op jit(solution)/shard_map/ppermute | solution.py:34

commit v13 on v7

--- a/solution.py
+++ b/solution.py
@@ -99,16 +99,23 @@
         wide[pl.ds(pl.multiple_of(to + 16 - c * 16, 16), 16), :] = other[rows, :]
 
 
-def tile_kernel(core, up, own, down, up2, own2, down2, out, wide):
-    for i, (mine, other) in enumerate(((up, up2), (own, own2), (down, down2))):
-        interleave(core[0], mine, other, wide, i * 512)
-    for i in range(3):
+def near_kernel(core, up, own, up2, own2, out, wide):
+    interleave(core[0], up, up2, wide, 0)
+    interleave(core[0], own, own2, wide, 512)
+    for i in range(2):
         out[:, i * 512 : (i + 1) * 512] = dot_t(own[...], wide[i * 512 : (i + 1) * 512, :]).astype(BF16)
+
+
+def tile_kernel(core, near, up, own, down, up2, down2, out, wide):
+    interleave(core[0], up, up2, wide, 0)
+    interleave(core[0], down, down2, wide, 512)
+    out[:, :1024] = near[...]
+    out[:, 1024:1536] = dot_t(own[...], wide[512:1024, :]).astype(BF16)
     for x in range(4):
         rows = slice(x * HALF, (x + 1) * HALF)
         cut = 1536 + x * ROWS
         if x > 0:
-            out[rows, 1536:cut] = dot_t(up[rows, :], wide[1024 : 1024 + x * ROWS, :]).astype(BF16)
+            out[rows, 1536:cut] = dot_t(up[rows, :], wide[512 : 512 + x * ROWS, :]).astype(BF16)
         if x < 3:
             out[rows, cut:] = dot_t(down[rows, :], wide[(x + 1) * ROWS : 512, :]).astype(BF16)
 
@@ -155,10 +162,15 @@
     up = moved(own, 1)
     down = moved(own, -1)
     own2 = swapped(own)
+    up2 = swapped(up)
+    near = call(
+        near_kernel, "make_near", [SMEM] + [VMEM] * 4, (256, 1024), BF16, core, up, own, up2, own2,
+        scratch=[pltpu.VMEM((1024, 2 * COLS), BF16)],
+    )
     partial = call(
         tile_kernel, "make_tiles", [SMEM] + [VMEM] * 6, (256, SPAN * ROWS), BF16,
-        core, up, own, down, swapped(up), own2, swapped(down),
-        scratch=[pltpu.VMEM((1536, 2 * COLS), BF16)],
+        core, near, up, own, down, up2, swapped(down),
+        scratch=[pltpu.VMEM((1024, 2 * COLS), BF16)],
     )
     partial = lax.all_to_all(partial.reshape(16, 16, SPAN * ROWS), ("x", "y"), 0, 0)
     total = call(sum_kernel, "sum_parts", [VMEM], (SPAN, 16, ROWS), F32, partial)

time: 111 us -> 110 us (level)
    pallas_call x5 -> x6, Pallas kernels: 6.22 us -> 6.49 us  [call(): pl.pallas_call(kernel, in_specs=specs, out_specs=out, out_shape=jax.Shape...]
  transfers between devices with their start and end apart: 15 -> 15, of which waited for: 8 -> 8; matrix products, arithmetic and copies ran while one was open for 1% -> 1% of each run, Pallas kernels for 1% -> 2%
where the time goes in v13:
time: 110 us; the launch traced here: 109 us
  starting transfers between devices  45.5 us (41%)
  waiting for transfers between devices  28.5 us (26%)
  blocking collectives  22.8 us (21%)
  Pallas kernels  6.49 us (6%)
  local copies, waits for them, and re-layouts  4.07 us (4%)
  other arithmetic  1.69 us (2%)
    ppermute x8, starting transfers between devices, moved(): lax.ppermute(x, 'z', [(i, i + by) for i in range(n) if 0 <= i + by < n])  28 us
    ppermute x8, waiting for transfers between devices, moved(): lax.ppermute(x, 'z', [(i, i + by) for i in range(n) if 0 <= i + by < n])  22.8 us
    all_to_all x1, blocking collectives, per_device(): lax.all_to_all(partial.reshape(16, 16, SPAN * ROWS), ('x', 'y'), 0, 0)  22.8 us
    ppermute x5, starting transfers between devices, swapped(): return lax.ppermute(x, 'core', [(0, 1), (1, 0)])  9.57 us
    pallas_call x6, Pallas kernels, call(): pl.pallas_call(kernel, in_specs=specs, out_specs=out, out_shape=jax.Shape...  6.49 us
    all_to_all x1, starting transfers between devices, per_device(): plane = lax.all_to_all(pieces, 'x', 0, 0)  4.3 us
    unnamed x10, local copies, waits for them, and re-layouts  4.02 us
    all_to_all x1, starting transfers between devices, per_device(): lax.all_to_all(tiles.reshape(8, SPAN, HALF, ROWS), ('x', 'core'), 0, 0)  3.6 us
  transfers between devices with their start and end apart: 15, of which 8 were waited for; matrix products, arithmetic and copies ran while one was open for 1% of the time, Pallas kernels for 2%

profile of v13, /device:TPU:96, one launch (start us, length us, event | category | flops | bytes accessed | tf_op | source)
XLA Modules:
  0.0 109.2 jit_solution(3046260355898608221)
XLA Ops:
  0.0 1.0 copy-done.1
  1.8 4.3 %all-to-all-start.1 = ((bf16[4,64,512]{2,1,0:T(8,128)(2,1)}), bf16[4,64,512]{2,1,0:T(8,128)(2,1)S(1)}, u32[]{:S(2)}, u32[]{:S(2)}) async-start(bf16[4,64,512]{2,1,0:T(8,128)(2,1)} %cut_orbitals.1), calls=%async_computation.1 | async-start | bytes 524288 | tf_op jit(solution)/shard_map/all_to_all | solution.py:140
  6.1 1.0 copy-done.2
  7.8 0.8 cut_integrals.1
  8.6 1.3 %copy-done = bf16[4,2,15,64,128]{4,3,2,1,0:T(8,128)(2,1)} copy-done((bf16[4,2,15,64,128]{4,3,2,1,0:T(8,128)(2,1)}, bf16[4,2,15,64,128]{4,3,2,1,0:T(8,128)(2,1)S(1)}, u32[]{:S(2)}) %copy-start) | copy-done | bytes 1966104
  9.9 2.9 %all-to-all-done.1.plane = bf16[4,64,512]{2,1,0:T(8,128)(2,1)S(1)} async-done(((bf16[4,64,512]{2,1,0:T(8,128)(2,1)}), bf16[4,64,512]{2,1,0:T(8,128)(2,1)S(1)}, u32[]{:S(2)}, u32[]{:S(2)}) %all-to-all-start.1) | async-done | bytes 262176 | tf_op jit(solution)/shard_map/all_to_all | solution.py:140
  12.8 3.6 %all-to-all-start = ((bf16[8,15,64,128]{3,2,1,0:T(8,128)(2,1)}), bf16[8,15,64,128]{3,2,1,0:T(8,128)(2,1)S(1)}, u32[]{:S(2)}, u32[]{:S(2)}) async-start(bf16[8,15,64,128]{3,2,1,0:T(8,128)(2,1)} %bitcast.8), calls=%async_computation | async-start | bytes 3932160 | tf_op jit(solution)/shard_map/all_to_all | solution.py:146
  16.4 6.4 %collective-permute-start.1 = (bf16[3,64,512]{2,1,0:T(8,128)(2,1)S(1)}, bf16[3,64,512]{2,1,0:T(8,128)(2,1)S(1)}, u32[]{:S(2)}, u32[]{:S(2)}) collective-permute-start(bf16[3,64,512]{2,1,0:T(8,128)(2,1)S(1)} %get-tuple-element.10), channel_id=1, source_target_pairs={{0,8},{4,12},{8,16},{12,20},{16,24},{20,28},{24,32},{28,36},{32,40... | collective-permute-start | bytes 589832 | tf_op jit(solution)/shard_map/ppermute | solution.py:34
  22.8 1.9 %collective-permute-start.3 = (bf16[3,64,512]{2,1,0:T(8,128)(2,1)S(1)}, bf16[3,64,512]{2,1,0:T(8,128)(2,1)S(1)}, u32[]{:S(2)}, u32[]{:S(2)}) collective-permute-start(bf16[3,64,512]{2,1,0:T(8,128)(2,1)S(1)} %get-tuple-element.9), channel_id=1, source_target_pairs={{8,0},{12,4},{16,8},{20,12},{24,16},{28,20},{32,24},{36,28},{40,32... | collective-permute-start | bytes 589832 | tf_op jit(solution)/shard_map/ppermute | solution.py:34
  24.7 2.0 %collective-permute-start = (bf16[4,64,512]{2,1,0:T(8,128)(2,1)S(1)}, bf16[4,64,512]{2,1,0:T(8,128)(2,1)S(1)}, u32[]{:S(2)}, u32[]{:S(2)}) collective-permute-start(bf16[4,64,512]{2,1,0:T(8,128)(2,1)S(1)} %all-to-all-done.1.plane), channel_id=1, source_target_pairs={{4,0},{8,4},{12,8},{16,12},{20,16},{24,20},{28,24},{32,28},{36,32}... | collective-permute-start | bytes 786440 | tf_op jit(solution)/shard_map/ppermute | solution.py:34
  26.8 5.0 %collective-permute-start.2 = (bf16[4,64,512]{2,1,0:T(8,128)(2,1)S(1)}, bf16[4,64,512]{2,1,0:T(8,128)(2,1)S(1)}, u32[]{:S(2)}, u32[]{:S(2)}) collective-permute-start(bf16[4,64,512]{2,1,0:T(8,128)(2,1)S(1)} %all-to-all-done.1.plane), channel_id=1, source_target_pairs={{0,4},{4,8},{8,12},{12,16},{16,20},{20,24},{24,28},{28,32},{32,36}... | collective-permute-start | bytes 786440 | tf_op jit(solution)/shard_map/ppermute | solution.py:34
  31.8 3.9 %collective-permute-done.3.above2 = bf16[3,64,512]{2,1,0:T(8,128)(2,1)S(1)} collective-permute-done((bf16[3,64,512]{2,1,0:T(8,128)(2,1)S(1)}, bf16[3,64,512]{2,1,0:T(8,128)(2,1)S(1)}, u32[]{:S(2)}, u32[]{:S(2)}) %collective-permute-start.3) | collective-permute-done | bytes 196640 | tf_op jit(solution)/shard_map/ppermute | solution.py:34
  35.8 0.9 pad_maximum_fusion
  36.7 1.9 %collective-permute-start.4 = (bf16[10,64,512]{2,1,0:T(8,128)(2,1)}, bf16[10,64,512]{2,1,0:T(8,128)(2,1)}, u32[]{:S(2)}, u32[]{:S(2)}) collective-permute-start(bf16[10,64,512]{2,1,0:T(8,128)(2,1)} %pad_maximum_fusion), channel_id=1, source_target_pairs={{0,64},{64,0},{1,65},{65,1},{2,66},{66,2},{3,67},{67,3},{4,68},{68... | collective-permute-start | bytes 1966088 | tf_op jit(solution)/shard_map/ppermute | solution.py:38
  38.6 3.7 %collective-permute-done.above = bf16[4,64,512]{2,1,0:T(8,128)(2,1)S(1)} collective-permute-done((bf16[4,64,512]{2,1,0:T(8,128)(2,1)S(1)}, bf16[4,64,512]{2,1,0:T(8,128)(2,1)S(1)}, u32[]{:S(2)}, u32[]{:S(2)}) %collective-permute-start) | collective-permute-done | bytes 262176 | tf_op jit(solution)/shard_map/ppermute | solution.py:34
  42.3 1.9 %collective-permute-start.5 = (bf16[8,64,512]{2,1,0:T(8,128)(2,1)S(1)}, bf16[8,64,512]{2,1,0:T(8,128)(2,1)S(1)}, u32[]{:S(2)}, u32[]{:S(2)}) collective-permute-start(bf16[8,64,512]{2,1,0:T(8,128)(2,1)S(1)} %pad_maximum_fusion.1), channel_id=1, source_target_pairs={{0,64},{64,0},{1,65},{65,1},{2,66},{66,2},{3,67},{67,3},{4,68},{68... | collective-permute-start | bytes 1572872 | tf_op jit(solution)/shard_map/ppermute | solution.py:38
  44.3 1.9 %collective-permute-done.5.second = bf16[8,64,512]{2,1,0:T(8,128)(2,1)S(1)} collective-permute-done((bf16[8,64,512]{2,1,0:T(8,128)(2,1)S(1)}, bf16[8,64,512]{2,1,0:T(8,128)(2,1)S(1)}, u32[]{:S(2)}, u32[]{:S(2)}) %collective-permute-start.5) | collective-permute-done | bytes 524320 | tf_op jit(solution)/shard_map/ppermute | solution.py:38
  46.1 2.4 %make_half.1.own = bf16[256,1024]{1,0:T(8,128)(2,1)S(1)} custom-call(s32[1]{0:T(128)} %bitcast.core, bf16[8,15,64,128]{3,2,1,0:T(8,128)(2,1)S(1)} %all-to-all-done.tiles, bf16[3,64,512]{2,1,0:T(8,128)(2,1)S(1)} %collective-permute-done.1.below2, bf16[4,64,512]{2,1,0:T(8,128)(2,1)S(1)} %collective-permute-done.2.below, ...), custom_call_target="tpu_custom_call" | custom-call | tf_op jit(solution)/shard_map/make_half/pallas_call | solution.py:21
  48.5 4.9 %collective-permute-start.6 = (bf16[256,1024]{1,0:T(8,128)(2,1)S(1)}, bf16[256,1024]{1,0:T(8,128)(2,1)S(1)}, u32[]{:S(2)}, u32[]{:S(2)}) collective-permute-start(bf16[256,1024]{1,0:T(8,128)(2,1)S(1)} %make_half.1.own), channel_id=1, source_target_pairs={{0,4},{4,8},{8,12},{12,16},{16,20},{20,24},{24,28},{28,32},{32,36}... | collective-permute-start | bytes 1572872 | tf_op jit(solution)/shard_map/ppermute | solution.py:34
  53.4 1.9 %collective-permute-start.9 = (bf16[256,1024]{1,0:T(8,128)(2,1)S(1)}, bf16[256,1024]{1,0:T(8,128)(2,1)S(1)}, u32[]{:S(2)}, u32[]{:S(2)}) collective-permute-start(bf16[256,1024]{1,0:T(8,128)(2,1)S(1)} %make_half.1.own), channel_id=1, source_target_pairs={{4,0},{8,4},{12,8},{16,12},{20,16},{24,20},{28,24},{32,28},{36,32}... | collective-permute-start | bytes 1572872 | tf_op jit(solution)/shard_map/ppermute | solution.py:34
  55.3 1.9 %collective-permute-start.8 = (bf16[256,1024]{1,0:T(8,128)(2,1)S(1)}, bf16[256,1024]{1,0:T(8,128)(2,1)S(1)}, u32[]{:S(2)}, u32[]{:S(2)}) collective-permute-start(bf16[256,1024]{1,0:T(8,128)(2,1)S(1)} %make_half.1.own), channel_id=1, source_target_pairs={{0,64},{64,0},{1,65},{65,1},{2,66},{66,2},{3,67},{67,3},{4,68},{68... | collective-permute-start | bytes 1572872 | tf_op jit(solution)/shard_map/ppermute | solution.py:38
  57.3 7.6 %collective-permute-done.6.up = bf16[256,1024]{1,0:T(8,128)(2,1)S(1)} collective-permute-done((bf16[256,1024]{1,0:T(8,128)(2,1)S(1)}, bf16[256,1024]{1,0:T(8,128)(2,1)S(1)}, u32[]{:S(2)}, u32[]{:S(2)}) %collective-permute-start.6) | collective-permute-done | bytes 524320 | tf_op jit(solution)/shard_map/ppermute | solution.py:34
  64.9 1.9 %collective-permute-start.7 = (bf16[256,1024]{1,0:T(8,128)(2,1)S(1)}, bf16[256,1024]{1,0:T(8,128)(2,1)S(1)}, u32[]{:S(2)}, u32[]{:S(2)}) collective-permute-start(bf16[256,1024]{1,0:T(8,128)(2,1)S(1)} %collective-permute-done.6.up), channel_id=1, source_target_pairs={{0,64},{64,0},{1,65},{65,1},{2,66},{66,2},{3,67},{67,3},{4,68},{68... | collective-permute-start | bytes 1572872 | tf_op jit(solution)/shard_map/ppermute | solution.py:38
  66.8 3.4 %collective-permute-done.9.down = bf16[256,1024]{1,0:T(8,128)(2,1)S(1)} collective-permute-done((bf16[256,1024]{1,0:T(8,128)(2,1)S(1)}, bf16[256,1024]{1,0:T(8,128)(2,1)S(1)}, u32[]{:S(2)}, u32[]{:S(2)}) %collective-permute-start.9) | collective-permute-done | bytes 524320 | tf_op jit(solution)/shard_map/ppermute | solution.py:34
  70.2 1.9 %collective-permute-start.10 = (bf16[256,1024]{1,0:T(8,128)(2,1)S(1)}, bf16[256,1024]{1,0:T(8,128)(2,1)S(1)}, u32[]{:S(2)}, u32[]{:S(2)}) collective-permute-start(bf16[256,1024]{1,0:T(8,128)(2,1)S(1)} %collective-permute-done.9.down), channel_id=1, source_target_pairs={{0,64},{64,0},{1,65},{65,1},{2,66},{66,2},{3,67},{67,3},{4,68},{68... | collective-permute-start | bytes 1572872 | tf_op jit(solution)/shard_map/ppermute | solution.py:38
  72.1 0.9 make_near.1.near
  73.0 1.0 collective-permute-done.10.down2
  74.0 1.5 %make_tiles.1 = bf16[256,1920]{1,0:T(8,128)(2,1)S(1)} custom-call(s32[1]{0:T(128)} %bitcast.core, bf16[256,1024]{1,0:T(8,128)(2,1)S(1)} %make_near.1.near, bf16[256,1024]{1,0:T(8,128)(2,1)S(1)} %collective-permute-done.6.up, bf16[256,1024]{1,0:T(8,128)(2,1)S(1)} %make_half.1.own, bf16[256,1024]{1,0:T(8,128)(2,1)S(1)} %collective-permute-done.9.down, ...), custom_call_target="tpu_custom_call" | custom-call | tf_op jit(solution)/shard_map/make_tiles/pallas_call | solution.py:21
  75.5 22.8 %all_to_all.15.parts = bf16[16,16,1920]{2,1,0:T(8,128)(2,1)S(1)} all-to-all(bf16[16,16,1920]{2,1,0:T(8,128)(2,1)S(1)} %bitcast.9), channel_id=1, replica_groups=mesh['y'=4,'core'=2,'z'=16,'x'=4] {'x','y'}, dimensions={0} | all-to-all | bytes 1966080 | tf_op jit(solution)/shard_map/all_to_all | solution.py:175
  98.4 3.1 %collective-permute-start.11 = (f32[3,16,128]{2,1,0:T(8,128)S(1)}, f32[3,16,128]{2,1,0:T(8,128)S(1)}, u32[]{:S(2)}, u32[]{:S(2)}) collective-permute-start(f32[3,16,128]{2,1,0:T(8,128)S(1)} %slice.18), channel_id=1, source_target_pairs={{0,4},{4,8},{8,12},{12,16},{16,20},{20,24},{24,28},{28,32},{32,36}... | collective-permute-start | bytes 73736 | tf_op jit(solution)/shard_map/ppermute | solution.py:34
  101.6 2.7 %collective-permute-start.12 = (f32[3,16,128]{2,1,0:T(8,128)S(1)}, f32[3,16,128]{2,1,0:T(8,128)S(1)}, u32[]{:S(2)}, u32[]{:S(2)}) collective-permute-start(f32[3,16,128]{2,1,0:T(8,128)S(1)} %slice.18), channel_id=1, source_target_pairs={{4,0},{8,4},{12,8},{16,12},{20,16},{24,20},{28,24},{32,28},{36,32}... | collective-permute-start | bytes 73736 | tf_op jit(solution)/shard_map/ppermute | solution.py:34
  104.4 4.2 %collective-permute-done.12 = f32[3,16,128]{2,1,0:T(8,128)S(1)} collective-permute-done((f32[3,16,128]{2,1,0:T(8,128)S(1)}, f32[3,16,128]{2,1,0:T(8,128)S(1)}, u32[]{:S(2)}, u32[]{:S(2)}) %collective-permute-start.12) | collective-permute-done | bytes 24608 | tf_op jit(solution)/shard_map/ppermute | solution.py:34
  (22 shorter events, 2.4 us)
Async XLA Ops:
  0.0 1.0 copy-start.1
  1.8 11.0 %all-to-all-start.1 = ((bf16[4,64,512]{2,1,0:T(8,128)(2,1)}), bf16[4,64,512]{2,1,0:T(8,128)(2,1)S(1)}, u32[]{:S(2)}, u32[]{:S(2)}) async-start(bf16[4,64,512]{2,1,0:T(8,128)(2,1)} %cut_orbitals.1), calls=%async_computation.1 | async-start | bytes 524288 | tf_op jit(solution)/shard_map/all_to_all | solution.py:140
  6.1 1.0 copy-start.2
  7.1 0.7 copy-start.3
  8.6 1.3 %copy-start = (bf16[4,2,15,64,128]{4,3,2,1,0:T(8,128)(2,1)}, bf16[4,2,15,64,128]{4,3,2,1,0:T(8,128)(2,1)S(1)}, u32[]{:S(2)}) copy-start(bf16[4,2,15,64,128]{4,3,2,1,0:T(8,128)(2,1)S(1)} %cut_integrals.1) | copy-start | bytes 5898244
  12.8 29.5 %all-to-all-start = ((bf16[8,15,64,128]{3,2,1,0:T(8,128)(2,1)}), bf16[8,15,64,128]{3,2,1,0:T(8,128)(2,1)S(1)}, u32[]{:S(2)}, u32[]{:S(2)}) async-start(bf16[8,15,64,128]{3,2,1,0:T(8,128)(2,1)} %bitcast.8), calls=%async_computation | async-start | bytes 3932160 | tf_op jit(solution)/shard_map/all_to_all | solution.py:146
  16.4 15.4 %collective-permute-start.1 = (bf16[3,64,512]{2,1,0:T(8,128)(2,1)S(1)}, bf16[3,64,512]{2,1,0:T(8,128)(2,1)S(1)}, u32[]{:S(2)}, u32[]{:S(2)}) collective-permute-start(bf16[3,64,512]{2,1,0:T(8,128)(2,1)S(1)} %get-tuple-element.10), channel_id=1, source_target_pairs={{0,8},{4,12},{8,16},{12,20},{16,24},{20,28},{24,32},{28,36},{32,40... | collective-permute-start | bytes 589832 | tf_op jit(solution)/shard_map/ppermute | solution.py:34
  22.8 12.9 %collective-permute-start.3 = (bf16[3,64,512]{2,1,0:T(8,128)(2,1)S(1)}, bf16[3,64,512]{2,1,0:T(8,128)(2,1)S(1)}, u32[]{:S(2)}, u32[]{:S(2)}) collective-permute-start(bf16[3,64,512]{2,1,0:T(8,128)(2,1)S(1)} %get-tuple-element.9), channel_id=1, source_target_pairs={{8,0},{12,4},{16,8},{20,12},{24,16},{28,20},{32,24},{36,28},{40,32... | collective-permute-start | bytes 589832 | tf_op jit(solution)/shard_map/ppermute | solution.py:34
  24.7 17.5 %collective-permute-start = (bf16[4,64,512]{2,1,0:T(8,128)(2,1)S(1)}, bf16[4,64,512]{2,1,0:T(8,128)(2,1)S(1)}, u32[]{:S(2)}, u32[]{:S(2)}) collective-permute-start(bf16[4,64,512]{2,1,0:T(8,128)(2,1)S(1)} %all-to-all-done.1.plane), channel_id=1, source_target_pairs={{4,0},{8,4},{12,8},{16,12},{20,16},{24,20},{28,24},{32,28},{36,32}... | collective-permute-start | bytes 786440 | tf_op jit(solution)/shard_map/ppermute | solution.py:34
  26.8 15.5 %collective-permute-start.2 = (bf16[4,64,512]{2,1,0:T(8,128)(2,1)S(1)}, bf16[4,64,512]{2,1,0:T(8,128)(2,1)S(1)}, u32[]{:S(2)}, u32[]{:S(2)}) collective-permute-start(bf16[4,64,512]{2,1,0:T(8,128)(2,1)S(1)} %all-to-all-done.1.plane), channel_id=1, source_target_pairs={{0,4},{4,8},{8,12},{12,16},{16,20},{20,24},{24,28},{28,32},{32,36}... | collective-permute-start | bytes 786440 | tf_op jit(solution)/shard_map/ppermute | solution.py:34
  36.7 7.6 %collective-permute-start.4 = (bf16[10,64,512]{2,1,0:T(8,128)(2,1)}, bf16[10,64,512]{2,1,0:T(8,128)(2,1)}, u32[]{:S(2)}, u32[]{:S(2)}) collective-permute-start(bf16[10,64,512]{2,1,0:T(8,128)(2,1)} %pad_maximum_fusion), channel_id=1, source_target_pairs={{0,64},{64,0},{1,65},{65,1},{2,66},{66,2},{3,67},{67,3},{4,68},{68... | collective-permute-start | bytes 1966088 | tf_op jit(solution)/shard_map/ppermute | solution.py:38
  42.3 3.8 %collective-permute-start.5 = (bf16[8,64,512]{2,1,0:T(8,128)(2,1)S(1)}, bf16[8,64,512]{2,1,0:T(8,128)(2,1)S(1)}, u32[]{:S(2)}, u32[]{:S(2)}) collective-permute-start(bf16[8,64,512]{2,1,0:T(8,128)(2,1)S(1)} %pad_maximum_fusion.1), channel_id=1, source_target_pairs={{0,64},{64,0},{1,65},{65,1},{2,66},{66,2},{3,67},{67,3},{4,68},{68... | collective-permute-start | bytes 1572872 | tf_op jit(solution)/shard_map/ppermute | solution.py:38
  48.5 16.3 %collective-permute-start.6 = (bf16[256,1024]{1,0:T(8,128)(2,1)S(1)}, bf16[256,1024]{1,0:T(8,128)(2,1)S(1)}, u32[]{:S(2)}, u32[]{:S(2)}) collective-permute-start(bf16[256,1024]{1,0:T(8,128)(2,1)S(1)} %make_half.1.own), channel_id=1, source_target_pairs={{0,4},{4,8},{8,12},{12,16},{16,20},{20,24},{24,28},{28,32},{32,36}... | collective-permute-start | bytes 1572872 | tf_op jit(solution)/shard_map/ppermute | solution.py:34
  53.4 16.8 %collective-permute-start.9 = (bf16[256,1024]{1,0:T(8,128)(2,1)S(1)}, bf16[256,1024]{1,0:T(8,128)(2,1)S(1)}, u32[]{:S(2)}, u32[]{:S(2)}) collective-permute-start(bf16[256,1024]{1,0:T(8,128)(2,1)S(1)} %make_half.1.own), channel_id=1, source_target_pairs={{4,0},{8,4},{12,8},{16,12},{20,16},{24,20},{28,24},{32,28},{36,32}... | collective-permute-start | bytes 1572872 | tf_op jit(solution)/shard_map/ppermute | solution.py:34
  55.3 16.8 %collective-permute-start.8 = (bf16[256,1024]{1,0:T(8,128)(2,1)S(1)}, bf16[256,1024]{1,0:T(8,128)(2,1)S(1)}, u32[]{:S(2)}, u32[]{:S(2)}) collective-permute-start(bf16[256,1024]{1,0:T(8,128)(2,1)S(1)} %make_half.1.own), channel_id=1, source_target_pairs={{0,64},{64,0},{1,65},{65,1},{2,66},{66,2},{3,67},{67,3},{4,68},{68... | collective-permute-start | bytes 1572872 | tf_op jit(solution)/shard_map/ppermute | solution.py:38
  64.9 7.3 %collective-permute-start.7 = (bf16[256,1024]{1,0:T(8,128)(2,1)S(1)}, bf16[256,1024]{1,0:T(8,128)(2,1)S(1)}, u32[]{:S(2)}, u32[]{:S(2)}) collective-permute-start(bf16[256,1024]{1,0:T(8,128)(2,1)S(1)} %collective-permute-done.6.up), channel_id=1, source_target_pairs={{0,64},{64,0},{1,65},{65,1},{2,66},{66,2},{3,67},{67,3},{4,68},{68... | collective-permute-start | bytes 1572872 | tf_op jit(solution)/shard_map/ppermute | solution.py:38
  70.2 3.8 %collective-permute-start.10 = (bf16[256,1024]{1,0:T(8,128)(2,1)S(1)}, bf16[256,1024]{1,0:T(8,128)(2,1)S(1)}, u32[]{:S(2)}, u32[]{:S(2)}) collective-permute-start(bf16[256,1024]{1,0:T(8,128)(2,1)S(1)} %collective-permute-done.9.down), channel_id=1, source_target_pairs={{0,64},{64,0},{1,65},{65,1},{2,66},{66,2},{3,67},{67,3},{4,68},{68... | collective-permute-start | bytes 1572872 | tf_op jit(solution)/shard_map/ppermute | solution.py:38
  75.5 28.8 %copy-start.4 = (s32[1,15]{1,0:T(1,128)S(1)}, s32[1,15]{1,0:T(1,128)}, u32[]{:S(2)}) copy-start(s32[1,15]{1,0:T(1,128)} %mask.1) | copy-start | bytes 184
  98.4 5.9 %collective-permute-start.11 = (f32[3,16,128]{2,1,0:T(8,128)S(1)}, f32[3,16,128]{2,1,0:T(8,128)S(1)}, u32[]{:S(2)}, u32[]{:S(2)}) collective-permute-start(f32[3,16,128]{2,1,0:T(8,128)S(1)} %slice.18), channel_id=1, source_target_pairs={{0,4},{4,8},{8,12},{12,16},{16,20},{20,24},{24,28},{28,32},{32,36}... | collective-permute-start | bytes 73736 | tf_op jit(solution)/shard_map/ppermute | solution.py:34
  101.6 6.9 %collective-permute-start.12 = (f32[3,16,128]{2,1,0:T(8,128)S(1)}, f32[3,16,128]{2,1,0:T(8,128)S(1)}, u32[]{:S(2)}, u32[]{:S(2)}) collective-permute-start(f32[3,16,128]{2,1,0:T(8,128)S(1)} %slice.18), channel_id=1, source_target_pairs={{4,0},{8,4},{12,8},{16,12},{20,16},{24,20},{28,24},{32,28},{36,32}... | collective-permute-start | bytes 73736 | tf_op jit(solution)/shard_map/ppermute | solution.py:34

commit v14 on v13

--- a/solution.py
+++ b/solution.py
@@ -58,7 +58,7 @@
             for k in range(4):
                 at = k * 32 + core * 16
                 for x in range(4):
-                    out[x, core, s, k * 16 : k * 16 + 16, :] = tile[at : at + 16]
+                    out[core, x, s, k * 16 : k * 16 + 16, :] = tile[at : at + 16]
 
 
 def half_kernel(core, tiles, below2, below, plane, above, above2, first, second, half, window, sems):
@@ -80,7 +80,7 @@
     for a in range(4):
         near = window[a : a + SPAN].reshape(SPAN * ROWS, COLS)
         wide = jnp.concatenate(
-            [tiles[2 * a : 2 * a + 2, s].reshape(2 * HALF, ROWS) for s in range(SPAN)], 1
+            [jnp.concatenate([tiles[a, s], tiles[4 + a, s]], 0) for s in range(SPAN)], 1
         )
         made = jnp.dot(wide, near, preferred_element_type=F32).astype(BF16)
         half[a * HALF : (a + 1) * HALF, :COLS] = made[:HALF]
@@ -140,10 +140,10 @@
     plane = lax.all_to_all(pieces, "x", 0, 0)
 
     tiles = call(
-        integral_kernel, "cut_integrals", [SMEM, VMEM], (4, 2, SPAN, HALF, ROWS), BF16,
+        integral_kernel, "cut_integrals", [SMEM, VMEM], (2, 4, SPAN, HALF, ROWS), BF16,
         pair_mask, integrals[0, 0],
     )
-    tiles = lax.all_to_all(tiles.reshape(8, SPAN, HALF, ROWS), ("x", "core"), 0, 0)
+    tiles = lax.all_to_all(tiles.reshape(8, SPAN, HALF, ROWS), ("core", "x"), 0, 0)
 
     below2 = moved(plane[1:], 2)
     above2 = moved(plane[:3], -2)

time: 110 us -> 110 us (level)
  no operation moved by 1% of the time
where the time goes in v14:
time: 110 us; the launch traced here: 109 us
  starting transfers between devices  44.9 us (41%)
  waiting for transfers between devices  28.5 us (26%)
  blocking collectives  23.3 us (21%)
  Pallas kernels  6.5 us (6%)
  local copies, waits for them, and re-layouts  4.07 us (4%)
  other arithmetic  1.69 us (2%)
    ppermute x8, starting transfers between devices, moved(): lax.ppermute(x, 'z', [(i, i + by) for i in range(n) if 0 <= i + by < n])  27.4 us
    all_to_all x1, blocking collectives, per_device(): lax.all_to_all(partial.reshape(16, 16, SPAN * ROWS), ('x', 'y'), 0, 0)  23.3 us
    ppermute x8, waiting for transfers between devices, moved(): lax.ppermute(x, 'z', [(i, i + by) for i in range(n) if 0 <= i + by < n])  22.8 us
    ppermute x5, starting transfers between devices, swapped(): return lax.ppermute(x, 'core', [(0, 1), (1, 0)])  9.57 us
    pallas_call x6, Pallas kernels, call(): pl.pallas_call(kernel, in_specs=specs, out_specs=out, out_shape=jax.Shape...  6.5 us
    all_to_all x1, starting transfers between devices, per_device(): plane = lax.all_to_all(pieces, 'x', 0, 0)  4.3 us
    unnamed x10, local copies, waits for them, and re-layouts  4.02 us
    all_to_all x1, starting transfers between devices, per_device(): lax.all_to_all(tiles.reshape(8, SPAN, HALF, ROWS), ('core', 'x'), 0, 0)  3.6 us
  transfers between devices with their start and end apart: 15, of which 8 were waited for; matrix products, arithmetic and copies ran while one was open for 1% of the time, Pallas kernels for 2%

profile of v14, /device:TPU:96, one launch (start us, length us, event | category | flops | bytes accessed | tf_op | source)
XLA Modules:
  0.0 109.2 jit_solution(16112682479996706161)
XLA Ops:
  0.0 1.0 copy-done.1
  1.8 4.3 %all-to-all-start.1 = ((bf16[4,64,512]{2,1,0:T(8,128)(2,1)}), bf16[4,64,512]{2,1,0:T(8,128)(2,1)S(1)}, u32[]{:S(2)}, u32[]{:S(2)}) async-start(bf16[4,64,512]{2,1,0:T(8,128)(2,1)} %cut_orbitals.1), calls=%async_computation.1 | async-start | bytes 524288 | tf_op jit(solution)/shard_map/all_to_all | solution.py:140
  6.1 1.0 copy-done.2
  7.8 0.8 cut_integrals.1
  8.6 1.3 %copy-done = bf16[2,4,15,64,128]{4,3,2,1,0:T(8,128)(2,1)} copy-done((bf16[2,4,15,64,128]{4,3,2,1,0:T(8,128)(2,1)}, bf16[2,4,15,64,128]{4,3,2,1,0:T(8,128)(2,1)S(1)}, u32[]{:S(2)}) %copy-start) | copy-done | bytes 1966104
  9.9 2.9 %all-to-all-done.1.plane = bf16[4,64,512]{2,1,0:T(8,128)(2,1)S(1)} async-done(((bf16[4,64,512]{2,1,0:T(8,128)(2,1)}), bf16[4,64,512]{2,1,0:T(8,128)(2,1)S(1)}, u32[]{:S(2)}, u32[]{:S(2)}) %all-to-all-start.1) | async-done | bytes 262176 | tf_op jit(solution)/shard_map/all_to_all | solution.py:140
  12.8 3.6 %all-to-all-start = ((bf16[8,15,64,128]{3,2,1,0:T(8,128)(2,1)}), bf16[8,15,64,128]{3,2,1,0:T(8,128)(2,1)S(1)}, u32[]{:S(2)}, u32[]{:S(2)}) async-start(bf16[8,15,64,128]{3,2,1,0:T(8,128)(2,1)} %bitcast.8), calls=%async_computation | async-start | bytes 3932160 | tf_op jit(solution)/shard_map/all_to_all | solution.py:146
  16.4 6.4 %collective-permute-start.1 = (bf16[3,64,512]{2,1,0:T(8,128)(2,1)S(1)}, bf16[3,64,512]{2,1,0:T(8,128)(2,1)S(1)}, u32[]{:S(2)}, u32[]{:S(2)}) collective-permute-start(bf16[3,64,512]{2,1,0:T(8,128)(2,1)S(1)} %get-tuple-element.10), channel_id=1, source_target_pairs={{0,8},{4,12},{8,16},{12,20},{16,24},{20,28},{24,32},{28,36},{32,40... | collective-permute-start | bytes 589832 | tf_op jit(solution)/shard_map/ppermute | solution.py:34
  22.8 1.9 %collective-permute-start.3 = (bf16[3,64,512]{2,1,0:T(8,128)(2,1)S(1)}, bf16[3,64,512]{2,1,0:T(8,128)(2,1)S(1)}, u32[]{:S(2)}, u32[]{:S(2)}) collective-permute-start(bf16[3,64,512]{2,1,0:T(8,128)(2,1)S(1)} %get-tuple-element.9), channel_id=1, source_target_pairs={{8,0},{12,4},{16,8},{20,12},{24,16},{28,20},{32,24},{36,28},{40,32... | collective-permute-start | bytes 589832 | tf_op jit(solution)/shard_map/ppermute | solution.py:34
  24.7 2.0 %collective-permute-start = (bf16[4,64,512]{2,1,0:T(8,128)(2,1)S(1)}, bf16[4,64,512]{2,1,0:T(8,128)(2,1)S(1)}, u32[]{:S(2)}, u32[]{:S(2)}) collective-permute-start(bf16[4,64,512]{2,1,0:T(8,128)(2,1)S(1)} %all-to-all-done.1.plane), channel_id=1, source_target_pairs={{4,0},{8,4},{12,8},{16,12},{20,16},{24,20},{28,24},{32,28},{36,32}... | collective-permute-start | bytes 786440 | tf_op jit(solution)/shard_map/ppermute | solution.py:34
  26.8 5.0 %collective-permute-start.2 = (bf16[4,64,512]{2,1,0:T(8,128)(2,1)S(1)}, bf16[4,64,512]{2,1,0:T(8,128)(2,1)S(1)}, u32[]{:S(2)}, u32[]{:S(2)}) collective-permute-start(bf16[4,64,512]{2,1,0:T(8,128)(2,1)S(1)} %all-to-all-done.1.plane), channel_id=1, source_target_pairs={{0,4},{4,8},{8,12},{12,16},{16,20},{20,24},{24,28},{28,32},{32,36}... | collective-permute-start | bytes 786440 | tf_op jit(solution)/shard_map/ppermute | solution.py:34
  31.8 3.9 %collective-permute-done.3.above2 = bf16[3,64,512]{2,1,0:T(8,128)(2,1)S(1)} collective-permute-done((bf16[3,64,512]{2,1,0:T(8,128)(2,1)S(1)}, bf16[3,64,512]{2,1,0:T(8,128)(2,1)S(1)}, u32[]{:S(2)}, u32[]{:S(2)}) %collective-permute-start.3) | collective-permute-done | bytes 196640 | tf_op jit(solution)/shard_map/ppermute | solution.py:34
  35.8 0.9 pad_maximum_fusion
  36.7 1.9 %collective-permute-start.4 = (bf16[10,64,512]{2,1,0:T(8,128)(2,1)}, bf16[10,64,512]{2,1,0:T(8,128)(2,1)}, u32[]{:S(2)}, u32[]{:S(2)}) collective-permute-start(bf16[10,64,512]{2,1,0:T(8,128)(2,1)} %pad_maximum_fusion), channel_id=1, source_target_pairs={{0,64},{64,0},{1,65},{65,1},{2,66},{66,2},{3,67},{67,3},{4,68},{68... | collective-permute-start | bytes 1966088 | tf_op jit(solution)/shard_map/ppermute | solution.py:38
  38.6 3.7 %collective-permute-done.above = bf16[4,64,512]{2,1,0:T(8,128)(2,1)S(1)} collective-permute-done((bf16[4,64,512]{2,1,0:T(8,128)(2,1)S(1)}, bf16[4,64,512]{2,1,0:T(8,128)(2,1)S(1)}, u32[]{:S(2)}, u32[]{:S(2)}) %collective-permute-start) | collective-permute-done | bytes 262176 | tf_op jit(solution)/shard_map/ppermute | solution.py:34
  42.3 1.9 %collective-permute-start.5 = (bf16[8,64,512]{2,1,0:T(8,128)(2,1)S(1)}, bf16[8,64,512]{2,1,0:T(8,128)(2,1)S(1)}, u32[]{:S(2)}, u32[]{:S(2)}) collective-permute-start(bf16[8,64,512]{2,1,0:T(8,128)(2,1)S(1)} %pad_maximum_fusion.1), channel_id=1, source_target_pairs={{0,64},{64,0},{1,65},{65,1},{2,66},{66,2},{3,67},{67,3},{4,68},{68... | collective-permute-start | bytes 1572872 | tf_op jit(solution)/shard_map/ppermute | solution.py:38
  44.3 1.9 %collective-permute-done.5.second = bf16[8,64,512]{2,1,0:T(8,128)(2,1)S(1)} collective-permute-done((bf16[8,64,512]{2,1,0:T(8,128)(2,1)S(1)}, bf16[8,64,512]{2,1,0:T(8,128)(2,1)S(1)}, u32[]{:S(2)}, u32[]{:S(2)}) %collective-permute-start.5) | collective-permute-done | bytes 524320 | tf_op jit(solution)/shard_map/ppermute | solution.py:38
  46.1 2.4 %make_half.1.own = bf16[256,1024]{1,0:T(8,128)(2,1)S(1)} custom-call(s32[1]{0:T(128)} %bitcast.core, bf16[8,15,64,128]{3,2,1,0:T(8,128)(2,1)S(1)} %all-to-all-done.tiles, bf16[3,64,512]{2,1,0:T(8,128)(2,1)S(1)} %collective-permute-done.1.below2, bf16[4,64,512]{2,1,0:T(8,128)(2,1)S(1)} %collective-permute-done.2.below, ...), custom_call_target="tpu_custom_call" | custom-call | tf_op jit(solution)/shard_map/make_half/pallas_call | solution.py:21
  48.5 4.3 %collective-permute-start.6 = (bf16[256,1024]{1,0:T(8,128)(2,1)S(1)}, bf16[256,1024]{1,0:T(8,128)(2,1)S(1)}, u32[]{:S(2)}, u32[]{:S(2)}) collective-permute-start(bf16[256,1024]{1,0:T(8,128)(2,1)S(1)} %make_half.1.own), channel_id=1, source_target_pairs={{0,4},{4,8},{8,12},{12,16},{16,20},{20,24},{24,28},{28,32},{32,36}... | collective-permute-start | bytes 1572872 | tf_op jit(solution)/shard_map/ppermute | solution.py:34
  52.8 1.9 %collective-permute-start.9 = (bf16[256,1024]{1,0:T(8,128)(2,1)S(1)}, bf16[256,1024]{1,0:T(8,128)(2,1)S(1)}, u32[]{:S(2)}, u32[]{:S(2)}) collective-permute-start(bf16[256,1024]{1,0:T(8,128)(2,1)S(1)} %make_half.1.own), channel_id=1, source_target_pairs={{4,0},{8,4},{12,8},{16,12},{20,16},{24,20},{28,24},{32,28},{36,32}... | collective-permute-start | bytes 1572872 | tf_op jit(solution)/shard_map/ppermute | solution.py:34
  54.7 1.9 %collective-permute-start.8 = (bf16[256,1024]{1,0:T(8,128)(2,1)S(1)}, bf16[256,1024]{1,0:T(8,128)(2,1)S(1)}, u32[]{:S(2)}, u32[]{:S(2)}) collective-permute-start(bf16[256,1024]{1,0:T(8,128)(2,1)S(1)} %make_half.1.own), channel_id=1, source_target_pairs={{0,64},{64,0},{1,65},{65,1},{2,66},{66,2},{3,67},{67,3},{4,68},{68... | collective-permute-start | bytes 1572872 | tf_op jit(solution)/shard_map/ppermute | solution.py:38
  56.7 7.7 %collective-permute-done.6.up = bf16[256,1024]{1,0:T(8,128)(2,1)S(1)} collective-permute-done((bf16[256,1024]{1,0:T(8,128)(2,1)S(1)}, bf16[256,1024]{1,0:T(8,128)(2,1)S(1)}, u32[]{:S(2)}, u32[]{:S(2)}) %collective-permute-start.6) | collective-permute-done | bytes 524320 | tf_op jit(solution)/shard_map/ppermute | solution.py:34
  64.4 1.9 %collective-permute-start.7 = (bf16[256,1024]{1,0:T(8,128)(2,1)S(1)}, bf16[256,1024]{1,0:T(8,128)(2,1)S(1)}, u32[]{:S(2)}, u32[]{:S(2)}) collective-permute-start(bf16[256,1024]{1,0:T(8,128)(2,1)S(1)} %collective-permute-done.6.up), channel_id=1, source_target_pairs={{0,64},{64,0},{1,65},{65,1},{2,66},{66,2},{3,67},{67,3},{4,68},{68... | collective-permute-start | bytes 1572872 | tf_op jit(solution)/shard_map/ppermute | solution.py:38
  66.3 3.3 %collective-permute-done.9.down = bf16[256,1024]{1,0:T(8,128)(2,1)S(1)} collective-permute-done((bf16[256,1024]{1,0:T(8,128)(2,1)S(1)}, bf16[256,1024]{1,0:T(8,128)(2,1)S(1)}, u32[]{:S(2)}, u32[]{:S(2)}) %collective-permute-start.9) | collective-permute-done | bytes 524320 | tf_op jit(solution)/shard_map/ppermute | solution.py:34
  69.6 1.9 %collective-permute-start.10 = (bf16[256,1024]{1,0:T(8,128)(2,1)S(1)}, bf16[256,1024]{1,0:T(8,128)(2,1)S(1)}, u32[]{:S(2)}, u32[]{:S(2)}) collective-permute-start(bf16[256,1024]{1,0:T(8,128)(2,1)S(1)} %collective-permute-done.9.down), channel_id=1, source_target_pairs={{0,64},{64,0},{1,65},{65,1},{2,66},{66,2},{3,67},{67,3},{4,68},{68... | collective-permute-start | bytes 1572872 | tf_op jit(solution)/shard_map/ppermute | solution.py:38
  71.5 0.9 make_near.1.near
  72.4 1.0 collective-permute-done.10.down2
  73.4 1.5 %make_tiles.1 = bf16[256,1920]{1,0:T(8,128)(2,1)S(1)} custom-call(s32[1]{0:T(128)} %bitcast.core, bf16[256,1024]{1,0:T(8,128)(2,1)S(1)} %make_near.1.near, bf16[256,1024]{1,0:T(8,128)(2,1)S(1)} %collective-permute-done.6.up, bf16[256,1024]{1,0:T(8,128)(2,1)S(1)} %make_half.1.own, bf16[256,1024]{1,0:T(8,128)(2,1)S(1)} %collective-permute-done.9.down, ...), custom_call_target="tpu_custom_call" | custom-call | tf_op jit(solution)/shard_map/make_tiles/pallas_call | solution.py:21
  74.9 23.3 %all_to_all.15.parts = bf16[16,16,1920]{2,1,0:T(8,128)(2,1)S(1)} all-to-all(bf16[16,16,1920]{2,1,0:T(8,128)(2,1)S(1)} %bitcast.9), channel_id=1, replica_groups=mesh['y'=4,'core'=2,'z'=16,'x'=4] {'x','y'}, dimensions={0} | all-to-all | bytes 1966080 | tf_op jit(solution)/shard_map/all_to_all | solution.py:175
  98.4 3.1 %collective-permute-start.11 = (f32[3,16,128]{2,1,0:T(8,128)S(1)}, f32[3,16,128]{2,1,0:T(8,128)S(1)}, u32[]{:S(2)}, u32[]{:S(2)}) collective-permute-start(f32[3,16,128]{2,1,0:T(8,128)S(1)} %slice.18), channel_id=1, source_target_pairs={{0,4},{4,8},{8,12},{12,16},{16,20},{20,24},{24,28},{28,32},{32,36}... | collective-permute-start | bytes 73736 | tf_op jit(solution)/shard_map/ppermute | solution.py:34
  101.6 2.7 %collective-permute-start.12 = (f32[3,16,128]{2,1,0:T(8,128)S(1)}, f32[3,16,128]{2,1,0:T(8,128)S(1)}, u32[]{:S(2)}, u32[]{:S(2)}) collective-permute-start(f32[3,16,128]{2,1,0:T(8,128)S(1)} %slice.18), channel_id=1, source_target_pairs={{4,0},{8,4},{12,8},{16,12},{20,16},{24,20},{28,24},{32,28},{36,32}... | collective-permute-start | bytes 73736 | tf_op jit(solution)/shard_map/ppermute | solution.py:34
  104.3 4.2 %collective-permute-done.12 = f32[3,16,128]{2,1,0:T(8,128)S(1)} collective-permute-done((f32[3,16,128]{2,1,0:T(8,128)S(1)}, f32[3,16,128]{2,1,0:T(8,128)S(1)}, u32[]{:S(2)}, u32[]{:S(2)}) %collective-permute-start.12) | collective-permute-done | bytes 24608 | tf_op jit(solution)/shard_map/ppermute | solution.py:34
  (22 shorter events, 2.4 us)
Async XLA Ops:
  0.0 1.0 copy-start.1
  1.8 11.0 %all-to-all-start.1 = ((bf16[4,64,512]{2,1,0:T(8,128)(2,1)}), bf16[4,64,512]{2,1,0:T(8,128)(2,1)S(1)}, u32[]{:S(2)}, u32[]{:S(2)}) async-start(bf16[4,64,512]{2,1,0:T(8,128)(2,1)} %cut_orbitals.1), calls=%async_computation.1 | async-start | bytes 524288 | tf_op jit(solution)/shard_map/all_to_all | solution.py:140
  6.1 1.0 copy-start.2
  7.1 0.7 copy-start.3
  8.6 1.3 %copy-start = (bf16[2,4,15,64,128]{4,3,2,1,0:T(8,128)(2,1)}, bf16[2,4,15,64,128]{4,3,2,1,0:T(8,128)(2,1)S(1)}, u32[]{:S(2)}) copy-start(bf16[2,4,15,64,128]{4,3,2,1,0:T(8,128)(2,1)S(1)} %cut_integrals.1) | copy-start | bytes 5898244
  12.8 29.5 %all-to-all-start = ((bf16[8,15,64,128]{3,2,1,0:T(8,128)(2,1)}), bf16[8,15,64,128]{3,2,1,0:T(8,128)(2,1)S(1)}, u32[]{:S(2)}, u32[]{:S(2)}) async-start(bf16[8,15,64,128]{3,2,1,0:T(8,128)(2,1)} %bitcast.8), calls=%async_computation | async-start | bytes 3932160 | tf_op jit(solution)/shard_map/all_to_all | solution.py:146
  16.4 15.4 %collective-permute-start.1 = (bf16[3,64,512]{2,1,0:T(8,128)(2,1)S(1)}, bf16[3,64,512]{2,1,0:T(8,128)(2,1)S(1)}, u32[]{:S(2)}, u32[]{:S(2)}) collective-permute-start(bf16[3,64,512]{2,1,0:T(8,128)(2,1)S(1)} %get-tuple-element.10), channel_id=1, source_target_pairs={{0,8},{4,12},{8,16},{12,20},{16,24},{20,28},{24,32},{28,36},{32,40... | collective-permute-start | bytes 589832 | tf_op jit(solution)/shard_map/ppermute | solution.py:34
  22.8 12.9 %collective-permute-start.3 = (bf16[3,64,512]{2,1,0:T(8,128)(2,1)S(1)}, bf16[3,64,512]{2,1,0:T(8,128)(2,1)S(1)}, u32[]{:S(2)}, u32[]{:S(2)}) collective-permute-start(bf16[3,64,512]{2,1,0:T(8,128)(2,1)S(1)} %get-tuple-element.9), channel_id=1, source_target_pairs={{8,0},{12,4},{16,8},{20,12},{24,16},{28,20},{32,24},{36,28},{40,32... | collective-permute-start | bytes 589832 | tf_op jit(solution)/shard_map/ppermute | solution.py:34
  24.7 17.5 %collective-permute-start = (bf16[4,64,512]{2,1,0:T(8,128)(2,1)S(1)}, bf16[4,64,512]{2,1,0:T(8,128)(2,1)S(1)}, u32[]{:S(2)}, u32[]{:S(2)}) collective-permute-start(bf16[4,64,512]{2,1,0:T(8,128)(2,1)S(1)} %all-to-all-done.1.plane), channel_id=1, source_target_pairs={{4,0},{8,4},{12,8},{16,12},{20,16},{24,20},{28,24},{32,28},{36,32}... | collective-permute-start | bytes 786440 | tf_op jit(solution)/shard_map/ppermute | solution.py:34
  26.8 15.5 %collective-permute-start.2 = (bf16[4,64,512]{2,1,0:T(8,128)(2,1)S(1)}, bf16[4,64,512]{2,1,0:T(8,128)(2,1)S(1)}, u32[]{:S(2)}, u32[]{:S(2)}) collective-permute-start(bf16[4,64,512]{2,1,0:T(8,128)(2,1)S(1)} %all-to-all-done.1.plane), channel_id=1, source_target_pairs={{0,4},{4,8},{8,12},{12,16},{16,20},{20,24},{24,28},{28,32},{32,36}... | collective-permute-start | bytes 786440 | tf_op jit(solution)/shard_map/ppermute | solution.py:34
  36.7 7.6 %collective-permute-start.4 = (bf16[10,64,512]{2,1,0:T(8,128)(2,1)}, bf16[10,64,512]{2,1,0:T(8,128)(2,1)}, u32[]{:S(2)}, u32[]{:S(2)}) collective-permute-start(bf16[10,64,512]{2,1,0:T(8,128)(2,1)} %pad_maximum_fusion), channel_id=1, source_target_pairs={{0,64},{64,0},{1,65},{65,1},{2,66},{66,2},{3,67},{67,3},{4,68},{68... | collective-permute-start | bytes 1966088 | tf_op jit(solution)/shard_map/ppermute | solution.py:38
  42.3 3.8 %collective-permute-start.5 = (bf16[8,64,512]{2,1,0:T(8,128)(2,1)S(1)}, bf16[8,64,512]{2,1,0:T(8,128)(2,1)S(1)}, u32[]{:S(2)}, u32[]{:S(2)}) collective-permute-start(bf16[8,64,512]{2,1,0:T(8,128)(2,1)S(1)} %pad_maximum_fusion.1), channel_id=1, source_target_pairs={{0,64},{64,0},{1,65},{65,1},{2,66},{66,2},{3,67},{67,3},{4,68},{68... | collective-permute-start | bytes 1572872 | tf_op jit(solution)/shard_map/ppermute | solution.py:38
  48.5 15.9 %collective-permute-start.6 = (bf16[256,1024]{1,0:T(8,128)(2,1)S(1)}, bf16[256,1024]{1,0:T(8,128)(2,1)S(1)}, u32[]{:S(2)}, u32[]{:S(2)}) collective-permute-start(bf16[256,1024]{1,0:T(8,128)(2,1)S(1)} %make_half.1.own), channel_id=1, source_target_pairs={{0,4},{4,8},{8,12},{12,16},{16,20},{20,24},{24,28},{28,32},{32,36}... | collective-permute-start | bytes 1572872 | tf_op jit(solution)/shard_map/ppermute | solution.py:34
  52.8 16.8 %collective-permute-start.9 = (bf16[256,1024]{1,0:T(8,128)(2,1)S(1)}, bf16[256,1024]{1,0:T(8,128)(2,1)S(1)}, u32[]{:S(2)}, u32[]{:S(2)}) collective-permute-start(bf16[256,1024]{1,0:T(8,128)(2,1)S(1)} %make_half.1.own), channel_id=1, source_target_pairs={{4,0},{8,4},{12,8},{16,12},{20,16},{24,20},{28,24},{32,28},{36,32}... | collective-permute-start | bytes 1572872 | tf_op jit(solution)/shard_map/ppermute | solution.py:34
  54.7 16.8 %collective-permute-start.8 = (bf16[256,1024]{1,0:T(8,128)(2,1)S(1)}, bf16[256,1024]{1,0:T(8,128)(2,1)S(1)}, u32[]{:S(2)}, u32[]{:S(2)}) collective-permute-start(bf16[256,1024]{1,0:T(8,128)(2,1)S(1)} %make_half.1.own), channel_id=1, source_target_pairs={{0,64},{64,0},{1,65},{65,1},{2,66},{66,2},{3,67},{67,3},{4,68},{68... | collective-permute-start | bytes 1572872 | tf_op jit(solution)/shard_map/ppermute | solution.py:38
  64.4 7.1 %collective-permute-start.7 = (bf16[256,1024]{1,0:T(8,128)(2,1)S(1)}, bf16[256,1024]{1,0:T(8,128)(2,1)S(1)}, u32[]{:S(2)}, u32[]{:S(2)}) collective-permute-start(bf16[256,1024]{1,0:T(8,128)(2,1)S(1)} %collective-permute-done.6.up), channel_id=1, source_target_pairs={{0,64},{64,0},{1,65},{65,1},{2,66},{66,2},{3,67},{67,3},{4,68},{68... | collective-permute-start | bytes 1572872 | tf_op jit(solution)/shard_map/ppermute | solution.py:38
  69.6 3.8 %collective-permute-start.10 = (bf16[256,1024]{1,0:T(8,128)(2,1)S(1)}, bf16[256,1024]{1,0:T(8,128)(2,1)S(1)}, u32[]{:S(2)}, u32[]{:S(2)}) collective-permute-start(bf16[256,1024]{1,0:T(8,128)(2,1)S(1)} %collective-permute-done.9.down), channel_id=1, source_target_pairs={{0,64},{64,0},{1,65},{65,1},{2,66},{66,2},{3,67},{67,3},{4,68},{68... | collective-permute-start | bytes 1572872 | tf_op jit(solution)/shard_map/ppermute | solution.py:38
  74.9 29.4 %copy-start.4 = (s32[1,15]{1,0:T(1,128)S(1)}, s32[1,15]{1,0:T(1,128)}, u32[]{:S(2)}) copy-start(s32[1,15]{1,0:T(1,128)} %mask.1) | copy-start | bytes 184
  98.4 5.9 %collective-permute-start.11 = (f32[3,16,128]{2,1,0:T(8,128)S(1)}, f32[3,16,128]{2,1,0:T(8,128)S(1)}, u32[]{:S(2)}, u32[]{:S(2)}) collective-permute-start(f32[3,16,128]{2,1,0:T(8,128)S(1)} %slice.18), channel_id=1, source_target_pairs={{0,4},{4,8},{8,12},{12,16},{16,20},{20,24},{24,28},{28,32},{32,36}... | collective-permute-start | bytes 73736 | tf_op jit(solution)/shard_map/ppermute | solution.py:34
  101.6 6.9 %collective-permute-start.12 = (f32[3,16,128]{2,1,0:T(8,128)S(1)}, f32[3,16,128]{2,1,0:T(8,128)S(1)}, u32[]{:S(2)}, u32[]{:S(2)}) collective-permute-start(f32[3,16,128]{2,1,0:T(8,128)S(1)} %slice.18), channel_id=1, source_target_pairs={{4,0},{8,4},{12,8},{16,12},{20,16},{24,20},{28,24},{32,28},{36,32}... | collective-permute-start | bytes 73736 | tf_op jit(solution)/shard_map/ppermute | solution.py:34

commit v15 on v10

--- a/solution.py
+++ b/solution.py
@@ -102,16 +102,23 @@
         wide[pl.ds(pl.multiple_of(to + 16 - c * 16, 16), 16), :] = other[rows, :]
 
 
-def tile_kernel(core, up, own, down, up2, own2, down2, out, wide):
-    for i, (mine, other) in enumerate(((up, up2), (own, own2), (down, down2))):
-        interleave(core[0], mine, other, wide, i * 512)
-    for i in range(3):
+def near_kernel(core, up, own, up2, own2, out, wide):
+    interleave(core[0], up, up2, wide, 0)
+    interleave(core[0], own, own2, wide, 512)
+    for i in range(2):
         out[:, i * 512 : (i + 1) * 512] = dot_t(own[...], wide[i * 512 : (i + 1) * 512, :]).astype(BF16)
+
+
+def tile_kernel(core, near, up, own, down, up2, down2, out, wide):
+    interleave(core[0], up, up2, wide, 0)
+    interleave(core[0], down, down2, wide, 512)
+    out[:, :1024] = near[...]
+    out[:, 1024:1536] = dot_t(own[...], wide[512:1024, :]).astype(BF16)
     for x in range(4):
         rows = slice(x * HALF, (x + 1) * HALF)
         cut = 1536 + x * ROWS
         if x > 0:
-            out[rows, 1536:cut] = dot_t(up[rows, :], wide[1024 : 1024 + x * ROWS, :]).astype(BF16)
+            out[rows, 1536:cut] = dot_t(up[rows, :], wide[512 : 512 + x * ROWS, :]).astype(BF16)
         if x < 3:
             out[rows, cut:] = dot_t(down[rows, :], wide[(x + 1) * ROWS : 512, :]).astype(BF16)
 
@@ -160,10 +167,15 @@
     up = moved(own, 1)
     down = moved(own, -1)
     own2 = swapped(own)
+    up2 = swapped(up)
+    near = call(
+        near_kernel, "make_near", [SMEM] + [VMEM] * 4, (256, 1024), BF16, core, up, own, up2, own2,
+        scratch=[pltpu.VMEM((1024, 2 * COLS), BF16)],
+    )
     partial = call(
         tile_kernel, "make_tiles", [SMEM] + [VMEM] * 6, (256, SPAN * ROWS), BF16,
-        core, up, own, down, swapped(up), own2, swapped(down),
-        scratch=[pltpu.VMEM((1536, 2 * COLS), BF16)],
+        core, near, up, own, down, up2, swapped(down),
+        scratch=[pltpu.VMEM((1024, 2 * COLS), BF16)],
     )
     partial = lax.all_to_all(partial.reshape(16, 16, SPAN * ROWS), ("x", "y"), 0, 0)
     total = call(sum_kernel, "sum_parts", [VMEM], (SPAN, 16, ROWS), F32, partial)

time: 112 us -> 112 us (level)
  waiting for transfers between devices: 28.1 us -> 30 us
  starting transfers between devices: 47.1 us -> 45.5 us
    ppermute x8, waiting for transfers between devices: 21.8 us -> 24.3 us  [moved(): lax.ppermute(x, 'z', [(i, i + by) for i in range(n) if 0 <= i + by < n])]
    pallas_call x6 -> x7, Pallas kernels: 8.1 us -> 8.36 us  [call(): pl.pallas_call(kernel, in_specs=specs, out_specs=out, out_shape=jax.Shape...]
  transfers between devices with their start and end apart: 15 -> 15, of which waited for: 8 -> 9; matrix products, arithmetic and copies ran while one was open for 0% -> 0% of each run, Pallas kernels for 2% -> 3%
where the time goes in v15:
time: 112 us; the launch traced here: 111 us
  starting transfers between devices  45.5 us (41%)
  waiting for transfers between devices  30 us (27%)
  blocking collectives  23.7 us (21%)
  Pallas kernels  8.36 us (7%)
  local copies, waits for them, and re-layouts  2.77 us (2%)
    ppermute x8, starting transfers between devices, moved(): lax.ppermute(x, 'z', [(i, i + by) for i in range(n) if 0 <= i + by < n])  27.3 us
    ppermute x8, waiting for transfers between devices, moved(): lax.ppermute(x, 'z', [(i, i + by) for i in range(n) if 0 <= i + by < n])  24.3 us
    all_to_all x1, blocking collectives, per_device(): lax.all_to_all(partial.reshape(16, 16, SPAN * ROWS), ('x', 'y'), 0, 0)  23.7 us
    ppermute x5, starting transfers between devices, swapped(): return lax.ppermute(x, 'core', [(0, 1), (1, 0)])  9.58 us
    pallas_call x7, Pallas kernels, call(): pl.pallas_call(kernel, in_specs=specs, out_specs=out, out_shape=jax.Shape...  8.36 us
    all_to_all x1, starting transfers between devices, per_device(): lax.all_to_all(tiles.reshape(8, SPAN, HALF, ROWS), ('x', 'core'), 0, 0)  4.32 us
    all_to_all x1, starting transfers between devices, per_device(): plane = lax.all_to_all(pieces, 'x', 0, 0)  4.3 us
    all_to_all x1, waiting for transfers between devices, per_device(): plane = lax.all_to_all(pieces, 'x', 0, 0)  2.91 us
  transfers between devices with their start and end apart: 15, of which 9 were waited for; matrix products, arithmetic and copies ran while one was open for 0% of the time, Pallas kernels for 3%

profile of v15, /device:TPU:96, one launch (start us, length us, event | category | flops | bytes accessed | tf_op | source)
XLA Modules:
  0.0 111.5 jit_solution(7811030469619900587)
XLA Ops:
  0.0 1.0 copy-done
  1.8 4.3 %all-to-all-start.1 = ((bf16[4,64,512]{2,1,0:T(8,128)(2,1)}), bf16[4,64,512]{2,1,0:T(8,128)(2,1)S(1)}, u32[]{:S(2)}, u32[]{:S(2)}) async-start(bf16[4,64,512]{2,1,0:T(8,128)(2,1)} %cut_orbitals.1), calls=%async_computation.1 | async-start | bytes 524288 | tf_op jit(solution)/shard_map/all_to_all | solution.py:143
  6.1 1.0 copy-done.1
  7.8 2.1 %cut_integrals.1 = bf16[4,2,15,64,128]{4,3,2,1,0:T(8,128)(2,1)} custom-call(s32[1,15]{1,0:T(1,128)S(1)} %copy-done.2, bf16[15,128,128]{2,1,0:T(8,128)(2,1)S(1)} %bitcast.9), custom_call_target="tpu_custom_call" | custom-call | tf_op jit(solution)/shard_map/cut_integrals/pallas_call | solution.py:21
  9.9 2.9 %all-to-all-done.1.plane = bf16[4,64,512]{2,1,0:T(8,128)(2,1)S(1)} async-done(((bf16[4,64,512]{2,1,0:T(8,128)(2,1)}), bf16[4,64,512]{2,1,0:T(8,128)(2,1)S(1)}, u32[]{:S(2)}, u32[]{:S(2)}) %all-to-all-start.1) | async-done | bytes 262176 | tf_op jit(solution)/shard_map/all_to_all | solution.py:143
  12.8 4.3 %all-to-all-start = ((bf16[8,15,64,128]{3,2,1,0:T(8,128)(2,1)}), bf16[8,15,64,128]{3,2,1,0:T(8,128)(2,1)}, u32[]{:S(2)}, u32[]{:S(2)}) async-start(bf16[8,15,64,128]{3,2,1,0:T(8,128)(2,1)} %bitcast.2), calls=%async_computation | async-start | bytes 3932160 | tf_op jit(solution)/shard_map/all_to_all | solution.py:149
  17.1 6.4 %collective-permute-start = (bf16[3,64,512]{2,1,0:T(8,128)(2,1)S(1)}, bf16[3,64,512]{2,1,0:T(8,128)(2,1)S(1)}, u32[]{:S(2)}, u32[]{:S(2)}) collective-permute-start(bf16[3,64,512]{2,1,0:T(8,128)(2,1)S(1)} %get-tuple-element.6), channel_id=1, source_target_pairs={{0,8},{4,12},{8,16},{12,20},{16,24},{20,28},{24,32},{28,36},{32,40... | collective-permute-start | bytes 589832 | tf_op jit(solution)/shard_map/ppermute | solution.py:34
  23.5 1.9 %collective-permute-start.3 = (bf16[3,64,512]{2,1,0:T(8,128)(2,1)S(1)}, bf16[3,64,512]{2,1,0:T(8,128)(2,1)S(1)}, u32[]{:S(2)}, u32[]{:S(2)}) collective-permute-start(bf16[3,64,512]{2,1,0:T(8,128)(2,1)S(1)} %get-tuple-element.5), channel_id=1, source_target_pairs={{8,0},{12,4},{16,8},{20,12},{24,16},{28,20},{32,24},{36,28},{40,32... | collective-permute-start | bytes 589832 | tf_op jit(solution)/shard_map/ppermute | solution.py:34
  25.5 4.7 %collective-permute-start.1 = (bf16[4,64,512]{2,1,0:T(8,128)(2,1)S(1)}, bf16[4,64,512]{2,1,0:T(8,128)(2,1)S(1)}, u32[]{:S(2)}, u32[]{:S(2)}) collective-permute-start(bf16[4,64,512]{2,1,0:T(8,128)(2,1)S(1)} %all-to-all-done.1.plane), channel_id=1, source_target_pairs={{0,4},{4,8},{8,12},{12,16},{16,20},{20,24},{24,28},{28,32},{32,36}... | collective-permute-start | bytes 786440 | tf_op jit(solution)/shard_map/ppermute | solution.py:34
  30.2 1.9 %collective-permute-start.2 = (bf16[4,64,512]{2,1,0:T(8,128)(2,1)S(1)}, bf16[4,64,512]{2,1,0:T(8,128)(2,1)S(1)}, u32[]{:S(2)}, u32[]{:S(2)}) collective-permute-start(bf16[4,64,512]{2,1,0:T(8,128)(2,1)S(1)} %all-to-all-done.1.plane), channel_id=1, source_target_pairs={{4,0},{8,4},{12,8},{16,12},{20,16},{24,20},{28,24},{32,28},{36,32}... | collective-permute-start | bytes 786440 | tf_op jit(solution)/shard_map/ppermute | solution.py:34
  32.1 2.9 %collective-permute-done.3.above2 = bf16[3,64,512]{2,1,0:T(8,128)(2,1)S(1)} collective-permute-done((bf16[3,64,512]{2,1,0:T(8,128)(2,1)S(1)}, bf16[3,64,512]{2,1,0:T(8,128)(2,1)S(1)}, u32[]{:S(2)}, u32[]{:S(2)}) %collective-permute-start.3) | collective-permute-done | bytes 196640 | tf_op jit(solution)/shard_map/ppermute | solution.py:34
  35.1 1.9 %collective-permute-start.4 = (bf16[10,64,512]{2,1,0:T(8,128)(2,1)S(1)}, bf16[10,64,512]{2,1,0:T(8,128)(2,1)S(1)}, u32[]{:S(2)}, u32[]{:S(2)}) collective-permute-start(bf16[10,64,512]{2,1,0:T(8,128)(2,1)S(1)} %pad_maximum_fusion), channel_id=1, source_target_pairs={{0,64},{64,0},{1,65},{65,1},{2,66},{66,2},{3,67},{67,3},{4,68},{68... | collective-permute-start | bytes 1966088 | tf_op jit(solution)/shard_map/ppermute | solution.py:38
  37.0 1.1 collective-permute-done.1.below
  38.1 4.8 %collective-permute-done.2.above = bf16[4,64,512]{2,1,0:T(8,128)(2,1)S(1)} collective-permute-done((bf16[4,64,512]{2,1,0:T(8,128)(2,1)S(1)}, bf16[4,64,512]{2,1,0:T(8,128)(2,1)S(1)}, u32[]{:S(2)}, u32[]{:S(2)}) %collective-permute-start.2) | collective-permute-done | bytes 262176 | tf_op jit(solution)/shard_map/ppermute | solution.py:34
  43.0 1.9 %collective-permute-start.5 = (bf16[8,64,512]{2,1,0:T(8,128)(2,1)S(1)}, bf16[8,64,512]{2,1,0:T(8,128)(2,1)S(1)}, u32[]{:S(2)}, u32[]{:S(2)}) collective-permute-start(bf16[8,64,512]{2,1,0:T(8,128)(2,1)S(1)} %pad_maximum_fusion.1), channel_id=1, source_target_pairs={{0,64},{64,0},{1,65},{65,1},{2,66},{66,2},{3,67},{67,3},{4,68},{68... | collective-permute-start | bytes 1572872 | tf_op jit(solution)/shard_map/ppermute | solution.py:38
  44.9 1.9 %collective-permute-done.5.second = bf16[8,64,512]{2,1,0:T(8,128)(2,1)S(1)} collective-permute-done((bf16[8,64,512]{2,1,0:T(8,128)(2,1)S(1)}, bf16[8,64,512]{2,1,0:T(8,128)(2,1)S(1)}, u32[]{:S(2)}, u32[]{:S(2)}) %collective-permute-start.5) | collective-permute-done | bytes 524320 | tf_op jit(solution)/shard_map/ppermute | solution.py:38
  46.9 2.9 %make_half.1.own = bf16[256,1024]{1,0:T(8,128)(2,1)S(1)} custom-call(bf16[8,15,64,128]{3,2,1,0:T(8,128)(2,1)} %all-to-all-done.gathered, bf16[18,2,64,512]{3,2,1,0:T(8,128)(2,1)S(1)} %place_orbitals.1.window), custom_call_target="tpu_custom_call" | custom-call | tf_op jit(solution)/shard_map/make_half/pallas_call | solution.py:21
  49.8 4.6 %collective-permute-start.6 = (bf16[256,1024]{1,0:T(8,128)(2,1)S(1)}, bf16[256,1024]{1,0:T(8,128)(2,1)S(1)}, u32[]{:S(2)}, u32[]{:S(2)}) collective-permute-start(bf16[256,1024]{1,0:T(8,128)(2,1)S(1)} %make_half.1.own), channel_id=1, source_target_pairs={{0,4},{4,8},{8,12},{12,16},{16,20},{20,24},{24,28},{28,32},{32,36}... | collective-permute-start | bytes 1572872 | tf_op jit(solution)/shard_map/ppermute | solution.py:34
  54.4 1.9 %collective-permute-start.9 = (bf16[256,1024]{1,0:T(8,128)(2,1)S(1)}, bf16[256,1024]{1,0:T(8,128)(2,1)S(1)}, u32[]{:S(2)}, u32[]{:S(2)}) collective-permute-start(bf16[256,1024]{1,0:T(8,128)(2,1)S(1)} %make_half.1.own), channel_id=1, source_target_pairs={{4,0},{8,4},{12,8},{16,12},{20,16},{24,20},{28,24},{32,28},{36,32}... | collective-permute-start | bytes 1572872 | tf_op jit(solution)/shard_map/ppermute | solution.py:34
  56.3 1.9 %collective-permute-start.8 = (bf16[256,1024]{1,0:T(8,128)(2,1)S(1)}, bf16[256,1024]{1,0:T(8,128)(2,1)S(1)}, u32[]{:S(2)}, u32[]{:S(2)}) collective-permute-start(bf16[256,1024]{1,0:T(8,128)(2,1)S(1)} %make_half.1.own), channel_id=1, source_target_pairs={{0,64},{64,0},{1,65},{65,1},{2,66},{66,2},{3,67},{67,3},{4,68},{68... | collective-permute-start | bytes 1572872 | tf_op jit(solution)/shard_map/ppermute | solution.py:38
  58.3 7.6 %collective-permute-done.6.up = bf16[256,1024]{1,0:T(8,128)(2,1)S(1)} collective-permute-done((bf16[256,1024]{1,0:T(8,128)(2,1)S(1)}, bf16[256,1024]{1,0:T(8,128)(2,1)S(1)}, u32[]{:S(2)}, u32[]{:S(2)}) %collective-permute-start.6) | collective-permute-done | bytes 524320 | tf_op jit(solution)/shard_map/ppermute | solution.py:34
  65.9 1.9 %collective-permute-start.7 = (bf16[256,1024]{1,0:T(8,128)(2,1)S(1)}, bf16[256,1024]{1,0:T(8,128)(2,1)S(1)}, u32[]{:S(2)}, u32[]{:S(2)}) collective-permute-start(bf16[256,1024]{1,0:T(8,128)(2,1)S(1)} %collective-permute-done.6.up), channel_id=1, source_target_pairs={{0,64},{64,0},{1,65},{65,1},{2,66},{66,2},{3,67},{67,3},{4,68},{68... | collective-permute-start | bytes 1572872 | tf_op jit(solution)/shard_map/ppermute | solution.py:38
  67.8 3.4 %collective-permute-done.9.down = bf16[256,1024]{1,0:T(8,128)(2,1)S(1)} collective-permute-done((bf16[256,1024]{1,0:T(8,128)(2,1)S(1)}, bf16[256,1024]{1,0:T(8,128)(2,1)S(1)}, u32[]{:S(2)}, u32[]{:S(2)}) %collective-permute-start.9) | collective-permute-done | bytes 524320 | tf_op jit(solution)/shard_map/ppermute | solution.py:34
  71.2 1.9 %collective-permute-start.10 = (bf16[256,1024]{1,0:T(8,128)(2,1)S(1)}, bf16[256,1024]{1,0:T(8,128)(2,1)S(1)}, u32[]{:S(2)}, u32[]{:S(2)}) collective-permute-start(bf16[256,1024]{1,0:T(8,128)(2,1)S(1)} %collective-permute-done.9.down), channel_id=1, source_target_pairs={{0,64},{64,0},{1,65},{65,1},{2,66},{66,2},{3,67},{67,3},{4,68},{68... | collective-permute-start | bytes 1572872 | tf_op jit(solution)/shard_map/ppermute | solution.py:38
  73.1 0.9 make_near.1.near
  74.0 1.0 collective-permute-done.10.down2
  75.0 1.5 %make_tiles.1 = bf16[256,1920]{1,0:T(8,128)(2,1)S(1)} custom-call(s32[1]{0:T(128)} %bitcast.core, bf16[256,1024]{1,0:T(8,128)(2,1)S(1)} %make_near.1.near, bf16[256,1024]{1,0:T(8,128)(2,1)S(1)} %collective-permute-done.6.up, bf16[256,1024]{1,0:T(8,128)(2,1)S(1)} %make_half.1.own, bf16[256,1024]{1,0:T(8,128)(2,1)S(1)} %collective-permute-done.9.down, ...), custom_call_target="tpu_custom_call" | custom-call | tf_op jit(solution)/shard_map/make_tiles/pallas_call | solution.py:21
  76.5 23.7 %all_to_all.15.parts = bf16[16,16,1920]{2,1,0:T(8,128)(2,1)S(1)} all-to-all(bf16[16,16,1920]{2,1,0:T(8,128)(2,1)S(1)} %bitcast.8), channel_id=1, replica_groups=mesh['y'=4,'core'=2,'z'=16,'x'=4] {'x','y'}, dimensions={0} | all-to-all | bytes 1966080 | tf_op jit(solution)/shard_map/all_to_all | solution.py:180
  100.4 3.4 %collective-permute-start.11 = (f32[3,16,128]{2,1,0:T(8,128)S(1)}, f32[3,16,128]{2,1,0:T(8,128)S(1)}, u32[]{:S(2)}, u32[]{:S(2)}) collective-permute-start(f32[3,16,128]{2,1,0:T(8,128)S(1)} %slice.18), channel_id=1, source_target_pairs={{0,4},{4,8},{8,12},{12,16},{16,20},{20,24},{24,28},{28,32},{32,36}... | collective-permute-start | bytes 73736 | tf_op jit(solution)/shard_map/ppermute | solution.py:34
  103.8 2.4 %collective-permute-start.12 = (f32[3,16,128]{2,1,0:T(8,128)S(1)}, f32[3,16,128]{2,1,0:T(8,128)S(1)}, u32[]{:S(2)}, u32[]{:S(2)}) collective-permute-start(f32[3,16,128]{2,1,0:T(8,128)S(1)} %slice.18), channel_id=1, source_target_pairs={{4,0},{8,4},{12,8},{16,12},{20,16},{24,20},{28,24},{32,28},{36,32}... | collective-permute-start | bytes 73736 | tf_op jit(solution)/shard_map/ppermute | solution.py:34
  106.3 4.5 %collective-permute-done.12 = f32[3,16,128]{2,1,0:T(8,128)S(1)} collective-permute-done((f32[3,16,128]{2,1,0:T(8,128)S(1)}, f32[3,16,128]{2,1,0:T(8,128)S(1)}, u32[]{:S(2)}, u32[]{:S(2)}) %collective-permute-start.12) | collective-permute-done | bytes 24608 | tf_op jit(solution)/shard_map/ppermute | solution.py:34
  110.7 0.7 fusion.3
  (21 shorter events, 1.9 us)
Async XLA Ops:
  0.0 1.0 copy-start
  1.8 11.0 %all-to-all-start.1 = ((bf16[4,64,512]{2,1,0:T(8,128)(2,1)}), bf16[4,64,512]{2,1,0:T(8,128)(2,1)S(1)}, u32[]{:S(2)}, u32[]{:S(2)}) async-start(bf16[4,64,512]{2,1,0:T(8,128)(2,1)} %cut_orbitals.1), calls=%async_computation.1 | async-start | bytes 524288 | tf_op jit(solution)/shard_map/all_to_all | solution.py:143
  6.1 1.0 copy-start.1
  7.1 0.7 copy-start.2
  12.8 34.2 %all-to-all-start = ((bf16[8,15,64,128]{3,2,1,0:T(8,128)(2,1)}), bf16[8,15,64,128]{3,2,1,0:T(8,128)(2,1)}, u32[]{:S(2)}, u32[]{:S(2)}) async-start(bf16[8,15,64,128]{3,2,1,0:T(8,128)(2,1)} %bitcast.2), calls=%async_computation | async-start | bytes 3932160 | tf_op jit(solution)/shard_map/all_to_all | solution.py:149
  17.1 15.0 %collective-permute-start = (bf16[3,64,512]{2,1,0:T(8,128)(2,1)S(1)}, bf16[3,64,512]{2,1,0:T(8,128)(2,1)S(1)}, u32[]{:S(2)}, u32[]{:S(2)}) collective-permute-start(bf16[3,64,512]{2,1,0:T(8,128)(2,1)S(1)} %get-tuple-element.6), channel_id=1, source_target_pairs={{0,8},{4,12},{8,16},{12,20},{16,24},{20,28},{24,32},{28,36},{32,40... | collective-permute-start | bytes 589832 | tf_op jit(solution)/shard_map/ppermute | solution.py:34
  23.5 11.5 %collective-permute-start.3 = (bf16[3,64,512]{2,1,0:T(8,128)(2,1)S(1)}, bf16[3,64,512]{2,1,0:T(8,128)(2,1)S(1)}, u32[]{:S(2)}, u32[]{:S(2)}) collective-permute-start(bf16[3,64,512]{2,1,0:T(8,128)(2,1)S(1)} %get-tuple-element.5), channel_id=1, source_target_pairs={{8,0},{12,4},{16,8},{20,12},{24,16},{28,20},{32,24},{36,28},{40,32... | collective-permute-start | bytes 589832 | tf_op jit(solution)/shard_map/ppermute | solution.py:34
  25.5 12.7 %collective-permute-start.1 = (bf16[4,64,512]{2,1,0:T(8,128)(2,1)S(1)}, bf16[4,64,512]{2,1,0:T(8,128)(2,1)S(1)}, u32[]{:S(2)}, u32[]{:S(2)}) collective-permute-start(bf16[4,64,512]{2,1,0:T(8,128)(2,1)S(1)} %all-to-all-done.1.plane), channel_id=1, source_target_pairs={{0,4},{4,8},{8,12},{12,16},{16,20},{20,24},{24,28},{28,32},{32,36}... | collective-permute-start | bytes 786440 | tf_op jit(solution)/shard_map/ppermute | solution.py:34
  30.2 12.8 %collective-permute-start.2 = (bf16[4,64,512]{2,1,0:T(8,128)(2,1)S(1)}, bf16[4,64,512]{2,1,0:T(8,128)(2,1)S(1)}, u32[]{:S(2)}, u32[]{:S(2)}) collective-permute-start(bf16[4,64,512]{2,1,0:T(8,128)(2,1)S(1)} %all-to-all-done.1.plane), channel_id=1, source_target_pairs={{4,0},{8,4},{12,8},{16,12},{20,16},{24,20},{28,24},{32,28},{36,32}... | collective-permute-start | bytes 786440 | tf_op jit(solution)/shard_map/ppermute | solution.py:34
  35.1 11.7 %collective-permute-start.4 = (bf16[10,64,512]{2,1,0:T(8,128)(2,1)S(1)}, bf16[10,64,512]{2,1,0:T(8,128)(2,1)S(1)}, u32[]{:S(2)}, u32[]{:S(2)}) collective-permute-start(bf16[10,64,512]{2,1,0:T(8,128)(2,1)S(1)} %pad_maximum_fusion), channel_id=1, source_target_pairs={{0,64},{64,0},{1,65},{65,1},{2,66},{66,2},{3,67},{67,3},{4,68},{68... | collective-permute-start | bytes 1966088 | tf_op jit(solution)/shard_map/ppermute | solution.py:38
  43.0 3.8 %collective-permute-start.5 = (bf16[8,64,512]{2,1,0:T(8,128)(2,1)S(1)}, bf16[8,64,512]{2,1,0:T(8,128)(2,1)S(1)}, u32[]{:S(2)}, u32[]{:S(2)}) collective-permute-start(bf16[8,64,512]{2,1,0:T(8,128)(2,1)S(1)} %pad_maximum_fusion.1), channel_id=1, source_target_pairs={{0,64},{64,0},{1,65},{65,1},{2,66},{66,2},{3,67},{67,3},{4,68},{68... | collective-permute-start | bytes 1572872 | tf_op jit(solution)/shard_map/ppermute | solution.py:38
  49.8 16.0 %collective-permute-start.6 = (bf16[256,1024]{1,0:T(8,128)(2,1)S(1)}, bf16[256,1024]{1,0:T(8,128)(2,1)S(1)}, u32[]{:S(2)}, u32[]{:S(2)}) collective-permute-start(bf16[256,1024]{1,0:T(8,128)(2,1)S(1)} %make_half.1.own), channel_id=1, source_target_pairs={{0,4},{4,8},{8,12},{12,16},{16,20},{20,24},{24,28},{28,32},{32,36}... | collective-permute-start | bytes 1572872 | tf_op jit(solution)/shard_map/ppermute | solution.py:34
  54.4 16.8 %collective-permute-start.9 = (bf16[256,1024]{1,0:T(8,128)(2,1)S(1)}, bf16[256,1024]{1,0:T(8,128)(2,1)S(1)}, u32[]{:S(2)}, u32[]{:S(2)}) collective-permute-start(bf16[256,1024]{1,0:T(8,128)(2,1)S(1)} %make_half.1.own), channel_id=1, source_target_pairs={{4,0},{8,4},{12,8},{16,12},{20,16},{24,20},{28,24},{32,28},{36,32}... | collective-permute-start | bytes 1572872 | tf_op jit(solution)/shard_map/ppermute | solution.py:34
  56.3 16.8 %collective-permute-start.8 = (bf16[256,1024]{1,0:T(8,128)(2,1)S(1)}, bf16[256,1024]{1,0:T(8,128)(2,1)S(1)}, u32[]{:S(2)}, u32[]{:S(2)}) collective-permute-start(bf16[256,1024]{1,0:T(8,128)(2,1)S(1)} %make_half.1.own), channel_id=1, source_target_pairs={{0,64},{64,0},{1,65},{65,1},{2,66},{66,2},{3,67},{67,3},{4,68},{68... | collective-permute-start | bytes 1572872 | tf_op jit(solution)/shard_map/ppermute | solution.py:38
  65.9 7.3 %collective-permute-start.7 = (bf16[256,1024]{1,0:T(8,128)(2,1)S(1)}, bf16[256,1024]{1,0:T(8,128)(2,1)S(1)}, u32[]{:S(2)}, u32[]{:S(2)}) collective-permute-start(bf16[256,1024]{1,0:T(8,128)(2,1)S(1)} %collective-permute-done.6.up), channel_id=1, source_target_pairs={{0,64},{64,0},{1,65},{65,1},{2,66},{66,2},{3,67},{67,3},{4,68},{68... | collective-permute-start | bytes 1572872 | tf_op jit(solution)/shard_map/ppermute | solution.py:38
  71.2 3.8 %collective-permute-start.10 = (bf16[256,1024]{1,0:T(8,128)(2,1)S(1)}, bf16[256,1024]{1,0:T(8,128)(2,1)S(1)}, u32[]{:S(2)}, u32[]{:S(2)}) collective-permute-start(bf16[256,1024]{1,0:T(8,128)(2,1)S(1)} %collective-permute-done.9.down), channel_id=1, source_target_pairs={{0,64},{64,0},{1,65},{65,1},{2,66},{66,2},{3,67},{67,3},{4,68},{68... | collective-permute-start | bytes 1572872 | tf_op jit(solution)/shard_map/ppermute | solution.py:38
  76.5 29.7 %copy-start.3 = (s32[1,15]{1,0:T(1,128)S(1)}, s32[1,15]{1,0:T(1,128)}, u32[]{:S(2)}) copy-start(s32[1,15]{1,0:T(1,128)} %mask.1) | copy-start | bytes 184
  100.4 5.9 %collective-permute-start.11 = (f32[3,16,128]{2,1,0:T(8,128)S(1)}, f32[3,16,128]{2,1,0:T(8,128)S(1)}, u32[]{:S(2)}, u32[]{:S(2)}) collective-permute-start(f32[3,16,128]{2,1,0:T(8,128)S(1)} %slice.18), channel_id=1, source_target_pairs={{0,4},{4,8},{8,12},{12,16},{16,20},{20,24},{24,28},{28,32},{32,36}... | collective-permute-start | bytes 73736 | tf_op jit(solution)/shard_map/ppermute | solution.py:34
  103.8 6.9 %collective-permute-start.12 = (f32[3,16,128]{2,1,0:T(8,128)S(1)}, f32[3,16,128]{2,1,0:T(8,128)S(1)}, u32[]{:S(2)}, u32[]{:S(2)}) collective-permute-start(f32[3,16,128]{2,1,0:T(8,128)S(1)} %slice.18), channel_id=1, source_target_pairs={{4,0},{8,4},{12,8},{16,12},{20,16},{24,20},{28,24},{32,28},{36,32}... | collective-permute-start | bytes 73736 | tf_op jit(solution)/shard_map/ppermute | solution.py:34
